TPU v7x, 512 devices: a whole 4x8x8 slice. The times are simulated.
512 devices in a mesh: dp: 8 (over x, z_hi), mp: 64 (over z_lo, y, core).
Axes of the slice: x: 4, y: 8, z: 8 (z_hi: 2, z_lo: 4; z = z_hi * 4 + z_lo), core: 2. Of those that a mesh axis runs over, the one named last changes fastest.
Arguments:
- acts: bfloat16 [2048, 28672], P('dp', 'mp'), may hold values from -6 to 6
- grads: bfloat16 [2048, 8192], P('dp', 'mp'), may hold values from -6 to 6
- basis_in: bfloat16 [3584, 28672], P('mp'), may hold values from -0.03125 to 0.03125
- basis_out: bfloat16 [512, 8192], P('mp'), may hold values from -0.0625 to 0.0625
- doc_lengths: int32 [8, 4], P('dp'), may hold values from 1 to 128, 256 in all within a row
Outputs:
- correction: float32 [512, 3584], P('dp', 'mp')
Inputs may be any that keep to these rules, and one draw needn't show every extreme that they name: `doc_lengths`: each row holds 4 lengths that sum to 256; the largest of each row is exactly 128.
All inputs are finite; a program needn't handle non-finite values.
Results may differ from a plain program's by a relative error of at most 0.0019.
Values may be sent and summed in bfloat16 or wider, within the bound.
No kernel may reach another device: no remote copies, remote signals or barrier semaphores. Data moves between devices by JAX's collectives and lax.ppermute only.
A program may use at most 64 MiB of HBM per device.

v0:
```python
import jax
import jax.numpy as jnp
from jax import lax
from jax.sharding import PartitionSpec as P


def make_masks(lengths, count, dtype):
    starts = jnp.cumsum(lengths, axis=1) - lengths
    ends = starts + lengths
    position = jnp.arange(count, dtype=jnp.int32)
    inside = (position[None, None, :] >= starts[:, :, None]) & (
        position[None, None, :] < ends[:, :, None]
    )
    return inside.astype(dtype)


def doc_squares(grad_rows, act_rows, masks):
    groups, width_in, count = act_rows.shape
    docs = masks.shape[1]
    masked = act_rows[:, None, :, :] * masks[:, :, None, :]
    masked = masked.reshape(groups, docs * width_in, count)
    product = lax.dot_general(
        grad_rows, masked, (((2,), (2,)), ((0,), (0,))), preferred_element_type=jnp.float32
    )
    product = product.reshape(groups, grad_rows.shape[1], docs, width_in)
    return jnp.sum(product * product, axis=(0, 2))


def body(acts, grads, basis_in, basis_out, doc_lengths):
    count = acts.shape[0]
    contract = (((1,), (1,)), ((), ()))
    in_rows = lax.all_to_all(basis_in, "mp", split_axis=1, concat_axis=0, tiled=True)
    out_rows = lax.all_to_all(basis_out, "mp", split_axis=1, concat_axis=0, tiled=True)
    part = in_rows
    act_proj = lax.psum_scatter(
        lax.dot_general(part, acts, contract, preferred_element_type=jnp.float32),
        "mp",
        scatter_dimension=0,
        tiled=True,
    ).astype(jnp.bfloat16)
    part = out_rows
    grad_proj = lax.psum_scatter(
        lax.dot_general(part, grads, contract, preferred_element_type=jnp.float32),
        "mp",
        scatter_dimension=0,
        tiled=True,
    ).astype(jnp.bfloat16)
    grad_whole = lax.all_gather(grad_proj, "mp", axis=0, tiled=True)
    groups = lax.axis_size("dp")
    masks = make_masks(doc_lengths, count, act_proj.dtype)
    local_sum = doc_squares(grad_whole[None], act_proj[None], masks)
    summed = lax.psum_scatter(local_sum, "dp", scatter_dimension=0, tiled=True)
    return summed / jnp.float32(count * groups)


def solution(mesh):
    in_specs = (P("dp", "mp"), P("dp", "mp"), P("mp", None), P("mp", None), P("dp", None))
    out_specs = P("dp", "mp")
    return jax.shard_map(body, mesh=mesh, in_specs=in_specs, out_specs=out_specs, check_vma=False)
```

profile of v0, /device:TPU:1, one launch (start us, length us, event | category | flops | bytes accessed | tf_op | source)
XLA Modules:
  0.0 723.6 jit_solution(5881813522939112463)
XLA Ops:
  6.5 0.0 copy-start
  6.5 14.7 %all-to-all-start = ((bf16[8,64,128]{2,0,1:T(8,128)(2,1)}), bf16[8,64,128]{2,0,1:T(8,128)(2,1)S(1)}, u32[]{:S(2)}, u32[]{:S(2)}) async-start(bf16[8,64,128]{2,0,1:T(8,128)(2,1)} %bitcast.19), calls=%async_computation | async-start | bytes 262144 | tf_op jit(solution)/shard_map/all_to_all | solution.py:33
  21.3 6.7 all_to_all.32
  27.9 5.9 copy.7
  33.9 0.0 copy-start.1
  33.9 0.0 all-to-all-done
  33.9 11.0 %all-to-all-start.1 = ((bf16[56,64,448]{2,0,1:T(8,128)(2,1)}), bf16[56,64,448]{2,0,1:T(8,128)(2,1)}, u32[]{:S(2)}, u32[]{:S(2)}) async-start(bf16[56,64,448]{2,0,1:T(8,128)(2,1)} %copy.7), calls=%async_computation.2 | async-start | bytes 7340032 | tf_op jit(solution)/shard_map/all_to_all | solution.py:32
  44.9 0.0 reduce-scatter.6.cloned.1.call-start
  44.9 0.0 copy-done.1
  44.9 1.0 fusion.2
  46.0 0.0 reduce-scatter.6.cloned.1.call-update
  46.0 0.0 reduce-scatter.8.cloned.1.call-start
  46.0 84.6 %all-to-all-done.1 = bf16[56,64,448]{2,0,1:T(8,128)(2,1)} async-done(((bf16[56,64,448]{2,0,1:T(8,128)(2,1)}), bf16[56,64,448]{2,0,1:T(8,128)(2,1)}, u32[]{:S(2)}, u32[]{:S(2)}) %all-to-all-start.1) | async-done | bytes 3211296 | tf_op jit(solution)/shard_map/all_to_all | solution.py:32
  130.6 0.0 copy-done
  130.6 5.0 fusion.9
  135.6 0.0 copy-start.2
  135.6 0.0 reduce-scatter.8.cloned.1.call-update
  135.7 0.0 reduce-scatter.10.cloned.1.call-start
  135.7 0.6 copy-done.2
  136.3 0.2 reduce_window_sum.11
  136.5 0.1 fusion.8
  136.6 205.8 %reduce-scatter.6.cloned.1.call-done = f32[8,256]{1,0:T(8,128)} async-done(((f32[512,256]{1,0:T(8,128)}), f32[8,256]{1,0:T(8,128)}) %reduce-scatter.6.cloned.1.call-update) | async-done | bytes 8208 | tf_op jit(solution)/shard_map/reduce_scatter | solution.py:42
  342.4 0.7 convert_element_type.15
  343.1 75.3 %all_gather.3 = bf16[512,256]{1,0:T(8,128)(2,1)S(1)} all-gather(bf16[8,256]{1,0:T(8,128)(2,1)S(1)} %convert_element_type.15), channel_id=1, replica_groups=mesh['dp'=8,'mp'=64] {'mp'}, dimensions={0}, use_global_device_ids=true | all-gather | bytes 266240 | tf_op jit(solution)/shard_map/all_gather | solution.py:48
  418.4 206.3 %reduce-scatter.8.cloned.1.call-done = f32[56,256]{1,0:T(8,128)} async-done(((f32[3584,256]{1,0:T(8,128)}), f32[56,256]{1,0:T(8,128)}) %reduce-scatter.8.cloned.1.call-update) | async-done | bytes 57360 | tf_op jit(solution)/shard_map/reduce_scatter | solution.py:35
  624.7 0.8 convert_element_type.16
  625.6 0.3 fusion
  625.8 0.8 copy.8
  626.6 0.0 reduce-scatter.10.cloned.1.call-update
  626.7 89.0 %reduce-scatter.10.cloned.1.call-done = f32[64,56]{1,0:T(8,128)} async-done(((f32[512,56]{1,0:T(8,128)}), f32[64,56]{1,0:T(8,128)}) %reduce-scatter.10.cloned.1.call-update) | async-done | bytes 14352
  715.7 0.8 copy.9
  716.5 0.6 broadcast_multiply_fusion
  (1 shorter events, 0.0 us)
Async XLA Ops:
  6.5 124.1 %copy-start = (bf16[256,448]{0,1:T(8,128)(2,1)S(1)}, bf16[256,448]{0,1:T(8,128)(2,1)}, u32[]{:S(2)}) copy-start(bf16[256,448]{0,1:T(8,128)(2,1)} %param.5) | copy-start | bytes 688132
  6.5 27.3 %all-to-all-start = ((bf16[8,64,128]{2,0,1:T(8,128)(2,1)}), bf16[8,64,128]{2,0,1:T(8,128)(2,1)S(1)}, u32[]{:S(2)}, u32[]{:S(2)}) async-start(bf16[8,64,128]{2,0,1:T(8,128)(2,1)} %bitcast.19), calls=%async_computation | async-start | bytes 262144 | tf_op jit(solution)/shard_map/all_to_all | solution.py:33
  33.9 11.1 %copy-start.1 = (bf16[256,128]{1,0:T(8,128)(2,1)S(1)}, bf16[256,128]{1,0:T(8,128)(2,1)}, u32[]{:S(2)}) copy-start(bf16[256,128]{1,0:T(8,128)(2,1)} %param.6) | copy-start | bytes 196612
  33.9 96.8 %all-to-all-start.1 = ((bf16[56,64,448]{2,0,1:T(8,128)(2,1)}), bf16[56,64,448]{2,0,1:T(8,128)(2,1)}, u32[]{:S(2)}, u32[]{:S(2)}) async-start(bf16[56,64,448]{2,0,1:T(8,128)(2,1)} %copy.7), calls=%async_computation.2 | async-start | bytes 7340032 | tf_op jit(solution)/shard_map/all_to_all | solution.py:32
  44.9 297.5 %reduce-scatter.6.cloned.1.call-start = ((), (), s32[]{:S(2)}) async-start(), calls=%async_computation.5 | async-start | bytes 532480 | tf_op jit(solution)/shard_map/reduce_scatter | solution.py:42
  46.0 578.8 %reduce-scatter.8.cloned.1.call-start = ((), (), s32[]{:S(2)}) async-start(), calls=%async_computation.6 | async-start | bytes 3727360 | tf_op jit(solution)/shard_map/reduce_scatter | solution.py:35
  135.6 0.7 copy-start.2
  135.7 580.0 %reduce-scatter.10.cloned.1.call-start = ((), (), s32[]{:S(2)}) async-start(), calls=%async_computation.7 | async-start | bytes 294912
Sparse Core Ops, SparseCore 0:
  48.5 293.8 reduce-scatter.5
  345.4 279.3 reduce-scatter.7
  629.2 86.4 reduce-scatter.9
where the time goes:
time: 725 us; the launch traced here: 724 us
  waiting for transfers between devices  586 us (81%)
  blocking collectives  75.3 us (10%)
  starting transfers between devices  25.9 us (4%)
  local copies, waits for them, and re-layouts  14.8 us (2%)
  between operations  13.2 us (2%)
    reduce_scatter x1, waiting for transfers between devices, body(): lax.psum_scatter(lax.dot_general(part, acts, contract, preferred_element_...  206 us
    reduce_scatter x1, waiting for transfers between devices, body(): lax.psum_scatter(lax.dot_general(part, grads, contract, preferred_element...  206 us
    unnamed x4, waiting for transfers between devices  89 us
    all_to_all x1, waiting for transfers between devices, body(): lax.all_to_all(basis_in, 'mp', split_axis=1, concat_axis=0, tiled=True)  84.6 us
    all_gather x1, blocking collectives, body(): grad_whole = lax.all_gather(grad_proj, 'mp', axis=0, tiled=True)  75.3 us
    all_to_all x1, starting transfers between devices, body(): lax.all_to_all(basis_out, 'mp', split_axis=1, concat_axis=0, tiled=True)  14.7 us
  transfers between devices with their start and end apart: 5, of which 4 were waited for; matrix products, arithmetic and copies ran while one was open for 2% of the time, Pallas kernels for 0%

commit v1 on v0

v1 whole, which is shorter than its diff:
```python
import functools

import jax
import jax.numpy as jnp
from jax import lax
from jax.experimental import pallas as pl
from jax.experimental.pallas import tpu as pltpu
from jax.sharding import Mesh, PartitionSpec as P

NX, NZH, NZL, NY, NC = 4, 2, 4, 8, 2
CHIPS = NZL * NY
BF16, F32 = jnp.bfloat16, jnp.float32
SMEM = pl.BlockSpec(memory_space=pltpu.SMEM)
VMEM = pl.BlockSpec(memory_space=pltpu.VMEM)


def from_offset(value, axis, size, offset):
    return lax.ppermute(value, axis, [((i + offset) % size, i) for i in range(size)])


def call(kernel, shapes, scratch, operands, flops):
    size = sum(a.size * a.dtype.itemsize for a in operands)
    return pl.pallas_call(
        kernel,
        out_shape=shapes,
        in_specs=[SMEM] + [VMEM] * (len(operands) - 1),
        out_specs=jax.tree.map(lambda _: VMEM, shapes),
        scratch_shapes=scratch,
        compiler_params=pltpu.CompilerParams(vmem_limit_bytes=40 << 20),
        cost_estimate=pl.CostEstimate(flops=flops, bytes_accessed=size, transcendentals=0),
    )(*operands)


def in_vmem(value):
    return pltpu.with_memory_space_constraint(value, pltpu.VMEM)


def in_hbm(shape):
    return pltpu.HBM(shape, BF16)


def project(place, packed_ref, *refs):
    own, other, (parts_ref, acts, grads, wide, low) = refs[:NX], refs[NX : 2 * NX], refs[2 * NX :]
    x, core = place[0], place[2]
    fin = acts.shape[0] // NC
    fout = grads.shape[1]
    tokens, height = acts.shape[1], CHIPS * 16
    for pieces, which in ((own, core), (other, 1 - core)):
        for s in range(NX):
            cols = slice(s * 256, (s + 1) * 256)
            acts[pl.ds(pl.multiple_of(which * fin, 16), fin), cols] = pieces[s][:fin, :]
            grads[which, :, cols] = pieces[s][fin:, :]
    left = packed_ref[:, :, : NC * fin].reshape(height, NC * fin)

    def columns(n, carry):
        cols = pl.ds(pl.multiple_of(n * 256, 256), 256)
        part = jnp.dot(left, acts[:, cols], preferred_element_type=F32)
        for h in range(2):
            wide[pl.ds(pl.multiple_of((n * 2 + h) * height, height), height), :] = part[:, h * 128 : (h + 1) * 128]
        return carry

    lax.fori_loop(0, tokens // 256, columns, 0)
    rows = packed_ref[pl.ds(x * 8, 8), :, NC * fin :].astype(F32).reshape(8, NC, 8, fout)
    part = jnp.zeros((64, tokens), F32)
    for c in range(NC):
        part += jnp.dot(rows[:, c].reshape(64, fout).astype(BF16), grads[c], preferred_element_type=F32)
    rest = part - part.astype(BF16).astype(F32)
    for half in range(2):
        for t in range(8):
            block = slice(half * 32, half * 32 + 32), slice(t * 128, (t + 1) * 128)
            wide[pl.ds(t * height + 14 + half, CHIPS, stride=16), :] = part[block]
            low[pl.ds(half * 8 + t, CHIPS, stride=16), :] = rest[block]
    for t in range(8):
        parts_ref[:, :, t * 128 : (t + 1) * 128] = wide[t * height : (t + 1) * height].astype(BF16).reshape(CHIPS, 16, 128)
    parts_ref[:, :, tokens:] = low[...].astype(BF16).reshape(CHIPS, 16, 128)


def add_up(place, lens_ref, parts_ref, in_ref, out_ref, wide, narrow):
    x = place[0]
    tokens = wide.shape[1]
    total = parts_ref[0].astype(F32)
    for i in range(1, CHIPS):
        total = total + parts_ref[i].astype(F32)
    for s in range(NX):
        source = lax.rem(x + s, NX)
        wide[:, pl.ds(pl.multiple_of(source * 256, 256), 256)] = total[:, s * 256 : (s + 1) * 256]
        for half in range(2):
            for h in range(2):
                col, row = s * 2 + h, half * 8 + s * 2 + h
                value = total[14 + half : 15 + half, col * 128 : (col + 1) * 128] + total[row : row + 1, tokens:]
                narrow[pl.ds(half * 8 + source * 2 + h, 1), :] = value
    wide[14:15, :128] = lens_ref[...]
    in_ref[...] = wide[...].astype(BF16)
    out_ref[...] = jnp.broadcast_to(narrow[...].astype(BF16)[None], out_ref.shape)


def documents(which, place, out_ref, piece0, piece1, piece2, piece3, total_ref, rows_in, rows_out):
    x, zh = place[0], place[1]
    block = lax.rem(zh + which, NZH)
    for s, ref in enumerate((piece0, piece1, piece2, piece3)):
        rows_in[lax.rem(x + s, NX)] = ref[...]
    rows_out[...] = out_ref[...].astype(F32).reshape(64 * 16, 128)
    position = lax.broadcasted_iota(jnp.int32, (1, 256), 1).astype(F32)
    total = jnp.zeros((NX * 16, 64), F32)
    for g in range(NX):
        left = rows_in[:, :, g * 256 : (g + 1) * 256].astype(F32).reshape(NX * 16, 256)
        lens = rows_in[g, :, :128].astype(F32)[14:15, :4]
        right = []
        for h in range(2):
            cut = [
                rows_out[pl.ds((zl * 16 + core) * 16 + block * 8 + g * 2 + h, NY, stride=32), :]
                for zl in range(NZL)
                for core in range(NC)
            ]
            right.append(jnp.concatenate(cut, axis=0))
        right = jnp.concatenate(right, axis=1).astype(BF16)
        masked, start = [], jnp.zeros((1, 1), F32)
        for d in range(4):
            end = start + lens[:, d : d + 1]
            inside = (position >= start) & (position < end)
            masked.append(jnp.where(inside, left, 0.0).astype(BF16))
            start = end
        product = lax.dot_general(
            jnp.concatenate(masked, axis=0), right, (((1,), (1,)), ((), ())), preferred_element_type=F32
        )
        for d in range(4):
            one = product[d * 64 : (d + 1) * 64]
            total = total + one * one
    total = total * (1.0 / 2048.0)
    for i in range(NX):
        total_ref[i * 14 : (i + 1) * 14, :] = total[i * 16 : i * 16 + 14]


def body(acts, grads, basis_in, basis_out, doc_lengths):
    x, zh, core = lax.axis_index("x"), lax.axis_index("zh"), lax.axis_index("core")
    place = jnp.stack([x, zh, core]).astype(jnp.int32)
    tok, fin = acts.shape
    fout = grads.shape[1]
    rows = basis_in.shape[0] // NX
    tokens = NX * tok

    mine = lax.dynamic_slice_in_dim(basis_in, x * rows, rows, 0)
    mine = jnp.pad(mine, ((0, 16 - rows), (0, 0))).reshape(16, CHIPS, NC * fin).swapaxes(0, 1)
    mine_out = basis_out.reshape(8, CHIPS, NC, fout).transpose(1, 2, 0, 3).reshape(CHIPS, 16, fout)
    packed = jnp.concatenate([mine, mine_out], axis=2)
    packed, acts, grads = lax.optimization_barrier((packed, acts, grads))
    packed = lax.all_to_all(packed, ("zl", "y"), split_axis=0, concat_axis=0, tiled=True)

    payload = jnp.concatenate([acts.T, grads.T], axis=0)
    own = [payload] + [from_offset(payload, "x", NX, s) for s in range(1, NX)]
    other = [from_offset(v, "core", NC, 1) for v in own]

    parts = call(
        project,
        in_hbm((CHIPS, 16, tokens + 128)),
        [
            pltpu.VMEM((NC * fin, tokens), BF16),
            pltpu.VMEM((NC, fout, tokens), BF16),
            pltpu.VMEM((8 * CHIPS * 16, 128), F32),
            pltpu.VMEM((CHIPS * 16, 128), F32),
        ],
        (place, *map(in_vmem, (packed, *own, *other))),
        2 * 512 * 1024 * 1024,
    )
    parts = lax.all_to_all(parts, ("zl", "y"), split_axis=0, concat_axis=0, tiled=True)
    lens = jnp.pad(doc_lengths.astype(F32), ((0, 0), (0, 124)))
    proj_in, proj_out = call(
        add_up,
        (jax.ShapeDtypeStruct((16, tokens), BF16), in_hbm((64, 16, 128))),
        [pltpu.VMEM((16, tokens), F32), pltpu.VMEM((16, 128), F32)],
        (place, lens, in_vmem(parts)),
        32 * 16 * 1152,
    )

    proj_out = lax.all_to_all(proj_out, ("zl", "y", "core"), split_axis=0, concat_axis=0, tiled=True)
    pieces = [proj_in] + [from_offset(proj_in, "x", NX, s) for s in range(1, NX)]
    operands = (place, *map(in_vmem, (proj_out, *pieces)))
    totals = [
        call(
            functools.partial(documents, which),
            jax.ShapeDtypeStruct((NX * rows, 64), F32),
            [pltpu.VMEM((NX, 16, tokens), BF16), pltpu.VMEM((64 * 16, 128), F32)],
            operands,
            2 * 4 * 256 * 256 * 64,
        )
        for which in range(NZH)
    ]
    return (totals[0] + from_offset(totals[1], "zh", NZH, 1)).T


def solution(mesh):
    fine = Mesh(mesh.devices.reshape(NX, NZH, NZL, NY, NC), ("x", "zh", "zl", "y", "core"))
    dp, mp = ("x", "zh"), ("zl", "y", "core")
    in_specs = (P(dp, mp), P(dp, mp), P(mp, None), P(mp, None), P(dp, None))
    return jax.shard_map(body, mesh=fine, in_specs=in_specs, out_specs=P(dp, mp), check_vma=False)
```

time: 725 us -> 129 us (0.18)
  waiting for transfers between devices: 586 us -> 34 us
  blocking collectives: 75.3 us -> 0 us
  starting transfers between devices: 25.9 us -> 73.7 us
  between operations: 13.2 us -> 0.23 us
  Pallas kernels: 0 us -> 9.75 us
  local copies, waits for them, and re-layouts: 14.8 us -> 6.5 us
    reduce_scatter x2 -> x0, waiting for transfers between devices: 412 us -> none  [the longest x1 206 us: body(): lax.psum_scatter(lax.dot_general(part, acts, contract, preferred_element_...]
    unnamed x4 -> x0, waiting for transfers between devices: 89 us -> none
    all_gather x1 -> x0, blocking collectives: 75.3 us -> none  [body(): grad_whole = lax.all_gather(grad_proj, 'mp', axis=0, tiled=True)]
    all_to_all x2 -> x3, waiting for transfers between devices: 84.6 us -> 27.9 us  [the longest x1 27.9 us: body(): lax.all_to_all(parts, ('zl', 'y'), split_axis=0, concat_axis=0, tiled=True)]
    ppermute x0 -> x11, starting transfers between devices: none -> 40.5 us  [from_offset(): lax.ppermute(value, axis, [((i + offset) % size, i) for i in range(size)])]
    all_to_all x2 -> x0, local copies, waits for them, and re-layouts: 12.6 us -> none  [body(): lax.all_to_all(basis_in, 'mp', split_axis=1, concat_axis=0, tiled=True)]
    pallas_call x0 -> x4, Pallas kernels: none -> 9.75 us  [call(): pl.pallas_call(kernel, out_shape=shapes, in_specs=[SMEM] + [VMEM] * (len(...]
    all_to_all x2 -> x3, starting transfers between devices: 25.7 us -> 33.2 us  [the longest x1 13.6 us: body(): lax.all_to_all(packed, ('zl', 'y'), split_axis=0, concat_axis=0, tiled=True)]
  transfers between devices with their start and end apart: 5 -> 14, of which waited for: 4 -> 6; matrix products, arithmetic and copies ran while one was open for 2% -> 1% of each run, Pallas kernels for 0% -> 1%
where the time goes in v1:
time: 129 us; the launch traced here: 127 us
  starting transfers between devices  73.7 us (57%)
  waiting for transfers between devices  34 us (26%)
  Pallas kernels  9.75 us (8%)
  local copies, waits for them, and re-layouts  6.5 us (5%)
  other arithmetic  2.84 us (2%)
    ppermute x11, starting transfers between devices, from_offset(): lax.ppermute(value, axis, [((i + offset) % size, i) for i in range(size)])  40.5 us
    all_to_all x1, waiting for transfers between devices, body(): lax.all_to_all(parts, ('zl', 'y'), split_axis=0, concat_axis=0, tiled=True)  27.9 us
    all_to_all x1, starting transfers between devices, body(): lax.all_to_all(packed, ('zl', 'y'), split_axis=0, concat_axis=0, tiled=True)  13.6 us
    all_to_all x1, starting transfers between devices, body(): lax.all_to_all(proj_out, ('zl', 'y', 'core'), split_axis=0, concat_axis=0...  9.86 us
    pallas_call x4, Pallas kernels, call(): pl.pallas_call(kernel, out_shape=shapes, in_specs=[SMEM] + [VMEM] * (len(...  9.75 us
    all_to_all x1, starting transfers between devices, body(): lax.all_to_all(parts, ('zl', 'y'), split_axis=0, concat_axis=0, tiled=True)  9.74 us
    ppermute x11, waiting for transfers between devices, from_offset(): lax.ppermute(value, axis, [((i + offset) % size, i) for i in range(size)])  6.11 us
    unnamed x16, local copies, waits for them, and re-layouts  5.37 us
  transfers between devices with their start and end apart: 14, of which 6 were waited for; matrix products, arithmetic and copies ran while one was open for 1% of the time, Pallas kernels for 1%

profile of v1, /device:TPU:1, one launch (start us, length us, event | category | flops | bytes accessed | tf_op | source)
XLA Modules:
  0.0 127.0 jit_solution(294046713648877011)
XLA Ops:
  0.0 1.9 %copy-done = bf16[56,28672]{1,0:T(8,128)(2,1)S(1)} copy-done((bf16[56,28672]{1,0:T(8,128)(2,1)S(1)}, bf16[56,28672]{1,0:T(8,128)(2,1)}, u32[]{:S(2)}) %copy-start) | copy-done | bytes 3211288
  2.3 0.7 copy-done.5
  3.1 1.1 pad_maximum_fusion
  4.2 13.6 %all-to-all-start = ((bf16[32,16,1024]{2,1,0:T(8,128)(2,1)}), bf16[32,16,1024]{2,1,0:T(8,128)(2,1)}, u32[]{:S(2)}, u32[]{:S(2)}) async-start(bf16[32,16,1024]{2,1,0:T(8,128)(2,1)} %pad_maximum_fusion), calls=%async_computation | async-start | bytes 2097152 | tf_op jit(solution)/shard_map/all_to_all | solution.py:147
  17.8 0.7 copy.8
  18.6 1.0 pad_maximum_fusion.1.refs_0_
  19.6 4.4 %collective-permute-start = (bf16[576,256]{1,0:T(8,128)(2,1)S(1)}, bf16[576,256]{1,0:T(8,128)(2,1)}, u32[]{:S(2)}, u32[]{:S(2)}) collective-permute-start(bf16[576,256]{1,0:T(8,128)(2,1)S(1)} %pad_maximum_fusion.1.refs_0_), channel_id=1, source_target_pairs={{128,0},{256,128},{384,256},{0,384},{129,1},{257,129},{385,257},{1... | collective-permute-start | bytes 884744 | tf_op jit(solution)/shard_map/ppermute | solution.py:18
  24.0 2.4 %collective-permute-start.1 = (bf16[576,256]{1,0:T(8,128)(2,1)S(1)}, bf16[576,256]{1,0:T(8,128)(2,1)}, u32[]{:S(2)}, u32[]{:S(2)}) collective-permute-start(bf16[576,256]{1,0:T(8,128)(2,1)S(1)} %pad_maximum_fusion.1.refs_0_), channel_id=1, source_target_pairs={{256,0},{384,128},{0,256},{128,384},{257,1},{385,129},{1,257},{129... | collective-permute-start | bytes 884744 | tf_op jit(solution)/shard_map/ppermute | solution.py:18
  26.4 2.5 %collective-permute-start.2 = (bf16[576,256]{1,0:T(8,128)(2,1)S(1)}, bf16[576,256]{1,0:T(8,128)(2,1)}, u32[]{:S(2)}, u32[]{:S(2)}) collective-permute-start(bf16[576,256]{1,0:T(8,128)(2,1)S(1)} %pad_maximum_fusion.1.refs_0_), channel_id=1, source_target_pairs={{384,0},{0,128},{128,256},{256,384},{385,1},{1,129},{129,257},{257... | collective-permute-start | bytes 884744 | tf_op jit(solution)/shard_map/ppermute | solution.py:18
  28.9 3.7 %collective-permute-start.3 = (bf16[576,256]{1,0:T(8,128)(2,1)S(1)}, bf16[576,256]{1,0:T(8,128)(2,1)}, u32[]{:S(2)}, u32[]{:S(2)}) collective-permute-start(bf16[576,256]{1,0:T(8,128)(2,1)S(1)} %pad_maximum_fusion.1.refs_0_), channel_id=1, source_target_pairs={{1,0},{0,1},{3,2},{2,3},{5,4},{4,5},{7,6},{6,7},{9,8},{8,9},{11,10... | collective-permute-start | bytes 884744 | tf_op jit(solution)/shard_map/ppermute | solution.py:18
  32.6 6.8 %collective-permute-start.4 = (bf16[576,256]{1,0:T(8,128)(2,1)}, bf16[576,256]{1,0:T(8,128)(2,1)}, u32[]{:S(2)}, u32[]{:S(2)}) collective-permute-start(bf16[576,256]{1,0:T(8,128)(2,1)} %collective-permute-done.refs_1_), channel_id=1, source_target_pairs={{1,0},{0,1},{3,2},{2,3},{5,4},{4,5},{7,6},{6,7},{9,8},{8,9},{11,10... | collective-permute-start | bytes 884744 | tf_op jit(solution)/shard_map/ppermute | solution.py:18
  39.4 1.9 %collective-permute-start.5 = (bf16[576,256]{1,0:T(8,128)(2,1)}, bf16[576,256]{1,0:T(8,128)(2,1)}, u32[]{:S(2)}, u32[]{:S(2)}) collective-permute-start(bf16[576,256]{1,0:T(8,128)(2,1)} %collective-permute-done.1.refs_2_), channel_id=1, source_target_pairs={{1,0},{0,1},{3,2},{2,3},{5,4},{4,5},{7,6},{6,7},{9,8},{8,9},{11,10... | collective-permute-start | bytes 884744 | tf_op jit(solution)/shard_map/ppermute | solution.py:18
  41.4 1.4 %collective-permute-done.2.refs_3_ = bf16[576,256]{1,0:T(8,128)(2,1)} collective-permute-done((bf16[576,256]{1,0:T(8,128)(2,1)S(1)}, bf16[576,256]{1,0:T(8,128)(2,1)}, u32[]{:S(2)}, u32[]{:S(2)}) %collective-permute-start.2) | collective-permute-done | bytes 294944 | tf_op jit(solution)/shard_map/ppermute | solution.py:18
  42.7 2.4 %collective-permute-start.6 = (bf16[576,256]{1,0:T(8,128)(2,1)}, bf16[576,256]{1,0:T(8,128)(2,1)}, u32[]{:S(2)}, u32[]{:S(2)}) collective-permute-start(bf16[576,256]{1,0:T(8,128)(2,1)} %collective-permute-done.2.refs_3_), channel_id=1, source_target_pairs={{1,0},{0,1},{3,2},{2,3},{5,4},{4,5},{7,6},{6,7},{9,8},{8,9},{11,10... | collective-permute-start | bytes 884744 | tf_op jit(solution)/shard_map/ppermute | solution.py:18
  45.2 1.4 %collective-permute-done.6.refs_7_ = bf16[576,256]{1,0:T(8,128)(2,1)} collective-permute-done((bf16[576,256]{1,0:T(8,128)(2,1)}, bf16[576,256]{1,0:T(8,128)(2,1)}, u32[]{:S(2)}, u32[]{:S(2)}) %collective-permute-start.6) | collective-permute-done | bytes 294944 | tf_op jit(solution)/shard_map/ppermute | solution.py:18
  46.6 5.6 %shard_map.55 = bf16[32,16,1152]{2,1,0:T(8,128)(2,1)} custom-call(s32[3]{0:T(128)S(1)} %pad_add_fusion.place, bf16[32,16,1024]{2,1,0:T(8,128)(2,1)} %all-to-all-done.packed_ref, bf16[576,256]{1,0:T(8,128)(2,1)S(1)} %pad_maximum_fusion.1.refs_0_, bf16[576,256]{1,0:T(8,128)(2,1)} %collective-permute-done.refs_1_, ...), custom_call_target="tpu_custom_call" | custom-call | flops 1073741824 | bytes 3407884 | tf_op jit(solution)/shard_map/pallas_call | solution.py:23
  52.2 9.7 %all-to-all-start.1 = ((bf16[32,16,1152]{2,1,0:T(8,128)(2,1)}), bf16[32,16,1152]{2,1,0:T(8,128)(2,1)}, u32[]{:S(2)}, u32[]{:S(2)}) async-start(bf16[32,16,1152]{2,1,0:T(8,128)(2,1)} %shard_map.55), calls=%async_computation.1 | async-start | bytes 2359296 | tf_op jit(solution)/shard_map/all_to_all | solution.py:165
  62.0 27.9 %all-to-all-done.1.parts_ref = bf16[32,16,1152]{2,1,0:T(8,128)(2,1)} async-done(((bf16[32,16,1152]{2,1,0:T(8,128)(2,1)}), bf16[32,16,1152]{2,1,0:T(8,128)(2,1)}, u32[]{:S(2)}, u32[]{:S(2)}) %all-to-all-start.1) | async-done | bytes 1179680 | tf_op jit(solution)/shard_map/all_to_all | solution.py:165
  89.9 2.2 %shard_map.56 = (bf16[16,1024]{1,0:T(8,128)(2,1)S(1)}, bf16[64,16,128]{2,1,0:T(8,128)(2,1)}) custom-call(s32[3]{0:T(128)S(1)} %pad_add_fusion.place, f32[1,128]{1,0:T(1,128)S(1)} %pad.8.lens_ref, bf16[32,16,1152]{2,1,0:T(8,128)(2,1)} %all-to-all-done.1.parts_ref), custom_call_target="tpu_custom_call" | custom-call | flops 589824 | bytes 1180172 | tf_op jit(solution)/shard_map/pallas_call | solution.py:23
  92.0 9.9 %all-to-all-start.2 = ((bf16[64,16,128]{2,1,0:T(8,128)(2,1)}), bf16[64,16,128]{2,1,0:T(8,128)(2,1)S(1)}, u32[]{:S(2)}, u32[]{:S(2)}) async-start(bf16[64,16,128]{2,1,0:T(8,128)(2,1)} %get-tuple-element.13), calls=%async_computation.2 | async-start | bytes 524288 | tf_op jit(solution)/shard_map/all_to_all | solution.py:175
  101.9 4.0 %collective-permute-start.7 = (bf16[16,1024]{1,0:T(8,128)(2,1)S(1)}, bf16[16,1024]{1,0:T(8,128)(2,1)S(1)}, u32[]{:S(2)}, u32[]{:S(2)}) collective-permute-start(bf16[16,1024]{1,0:T(8,128)(2,1)S(1)} %get-tuple-element.14.piece0), channel_id=1, source_target_pairs={{128,0},{256,128},{384,256},{0,384},{129,1},{257,129},{385,257},{1... | collective-permute-start | bytes 98312 | tf_op jit(solution)/shard_map/ppermute | solution.py:18
  106.0 1.9 %collective-permute-start.8 = (bf16[16,1024]{1,0:T(8,128)(2,1)S(1)}, bf16[16,1024]{1,0:T(8,128)(2,1)S(1)}, u32[]{:S(2)}, u32[]{:S(2)}) collective-permute-start(bf16[16,1024]{1,0:T(8,128)(2,1)S(1)} %get-tuple-element.14.piece0), channel_id=1, source_target_pairs={{256,0},{384,128},{0,256},{128,384},{257,1},{385,129},{1,257},{129... | collective-permute-start | bytes 98312 | tf_op jit(solution)/shard_map/ppermute | solution.py:18
  107.9 2.5 %collective-permute-start.9 = (bf16[16,1024]{1,0:T(8,128)(2,1)S(1)}, bf16[16,1024]{1,0:T(8,128)(2,1)S(1)}, u32[]{:S(2)}, u32[]{:S(2)}) collective-permute-start(bf16[16,1024]{1,0:T(8,128)(2,1)S(1)} %get-tuple-element.14.piece0), channel_id=1, source_target_pairs={{384,0},{0,128},{128,256},{256,384},{385,1},{1,129},{129,257},{257... | collective-permute-start | bytes 98312 | tf_op jit(solution)/shard_map/ppermute | solution.py:18
  110.4 2.0 %collective-permute-done.8.piece2 = bf16[16,1024]{1,0:T(8,128)(2,1)S(1)} collective-permute-done((bf16[16,1024]{1,0:T(8,128)(2,1)S(1)}, bf16[16,1024]{1,0:T(8,128)(2,1)S(1)}, u32[]{:S(2)}, u32[]{:S(2)}) %collective-permute-start.8) | collective-permute-done | bytes 32800 | tf_op jit(solution)/shard_map/ppermute | solution.py:18
  112.4 0.6 copy-done.1
  113.0 1.0 collective-permute-done.9.piece3
  114.7 0.8 copy-done.2
  115.4 0.8 copy-done.4
  116.2 1.0 shard_map.58
  117.2 7.9 %collective-permute-start.10 = (f32[56,64]{1,0:T(8,128)S(1)}, f32[56,64]{1,0:T(8,128)S(1)}, u32[]{:S(2)}, u32[]{:S(2)}) collective-permute-start(f32[56,64]{1,0:T(8,128)S(1)} %shard_map.58), channel_id=1, source_target_pairs={{64,0},{0,64},{65,1},{1,65},{66,2},{2,66},{67,3},{3,67},{68,4},{4,... | collective-permute-start | bytes 43016 | tf_op jit(solution)/shard_map/ppermute | solution.py:18
  125.1 1.0 shard_map.57
  126.4 0.6 add_bitcast_fusion
  (26 shorter events, 1.4 us)
Async XLA Ops:
  0.0 1.9 %copy-start = (bf16[56,28672]{1,0:T(8,128)(2,1)S(1)}, bf16[56,28672]{1,0:T(8,128)(2,1)}, u32[]{:S(2)}) copy-start(bf16[56,28672]{1,0:T(8,128)(2,1)} %param.7) | copy-start | bytes 9633796
  2.2 0.9 copy-start.5
  3.1 14.8 %copy-start.6 = (bf16[256,128]{1,0:T(8,128)(2,1)S(1)}, bf16[256,128]{1,0:T(8,128)(2,1)}, u32[]{:S(2)}) copy-start(bf16[256,128]{1,0:T(8,128)(2,1)} %param.6) | copy-start | bytes 196612
  4.2 42.4 %all-to-all-start = ((bf16[32,16,1024]{2,1,0:T(8,128)(2,1)}), bf16[32,16,1024]{2,1,0:T(8,128)(2,1)}, u32[]{:S(2)}, u32[]{:S(2)}) async-start(bf16[32,16,1024]{2,1,0:T(8,128)(2,1)} %pad_maximum_fusion), calls=%async_computation | async-start | bytes 2097152 | tf_op jit(solution)/shard_map/all_to_all | solution.py:147
  19.6 13.1 %collective-permute-start = (bf16[576,256]{1,0:T(8,128)(2,1)S(1)}, bf16[576,256]{1,0:T(8,128)(2,1)}, u32[]{:S(2)}, u32[]{:S(2)}) collective-permute-start(bf16[576,256]{1,0:T(8,128)(2,1)S(1)} %pad_maximum_fusion.1.refs_0_), channel_id=1, source_target_pairs={{128,0},{256,128},{384,256},{0,384},{129,1},{257,129},{385,257},{1... | collective-permute-start | bytes 884744 | tf_op jit(solution)/shard_map/ppermute | solution.py:18
  24.0 15.5 %collective-permute-start.1 = (bf16[576,256]{1,0:T(8,128)(2,1)S(1)}, bf16[576,256]{1,0:T(8,128)(2,1)}, u32[]{:S(2)}, u32[]{:S(2)}) collective-permute-start(bf16[576,256]{1,0:T(8,128)(2,1)S(1)} %pad_maximum_fusion.1.refs_0_), channel_id=1, source_target_pairs={{256,0},{384,128},{0,256},{128,384},{257,1},{385,129},{1,257},{129... | collective-permute-start | bytes 884744 | tf_op jit(solution)/shard_map/ppermute | solution.py:18
  26.4 16.3 %collective-permute-start.2 = (bf16[576,256]{1,0:T(8,128)(2,1)S(1)}, bf16[576,256]{1,0:T(8,128)(2,1)}, u32[]{:S(2)}, u32[]{:S(2)}) collective-permute-start(bf16[576,256]{1,0:T(8,128)(2,1)S(1)} %pad_maximum_fusion.1.refs_0_), channel_id=1, source_target_pairs={{384,0},{0,128},{128,256},{256,384},{385,1},{1,129},{129,257},{257... | collective-permute-start | bytes 884744 | tf_op jit(solution)/shard_map/ppermute | solution.py:18
  28.9 16.3 %collective-permute-start.3 = (bf16[576,256]{1,0:T(8,128)(2,1)S(1)}, bf16[576,256]{1,0:T(8,128)(2,1)}, u32[]{:S(2)}, u32[]{:S(2)}) collective-permute-start(bf16[576,256]{1,0:T(8,128)(2,1)S(1)} %pad_maximum_fusion.1.refs_0_), channel_id=1, source_target_pairs={{1,0},{0,1},{3,2},{2,3},{5,4},{4,5},{7,6},{6,7},{9,8},{8,9},{11,10... | collective-permute-start | bytes 884744 | tf_op jit(solution)/shard_map/ppermute | solution.py:18
  32.6 12.6 %collective-permute-start.4 = (bf16[576,256]{1,0:T(8,128)(2,1)}, bf16[576,256]{1,0:T(8,128)(2,1)}, u32[]{:S(2)}, u32[]{:S(2)}) collective-permute-start(bf16[576,256]{1,0:T(8,128)(2,1)} %collective-permute-done.refs_1_), channel_id=1, source_target_pairs={{1,0},{0,1},{3,2},{2,3},{5,4},{4,5},{7,6},{6,7},{9,8},{8,9},{11,10... | collective-permute-start | bytes 884744 | tf_op jit(solution)/shard_map/ppermute | solution.py:18
  39.4 5.8 %collective-permute-start.5 = (bf16[576,256]{1,0:T(8,128)(2,1)}, bf16[576,256]{1,0:T(8,128)(2,1)}, u32[]{:S(2)}, u32[]{:S(2)}) collective-permute-start(bf16[576,256]{1,0:T(8,128)(2,1)} %collective-permute-done.1.refs_2_), channel_id=1, source_target_pairs={{1,0},{0,1},{3,2},{2,3},{5,4},{4,5},{7,6},{6,7},{9,8},{8,9},{11,10... | collective-permute-start | bytes 884744 | tf_op jit(solution)/shard_map/ppermute | solution.py:18
  42.7 3.9 %collective-permute-start.6 = (bf16[576,256]{1,0:T(8,128)(2,1)}, bf16[576,256]{1,0:T(8,128)(2,1)}, u32[]{:S(2)}, u32[]{:S(2)}) collective-permute-start(bf16[576,256]{1,0:T(8,128)(2,1)} %collective-permute-done.2.refs_3_), channel_id=1, source_target_pairs={{1,0},{0,1},{3,2},{2,3},{5,4},{4,5},{7,6},{6,7},{9,8},{8,9},{11,10... | collective-permute-start | bytes 884744 | tf_op jit(solution)/shard_map/ppermute | solution.py:18
  52.2 9.8 %copy-start.7 = (s32[1,4]{1,0:T(1,128)S(1)}, s32[1,4]{1,0:T(1,128)}, u32[]{:S(2)}) copy-start(s32[1,4]{1,0:T(1,128)} %param.9) | copy-start | bytes 52
  52.2 37.7 %all-to-all-start.1 = ((bf16[32,16,1152]{2,1,0:T(8,128)(2,1)}), bf16[32,16,1152]{2,1,0:T(8,128)(2,1)}, u32[]{:S(2)}, u32[]{:S(2)}) async-start(bf16[32,16,1152]{2,1,0:T(8,128)(2,1)} %shard_map.55), calls=%async_computation.1 | async-start | bytes 2359296 | tf_op jit(solution)/shard_map/all_to_all | solution.py:165
  92.0 22.6 %all-to-all-start.2 = ((bf16[64,16,128]{2,1,0:T(8,128)(2,1)}), bf16[64,16,128]{2,1,0:T(8,128)(2,1)S(1)}, u32[]{:S(2)}, u32[]{:S(2)}) async-start(bf16[64,16,128]{2,1,0:T(8,128)(2,1)} %get-tuple-element.13), calls=%async_computation.2 | async-start | bytes 524288 | tf_op jit(solution)/shard_map/all_to_all | solution.py:175
  101.9 8.5 %collective-permute-start.7 = (bf16[16,1024]{1,0:T(8,128)(2,1)S(1)}, bf16[16,1024]{1,0:T(8,128)(2,1)S(1)}, u32[]{:S(2)}, u32[]{:S(2)}) collective-permute-start(bf16[16,1024]{1,0:T(8,128)(2,1)S(1)} %get-tuple-element.14.piece0), channel_id=1, source_target_pairs={{128,0},{256,128},{384,256},{0,384},{129,1},{257,129},{385,257},{1... | collective-permute-start | bytes 98312 | tf_op jit(solution)/shard_map/ppermute | solution.py:18
  106.0 6.5 %collective-permute-start.8 = (bf16[16,1024]{1,0:T(8,128)(2,1)S(1)}, bf16[16,1024]{1,0:T(8,128)(2,1)S(1)}, u32[]{:S(2)}, u32[]{:S(2)}) collective-permute-start(bf16[16,1024]{1,0:T(8,128)(2,1)S(1)} %get-tuple-element.14.piece0), channel_id=1, source_target_pairs={{256,0},{384,128},{0,256},{128,384},{257,1},{385,129},{1,257},{129... | collective-permute-start | bytes 98312 | tf_op jit(solution)/shard_map/ppermute | solution.py:18
  107.9 6.2 %collective-permute-start.9 = (bf16[16,1024]{1,0:T(8,128)(2,1)S(1)}, bf16[16,1024]{1,0:T(8,128)(2,1)S(1)}, u32[]{:S(2)}, u32[]{:S(2)}) collective-permute-start(bf16[16,1024]{1,0:T(8,128)(2,1)S(1)} %get-tuple-element.14.piece0), channel_id=1, source_target_pairs={{384,0},{0,128},{128,256},{256,384},{385,1},{1,129},{129,257},{257... | collective-permute-start | bytes 98312 | tf_op jit(solution)/shard_map/ppermute | solution.py:18
  112.4 0.6 copy-start.1
  114.1 0.6 copy-start.3
  114.7 0.8 copy-start.2
  115.4 0.8 copy-start.4
  117.2 9.2 %collective-permute-start.10 = (f32[56,64]{1,0:T(8,128)S(1)}, f32[56,64]{1,0:T(8,128)S(1)}, u32[]{:S(2)}, u32[]{:S(2)}) collective-permute-start(f32[56,64]{1,0:T(8,128)S(1)} %shard_map.58), channel_id=1, source_target_pairs={{64,0},{0,64},{65,1},{1,65},{66,2},{2,66},{67,3},{3,67},{68,4},{4,... | collective-permute-start | bytes 43016 | tf_op jit(solution)/shard_map/ppermute | solution.py:18

commit v2 on v1

--- a/solution.py
+++ b/solution.py
@@ -12,19 +12,20 @@
 BF16, F32 = jnp.bfloat16, jnp.float32
 SMEM = pl.BlockSpec(memory_space=pltpu.SMEM)
 VMEM = pl.BlockSpec(memory_space=pltpu.VMEM)
+ANY = pl.BlockSpec(memory_space=pl.ANY)
 
 
 def from_offset(value, axis, size, offset):
     return lax.ppermute(value, axis, [((i + offset) % size, i) for i in range(size)])
 
 
-def call(kernel, shapes, scratch, operands, flops):
+def call(kernel, shapes, scratch, operands, flops, space=VMEM):
     size = sum(a.size * a.dtype.itemsize for a in operands)
     return pl.pallas_call(
         kernel,
         out_shape=shapes,
-        in_specs=[SMEM] + [VMEM] * (len(operands) - 1),
-        out_specs=jax.tree.map(lambda _: VMEM, shapes),
+        in_specs=[SMEM] + [space] * (len(operands) - 1),
+        out_specs=jax.tree.map(lambda _: space, shapes),
         scratch_shapes=scratch,
         compiler_params=pltpu.CompilerParams(vmem_limit_bytes=40 << 20),
         cost_estimate=pl.CostEstimate(flops=flops, bytes_accessed=size, transcendentals=0),
@@ -35,44 +36,86 @@
     return pltpu.with_memory_space_constraint(value, pltpu.VMEM)
 
 
+def from_hbm(value):
+    return pltpu.with_memory_space_constraint(value, pltpu.HBM)
+
+
 def in_hbm(shape):
     return pltpu.HBM(shape, BF16)
 
 
+def pack(place, basis_ref, out_rows_ref, acts_ref, grads_ref, packed_ref, payload_ref):
+    first = place[0] * 14
+    row = lax.broadcasted_iota(jnp.int32, (16, 56), 0)
+    pick = (lax.broadcasted_iota(jnp.int32, (16, 56), 1) == row + first) & (row < 14)
+    pick = pick.astype(F32).astype(BF16)
+    width = basis_ref.shape[1] // packed_ref.shape[0]
+    fout = grads_ref.shape[1]
+    for c in range(packed_ref.shape[0]):
+        rows = jnp.dot(pick, basis_ref[:, c * width : (c + 1) * width], preferred_element_type=F32)
+        packed_ref[c, :, :width] = rows.astype(BF16)
+        out = out_rows_ref[:, c * NC * fout : (c + 1) * NC * fout].astype(F32)
+        packed_ref[c, :, width:] = jnp.concatenate([out[:, :fout], out[:, fout:]], axis=0).astype(BF16)
+
+    @pl.when(pl.program_id(0) == 0)
+    def _():
+        fin = acts_ref.shape[0]
+        payload_ref[:fin, :] = acts_ref[...]
+        payload_ref[fin:, :] = grads_ref[...].astype(F32).T.astype(BF16)
+
+
 def project(place, packed_ref, *refs):
-    own, other, (parts_ref, acts, grads, wide, low) = refs[:NX], refs[NX : 2 * NX], refs[2 * NX :]
+    own, other, parts_ref = refs[:NX], refs[NX : 2 * NX], refs[2 * NX]
+    packed, acts, grads, wide, low, *outs, in_sems, out_sems = refs[2 * NX + 1 :]
     x, core = place[0], place[2]
     fin = acts.shape[0] // NC
     fout = grads.shape[1]
     tokens, height = acts.shape[1], CHIPS * 16
-    for pieces, which in ((own, core), (other, 1 - core)):
-        for s in range(NX):
-            cols = slice(s * 256, (s + 1) * 256)
-            acts[pl.ds(pl.multiple_of(which * fin, 16), fin), cols] = pieces[s][:fin, :]
-            grads[which, :, cols] = pieces[s][fin:, :]
-    left = packed_ref[:, :, : NC * fin].reshape(height, NC * fin)
-
-    def columns(n, carry):
-        cols = pl.ds(pl.multiple_of(n * 256, 256), 256)
+    first = pltpu.make_async_copy(packed_ref, packed, in_sems.at[16])
+    first.start()
+    copies = []
+    for s in range(NX):
+        cols = pl.ds(s * 256, 256)
+        for k, (pieces, which) in enumerate(((own, core), (other, 1 - core))):
+            rows = pl.ds(pl.multiple_of(which * fin, 16), fin)
+            copies.append(
+                [
+                    pltpu.make_async_copy(pieces[s].at[pl.ds(0, fin)], acts.at[rows, cols], in_sems.at[s * 4 + k * 2]),
+                    pltpu.make_async_copy(
+                        pieces[s].at[pl.ds(fin, fout)], grads.at[which, :, cols], in_sems.at[s * 4 + k * 2 + 1]
+                    ),
+                ]
+            )
+            for copy in copies[-1]:
+                copy.start()
+    first.wait()
+    left = packed[:, :, : NC * fin].reshape(height, NC * fin)
+    rows_out = packed[pl.ds(x * 8, 8), :, NC * fin :].astype(F32).reshape(8, NC, 8, fout)
+    rows_out = [rows_out[:, c].reshape(64, fout).astype(BF16) for c in range(NC)]
+    results = []
+    for s in range(NX):
+        for copy in copies[2 * s] + copies[2 * s + 1]:
+            copy.wait()
+        cols = slice(s * 256, (s + 1) * 256)
         part = jnp.dot(left, acts[:, cols], preferred_element_type=F32)
+        out = jnp.zeros((64, 256), F32)
+        for c in range(NC):
+            out += jnp.dot(rows_out[c], grads[c, :, cols], preferred_element_type=F32)
+        rest = out - out.astype(BF16).astype(F32)
         for h in range(2):
-            wide[pl.ds(pl.multiple_of((n * 2 + h) * height, height), height), :] = part[:, h * 128 : (h + 1) * 128]
-        return carry
-
-    lax.fori_loop(0, tokens // 256, columns, 0)
-    rows = packed_ref[pl.ds(x * 8, 8), :, NC * fin :].astype(F32).reshape(8, NC, 8, fout)
-    part = jnp.zeros((64, tokens), F32)
-    for c in range(NC):
-        part += jnp.dot(rows[:, c].reshape(64, fout).astype(BF16), grads[c], preferred_element_type=F32)
-    rest = part - part.astype(BF16).astype(F32)
-    for half in range(2):
-        for t in range(8):
-            block = slice(half * 32, half * 32 + 32), slice(t * 128, (t + 1) * 128)
-            wide[pl.ds(t * height + 14 + half, CHIPS, stride=16), :] = part[block]
-            low[pl.ds(half * 8 + t, CHIPS, stride=16), :] = rest[block]
-    for t in range(8):
-        parts_ref[:, :, t * 128 : (t + 1) * 128] = wide[t * height : (t + 1) * height].astype(BF16).reshape(CHIPS, 16, 128)
-    parts_ref[:, :, tokens:] = low[...].astype(BF16).reshape(CHIPS, 16, 128)
+            block = slice(h * 128, (h + 1) * 128)
+            wide[pl.ds(h * height, height), :] = part[:, block]
+            for half in range(2):
+                wide[pl.ds(h * height + 14 + half, CHIPS, stride=16), :] = out[half * 32 : half * 32 + 32, block]
+                low[pl.ds(half * 8 + s * 2 + h, CHIPS, stride=16), :] = rest[half * 32 : half * 32 + 32, block]
+            outs[s][:, :, block] = wide[h * height : (h + 1) * height].astype(BF16).reshape(CHIPS, 16, 128)
+        results.append(pltpu.make_async_copy(outs[s], parts_ref.at[:, :, pl.ds(s * 256, 256)], out_sems.at[s]))
+        results[-1].start()
+    outs[NX][...] = low[...].astype(BF16).reshape(CHIPS, 16, 128)
+    results.append(pltpu.make_async_copy(outs[NX], parts_ref.at[:, :, pl.ds(tokens, 128)], out_sems.at[NX]))
+    results[-1].start()
+    for result in results:
+        result.wait()
 
 
 def add_up(place, lens_ref, parts_ref, in_ref, out_ref, wide, narrow):
@@ -139,14 +182,27 @@
     rows = basis_in.shape[0] // NX
     tokens = NX * tok
 
-    mine = lax.dynamic_slice_in_dim(basis_in, x * rows, rows, 0)
-    mine = jnp.pad(mine, ((0, 16 - rows), (0, 0))).reshape(16, CHIPS, NC * fin).swapaxes(0, 1)
-    mine_out = basis_out.reshape(8, CHIPS, NC, fout).transpose(1, 2, 0, 3).reshape(CHIPS, 16, fout)
-    packed = jnp.concatenate([mine, mine_out], axis=2)
-    packed, acts, grads = lax.optimization_barrier((packed, acts, grads))
+    steps = 4
+    packed, payload = pl.pallas_call(
+        pack,
+        out_shape=(in_hbm((CHIPS, 16, NC * (fin + fout // 2))), jax.ShapeDtypeStruct((fin + fout, tok), BF16)),
+        grid=(steps,),
+        in_specs=[
+            SMEM,
+            pl.BlockSpec((4 * rows, CHIPS * NC * fin // steps), lambda i: (0, i)),
+            pl.BlockSpec((8, CHIPS * NC * fout // steps), lambda i: (0, i)),
+            pl.BlockSpec((fin, tok), lambda i: (0, 0)),
+            pl.BlockSpec((tok, fout), lambda i: (0, 0)),
+        ],
+        out_specs=(
+            pl.BlockSpec((CHIPS // steps, 16, NC * (fin + fout // 2)), lambda i: (i, 0, 0)),
+            pl.BlockSpec((fin + fout, tok), lambda i: (0, 0)),
+        ),
+        compiler_params=pltpu.CompilerParams(vmem_limit_bytes=40 << 20),
+        cost_estimate=pl.CostEstimate(flops=1 << 26, bytes_accessed=5 << 20, transcendentals=0),
+    )(place, from_hbm(basis_in), basis_out, acts.T, grads)
     packed = lax.all_to_all(packed, ("zl", "y"), split_axis=0, concat_axis=0, tiled=True)
 
-    payload = jnp.concatenate([acts.T, grads.T], axis=0)
     own = [payload] + [from_offset(payload, "x", NX, s) for s in range(1, NX)]
     other = [from_offset(v, "core", NC, 1) for v in own]
 
@@ -154,13 +210,19 @@
         project,
         in_hbm((CHIPS, 16, tokens + 128)),
         [
+            pltpu.VMEM((CHIPS, 16, NC * fin + fout), BF16),
             pltpu.VMEM((NC * fin, tokens), BF16),
             pltpu.VMEM((NC, fout, tokens), BF16),
-            pltpu.VMEM((8 * CHIPS * 16, 128), F32),
+            pltpu.VMEM((2 * CHIPS * 16, 128), F32),
             pltpu.VMEM((CHIPS * 16, 128), F32),
+            *[pltpu.VMEM((CHIPS, 16, 256), BF16)] * NX,
+            pltpu.VMEM((CHIPS, 16, 128), BF16),
+            pltpu.SemaphoreType.DMA((17,)),
+            pltpu.SemaphoreType.DMA((5,)),
         ],
-        (place, *map(in_vmem, (packed, *own, *other))),
+        (place, packed, *own, *other),
         2 * 512 * 1024 * 1024,
+        ANY,
     )
     parts = lax.all_to_all(parts, ("zl", "y"), split_axis=0, concat_axis=0, tiled=True)
     lens = jnp.pad(doc_lengths.astype(F32), ((0, 0), (0, 124)))
@@ -174,7 +236,7 @@
 
     proj_out = lax.all_to_all(proj_out, ("zl", "y", "core"), split_axis=0, concat_axis=0, tiled=True)
     pieces = [proj_in] + [from_offset(proj_in, "x", NX, s) for s in range(1, NX)]
-    operands = (place, *map(in_vmem, (proj_out, *pieces)))
+    operands = (place, in_vmem(proj_out), *map(from_hbm, pieces))
     totals = [
         call(
             functools.partial(documents, which),

time: 129 us -> 127 us (0.984)
  Pallas kernels: 9.75 us -> 13.3 us
  local copies, waits for them, and re-layouts: 6.5 us -> 3.2 us
  other arithmetic: 2.84 us -> 0.69 us
    pallas_call x4 -> x5, Pallas kernels: 9.75 us -> 13.3 us  [the longest x4 8.96 us: call(): pl.pallas_call(kernel, out_shape=shapes, in_specs=[SMEM] + [space] * (len...]
    unnamed x16, local copies, waits for them, and re-layouts: 5.37 us -> 3.19 us
    concatenate x2 -> x0, other arithmetic: 2.14 us -> none  [the longest x1 1.15 us: body(): packed = jnp.concatenate([mine, mine_out], axis=2)]
  transfers between devices with their start and end apart: 14 -> 14, of which waited for: 6 -> 6; matrix products, arithmetic and copies ran while one was open for 1% -> 0% of each run, Pallas kernels for 1% -> 1%
where the time goes in v2:
time: 127 us; the launch traced here: 125 us
  starting transfers between devices  73.4 us (58%)
  waiting for transfers between devices  34.1 us (27%)
  Pallas kernels  13.3 us (10%)
  local copies, waits for them, and re-layouts  3.2 us (3%)
    ppermute x11, starting transfers between devices, from_offset(): lax.ppermute(value, axis, [((i + offset) % size, i) for i in range(size)])  40.5 us
    all_to_all x1, waiting for transfers between devices, body(): lax.all_to_all(parts, ('zl', 'y'), split_axis=0, concat_axis=0, tiled=True)  27.9 us
    all_to_all x1, starting transfers between devices, body(): lax.all_to_all(packed, ('zl', 'y'), split_axis=0, concat_axis=0, tiled=True)  13.5 us
    all_to_all x1, starting transfers between devices, body(): lax.all_to_all(proj_out, ('zl', 'y', 'core'), split_axis=0, concat_axis=0...  9.85 us
    all_to_all x1, starting transfers between devices, body(): lax.all_to_all(parts, ('zl', 'y'), split_axis=0, concat_axis=0, tiled=True)  9.59 us
    pallas_call x4, Pallas kernels, call(): pl.pallas_call(kernel, out_shape=shapes, in_specs=[SMEM] + [space] * (len...  8.96 us
    ppermute x11, waiting for transfers between devices, from_offset(): lax.ppermute(value, axis, [((i + offset) % size, i) for i in range(size)])  6.07 us
    pallas_call x1, Pallas kernels, body(): pl.pallas_call(pack, out_shape=(in_hbm((CHIPS, 16, NC * (fin + fout // 2)...  4.36 us
  transfers between devices with their start and end apart: 14, of which 6 were waited for; matrix products, arithmetic and copies ran while one was open for 0% of the time, Pallas kernels for 1%

profile of v2, /device:TPU:1, one launch (start us, length us, event | category | flops | bytes accessed | tf_op | source)
XLA Modules:
  0.0 124.9 jit_solution(15517897013832929391)
XLA Ops:
  0.0 0.1 pad_add_fusion.place
  0.1 0.9 copy-done
  1.0 0.9 copy-done.1
  1.9 0.8 copy-done.3
  2.8 4.4 %shard_map.55 = (bf16[32,16,1024]{2,1,0:T(8,128)(2,1)}, bf16[576,256]{1,0:T(8,128)(2,1)S(1)}) custom-call(s32[3]{0:T(128)S(1)} %pad_add_fusion.place, bf16[56,28672]{1,0:T(8,128)(2,1)} %basis_ref.1, bf16[8,8192]{1,0:T(8,128)(2,1)S(1)} %copy-done.1, bf16[448,256]{1,0:T(8,128)(2,1)S(1)} %bitcast.6, bf16[256,128]{1,0:T(8,128)(2,1)S(1)} %copy-done.3), custom_call_target="tpu_custom_call" | custom-call | flops 67108864 | bytes 5242880 | tf_op jit(solution)/shard_map/pallas_call | solution.py:186
  7.1 13.5 %all-to-all-start = ((bf16[32,16,1024]{2,1,0:T(8,128)(2,1)}), bf16[32,16,1024]{2,1,0:T(8,128)(2,1)S(1)}, u32[]{:S(2)}, u32[]{:S(2)}) async-start(bf16[32,16,1024]{2,1,0:T(8,128)(2,1)} %get-tuple-element.9), calls=%async_computation | async-start | bytes 2097152 | tf_op jit(solution)/shard_map/all_to_all | solution.py:204
  20.6 4.4 %collective-permute-start = (bf16[576,256]{1,0:T(8,128)(2,1)S(1)}, bf16[576,256]{1,0:T(8,128)(2,1)S(1)}, u32[]{:S(2)}, u32[]{:S(2)}) collective-permute-start(bf16[576,256]{1,0:T(8,128)(2,1)S(1)} %get-tuple-element.10.refs_0_), channel_id=1, source_target_pairs={{128,0},{256,128},{384,256},{0,384},{129,1},{257,129},{385,257},{1... | collective-permute-start | bytes 884744 | tf_op jit(solution)/shard_map/ppermute | solution.py:19
  25.0 2.4 %collective-permute-start.1 = (bf16[576,256]{1,0:T(8,128)(2,1)S(1)}, bf16[576,256]{1,0:T(8,128)(2,1)S(1)}, u32[]{:S(2)}, u32[]{:S(2)}) collective-permute-start(bf16[576,256]{1,0:T(8,128)(2,1)S(1)} %get-tuple-element.10.refs_0_), channel_id=1, source_target_pairs={{256,0},{384,128},{0,256},{128,384},{257,1},{385,129},{1,257},{129... | collective-permute-start | bytes 884744 | tf_op jit(solution)/shard_map/ppermute | solution.py:19
  27.4 2.5 %collective-permute-start.2 = (bf16[576,256]{1,0:T(8,128)(2,1)S(1)}, bf16[576,256]{1,0:T(8,128)(2,1)S(1)}, u32[]{:S(2)}, u32[]{:S(2)}) collective-permute-start(bf16[576,256]{1,0:T(8,128)(2,1)S(1)} %get-tuple-element.10.refs_0_), channel_id=1, source_target_pairs={{384,0},{0,128},{128,256},{256,384},{385,1},{1,129},{129,257},{257... | collective-permute-start | bytes 884744 | tf_op jit(solution)/shard_map/ppermute | solution.py:19
  29.9 3.7 %collective-permute-start.3 = (bf16[576,256]{1,0:T(8,128)(2,1)S(1)}, bf16[576,256]{1,0:T(8,128)(2,1)S(1)}, u32[]{:S(2)}, u32[]{:S(2)}) collective-permute-start(bf16[576,256]{1,0:T(8,128)(2,1)S(1)} %get-tuple-element.10.refs_0_), channel_id=1, source_target_pairs={{1,0},{0,1},{3,2},{2,3},{5,4},{4,5},{7,6},{6,7},{9,8},{8,9},{11,10... | collective-permute-start | bytes 884744 | tf_op jit(solution)/shard_map/ppermute | solution.py:19
  33.7 6.8 %collective-permute-start.4 = (bf16[576,256]{1,0:T(8,128)(2,1)S(1)}, bf16[576,256]{1,0:T(8,128)(2,1)S(1)}, u32[]{:S(2)}, u32[]{:S(2)}) collective-permute-start(bf16[576,256]{1,0:T(8,128)(2,1)S(1)} %collective-permute-done.refs_1_), channel_id=1, source_target_pairs={{1,0},{0,1},{3,2},{2,3},{5,4},{4,5},{7,6},{6,7},{9,8},{8,9},{11,10... | collective-permute-start | bytes 884744 | tf_op jit(solution)/shard_map/ppermute | solution.py:19
  40.5 1.9 %collective-permute-start.5 = (bf16[576,256]{1,0:T(8,128)(2,1)S(1)}, bf16[576,256]{1,0:T(8,128)(2,1)S(1)}, u32[]{:S(2)}, u32[]{:S(2)}) collective-permute-start(bf16[576,256]{1,0:T(8,128)(2,1)S(1)} %collective-permute-done.1.refs_2_), channel_id=1, source_target_pairs={{1,0},{0,1},{3,2},{2,3},{5,4},{4,5},{7,6},{6,7},{9,8},{8,9},{11,10... | collective-permute-start | bytes 884744 | tf_op jit(solution)/shard_map/ppermute | solution.py:19
  42.4 1.3 %collective-permute-done.2.refs_3_ = bf16[576,256]{1,0:T(8,128)(2,1)S(1)} collective-permute-done((bf16[576,256]{1,0:T(8,128)(2,1)S(1)}, bf16[576,256]{1,0:T(8,128)(2,1)S(1)}, u32[]{:S(2)}, u32[]{:S(2)}) %collective-permute-start.2) | collective-permute-done | bytes 294944 | tf_op jit(solution)/shard_map/ppermute | solution.py:19
  43.6 2.4 %collective-permute-start.6 = (bf16[576,256]{1,0:T(8,128)(2,1)S(1)}, bf16[576,256]{1,0:T(8,128)(2,1)S(1)}, u32[]{:S(2)}, u32[]{:S(2)}) collective-permute-start(bf16[576,256]{1,0:T(8,128)(2,1)S(1)} %collective-permute-done.2.refs_3_), channel_id=1, source_target_pairs={{1,0},{0,1},{3,2},{2,3},{5,4},{4,5},{7,6},{6,7},{9,8},{8,9},{11,10... | collective-permute-start | bytes 884744 | tf_op jit(solution)/shard_map/ppermute | solution.py:19
  46.1 1.2 collective-permute-done.6.refs_7_
  47.2 4.9 %shard_map.56 = bf16[32,16,1152]{2,1,0:T(8,128)(2,1)} custom-call(s32[3]{0:T(128)S(1)} %pad_add_fusion.place, bf16[32,16,1024]{2,1,0:T(8,128)(2,1)S(1)} %all-to-all-done.packed_ref, bf16[576,256]{1,0:T(8,128)(2,1)S(1)} %get-tuple-element.10.refs_0_, bf16[576,256]{1,0:T(8,128)(2,1)S(1)} %collective-permute-done.refs_1_, ...), custom_call_target="tpu_custom_call" | custom-call | flops 1073741824 | bytes 3407884 | tf_op jit(solution)/shard_map/pallas_call | solution.py:24
  52.2 0.0 copy-start.7
  52.2 9.6 %all-to-all-start.1 = ((bf16[32,16,1152]{2,1,0:T(8,128)(2,1)}), bf16[32,16,1152]{2,1,0:T(8,128)(2,1)S(1)}, u32[]{:S(2)}, u32[]{:S(2)}) async-start(bf16[32,16,1152]{2,1,0:T(8,128)(2,1)} %shard_map.56), calls=%async_computation.1 | async-start | bytes 2359296 | tf_op jit(solution)/shard_map/all_to_all | solution.py:227
  61.8 27.9 %all-to-all-done.1.parts_ref = bf16[32,16,1152]{2,1,0:T(8,128)(2,1)S(1)} async-done(((bf16[32,16,1152]{2,1,0:T(8,128)(2,1)}), bf16[32,16,1152]{2,1,0:T(8,128)(2,1)S(1)}, u32[]{:S(2)}, u32[]{:S(2)}) %all-to-all-start.1) | async-done | bytes 1179680 | tf_op jit(solution)/shard_map/all_to_all | solution.py:227
  89.7 1.4 %shard_map.57 = (bf16[16,1024]{1,0:T(8,128)(2,1)S(1)}, bf16[64,16,128]{2,1,0:T(8,128)(2,1)}) custom-call(s32[3]{0:T(128)S(1)} %pad_add_fusion.place, f32[1,128]{1,0:T(1,128)S(1)} %pad.4.lens_ref, bf16[32,16,1152]{2,1,0:T(8,128)(2,1)S(1)} %all-to-all-done.1.parts_ref), custom_call_target="tpu_custom_call" | custom-call | flops 589824 | bytes 1180172 | tf_op jit(solution)/shard_map/pallas_call | solution.py:24
  91.1 9.9 %all-to-all-start.2 = ((bf16[64,16,128]{2,1,0:T(8,128)(2,1)}), bf16[64,16,128]{2,1,0:T(8,128)(2,1)S(1)}, u32[]{:S(2)}, u32[]{:S(2)}) async-start(bf16[64,16,128]{2,1,0:T(8,128)(2,1)} %get-tuple-element.11), calls=%async_computation.2 | async-start | bytes 524288 | tf_op jit(solution)/shard_map/all_to_all | solution.py:237
  101.0 4.1 %collective-permute-start.7 = (bf16[16,1024]{1,0:T(8,128)(2,1)S(1)}, bf16[16,1024]{1,0:T(8,128)(2,1)S(1)}, u32[]{:S(2)}, u32[]{:S(2)}) collective-permute-start(bf16[16,1024]{1,0:T(8,128)(2,1)S(1)} %get-tuple-element.12.piece0), channel_id=1, source_target_pairs={{128,0},{256,128},{384,256},{0,384},{129,1},{257,129},{385,257},{1... | collective-permute-start | bytes 98312 | tf_op jit(solution)/shard_map/ppermute | solution.py:19
  105.1 1.9 %collective-permute-start.8 = (bf16[16,1024]{1,0:T(8,128)(2,1)S(1)}, bf16[16,1024]{1,0:T(8,128)(2,1)S(1)}, u32[]{:S(2)}, u32[]{:S(2)}) collective-permute-start(bf16[16,1024]{1,0:T(8,128)(2,1)S(1)} %get-tuple-element.12.piece0), channel_id=1, source_target_pairs={{256,0},{384,128},{0,256},{128,384},{257,1},{385,129},{1,257},{129... | collective-permute-start | bytes 98312 | tf_op jit(solution)/shard_map/ppermute | solution.py:19
  107.0 2.5 %collective-permute-start.9 = (bf16[16,1024]{1,0:T(8,128)(2,1)S(1)}, bf16[16,1024]{1,0:T(8,128)(2,1)S(1)}, u32[]{:S(2)}, u32[]{:S(2)}) collective-permute-start(bf16[16,1024]{1,0:T(8,128)(2,1)S(1)} %get-tuple-element.12.piece0), channel_id=1, source_target_pairs={{384,0},{0,128},{128,256},{256,384},{385,1},{1,129},{129,257},{257... | collective-permute-start | bytes 98312 | tf_op jit(solution)/shard_map/ppermute | solution.py:19
  109.5 2.0 %collective-permute-done.8.piece2 = bf16[16,1024]{1,0:T(8,128)(2,1)S(1)} collective-permute-done((bf16[16,1024]{1,0:T(8,128)(2,1)S(1)}, bf16[16,1024]{1,0:T(8,128)(2,1)S(1)}, u32[]{:S(2)}, u32[]{:S(2)}) %collective-permute-start.8) | collective-permute-done | bytes 32800 | tf_op jit(solution)/shard_map/ppermute | solution.py:19
  111.5 1.6 %collective-permute-done.9.piece3 = bf16[16,1024]{1,0:T(8,128)(2,1)S(1)} collective-permute-done((bf16[16,1024]{1,0:T(8,128)(2,1)S(1)}, bf16[16,1024]{1,0:T(8,128)(2,1)S(1)}, u32[]{:S(2)}, u32[]{:S(2)}) %collective-permute-start.9) | collective-permute-done | bytes 32800 | tf_op jit(solution)/shard_map/ppermute | solution.py:19
  113.2 0.1 all-to-all-done.2.out_ref
  113.3 0.5 copy-done.6
  113.8 1.3 %shard_map.59 = f32[56,64]{1,0:T(8,128)S(1)} custom-call(s32[3]{0:T(128)S(1)} %pad_add_fusion.place, bf16[64,16,128]{2,1,0:T(8,128)(2,1)S(1)} %all-to-all-done.2.out_ref, bf16[16,1024]{1,0:T(8,128)(2,1)} %copy-done.2, bf16[16,1024]{1,0:T(8,128)(2,1)} %copy-done.4, bf16[16,1024]{1,0:T(8,128)(2,1)} %copy-done.5, bf16[16,1024]{1,0:T(8,128)(2,1)} %copy-done.6), custom_call_target="tpu_custom_call" | custom-call | flops 33554432 | bytes 393228 | tf_op jit(solution)/shard_map/pallas_call | solution.py:24
  115.1 7.9 %collective-permute-start.10 = (f32[56,64]{1,0:T(8,128)S(1)}, f32[56,64]{1,0:T(8,128)S(1)}, u32[]{:S(2)}, u32[]{:S(2)}) collective-permute-start(f32[56,64]{1,0:T(8,128)S(1)} %shard_map.59), channel_id=1, source_target_pairs={{64,0},{0,64},{65,1},{1,65},{66,2},{2,66},{67,3},{3,67},{68,4},{4,... | collective-permute-start | bytes 43016 | tf_op jit(solution)/shard_map/ppermute | solution.py:19
  123.0 1.3 %shard_map.58 = f32[56,64]{1,0:T(8,128)S(1)} custom-call(s32[3]{0:T(128)S(1)} %pad_add_fusion.place, bf16[64,16,128]{2,1,0:T(8,128)(2,1)S(1)} %all-to-all-done.2.out_ref, bf16[16,1024]{1,0:T(8,128)(2,1)} %copy-done.2, bf16[16,1024]{1,0:T(8,128)(2,1)} %copy-done.4, bf16[16,1024]{1,0:T(8,128)(2,1)} %copy-done.5, bf16[16,1024]{1,0:T(8,128)(2,1)} %copy-done.6), custom_call_target="tpu_custom_call" | custom-call | flops 33554432 | bytes 393228 | tf_op jit(solution)/shard_map/pallas_call | solution.py:24
  124.3 0.6 add_bitcast_fusion
  (21 shorter events, 0.1 us)
Async XLA Ops:
  0.1 0.9 copy-start
  1.0 0.9 copy-start.1
  1.9 0.8 copy-start.3
  7.1 40.1 %all-to-all-start = ((bf16[32,16,1024]{2,1,0:T(8,128)(2,1)}), bf16[32,16,1024]{2,1,0:T(8,128)(2,1)S(1)}, u32[]{:S(2)}, u32[]{:S(2)}) async-start(bf16[32,16,1024]{2,1,0:T(8,128)(2,1)} %get-tuple-element.9), calls=%async_computation | async-start | bytes 2097152 | tf_op jit(solution)/shard_map/all_to_all | solution.py:204
  20.6 13.1 %collective-permute-start = (bf16[576,256]{1,0:T(8,128)(2,1)S(1)}, bf16[576,256]{1,0:T(8,128)(2,1)S(1)}, u32[]{:S(2)}, u32[]{:S(2)}) collective-permute-start(bf16[576,256]{1,0:T(8,128)(2,1)S(1)} %get-tuple-element.10.refs_0_), channel_id=1, source_target_pairs={{128,0},{256,128},{384,256},{0,384},{129,1},{257,129},{385,257},{1... | collective-permute-start | bytes 884744 | tf_op jit(solution)/shard_map/ppermute | solution.py:19
  25.0 15.5 %collective-permute-start.1 = (bf16[576,256]{1,0:T(8,128)(2,1)S(1)}, bf16[576,256]{1,0:T(8,128)(2,1)S(1)}, u32[]{:S(2)}, u32[]{:S(2)}) collective-permute-start(bf16[576,256]{1,0:T(8,128)(2,1)S(1)} %get-tuple-element.10.refs_0_), channel_id=1, source_target_pairs={{256,0},{384,128},{0,256},{128,384},{257,1},{385,129},{1,257},{129... | collective-permute-start | bytes 884744 | tf_op jit(solution)/shard_map/ppermute | solution.py:19
  27.4 16.2 %collective-permute-start.2 = (bf16[576,256]{1,0:T(8,128)(2,1)S(1)}, bf16[576,256]{1,0:T(8,128)(2,1)S(1)}, u32[]{:S(2)}, u32[]{:S(2)}) collective-permute-start(bf16[576,256]{1,0:T(8,128)(2,1)S(1)} %get-tuple-element.10.refs_0_), channel_id=1, source_target_pairs={{384,0},{0,128},{128,256},{256,384},{385,1},{1,129},{129,257},{257... | collective-permute-start | bytes 884744 | tf_op jit(solution)/shard_map/ppermute | solution.py:19
  29.9 16.1 %collective-permute-start.3 = (bf16[576,256]{1,0:T(8,128)(2,1)S(1)}, bf16[576,256]{1,0:T(8,128)(2,1)S(1)}, u32[]{:S(2)}, u32[]{:S(2)}) collective-permute-start(bf16[576,256]{1,0:T(8,128)(2,1)S(1)} %get-tuple-element.10.refs_0_), channel_id=1, source_target_pairs={{1,0},{0,1},{3,2},{2,3},{5,4},{4,5},{7,6},{6,7},{9,8},{8,9},{11,10... | collective-permute-start | bytes 884744 | tf_op jit(solution)/shard_map/ppermute | solution.py:19
  33.7 12.4 %collective-permute-start.4 = (bf16[576,256]{1,0:T(8,128)(2,1)S(1)}, bf16[576,256]{1,0:T(8,128)(2,1)S(1)}, u32[]{:S(2)}, u32[]{:S(2)}) collective-permute-start(bf16[576,256]{1,0:T(8,128)(2,1)S(1)} %collective-permute-done.refs_1_), channel_id=1, source_target_pairs={{1,0},{0,1},{3,2},{2,3},{5,4},{4,5},{7,6},{6,7},{9,8},{8,9},{11,10... | collective-permute-start | bytes 884744 | tf_op jit(solution)/shard_map/ppermute | solution.py:19
  40.5 5.6 %collective-permute-start.5 = (bf16[576,256]{1,0:T(8,128)(2,1)S(1)}, bf16[576,256]{1,0:T(8,128)(2,1)S(1)}, u32[]{:S(2)}, u32[]{:S(2)}) collective-permute-start(bf16[576,256]{1,0:T(8,128)(2,1)S(1)} %collective-permute-done.1.refs_2_), channel_id=1, source_target_pairs={{1,0},{0,1},{3,2},{2,3},{5,4},{4,5},{7,6},{6,7},{9,8},{8,9},{11,10... | collective-permute-start | bytes 884744 | tf_op jit(solution)/shard_map/ppermute | solution.py:19
  43.6 3.6 %collective-permute-start.6 = (bf16[576,256]{1,0:T(8,128)(2,1)S(1)}, bf16[576,256]{1,0:T(8,128)(2,1)S(1)}, u32[]{:S(2)}, u32[]{:S(2)}) collective-permute-start(bf16[576,256]{1,0:T(8,128)(2,1)S(1)} %collective-permute-done.2.refs_3_), channel_id=1, source_target_pairs={{1,0},{0,1},{3,2},{2,3},{5,4},{4,5},{7,6},{6,7},{9,8},{8,9},{11,10... | collective-permute-start | bytes 884744 | tf_op jit(solution)/shard_map/ppermute | solution.py:19
  52.2 9.6 %copy-start.7 = (s32[1,4]{1,0:T(1,128)S(1)}, s32[1,4]{1,0:T(1,128)}, u32[]{:S(2)}) copy-start(s32[1,4]{1,0:T(1,128)} %param.9) | copy-start | bytes 52
  52.2 37.5 %all-to-all-start.1 = ((bf16[32,16,1152]{2,1,0:T(8,128)(2,1)}), bf16[32,16,1152]{2,1,0:T(8,128)(2,1)S(1)}, u32[]{:S(2)}, u32[]{:S(2)}) async-start(bf16[32,16,1152]{2,1,0:T(8,128)(2,1)} %shard_map.56), calls=%async_computation.1 | async-start | bytes 2359296 | tf_op jit(solution)/shard_map/all_to_all | solution.py:227
  91.1 22.1 %copy-start.2 = (bf16[16,1024]{1,0:T(8,128)(2,1)}, bf16[16,1024]{1,0:T(8,128)(2,1)S(1)}, u32[]{:S(2)}) copy-start(bf16[16,1024]{1,0:T(8,128)(2,1)S(1)} %get-tuple-element.12.piece0) | copy-start | bytes 98308
  91.1 22.1 %all-to-all-start.2 = ((bf16[64,16,128]{2,1,0:T(8,128)(2,1)}), bf16[64,16,128]{2,1,0:T(8,128)(2,1)S(1)}, u32[]{:S(2)}, u32[]{:S(2)}) async-start(bf16[64,16,128]{2,1,0:T(8,128)(2,1)} %get-tuple-element.11), calls=%async_computation.2 | async-start | bytes 524288 | tf_op jit(solution)/shard_map/all_to_all | solution.py:237
  101.0 8.5 %collective-permute-start.7 = (bf16[16,1024]{1,0:T(8,128)(2,1)S(1)}, bf16[16,1024]{1,0:T(8,128)(2,1)S(1)}, u32[]{:S(2)}, u32[]{:S(2)}) collective-permute-start(bf16[16,1024]{1,0:T(8,128)(2,1)S(1)} %get-tuple-element.12.piece0), channel_id=1, source_target_pairs={{128,0},{256,128},{384,256},{0,384},{129,1},{257,129},{385,257},{1... | collective-permute-start | bytes 98312 | tf_op jit(solution)/shard_map/ppermute | solution.py:19
  105.1 6.5 %collective-permute-start.8 = (bf16[16,1024]{1,0:T(8,128)(2,1)S(1)}, bf16[16,1024]{1,0:T(8,128)(2,1)S(1)}, u32[]{:S(2)}, u32[]{:S(2)}) collective-permute-start(bf16[16,1024]{1,0:T(8,128)(2,1)S(1)} %get-tuple-element.12.piece0), channel_id=1, source_target_pairs={{256,0},{384,128},{0,256},{128,384},{257,1},{385,129},{1,257},{129... | collective-permute-start | bytes 98312 | tf_op jit(solution)/shard_map/ppermute | solution.py:19
  107.0 6.2 %collective-permute-start.9 = (bf16[16,1024]{1,0:T(8,128)(2,1)S(1)}, bf16[16,1024]{1,0:T(8,128)(2,1)S(1)}, u32[]{:S(2)}, u32[]{:S(2)}) collective-permute-start(bf16[16,1024]{1,0:T(8,128)(2,1)S(1)} %get-tuple-element.12.piece0), channel_id=1, source_target_pairs={{384,0},{0,128},{128,256},{256,384},{385,1},{1,129},{129,257},{257... | collective-permute-start | bytes 98312 | tf_op jit(solution)/shard_map/ppermute | solution.py:19
  109.5 3.8 %copy-start.4 = (bf16[16,1024]{1,0:T(8,128)(2,1)}, bf16[16,1024]{1,0:T(8,128)(2,1)S(1)}, u32[]{:S(2)}) copy-start(bf16[16,1024]{1,0:T(8,128)(2,1)S(1)} %collective-permute-done.7.piece1) | copy-start | bytes 98308
  111.5 1.8 %copy-start.5 = (bf16[16,1024]{1,0:T(8,128)(2,1)}, bf16[16,1024]{1,0:T(8,128)(2,1)S(1)}, u32[]{:S(2)}) copy-start(bf16[16,1024]{1,0:T(8,128)(2,1)S(1)} %collective-permute-done.8.piece2) | copy-start | bytes 98308
  113.2 0.6 copy-start.6
  115.1 9.2 %collective-permute-start.10 = (f32[56,64]{1,0:T(8,128)S(1)}, f32[56,64]{1,0:T(8,128)S(1)}, u32[]{:S(2)}, u32[]{:S(2)}) collective-permute-start(f32[56,64]{1,0:T(8,128)S(1)} %shard_map.59), channel_id=1, source_target_pairs={{64,0},{0,64},{65,1},{1,65},{66,2},{2,66},{67,3},{3,67},{68,4},{4,... | collective-permute-start | bytes 43016 | tf_op jit(solution)/shard_map/ppermute | solution.py:19

commit v3 on v2

v3 whole, which is shorter than its diff:
```python
import functools

import jax
import jax.numpy as jnp
from jax import lax
from jax.experimental import pallas as pl
from jax.experimental.pallas import tpu as pltpu
from jax.sharding import Mesh, PartitionSpec as P

NX, NZH, NZL, NY, NC = 4, 2, 4, 8, 2
CHIPS = NZL * NY
BF16, F32 = jnp.bfloat16, jnp.float32
SMEM = pl.BlockSpec(memory_space=pltpu.SMEM)
VMEM = pl.BlockSpec(memory_space=pltpu.VMEM)
ANY = pl.BlockSpec(memory_space=pl.ANY)


def from_offset(value, axis, size, offset):
    return lax.ppermute(value, axis, [((i + offset) % size, i) for i in range(size)])


def call(kernel, shapes, scratch, operands, flops, in_specs=None, out_spec=VMEM):
    size = sum(a.size * a.dtype.itemsize for a in operands)
    return pl.pallas_call(
        kernel,
        out_shape=shapes,
        in_specs=in_specs or [SMEM] + [VMEM] * (len(operands) - 1),
        out_specs=jax.tree.map(lambda _: out_spec, shapes),
        scratch_shapes=scratch,
        compiler_params=pltpu.CompilerParams(vmem_limit_bytes=40 << 20),
        cost_estimate=pl.CostEstimate(flops=flops, bytes_accessed=size, transcendentals=0),
    )(*operands)


def in_vmem(value):
    return pltpu.with_memory_space_constraint(value, pltpu.VMEM)


def from_hbm(value):
    return pltpu.with_memory_space_constraint(value, pltpu.HBM)


def in_hbm(shape):
    return pltpu.HBM(shape, BF16)


def pack(place, basis_ref, out_rows_ref, acts_ref, grads_ref, packed_ref, payload_ref):
    width = basis_ref.shape[1] // packed_ref.shape[0]
    fout = grads_ref.shape[1]
    for x in range(NX):

        @pl.when(place[0] == x)
        def _():
            for c in range(packed_ref.shape[0]):
                rows = basis_ref[:, c * width : (c + 1) * width].astype(F32)[x * 14 : (x + 1) * 14]
                rows = jnp.concatenate([rows, jnp.zeros((2, width), F32)], axis=0)
                packed_ref[c, :, :width] = rows.astype(BF16)

    for c in range(packed_ref.shape[0]):
        out = out_rows_ref[:, c * NC * fout : (c + 1) * NC * fout].astype(F32)
        packed_ref[c, :, width:] = jnp.concatenate([out[:, :fout], out[:, fout:]], axis=0).astype(BF16)

    @pl.when(pl.program_id(0) == 0)
    def _():
        fin = acts_ref.shape[0]
        payload_ref[:fin, :] = acts_ref[...]
        payload_ref[fin:, :] = grads_ref[...].astype(F32).T.astype(BF16)


def project(place, packed_ref, *refs):
    own, other, parts_ref = refs[:NX], refs[NX : 2 * NX], refs[2 * NX]
    acts, grads, wide, low, *outs, sems = refs[2 * NX + 1 :]
    x, core = place[0], place[2]
    fin = acts.shape[0] // NC
    fout = grads.shape[1]
    tokens, height = acts.shape[1], CHIPS * 16
    left = packed_ref[:, :, : NC * fin].reshape(height, NC * fin)
    rows_out = packed_ref[pl.ds(x * 8, 8), :, NC * fin :].astype(F32).reshape(8, NC, 8, fout)
    rows_out = [rows_out[:, c].reshape(64, fout).astype(BF16) for c in range(NC)]
    results = []
    for s in range(NX):
        cols = slice(s * 256, (s + 1) * 256)
        for pieces, which in ((own, core), (other, 1 - core)):
            acts[pl.ds(pl.multiple_of(which * fin, 16), fin), cols] = pieces[s][:fin, :]
            grads[which, :, cols] = pieces[s][fin:, :]
        part = jnp.dot(left, acts[:, cols], preferred_element_type=F32)
        out = jnp.zeros((64, 256), F32)
        for c in range(NC):
            out += jnp.dot(rows_out[c], grads[c, :, cols], preferred_element_type=F32)
        rest = out - out.astype(BF16).astype(F32)
        for h in range(2):
            block = slice(h * 128, (h + 1) * 128)
            wide[pl.ds(h * height, height), :] = part[:, block]
            for half in range(2):
                wide[pl.ds(h * height + 14 + half, CHIPS, stride=16), :] = out[half * 32 : half * 32 + 32, block]
                low[pl.ds(half * 8 + s * 2 + h, CHIPS, stride=16), :] = rest[half * 32 : half * 32 + 32, block]
            outs[s][:, :, block] = wide[h * height : (h + 1) * height].astype(BF16).reshape(CHIPS, 16, 128)
        results.append(pltpu.make_async_copy(outs[s], parts_ref.at[:, :, pl.ds(s * 256, 256)], sems.at[s]))
        results[-1].start()
    outs[NX][...] = low[...].astype(BF16).reshape(CHIPS, 16, 128)
    results.append(pltpu.make_async_copy(outs[NX], parts_ref.at[:, :, pl.ds(tokens, 128)], sems.at[NX]))
    results[-1].start()
    for result in results:
        result.wait()


def add_up(place, lens_ref, parts_ref, in_ref, out_ref, wide, narrow):
    x = place[0]
    tokens = wide.shape[1]
    total = parts_ref[0].astype(F32)
    for i in range(1, CHIPS):
        total = total + parts_ref[i].astype(F32)
    for s in range(NX):
        source = lax.rem(x + s, NX)
        wide[:, pl.ds(pl.multiple_of(source * 256, 256), 256)] = total[:, s * 256 : (s + 1) * 256]
        for half in range(2):
            for h in range(2):
                col, row = s * 2 + h, half * 8 + s * 2 + h
                value = total[14 + half : 15 + half, col * 128 : (col + 1) * 128] + total[row : row + 1, tokens:]
                narrow[pl.ds(half * 8 + source * 2 + h, 1), :] = value
    wide[14:15, :128] = lens_ref[...]
    in_ref[...] = wide[...].astype(BF16)
    rows = narrow[...]
    for half in range(NZH):
        row = rows[half * 8 : half * 8 + 8].astype(BF16)
        out_ref[half * 64 : (half + 1) * 64] = jnp.broadcast_to(row[None], (64, 8, 128))


def documents(place, out_ref, *refs):
    pieces, (total_ref, rows_in, rows_out, sems) = refs[:NX], refs[NX:]
    x, zh = place[0], place[1]
    copies = []
    for s in range(NX):
        for half in range(NZH):
            there = rows_in.at[lax.rem(x + s, NX), lax.rem(half + zh, NZH)]
            copies.append(pltpu.make_async_copy(pieces[s].at[half], there, sems.at[s * NZH + half]))
            copies[-1].start()
    rows_out[...] = out_ref[...].astype(F32).reshape(128 * 8, 128)
    position = lax.broadcasted_iota(jnp.int32, (1, 256), 1).astype(F32)
    for copy in copies:
        copy.wait()
    total = jnp.zeros((NX * 16, 64), F32)
    for half in range(NZH):
        for g in range(NX):
            left = rows_in[:, half, :, g * 256 : (g + 1) * 256].astype(F32).reshape(NX * 16, 256)
            lens = rows_in[g, half, :, :128].astype(F32)[14:15, :4]
            right = []
            for h in range(2):
                cut = [
                    rows_out[pl.ds((half * 64 + zl * 16 + core) * 8 + g * 2 + h, NY, stride=16), :]
                    for zl in range(NZL)
                    for core in range(NC)
                ]
                right.append(jnp.concatenate(cut, axis=0))
            right = jnp.concatenate(right, axis=1).astype(BF16)
            masked, start = [], jnp.zeros((1, 1), F32)
            for d in range(4):
                end = start + lens[:, d : d + 1]
                inside = (position >= start) & (position < end)
                masked.append(jnp.where(inside, left, 0.0).astype(BF16))
                start = end
            product = lax.dot_general(
                jnp.concatenate(masked, axis=0), right, (((1,), (1,)), ((), ())), preferred_element_type=F32
            )
            for d in range(4):
                one = product[d * 64 : (d + 1) * 64]
                total = total + one * one
    total = total * (1.0 / 2048.0)
    for i in range(NX):
        total_ref[i * 14 : (i + 1) * 14, :] = total[i * 16 : i * 16 + 14]


def body(acts, grads, basis_in, basis_out, doc_lengths):
    x, zh, core = lax.axis_index("x"), lax.axis_index("zh"), lax.axis_index("core")
    place = jnp.stack([x, zh, core]).astype(jnp.int32)
    tok, fin = acts.shape
    fout = grads.shape[1]
    rows = basis_in.shape[0] // NX
    tokens = NX * tok

    steps = 4
    packed, payload = pl.pallas_call(
        pack,
        out_shape=(in_hbm((CHIPS, 16, NC * (fin + fout // 2))), jax.ShapeDtypeStruct((fin + fout, tok), BF16)),
        grid=(steps,),
        in_specs=[
            SMEM,
            pl.BlockSpec((4 * rows, CHIPS * NC * fin // steps), lambda i: (0, i)),
            pl.BlockSpec((8, CHIPS * NC * fout // steps), lambda i: (0, i)),
            pl.BlockSpec((fin, tok), lambda i: (0, 0)),
            pl.BlockSpec((tok, fout), lambda i: (0, 0)),
        ],
        out_specs=(
            pl.BlockSpec((CHIPS // steps, 16, NC * (fin + fout // 2)), lambda i: (i, 0, 0)),
            pl.BlockSpec((fin + fout, tok), lambda i: (0, 0)),
        ),
        compiler_params=pltpu.CompilerParams(vmem_limit_bytes=40 << 20),
        cost_estimate=pl.CostEstimate(flops=1 << 26, bytes_accessed=5 << 20, transcendentals=0),
    )(place, *map(from_hbm, (basis_in, basis_out, acts.T, grads)))
    packed = lax.all_to_all(packed, ("zl", "y"), split_axis=0, concat_axis=0, tiled=True)

    own = [payload] + [from_offset(payload, "x", NX, s) for s in range(1, NX)]
    other = [from_offset(v, "core", NC, 1) for v in own]

    parts = call(
        project,
        in_hbm((CHIPS, 16, tokens + 128)),
        [
            pltpu.VMEM((NC * fin, tokens), BF16),
            pltpu.VMEM((NC, fout, tokens), BF16),
            pltpu.VMEM((2 * CHIPS * 16, 128), F32),
            pltpu.VMEM((CHIPS * 16, 128), F32),
            *[pltpu.VMEM((CHIPS, 16, 256), BF16)] * NX,
            pltpu.VMEM((CHIPS, 16, 128), BF16),
            pltpu.SemaphoreType.DMA((5,)),
        ],
        (place, *map(in_vmem, (packed, *own, *other))),
        2 * 512 * 1024 * 1024,
        out_spec=ANY,
    )
    parts = lax.all_to_all(parts, ("zl", "y"), split_axis=0, concat_axis=0, tiled=True)
    lens = jnp.pad(doc_lengths.astype(F32), ((0, 0), (0, 124)))
    proj_in, proj_out = call(
        add_up,
        (jax.ShapeDtypeStruct((16, tokens), BF16), in_hbm((128, 8, 128))),
        [pltpu.VMEM((16, tokens), F32), pltpu.VMEM((16, 128), F32)],
        (place, lens, in_vmem(parts)),
        32 * 16 * 1152,
    )

    pair = jnp.stack([proj_in, from_offset(proj_in, "zh", NZH, 1)])
    proj_out = lax.all_to_all(proj_out, ("zh", "zl", "y", "core"), split_axis=0, concat_axis=0, tiled=True)
    pieces = [pair] + [from_offset(pair, "x", NX, s) for s in range(1, NX)]
    total = call(
        documents,
        jax.ShapeDtypeStruct((NX * rows, 64), F32),
        [
            pltpu.VMEM((NX, NZH, 16, tokens), BF16),
            pltpu.VMEM((128 * 8, 128), F32),
            pltpu.SemaphoreType.DMA((NX * NZH,)),
        ],
        (place, in_vmem(proj_out), *pieces),
        2 * 8 * 256 * 256 * 64,
        in_specs=[SMEM, VMEM] + [ANY] * NX,
    )
    return total.T


def solution(mesh):
    fine = Mesh(mesh.devices.reshape(NX, NZH, NZL, NY, NC), ("x", "zh", "zl", "y", "core"))
    dp, mp = ("x", "zh"), ("zl", "y", "core")
    in_specs = (P(dp, mp), P(dp, mp), P(mp, None), P(mp, None), P(dp, None))
    return jax.shard_map(body, mesh=fine, in_specs=in_specs, out_specs=P(dp, mp), check_vma=False)
```

time: 127 us -> 131 us (1.031)
  the two profiles are of different devices: /device:TPU:1 before, /device:TPU:64 now
where the time goes in v3:
time: 131 us
  starting transfers between devices  71.1 us (54%)
  waiting for transfers between devices  48.5 us (37%)
  Pallas kernels  10.9 us (8%)
    ppermute x11, starting transfers between devices, from_offset(): lax.ppermute(value, axis, [((i + offset) % size, i) for i in range(size)])  34.9 us
    all_to_all x1, waiting for transfers between devices, body(): lax.all_to_all(parts, ('zl', 'y'), split_axis=0, concat_axis=0, tiled=True)  29.1 us
    ppermute x11, waiting for transfers between devices, from_offset(): lax.ppermute(value, axis, [((i + offset) % size, i) for i in range(size)])  19.2 us
    all_to_all x1, starting transfers between devices, body(): lax.all_to_all(proj_out, ('zh', 'zl', 'y', 'core'), split_axis=0, concat_...  14 us
    all_to_all x1, starting transfers between devices, body(): lax.all_to_all(packed, ('zl', 'y'), split_axis=0, concat_axis=0, tiled=True)  12.3 us
    all_to_all x1, starting transfers between devices, body(): lax.all_to_all(parts, ('zl', 'y'), split_axis=0, concat_axis=0, tiled=True)  9.89 us
    pallas_call x3, Pallas kernels, call(): pl.pallas_call(kernel, out_shape=shapes, in_specs=in_specs or [SMEM] + [V...  6.83 us
    pallas_call x1, Pallas kernels, body(): pl.pallas_call(pack, out_shape=(in_hbm((CHIPS, 16, NC * (fin + fout // 2)...  4.04 us
  transfers between devices with their start and end apart: 14, of which 7 were waited for; matrix products, arithmetic and copies ran while one was open for 0% of the time, Pallas kernels for 0%

profile of v3, /device:TPU:64, one launch (start us, length us, event | category | flops | bytes accessed | tf_op | source)
XLA Modules:
  0.0 130.8 jit_solution(7859438978368747021)
XLA Ops:
  0.0 0.1 pad_add_fusion.place
  0.1 4.0 %shard_map.55 = (bf16[32,16,1024]{2,1,0:T(8,128)(2,1)}, bf16[576,256]{1,0:T(8,128)(2,1)S(1)}) custom-call(s32[3]{0:T(128)S(1)} %pad_add_fusion.place, bf16[56,28672]{1,0:T(8,128)(2,1)} %basis_ref.1, bf16[8,8192]{1,0:T(8,128)(2,1)} %out_rows_ref.1, bf16[448,256]{1,0:T(8,128)(2,1)} %bitcast.8, bf16[256,128]{1,0:T(8,128)(2,1)} %grads_ref.1), custom_call_target="tpu_custom_call" | custom-call | flops 67108864 | bytes 5242880 | tf_op jit(solution)/shard_map/pallas_call | solution.py:182
  4.1 12.3 %all-to-all-start = ((bf16[32,16,1024]{2,1,0:T(8,128)(2,1)}), bf16[32,16,1024]{2,1,0:T(8,128)(2,1)S(1)}, u32[]{:S(2)}, u32[]{:S(2)}) async-start(bf16[32,16,1024]{2,1,0:T(8,128)(2,1)} %get-tuple-element.9), calls=%async_computation | async-start | bytes 2097152 | tf_op jit(solution)/shard_map/all_to_all | solution.py:200
  16.5 4.7 %collective-permute-start = (bf16[576,256]{1,0:T(8,128)(2,1)S(1)}, bf16[576,256]{1,0:T(8,128)(2,1)S(1)}, u32[]{:S(2)}, u32[]{:S(2)}) collective-permute-start(bf16[576,256]{1,0:T(8,128)(2,1)S(1)} %get-tuple-element.10.refs_0_), channel_id=1, source_target_pairs={{128,0},{256,128},{384,256},{0,384},{129,1},{257,129},{385,257},{1... | collective-permute-start | bytes 884744 | tf_op jit(solution)/shard_map/ppermute | solution.py:19
  21.2 2.8 %collective-permute-start.1 = (bf16[576,256]{1,0:T(8,128)(2,1)S(1)}, bf16[576,256]{1,0:T(8,128)(2,1)S(1)}, u32[]{:S(2)}, u32[]{:S(2)}) collective-permute-start(bf16[576,256]{1,0:T(8,128)(2,1)S(1)} %get-tuple-element.10.refs_0_), channel_id=1, source_target_pairs={{256,0},{384,128},{0,256},{128,384},{257,1},{385,129},{1,257},{129... | collective-permute-start | bytes 884744 | tf_op jit(solution)/shard_map/ppermute | solution.py:19
  24.0 2.8 %collective-permute-start.2 = (bf16[576,256]{1,0:T(8,128)(2,1)S(1)}, bf16[576,256]{1,0:T(8,128)(2,1)S(1)}, u32[]{:S(2)}, u32[]{:S(2)}) collective-permute-start(bf16[576,256]{1,0:T(8,128)(2,1)S(1)} %get-tuple-element.10.refs_0_), channel_id=1, source_target_pairs={{384,0},{0,128},{128,256},{256,384},{385,1},{1,129},{129,257},{257... | collective-permute-start | bytes 884744 | tf_op jit(solution)/shard_map/ppermute | solution.py:19
  26.8 1.9 %collective-permute-start.3 = (bf16[576,256]{1,0:T(8,128)(2,1)S(1)}, bf16[576,256]{1,0:T(8,128)(2,1)S(1)}, u32[]{:S(2)}, u32[]{:S(2)}) collective-permute-start(bf16[576,256]{1,0:T(8,128)(2,1)S(1)} %get-tuple-element.10.refs_0_), channel_id=1, source_target_pairs={{1,0},{0,1},{3,2},{2,3},{5,4},{4,5},{7,6},{6,7},{9,8},{8,9},{11,10... | collective-permute-start | bytes 884744 | tf_op jit(solution)/shard_map/ppermute | solution.py:19
  28.7 4.5 %collective-permute-done.refs_1_ = bf16[576,256]{1,0:T(8,128)(2,1)S(1)} collective-permute-done((bf16[576,256]{1,0:T(8,128)(2,1)S(1)}, bf16[576,256]{1,0:T(8,128)(2,1)S(1)}, u32[]{:S(2)}, u32[]{:S(2)}) %collective-permute-start) | collective-permute-done | bytes 294944 | tf_op jit(solution)/shard_map/ppermute | solution.py:19
  33.2 1.9 %collective-permute-start.4 = (bf16[576,256]{1,0:T(8,128)(2,1)S(1)}, bf16[576,256]{1,0:T(8,128)(2,1)S(1)}, u32[]{:S(2)}, u32[]{:S(2)}) collective-permute-start(bf16[576,256]{1,0:T(8,128)(2,1)S(1)} %collective-permute-done.refs_1_), channel_id=1, source_target_pairs={{1,0},{0,1},{3,2},{2,3},{5,4},{4,5},{7,6},{6,7},{9,8},{8,9},{11,10... | collective-permute-start | bytes 884744 | tf_op jit(solution)/shard_map/ppermute | solution.py:19
  35.1 0.0 collective-permute-done.1.refs_2_
  35.1 2.4 %collective-permute-start.5 = (bf16[576,256]{1,0:T(8,128)(2,1)S(1)}, bf16[576,256]{1,0:T(8,128)(2,1)S(1)}, u32[]{:S(2)}, u32[]{:S(2)}) collective-permute-start(bf16[576,256]{1,0:T(8,128)(2,1)S(1)} %collective-permute-done.1.refs_2_), channel_id=1, source_target_pairs={{1,0},{0,1},{3,2},{2,3},{5,4},{4,5},{7,6},{6,7},{9,8},{8,9},{11,10... | collective-permute-start | bytes 884744 | tf_op jit(solution)/shard_map/ppermute | solution.py:19
  37.5 1.3 collective-permute-done.2.refs_3_
  38.8 1.9 %collective-permute-start.6 = (bf16[576,256]{1,0:T(8,128)(2,1)S(1)}, bf16[576,256]{1,0:T(8,128)(2,1)S(1)}, u32[]{:S(2)}, u32[]{:S(2)}) collective-permute-start(bf16[576,256]{1,0:T(8,128)(2,1)S(1)} %collective-permute-done.2.refs_3_), channel_id=1, source_target_pairs={{1,0},{0,1},{3,2},{2,3},{5,4},{4,5},{7,6},{6,7},{9,8},{8,9},{11,10... | collective-permute-start | bytes 884744 | tf_op jit(solution)/shard_map/ppermute | solution.py:19
  40.7 0.0 collective-permute-done.3.refs_4_
  40.8 0.0 collective-permute-done.5.refs_6_
  40.8 1.5 %collective-permute-done.6.refs_7_ = bf16[576,256]{1,0:T(8,128)(2,1)S(1)} collective-permute-done((bf16[576,256]{1,0:T(8,128)(2,1)S(1)}, bf16[576,256]{1,0:T(8,128)(2,1)S(1)}, u32[]{:S(2)}, u32[]{:S(2)}) %collective-permute-start.6) | collective-permute-done | bytes 294944 | tf_op jit(solution)/shard_map/ppermute | solution.py:19
  42.3 0.3 all-to-all-done.packed_ref
  42.5 3.2 %shard_map.56 = bf16[32,16,1152]{2,1,0:T(8,128)(2,1)} custom-call(s32[3]{0:T(128)S(1)} %pad_add_fusion.place, bf16[32,16,1024]{2,1,0:T(8,128)(2,1)S(1)} %all-to-all-done.packed_ref, bf16[576,256]{1,0:T(8,128)(2,1)S(1)} %get-tuple-element.10.refs_0_, bf16[576,256]{1,0:T(8,128)(2,1)S(1)} %collective-permute-done.refs_1_, ...), custom_call_target="tpu_custom_call" | custom-call | flops 1073741824 | bytes 3407884 | tf_op jit(solution)/shard_map/pallas_call | solution.py:24
  45.8 0.0 copy-start
  45.8 9.9 %all-to-all-start.1 = ((bf16[32,16,1152]{2,1,0:T(8,128)(2,1)}), bf16[32,16,1152]{2,1,0:T(8,128)(2,1)S(1)}, u32[]{:S(2)}, u32[]{:S(2)}) async-start(bf16[32,16,1152]{2,1,0:T(8,128)(2,1)} %shard_map.56), calls=%async_computation.1 | async-start | bytes 2359296 | tf_op jit(solution)/shard_map/all_to_all | solution.py:221
  55.7 29.1 %all-to-all-done.1.parts_ref = bf16[32,16,1152]{2,1,0:T(8,128)(2,1)S(1)} async-done(((bf16[32,16,1152]{2,1,0:T(8,128)(2,1)}), bf16[32,16,1152]{2,1,0:T(8,128)(2,1)S(1)}, u32[]{:S(2)}, u32[]{:S(2)}) %all-to-all-start.1) | async-done | bytes 1179680 | tf_op jit(solution)/shard_map/all_to_all | solution.py:221
  84.8 1.4 %shard_map.57 = (bf16[16,1024]{1,0:T(8,128)(2,1)S(1)}, bf16[128,8,128]{2,1,0:T(8,128)(2,1)}) custom-call(s32[3]{0:T(128)S(1)} %pad_add_fusion.place, f32[1,128]{1,0:T(1,128)S(1)} %pad.4.lens_ref, bf16[32,16,1152]{2,1,0:T(8,128)(2,1)S(1)} %all-to-all-done.1.parts_ref), custom_call_target="tpu_custom_call" | custom-call | flops 589824 | bytes 1180172 | tf_op jit(solution)/shard_map/pallas_call | solution.py:24
  86.2 14.0 %all-to-all-start.2 = ((bf16[128,8,128]{2,1,0:T(8,128)(2,1)}), bf16[128,8,128]{2,1,0:T(8,128)(2,1)S(1)}, u32[]{:S(2)}, u32[]{:S(2)}) async-start(bf16[128,8,128]{2,1,0:T(8,128)(2,1)} %get-tuple-element.11), calls=%async_computation.2 | async-start | bytes 524288 | tf_op jit(solution)/shard_map/all_to_all | solution.py:232
  100.2 6.8 %collective-permute-start.7 = (bf16[16,1024]{1,0:T(8,128)(2,1)S(1)}, bf16[16,1024]{1,0:T(8,128)(2,1)S(1)}, u32[]{:S(2)}, u32[]{:S(2)}) collective-permute-start(bf16[16,1024]{1,0:T(8,128)(2,1)S(1)} %get-tuple-element.12), channel_id=1, source_target_pairs={{64,0},{0,64},{65,1},{1,65},{66,2},{2,66},{67,3},{3,67},{68,4},{4,... | collective-permute-start | bytes 98312 | tf_op jit(solution)/shard_map/ppermute | solution.py:19
  107.0 6.8 %collective-permute-done.7 = bf16[16,1024]{1,0:T(8,128)(2,1)S(1)} collective-permute-done((bf16[16,1024]{1,0:T(8,128)(2,1)S(1)}, bf16[16,1024]{1,0:T(8,128)(2,1)S(1)}, u32[]{:S(2)}, u32[]{:S(2)}) %collective-permute-start.7) | collective-permute-done | bytes 32800 | tf_op jit(solution)/shard_map/ppermute | solution.py:19
  113.8 1.9 %collective-permute-start.10 = (bf16[2,16,1024]{2,1,0:T(8,128)(2,1)S(1)}, bf16[2,16,1024]{2,1,0:T(8,128)(2,1)S(1)}, u32[]{:S(2)}, u32[]{:S(2)}) collective-permute-start(bf16[2,16,1024]{2,1,0:T(8,128)(2,1)S(1)} %pad_maximum_fusion.refs_0_), channel_id=1, source_target_pairs={{384,0},{0,128},{128,256},{256,384},{385,1},{1,129},{129,257},{257... | collective-permute-start | bytes 196616 | tf_op jit(solution)/shard_map/ppermute | solution.py:19
  115.7 5.1 %collective-permute-start.8 = (bf16[2,16,1024]{2,1,0:T(8,128)(2,1)S(1)}, bf16[2,16,1024]{2,1,0:T(8,128)(2,1)S(1)}, u32[]{:S(2)}, u32[]{:S(2)}) collective-permute-start(bf16[2,16,1024]{2,1,0:T(8,128)(2,1)S(1)} %pad_maximum_fusion.refs_0_), channel_id=1, source_target_pairs={{128,0},{256,128},{384,256},{0,384},{129,1},{257,129},{385,257},{1... | collective-permute-start | bytes 196616 | tf_op jit(solution)/shard_map/ppermute | solution.py:19
  120.9 2.6 %collective-permute-start.9 = (bf16[2,16,1024]{2,1,0:T(8,128)(2,1)S(1)}, bf16[2,16,1024]{2,1,0:T(8,128)(2,1)S(1)}, u32[]{:S(2)}, u32[]{:S(2)}) collective-permute-start(bf16[2,16,1024]{2,1,0:T(8,128)(2,1)S(1)} %pad_maximum_fusion.refs_0_), channel_id=1, source_target_pairs={{256,0},{384,128},{0,256},{128,384},{257,1},{385,129},{1,257},{129... | collective-permute-start | bytes 196616 | tf_op jit(solution)/shard_map/ppermute | solution.py:19
  123.5 0.0 collective-permute-done.10.refs_3_
  123.5 5.0 %collective-permute-done.9.refs_2_ = bf16[2,16,1024]{2,1,0:T(8,128)(2,1)S(1)} collective-permute-done((bf16[2,16,1024]{2,1,0:T(8,128)(2,1)S(1)}, bf16[2,16,1024]{2,1,0:T(8,128)(2,1)S(1)}, u32[]{:S(2)}, u32[]{:S(2)}) %collective-permute-start.9) | collective-permute-done | bytes 65568 | tf_op jit(solution)/shard_map/ppermute | solution.py:19
  128.5 0.0 all-to-all-done.2.out_ref
  128.5 2.2 %shard_map.58 = f32[56,64]{1,0:T(8,128)} custom-call(s32[3]{0:T(128)S(1)} %pad_add_fusion.place, bf16[128,8,128]{2,1,0:T(8,128)(2,1)S(1)} %all-to-all-done.2.out_ref, bf16[2,16,1024]{2,1,0:T(8,128)(2,1)S(1)} %pad_maximum_fusion.refs_0_, bf16[2,16,1024]{2,1,0:T(8,128)(2,1)S(1)} %collective-permute-done.8.refs_1_, ...), custom_call_target="tpu_custom_call" | custom-call | flops 67108864 | bytes 524300 | tf_op jit(solution)/shard_map/pallas_call | solution.py:24
  (6 shorter events, 0.0 us)
Async XLA Ops:
  4.1 38.4 %all-to-all-start = ((bf16[32,16,1024]{2,1,0:T(8,128)(2,1)}), bf16[32,16,1024]{2,1,0:T(8,128)(2,1)S(1)}, u32[]{:S(2)}, u32[]{:S(2)}) async-start(bf16[32,16,1024]{2,1,0:T(8,128)(2,1)} %get-tuple-element.9), calls=%async_computation | async-start | bytes 2097152 | tf_op jit(solution)/shard_map/all_to_all | solution.py:200
  16.5 16.7 %collective-permute-start = (bf16[576,256]{1,0:T(8,128)(2,1)S(1)}, bf16[576,256]{1,0:T(8,128)(2,1)S(1)}, u32[]{:S(2)}, u32[]{:S(2)}) collective-permute-start(bf16[576,256]{1,0:T(8,128)(2,1)S(1)} %get-tuple-element.10.refs_0_), channel_id=1, source_target_pairs={{128,0},{256,128},{384,256},{0,384},{129,1},{257,129},{385,257},{1... | collective-permute-start | bytes 884744 | tf_op jit(solution)/shard_map/ppermute | solution.py:19
  21.2 13.9 %collective-permute-start.1 = (bf16[576,256]{1,0:T(8,128)(2,1)S(1)}, bf16[576,256]{1,0:T(8,128)(2,1)S(1)}, u32[]{:S(2)}, u32[]{:S(2)}) collective-permute-start(bf16[576,256]{1,0:T(8,128)(2,1)S(1)} %get-tuple-element.10.refs_0_), channel_id=1, source_target_pairs={{256,0},{384,128},{0,256},{128,384},{257,1},{385,129},{1,257},{129... | collective-permute-start | bytes 884744 | tf_op jit(solution)/shard_map/ppermute | solution.py:19
  24.0 14.9 %collective-permute-start.2 = (bf16[576,256]{1,0:T(8,128)(2,1)S(1)}, bf16[576,256]{1,0:T(8,128)(2,1)S(1)}, u32[]{:S(2)}, u32[]{:S(2)}) collective-permute-start(bf16[576,256]{1,0:T(8,128)(2,1)S(1)} %get-tuple-element.10.refs_0_), channel_id=1, source_target_pairs={{384,0},{0,128},{128,256},{256,384},{385,1},{1,129},{129,257},{257... | collective-permute-start | bytes 884744 | tf_op jit(solution)/shard_map/ppermute | solution.py:19
  26.8 14.0 %collective-permute-start.3 = (bf16[576,256]{1,0:T(8,128)(2,1)S(1)}, bf16[576,256]{1,0:T(8,128)(2,1)S(1)}, u32[]{:S(2)}, u32[]{:S(2)}) collective-permute-start(bf16[576,256]{1,0:T(8,128)(2,1)S(1)} %get-tuple-element.10.refs_0_), channel_id=1, source_target_pairs={{1,0},{0,1},{3,2},{2,3},{5,4},{4,5},{7,6},{6,7},{9,8},{8,9},{11,10... | collective-permute-start | bytes 884744 | tf_op jit(solution)/shard_map/ppermute | solution.py:19
  33.2 7.6 %collective-permute-start.4 = (bf16[576,256]{1,0:T(8,128)(2,1)S(1)}, bf16[576,256]{1,0:T(8,128)(2,1)S(1)}, u32[]{:S(2)}, u32[]{:S(2)}) collective-permute-start(bf16[576,256]{1,0:T(8,128)(2,1)S(1)} %collective-permute-done.refs_1_), channel_id=1, source_target_pairs={{1,0},{0,1},{3,2},{2,3},{5,4},{4,5},{7,6},{6,7},{9,8},{8,9},{11,10... | collective-permute-start | bytes 884744 | tf_op jit(solution)/shard_map/ppermute | solution.py:19
  35.1 5.6 %collective-permute-start.5 = (bf16[576,256]{1,0:T(8,128)(2,1)S(1)}, bf16[576,256]{1,0:T(8,128)(2,1)S(1)}, u32[]{:S(2)}, u32[]{:S(2)}) collective-permute-start(bf16[576,256]{1,0:T(8,128)(2,1)S(1)} %collective-permute-done.1.refs_2_), channel_id=1, source_target_pairs={{1,0},{0,1},{3,2},{2,3},{5,4},{4,5},{7,6},{6,7},{9,8},{8,9},{11,10... | collective-permute-start | bytes 884744 | tf_op jit(solution)/shard_map/ppermute | solution.py:19
  38.8 3.5 %collective-permute-start.6 = (bf16[576,256]{1,0:T(8,128)(2,1)S(1)}, bf16[576,256]{1,0:T(8,128)(2,1)S(1)}, u32[]{:S(2)}, u32[]{:S(2)}) collective-permute-start(bf16[576,256]{1,0:T(8,128)(2,1)S(1)} %collective-permute-done.2.refs_3_), channel_id=1, source_target_pairs={{1,0},{0,1},{3,2},{2,3},{5,4},{4,5},{7,6},{6,7},{9,8},{8,9},{11,10... | collective-permute-start | bytes 884744 | tf_op jit(solution)/shard_map/ppermute | solution.py:19
  45.8 9.9 %copy-start = (s32[1,4]{1,0:T(1,128)S(1)}, s32[1,4]{1,0:T(1,128)}, u32[]{:S(2)}) copy-start(s32[1,4]{1,0:T(1,128)} %param.9) | copy-start | bytes 52
  45.8 39.0 %all-to-all-start.1 = ((bf16[32,16,1152]{2,1,0:T(8,128)(2,1)}), bf16[32,16,1152]{2,1,0:T(8,128)(2,1)S(1)}, u32[]{:S(2)}, u32[]{:S(2)}) async-start(bf16[32,16,1152]{2,1,0:T(8,128)(2,1)} %shard_map.56), calls=%async_computation.1 | async-start | bytes 2359296 | tf_op jit(solution)/shard_map/all_to_all | solution.py:221
  86.2 42.4 %all-to-all-start.2 = ((bf16[128,8,128]{2,1,0:T(8,128)(2,1)}), bf16[128,8,128]{2,1,0:T(8,128)(2,1)S(1)}, u32[]{:S(2)}, u32[]{:S(2)}) async-start(bf16[128,8,128]{2,1,0:T(8,128)(2,1)} %get-tuple-element.11), calls=%async_computation.2 | async-start | bytes 524288 | tf_op jit(solution)/shard_map/all_to_all | solution.py:232
  100.2 13.6 %collective-permute-start.7 = (bf16[16,1024]{1,0:T(8,128)(2,1)S(1)}, bf16[16,1024]{1,0:T(8,128)(2,1)S(1)}, u32[]{:S(2)}, u32[]{:S(2)}) collective-permute-start(bf16[16,1024]{1,0:T(8,128)(2,1)S(1)} %get-tuple-element.12), channel_id=1, source_target_pairs={{64,0},{0,64},{65,1},{1,65},{66,2},{2,66},{67,3},{3,67},{68,4},{4,... | collective-permute-start | bytes 98312 | tf_op jit(solution)/shard_map/ppermute | solution.py:19
  113.8 9.7 %collective-permute-start.10 = (bf16[2,16,1024]{2,1,0:T(8,128)(2,1)S(1)}, bf16[2,16,1024]{2,1,0:T(8,128)(2,1)S(1)}, u32[]{:S(2)}, u32[]{:S(2)}) collective-permute-start(bf16[2,16,1024]{2,1,0:T(8,128)(2,1)S(1)} %pad_maximum_fusion.refs_0_), channel_id=1, source_target_pairs={{384,0},{0,128},{128,256},{256,384},{385,1},{1,129},{129,257},{257... | collective-permute-start | bytes 196616 | tf_op jit(solution)/shard_map/ppermute | solution.py:19
  115.7 7.8 %collective-permute-start.8 = (bf16[2,16,1024]{2,1,0:T(8,128)(2,1)S(1)}, bf16[2,16,1024]{2,1,0:T(8,128)(2,1)S(1)}, u32[]{:S(2)}, u32[]{:S(2)}) collective-permute-start(bf16[2,16,1024]{2,1,0:T(8,128)(2,1)S(1)} %pad_maximum_fusion.refs_0_), channel_id=1, source_target_pairs={{128,0},{256,128},{384,256},{0,384},{129,1},{257,129},{385,257},{1... | collective-permute-start | bytes 196616 | tf_op jit(solution)/shard_map/ppermute | solution.py:19
  120.9 7.7 %collective-permute-start.9 = (bf16[2,16,1024]{2,1,0:T(8,128)(2,1)S(1)}, bf16[2,16,1024]{2,1,0:T(8,128)(2,1)S(1)}, u32[]{:S(2)}, u32[]{:S(2)}) collective-permute-start(bf16[2,16,1024]{2,1,0:T(8,128)(2,1)S(1)} %pad_maximum_fusion.refs_0_), channel_id=1, source_target_pairs={{256,0},{384,128},{0,256},{128,384},{257,1},{385,129},{1,257},{129... | collective-permute-start | bytes 196616 | tf_op jit(solution)/shard_map/ppermute | solution.py:19

commit v4 on v1

--- a/solution.py
+++ b/solution.py
@@ -9,22 +9,24 @@
 
 NX, NZH, NZL, NY, NC = 4, 2, 4, 8, 2
 CHIPS = NZL * NY
+PARTS = 8
 BF16, F32 = jnp.bfloat16, jnp.float32
 SMEM = pl.BlockSpec(memory_space=pltpu.SMEM)
 VMEM = pl.BlockSpec(memory_space=pltpu.VMEM)
+ANY = pl.BlockSpec(memory_space=pl.ANY)
 
 
 def from_offset(value, axis, size, offset):
     return lax.ppermute(value, axis, [((i + offset) % size, i) for i in range(size)])
 
 
-def call(kernel, shapes, scratch, operands, flops):
+def call(kernel, shapes, scratch, operands, flops, in_specs=None, out_spec=VMEM):
     size = sum(a.size * a.dtype.itemsize for a in operands)
     return pl.pallas_call(
         kernel,
         out_shape=shapes,
-        in_specs=[SMEM] + [VMEM] * (len(operands) - 1),
-        out_specs=jax.tree.map(lambda _: VMEM, shapes),
+        in_specs=in_specs or [SMEM] + [VMEM] * (len(operands) - 1),
+        out_specs=jax.tree.map(lambda _: out_spec, shapes),
         scratch_shapes=scratch,
         compiler_params=pltpu.CompilerParams(vmem_limit_bytes=40 << 20),
         cost_estimate=pl.CostEstimate(flops=flops, bytes_accessed=size, transcendentals=0),
@@ -35,44 +37,90 @@
     return pltpu.with_memory_space_constraint(value, pltpu.VMEM)
 
 
+def from_hbm(value):
+    return pltpu.with_memory_space_constraint(value, pltpu.HBM)
+
+
 def in_hbm(shape):
     return pltpu.HBM(shape, BF16)
 
 
+def pack(place, basis_ref, out_rows_ref, acts_ref, grads_ref, packed_ref, payload_ref, *scratch):
+    basis, out_rows, grads, turned, packed, sems = scratch
+    fin, fout = acts_ref.shape[0], grads_ref.shape[1]
+    width, chips = NC * fin, CHIPS // PARTS
+    loads = [
+        pltpu.make_async_copy(out_rows_ref, out_rows, sems.at[0]),
+        pltpu.make_async_copy(grads_ref, grads, sems.at[1]),
+    ]
+    for i in range(PARTS):
+        cols = pl.ds(i * chips * width, chips * width)
+        loads.append(pltpu.make_async_copy(basis_ref.at[:, cols], basis.at[i], sems.at[2 + i]))
+    stores = [pltpu.make_async_copy(acts_ref, payload_ref.at[pl.ds(0, fin)], sems.at[2 + PARTS])]
+    for copy in loads + stores:
+        copy.start()
+    loads[0].wait()
+    for c in range(CHIPS):
+        out = out_rows[:, c * NC * fout : (c + 1) * NC * fout].astype(F32)
+        out = jnp.concatenate([out[:, :fout], out[:, fout:]], axis=0).astype(BF16)
+        packed[c // chips, c % chips, :, width:] = out
+    loads[1].wait()
+    turned[...] = grads[...].astype(F32).T.astype(BF16)
+    stores.append(pltpu.make_async_copy(turned, payload_ref.at[pl.ds(fin, fout)], sems.at[3 + PARTS]))
+    stores[-1].start()
+    for i in range(PARTS):
+        loads[2 + i].wait()
+        for x in range(NX):
+
+            @pl.when(place[0] == x)
+            def _():
+                for c in range(chips):
+                    rows = basis[i, :, c * width : (c + 1) * width].astype(F32)[x * 14 : (x + 1) * 14]
+                    rows = jnp.concatenate([rows, jnp.zeros((2, width), F32)], axis=0)
+                    packed[i, c, :, :width] = rows.astype(BF16)
+
+        there = packed_ref.at[pl.ds(i * chips, chips)]
+        stores.append(pltpu.make_async_copy(packed.at[i], there, sems.at[4 + PARTS + i]))
+        stores[-1].start()
+    for store in stores:
+        store.wait()
+
+
 def project(place, packed_ref, *refs):
-    own, other, (parts_ref, acts, grads, wide, low) = refs[:NX], refs[NX : 2 * NX], refs[2 * NX :]
+    own, other, parts_ref = refs[:NX], refs[NX : 2 * NX], refs[2 * NX]
+    acts, grads, wide, low, *outs, sems = refs[2 * NX + 1 :]
     x, core = place[0], place[2]
     fin = acts.shape[0] // NC
     fout = grads.shape[1]
     tokens, height = acts.shape[1], CHIPS * 16
-    for pieces, which in ((own, core), (other, 1 - core)):
-        for s in range(NX):
-            cols = slice(s * 256, (s + 1) * 256)
+    left = packed_ref[:, :, : NC * fin].reshape(height, NC * fin)
+    rows_out = packed_ref[pl.ds(x * 8, 8), :, NC * fin :].astype(F32).reshape(8, NC, 8, fout)
+    rows_out = [rows_out[:, c].reshape(64, fout).astype(BF16) for c in range(NC)]
+    results = []
+    for s in range(NX):
+        cols = slice(s * 256, (s + 1) * 256)
+        for pieces, which in ((own, core), (other, 1 - core)):
             acts[pl.ds(pl.multiple_of(which * fin, 16), fin), cols] = pieces[s][:fin, :]
             grads[which, :, cols] = pieces[s][fin:, :]
-    left = packed_ref[:, :, : NC * fin].reshape(height, NC * fin)
-
-    def columns(n, carry):
-        cols = pl.ds(pl.multiple_of(n * 256, 256), 256)
         part = jnp.dot(left, acts[:, cols], preferred_element_type=F32)
+        out = jnp.zeros((64, 256), F32)
+        for c in range(NC):
+            out += jnp.dot(rows_out[c], grads[c, :, cols], preferred_element_type=F32)
+        rest = out - out.astype(BF16).astype(F32)
         for h in range(2):
-            wide[pl.ds(pl.multiple_of((n * 2 + h) * height, height), height), :] = part[:, h * 128 : (h + 1) * 128]
-        return carry
-
-    lax.fori_loop(0, tokens // 256, columns, 0)
-    rows = packed_ref[pl.ds(x * 8, 8), :, NC * fin :].astype(F32).reshape(8, NC, 8, fout)
-    part = jnp.zeros((64, tokens), F32)
-    for c in range(NC):
-        part += jnp.dot(rows[:, c].reshape(64, fout).astype(BF16), grads[c], preferred_element_type=F32)
-    rest = part - part.astype(BF16).astype(F32)
-    for half in range(2):
-        for t in range(8):
-            block = slice(half * 32, half * 32 + 32), slice(t * 128, (t + 1) * 128)
-            wide[pl.ds(t * height + 14 + half, CHIPS, stride=16), :] = part[block]
-            low[pl.ds(half * 8 + t, CHIPS, stride=16), :] = rest[block]
-    for t in range(8):
-        parts_ref[:, :, t * 128 : (t + 1) * 128] = wide[t * height : (t + 1) * height].astype(BF16).reshape(CHIPS, 16, 128)
-    parts_ref[:, :, tokens:] = low[...].astype(BF16).reshape(CHIPS, 16, 128)
+            block = slice(h * 128, (h + 1) * 128)
+            wide[pl.ds(h * height, height), :] = part[:, block]
+            for half in range(2):
+                wide[pl.ds(h * height + 14 + half, CHIPS, stride=16), :] = out[half * 32 : half * 32 + 32, block]
+                low[pl.ds(half * 8 + s * 2 + h, CHIPS, stride=16), :] = rest[half * 32 : half * 32 + 32, block]
+            outs[s][:, :, block] = wide[h * height : (h + 1) * height].astype(BF16).reshape(CHIPS, 16, 128)
+        results.append(pltpu.make_async_copy(outs[s], parts_ref.at[:, :, pl.ds(s * 256, 256)], sems.at[s]))
+        results[-1].start()
+    outs[NX][...] = low[...].astype(BF16).reshape(CHIPS, 16, 128)
+    results.append(pltpu.make_async_copy(outs[NX], parts_ref.at[:, :, pl.ds(tokens, 128)], sems.at[NX]))
+    results[-1].start()
+    for result in results:
+        result.wait()
 
 
 def add_up(place, lens_ref, parts_ref, in_ref, out_ref, wide, narrow):
@@ -94,13 +142,18 @@
     out_ref[...] = jnp.broadcast_to(narrow[...].astype(BF16)[None], out_ref.shape)
 
 
-def documents(which, place, out_ref, piece0, piece1, piece2, piece3, total_ref, rows_in, rows_out):
+def documents(which, place, out_ref, *refs):
+    pieces, (total_ref, rows_in, rows_out, sems) = refs[:NX], refs[NX:]
     x, zh = place[0], place[1]
     block = lax.rem(zh + which, NZH)
-    for s, ref in enumerate((piece0, piece1, piece2, piece3)):
-        rows_in[lax.rem(x + s, NX)] = ref[...]
+    copies = []
+    for s in range(NX):
+        copies.append(pltpu.make_async_copy(pieces[s], rows_in.at[lax.rem(x + s, NX)], sems.at[s]))
+        copies[-1].start()
     rows_out[...] = out_ref[...].astype(F32).reshape(64 * 16, 128)
     position = lax.broadcasted_iota(jnp.int32, (1, 256), 1).astype(F32)
+    for copy in copies:
+        copy.wait()
     total = jnp.zeros((NX * 16, 64), F32)
     for g in range(NX):
         left = rows_in[:, :, g * 256 : (g + 1) * 256].astype(F32).reshape(NX * 16, 256)
@@ -139,14 +192,24 @@
     rows = basis_in.shape[0] // NX
     tokens = NX * tok
 
-    mine = lax.dynamic_slice_in_dim(basis_in, x * rows, rows, 0)
-    mine = jnp.pad(mine, ((0, 16 - rows), (0, 0))).reshape(16, CHIPS, NC * fin).swapaxes(0, 1)
-    mine_out = basis_out.reshape(8, CHIPS, NC, fout).transpose(1, 2, 0, 3).reshape(CHIPS, 16, fout)
-    packed = jnp.concatenate([mine, mine_out], axis=2)
-    packed, acts, grads = lax.optimization_barrier((packed, acts, grads))
+    packed, payload = call(
+        pack,
+        (in_hbm((CHIPS, 16, NC * fin + fout)), jax.ShapeDtypeStruct((fin + fout, tok), BF16)),
+        [
+            pltpu.VMEM((PARTS, 4 * rows, CHIPS // PARTS * NC * fin), BF16),
+            pltpu.VMEM((8, CHIPS * NC * fout), BF16),
+            pltpu.VMEM((tok, fout), BF16),
+            pltpu.VMEM((fout, tok), BF16),
+            pltpu.VMEM((PARTS, CHIPS // PARTS, 16, NC * fin + fout), BF16),
+            pltpu.SemaphoreType.DMA((2 * PARTS + 4,)),
+        ],
+        (place, *map(from_hbm, (basis_in, basis_out, acts.T, grads))),
+        1 << 20,
+        in_specs=[SMEM] + [ANY] * 4,
+        out_spec=ANY,
+    )
     packed = lax.all_to_all(packed, ("zl", "y"), split_axis=0, concat_axis=0, tiled=True)
 
-    payload = jnp.concatenate([acts.T, grads.T], axis=0)
     own = [payload] + [from_offset(payload, "x", NX, s) for s in range(1, NX)]
     other = [from_offset(v, "core", NC, 1) for v in own]
 
@@ -156,11 +219,15 @@
         [
             pltpu.VMEM((NC * fin, tokens), BF16),
             pltpu.VMEM((NC, fout, tokens), BF16),
-            pltpu.VMEM((8 * CHIPS * 16, 128), F32),
+            pltpu.VMEM((2 * CHIPS * 16, 128), F32),
             pltpu.VMEM((CHIPS * 16, 128), F32),
+            *[pltpu.VMEM((CHIPS, 16, 256), BF16)] * NX,
+            pltpu.VMEM((CHIPS, 16, 128), BF16),
+            pltpu.SemaphoreType.DMA((5,)),
         ],
         (place, *map(in_vmem, (packed, *own, *other))),
         2 * 512 * 1024 * 1024,
+        out_spec=ANY,
     )
     parts = lax.all_to_all(parts, ("zl", "y"), split_axis=0, concat_axis=0, tiled=True)
     lens = jnp.pad(doc_lengths.astype(F32), ((0, 0), (0, 124)))
@@ -174,14 +241,19 @@
 
     proj_out = lax.all_to_all(proj_out, ("zl", "y", "core"), split_axis=0, concat_axis=0, tiled=True)
     pieces = [proj_in] + [from_offset(proj_in, "x", NX, s) for s in range(1, NX)]
-    operands = (place, *map(in_vmem, (proj_out, *pieces)))
+    operands = (place, in_vmem(proj_out), *pieces)
     totals = [
         call(
             functools.partial(documents, which),
             jax.ShapeDtypeStruct((NX * rows, 64), F32),
-            [pltpu.VMEM((NX, 16, tokens), BF16), pltpu.VMEM((64 * 16, 128), F32)],
+            [
+                pltpu.VMEM((NX, 16, tokens), BF16),
+                pltpu.VMEM((64 * 16, 128), F32),
+                pltpu.SemaphoreType.DMA((NX,)),
+            ],
             operands,
             2 * 4 * 256 * 256 * 64,
+            in_specs=[SMEM, VMEM] + [ANY] * NX,
         )
         for which in range(NZH)
     ]

time: 129 us -> 120 us (0.930)
  local copies, waits for them, and re-layouts: 6.5 us -> 0.01 us
  other arithmetic: 2.84 us -> 0.69 us
    unnamed x16 -> x2, local copies, waits for them, and re-layouts: 5.37 us -> 0.01 us
    concatenate x2 -> x0, other arithmetic: 2.14 us -> none  [the longest x1 1.15 us: body(): packed = jnp.concatenate([mine, mine_out], axis=2)]
    pallas_call x4 -> x5, Pallas kernels: 9.75 us -> 10.4 us  [call(): pl.pallas_call(kernel, out_shape=shapes, in_specs=in_specs or [SMEM] + [V...]
  transfers between devices with their start and end apart: 14 -> 14, of which waited for: 6 -> 7; matrix products, arithmetic and copies ran while one was open for 1% -> 0% of each run, Pallas kernels for 1% -> 1%
where the time goes in v4:
time: 120 us; the launch traced here: 119 us
  starting transfers between devices  73.4 us (61%)
  waiting for transfers between devices  34.2 us (29%)
  Pallas kernels  10.4 us (9%)
    ppermute x11, starting transfers between devices, from_offset(): lax.ppermute(value, axis, [((i + offset) % size, i) for i in range(size)])  40.5 us
    all_to_all x1, waiting for transfers between devices, body(): lax.all_to_all(parts, ('zl', 'y'), split_axis=0, concat_axis=0, tiled=True)  27.8 us
    all_to_all x1, starting transfers between devices, body(): lax.all_to_all(packed, ('zl', 'y'), split_axis=0, concat_axis=0, tiled=True)  13.5 us
    pallas_call x5, Pallas kernels, call(): pl.pallas_call(kernel, out_shape=shapes, in_specs=in_specs or [SMEM] + [V...  10.4 us
    all_to_all x1, starting transfers between devices, body(): lax.all_to_all(proj_out, ('zl', 'y', 'core'), split_axis=0, concat_axis=0...  9.92 us
    all_to_all x1, starting transfers between devices, body(): lax.all_to_all(parts, ('zl', 'y'), split_axis=0, concat_axis=0, tiled=True)  9.58 us
    ppermute x11, waiting for transfers between devices, from_offset(): lax.ppermute(value, axis, [((i + offset) % size, i) for i in range(size)])  6.2 us
  transfers between devices with their start and end apart: 14, of which 7 were waited for; matrix products, arithmetic and copies ran while one was open for 0% of the time, Pallas kernels for 1%

profile of v4, /device:TPU:1, one launch (start us, length us, event | category | flops | bytes accessed | tf_op | source)
XLA Modules:
  0.0 119.0 jit_solution(10957357099361936559)
XLA Ops:
  0.0 0.1 pad_add_fusion.place
  0.1 3.3 %shard_map.55 = (bf16[32,16,1024]{2,1,0:T(8,128)(2,1)}, bf16[576,256]{1,0:T(8,128)(2,1)S(1)}) custom-call(s32[3]{0:T(128)S(1)} %pad_add_fusion.place, bf16[56,28672]{1,0:T(8,128)(2,1)} %basis_ref.1, bf16[8,8192]{1,0:T(8,128)(2,1)} %out_rows_ref.1, bf16[448,256]{1,0:T(8,128)(2,1)} %bitcast.6, bf16[256,128]{1,0:T(8,128)(2,1)} %grads_ref.1), custom_call_target="tpu_custom_call" | custom-call | flops 1048576 | bytes 3637260 | tf_op jit(solution)/shard_map/pallas_call | solution.py:25
  3.4 13.5 %all-to-all-start = ((bf16[32,16,1024]{2,1,0:T(8,128)(2,1)}), bf16[32,16,1024]{2,1,0:T(8,128)(2,1)S(1)}, u32[]{:S(2)}, u32[]{:S(2)}) async-start(bf16[32,16,1024]{2,1,0:T(8,128)(2,1)} %get-tuple-element.9), calls=%async_computation | async-start | bytes 2097152 | tf_op jit(solution)/shard_map/all_to_all | solution.py:211
  16.9 4.4 %collective-permute-start = (bf16[576,256]{1,0:T(8,128)(2,1)S(1)}, bf16[576,256]{1,0:T(8,128)(2,1)S(1)}, u32[]{:S(2)}, u32[]{:S(2)}) collective-permute-start(bf16[576,256]{1,0:T(8,128)(2,1)S(1)} %get-tuple-element.10.refs_0_), channel_id=1, source_target_pairs={{128,0},{256,128},{384,256},{0,384},{129,1},{257,129},{385,257},{1... | collective-permute-start | bytes 884744 | tf_op jit(solution)/shard_map/ppermute | solution.py:20
  21.3 2.5 %collective-permute-start.1 = (bf16[576,256]{1,0:T(8,128)(2,1)S(1)}, bf16[576,256]{1,0:T(8,128)(2,1)S(1)}, u32[]{:S(2)}, u32[]{:S(2)}) collective-permute-start(bf16[576,256]{1,0:T(8,128)(2,1)S(1)} %get-tuple-element.10.refs_0_), channel_id=1, source_target_pairs={{256,0},{384,128},{0,256},{128,384},{257,1},{385,129},{1,257},{129... | collective-permute-start | bytes 884744 | tf_op jit(solution)/shard_map/ppermute | solution.py:20
  23.8 2.5 %collective-permute-start.2 = (bf16[576,256]{1,0:T(8,128)(2,1)S(1)}, bf16[576,256]{1,0:T(8,128)(2,1)S(1)}, u32[]{:S(2)}, u32[]{:S(2)}) collective-permute-start(bf16[576,256]{1,0:T(8,128)(2,1)S(1)} %get-tuple-element.10.refs_0_), channel_id=1, source_target_pairs={{384,0},{0,128},{128,256},{256,384},{385,1},{1,129},{129,257},{257... | collective-permute-start | bytes 884744 | tf_op jit(solution)/shard_map/ppermute | solution.py:20
  26.3 3.7 %collective-permute-start.3 = (bf16[576,256]{1,0:T(8,128)(2,1)S(1)}, bf16[576,256]{1,0:T(8,128)(2,1)S(1)}, u32[]{:S(2)}, u32[]{:S(2)}) collective-permute-start(bf16[576,256]{1,0:T(8,128)(2,1)S(1)} %get-tuple-element.10.refs_0_), channel_id=1, source_target_pairs={{1,0},{0,1},{3,2},{2,3},{5,4},{4,5},{7,6},{6,7},{9,8},{8,9},{11,10... | collective-permute-start | bytes 884744 | tf_op jit(solution)/shard_map/ppermute | solution.py:20
  30.0 0.0 collective-permute-done.refs_1_
  30.0 6.8 %collective-permute-start.4 = (bf16[576,256]{1,0:T(8,128)(2,1)S(1)}, bf16[576,256]{1,0:T(8,128)(2,1)S(1)}, u32[]{:S(2)}, u32[]{:S(2)}) collective-permute-start(bf16[576,256]{1,0:T(8,128)(2,1)S(1)} %collective-permute-done.refs_1_), channel_id=1, source_target_pairs={{1,0},{0,1},{3,2},{2,3},{5,4},{4,5},{7,6},{6,7},{9,8},{8,9},{11,10... | collective-permute-start | bytes 884744 | tf_op jit(solution)/shard_map/ppermute | solution.py:20
  36.8 1.9 %collective-permute-start.5 = (bf16[576,256]{1,0:T(8,128)(2,1)S(1)}, bf16[576,256]{1,0:T(8,128)(2,1)S(1)}, u32[]{:S(2)}, u32[]{:S(2)}) collective-permute-start(bf16[576,256]{1,0:T(8,128)(2,1)S(1)} %collective-permute-done.1.refs_2_), channel_id=1, source_target_pairs={{1,0},{0,1},{3,2},{2,3},{5,4},{4,5},{7,6},{6,7},{9,8},{8,9},{11,10... | collective-permute-start | bytes 884744 | tf_op jit(solution)/shard_map/ppermute | solution.py:20
  38.7 1.3 %collective-permute-done.2.refs_3_ = bf16[576,256]{1,0:T(8,128)(2,1)S(1)} collective-permute-done((bf16[576,256]{1,0:T(8,128)(2,1)S(1)}, bf16[576,256]{1,0:T(8,128)(2,1)S(1)}, u32[]{:S(2)}, u32[]{:S(2)}) %collective-permute-start.2) | collective-permute-done | bytes 294944 | tf_op jit(solution)/shard_map/ppermute | solution.py:20
  39.9 2.4 %collective-permute-start.6 = (bf16[576,256]{1,0:T(8,128)(2,1)S(1)}, bf16[576,256]{1,0:T(8,128)(2,1)S(1)}, u32[]{:S(2)}, u32[]{:S(2)}) collective-permute-start(bf16[576,256]{1,0:T(8,128)(2,1)S(1)} %collective-permute-done.2.refs_3_), channel_id=1, source_target_pairs={{1,0},{0,1},{3,2},{2,3},{5,4},{4,5},{7,6},{6,7},{9,8},{8,9},{11,10... | collective-permute-start | bytes 884744 | tf_op jit(solution)/shard_map/ppermute | solution.py:20
  42.3 0.0 collective-permute-done.3.refs_4_
  42.4 0.0 collective-permute-done.4.refs_5_
  42.4 1.2 collective-permute-done.6.refs_7_
  43.5 3.2 %shard_map.56 = bf16[32,16,1152]{2,1,0:T(8,128)(2,1)} custom-call(s32[3]{0:T(128)S(1)} %pad_add_fusion.place, bf16[32,16,1024]{2,1,0:T(8,128)(2,1)S(1)} %all-to-all-done.packed_ref, bf16[576,256]{1,0:T(8,128)(2,1)S(1)} %get-tuple-element.10.refs_0_, bf16[576,256]{1,0:T(8,128)(2,1)S(1)} %collective-permute-done.refs_1_, ...), custom_call_target="tpu_custom_call" | custom-call | flops 1073741824 | bytes 3407884 | tf_op jit(solution)/shard_map/pallas_call | solution.py:25
  46.8 0.0 copy-start
  46.8 9.6 %all-to-all-start.1 = ((bf16[32,16,1152]{2,1,0:T(8,128)(2,1)}), bf16[32,16,1152]{2,1,0:T(8,128)(2,1)S(1)}, u32[]{:S(2)}, u32[]{:S(2)}) async-start(bf16[32,16,1152]{2,1,0:T(8,128)(2,1)} %shard_map.56), calls=%async_computation.1 | async-start | bytes 2359296 | tf_op jit(solution)/shard_map/all_to_all | solution.py:232
  56.4 27.8 %all-to-all-done.1.parts_ref = bf16[32,16,1152]{2,1,0:T(8,128)(2,1)S(1)} async-done(((bf16[32,16,1152]{2,1,0:T(8,128)(2,1)}), bf16[32,16,1152]{2,1,0:T(8,128)(2,1)S(1)}, u32[]{:S(2)}, u32[]{:S(2)}) %all-to-all-start.1) | async-done | bytes 1179680 | tf_op jit(solution)/shard_map/all_to_all | solution.py:232
  84.2 1.4 %shard_map.57 = (bf16[16,1024]{1,0:T(8,128)(2,1)S(1)}, bf16[64,16,128]{2,1,0:T(8,128)(2,1)}) custom-call(s32[3]{0:T(128)S(1)} %pad_add_fusion.place, f32[1,128]{1,0:T(1,128)S(1)} %pad.4.lens_ref, bf16[32,16,1152]{2,1,0:T(8,128)(2,1)S(1)} %all-to-all-done.1.parts_ref), custom_call_target="tpu_custom_call" | custom-call | flops 589824 | bytes 1180172 | tf_op jit(solution)/shard_map/pallas_call | solution.py:25
  85.6 9.9 %all-to-all-start.2 = ((bf16[64,16,128]{2,1,0:T(8,128)(2,1)}), bf16[64,16,128]{2,1,0:T(8,128)(2,1)S(1)}, u32[]{:S(2)}, u32[]{:S(2)}) async-start(bf16[64,16,128]{2,1,0:T(8,128)(2,1)} %get-tuple-element.11), calls=%async_computation.2 | async-start | bytes 524288 | tf_op jit(solution)/shard_map/all_to_all | solution.py:242
  95.6 4.0 %collective-permute-start.7 = (bf16[16,1024]{1,0:T(8,128)(2,1)S(1)}, bf16[16,1024]{1,0:T(8,128)(2,1)S(1)}, u32[]{:S(2)}, u32[]{:S(2)}) collective-permute-start(bf16[16,1024]{1,0:T(8,128)(2,1)S(1)} %get-tuple-element.12.refs_0_), channel_id=1, source_target_pairs={{128,0},{256,128},{384,256},{0,384},{129,1},{257,129},{385,257},{1... | collective-permute-start | bytes 98312 | tf_op jit(solution)/shard_map/ppermute | solution.py:20
  99.6 1.9 %collective-permute-start.8 = (bf16[16,1024]{1,0:T(8,128)(2,1)S(1)}, bf16[16,1024]{1,0:T(8,128)(2,1)S(1)}, u32[]{:S(2)}, u32[]{:S(2)}) collective-permute-start(bf16[16,1024]{1,0:T(8,128)(2,1)S(1)} %get-tuple-element.12.refs_0_), channel_id=1, source_target_pairs={{256,0},{384,128},{0,256},{128,384},{257,1},{385,129},{1,257},{129... | collective-permute-start | bytes 98312 | tf_op jit(solution)/shard_map/ppermute | solution.py:20
  101.6 2.5 %collective-permute-start.9 = (bf16[16,1024]{1,0:T(8,128)(2,1)S(1)}, bf16[16,1024]{1,0:T(8,128)(2,1)S(1)}, u32[]{:S(2)}, u32[]{:S(2)}) collective-permute-start(bf16[16,1024]{1,0:T(8,128)(2,1)S(1)} %get-tuple-element.12.refs_0_), channel_id=1, source_target_pairs={{384,0},{0,128},{128,256},{256,384},{385,1},{1,129},{129,257},{257... | collective-permute-start | bytes 98312 | tf_op jit(solution)/shard_map/ppermute | solution.py:20
  104.1 2.0 %collective-permute-done.8.refs_2_ = bf16[16,1024]{1,0:T(8,128)(2,1)S(1)} collective-permute-done((bf16[16,1024]{1,0:T(8,128)(2,1)S(1)}, bf16[16,1024]{1,0:T(8,128)(2,1)S(1)}, u32[]{:S(2)}, u32[]{:S(2)}) %collective-permute-start.8) | collective-permute-done | bytes 32800 | tf_op jit(solution)/shard_map/ppermute | solution.py:20
  106.1 1.6 %collective-permute-done.9.refs_3_ = bf16[16,1024]{1,0:T(8,128)(2,1)S(1)} collective-permute-done((bf16[16,1024]{1,0:T(8,128)(2,1)S(1)}, bf16[16,1024]{1,0:T(8,128)(2,1)S(1)}, u32[]{:S(2)}, u32[]{:S(2)}) %collective-permute-start.9) | collective-permute-done | bytes 32800 | tf_op jit(solution)/shard_map/ppermute | solution.py:20
  107.7 0.1 all-to-all-done.2.out_ref
  107.9 1.2 %shard_map.59 = f32[56,64]{1,0:T(8,128)S(1)} custom-call(s32[3]{0:T(128)S(1)} %pad_add_fusion.place, bf16[64,16,128]{2,1,0:T(8,128)(2,1)S(1)} %all-to-all-done.2.out_ref, bf16[16,1024]{1,0:T(8,128)(2,1)S(1)} %get-tuple-element.12.refs_0_, bf16[16,1024]{1,0:T(8,128)(2,1)S(1)} %collective-permute-done.7.refs_1_, ...), custom_call_target="tpu_custom_call" | custom-call | flops 33554432 | bytes 393228 | tf_op jit(solution)/shard_map/pallas_call | solution.py:25
  109.1 7.9 %collective-permute-start.10 = (f32[56,64]{1,0:T(8,128)S(1)}, f32[56,64]{1,0:T(8,128)S(1)}, u32[]{:S(2)}, u32[]{:S(2)}) collective-permute-start(f32[56,64]{1,0:T(8,128)S(1)} %shard_map.59), channel_id=1, source_target_pairs={{64,0},{0,64},{65,1},{1,65},{66,2},{2,66},{67,3},{3,67},{68,4},{4,... | collective-permute-start | bytes 43016 | tf_op jit(solution)/shard_map/ppermute | solution.py:20
  117.0 1.2 %shard_map.58 = f32[56,64]{1,0:T(8,128)S(1)} custom-call(s32[3]{0:T(128)S(1)} %pad_add_fusion.place, bf16[64,16,128]{2,1,0:T(8,128)(2,1)S(1)} %all-to-all-done.2.out_ref, bf16[16,1024]{1,0:T(8,128)(2,1)S(1)} %get-tuple-element.12.refs_0_, bf16[16,1024]{1,0:T(8,128)(2,1)S(1)} %collective-permute-done.7.refs_1_, ...), custom_call_target="tpu_custom_call" | custom-call | flops 33554432 | bytes 393228 | tf_op jit(solution)/shard_map/pallas_call | solution.py:25
  118.2 0.1 collective-permute-done.10
  118.4 0.6 add_bitcast_fusion
  (7 shorter events, 0.0 us)
Async XLA Ops:
  3.4 40.1 %all-to-all-start = ((bf16[32,16,1024]{2,1,0:T(8,128)(2,1)}), bf16[32,16,1024]{2,1,0:T(8,128)(2,1)S(1)}, u32[]{:S(2)}, u32[]{:S(2)}) async-start(bf16[32,16,1024]{2,1,0:T(8,128)(2,1)} %get-tuple-element.9), calls=%async_computation | async-start | bytes 2097152 | tf_op jit(solution)/shard_map/all_to_all | solution.py:211
  16.9 13.1 %collective-permute-start = (bf16[576,256]{1,0:T(8,128)(2,1)S(1)}, bf16[576,256]{1,0:T(8,128)(2,1)S(1)}, u32[]{:S(2)}, u32[]{:S(2)}) collective-permute-start(bf16[576,256]{1,0:T(8,128)(2,1)S(1)} %get-tuple-element.10.refs_0_), channel_id=1, source_target_pairs={{128,0},{256,128},{384,256},{0,384},{129,1},{257,129},{385,257},{1... | collective-permute-start | bytes 884744 | tf_op jit(solution)/shard_map/ppermute | solution.py:20
  21.3 15.5 %collective-permute-start.1 = (bf16[576,256]{1,0:T(8,128)(2,1)S(1)}, bf16[576,256]{1,0:T(8,128)(2,1)S(1)}, u32[]{:S(2)}, u32[]{:S(2)}) collective-permute-start(bf16[576,256]{1,0:T(8,128)(2,1)S(1)} %get-tuple-element.10.refs_0_), channel_id=1, source_target_pairs={{256,0},{384,128},{0,256},{128,384},{257,1},{385,129},{1,257},{129... | collective-permute-start | bytes 884744 | tf_op jit(solution)/shard_map/ppermute | solution.py:20
  23.8 16.2 %collective-permute-start.2 = (bf16[576,256]{1,0:T(8,128)(2,1)S(1)}, bf16[576,256]{1,0:T(8,128)(2,1)S(1)}, u32[]{:S(2)}, u32[]{:S(2)}) collective-permute-start(bf16[576,256]{1,0:T(8,128)(2,1)S(1)} %get-tuple-element.10.refs_0_), channel_id=1, source_target_pairs={{384,0},{0,128},{128,256},{256,384},{385,1},{1,129},{129,257},{257... | collective-permute-start | bytes 884744 | tf_op jit(solution)/shard_map/ppermute | solution.py:20
  26.3 16.1 %collective-permute-start.3 = (bf16[576,256]{1,0:T(8,128)(2,1)S(1)}, bf16[576,256]{1,0:T(8,128)(2,1)S(1)}, u32[]{:S(2)}, u32[]{:S(2)}) collective-permute-start(bf16[576,256]{1,0:T(8,128)(2,1)S(1)} %get-tuple-element.10.refs_0_), channel_id=1, source_target_pairs={{1,0},{0,1},{3,2},{2,3},{5,4},{4,5},{7,6},{6,7},{9,8},{8,9},{11,10... | collective-permute-start | bytes 884744 | tf_op jit(solution)/shard_map/ppermute | solution.py:20
  30.0 12.4 %collective-permute-start.4 = (bf16[576,256]{1,0:T(8,128)(2,1)S(1)}, bf16[576,256]{1,0:T(8,128)(2,1)S(1)}, u32[]{:S(2)}, u32[]{:S(2)}) collective-permute-start(bf16[576,256]{1,0:T(8,128)(2,1)S(1)} %collective-permute-done.refs_1_), channel_id=1, source_target_pairs={{1,0},{0,1},{3,2},{2,3},{5,4},{4,5},{7,6},{6,7},{9,8},{8,9},{11,10... | collective-permute-start | bytes 884744 | tf_op jit(solution)/shard_map/ppermute | solution.py:20
  36.8 5.6 %collective-permute-start.5 = (bf16[576,256]{1,0:T(8,128)(2,1)S(1)}, bf16[576,256]{1,0:T(8,128)(2,1)S(1)}, u32[]{:S(2)}, u32[]{:S(2)}) collective-permute-start(bf16[576,256]{1,0:T(8,128)(2,1)S(1)} %collective-permute-done.1.refs_2_), channel_id=1, source_target_pairs={{1,0},{0,1},{3,2},{2,3},{5,4},{4,5},{7,6},{6,7},{9,8},{8,9},{11,10... | collective-permute-start | bytes 884744 | tf_op jit(solution)/shard_map/ppermute | solution.py:20
  39.9 3.6 %collective-permute-start.6 = (bf16[576,256]{1,0:T(8,128)(2,1)S(1)}, bf16[576,256]{1,0:T(8,128)(2,1)S(1)}, u32[]{:S(2)}, u32[]{:S(2)}) collective-permute-start(bf16[576,256]{1,0:T(8,128)(2,1)S(1)} %collective-permute-done.2.refs_3_), channel_id=1, source_target_pairs={{1,0},{0,1},{3,2},{2,3},{5,4},{4,5},{7,6},{6,7},{9,8},{8,9},{11,10... | collective-permute-start | bytes 884744 | tf_op jit(solution)/shard_map/ppermute | solution.py:20
  46.8 9.6 %copy-start = (s32[1,4]{1,0:T(1,128)S(1)}, s32[1,4]{1,0:T(1,128)}, u32[]{:S(2)}) copy-start(s32[1,4]{1,0:T(1,128)} %param.9) | copy-start | bytes 52
  46.8 37.5 %all-to-all-start.1 = ((bf16[32,16,1152]{2,1,0:T(8,128)(2,1)}), bf16[32,16,1152]{2,1,0:T(8,128)(2,1)S(1)}, u32[]{:S(2)}, u32[]{:S(2)}) async-start(bf16[32,16,1152]{2,1,0:T(8,128)(2,1)} %shard_map.56), calls=%async_computation.1 | async-start | bytes 2359296 | tf_op jit(solution)/shard_map/all_to_all | solution.py:232
  85.6 22.2 %all-to-all-start.2 = ((bf16[64,16,128]{2,1,0:T(8,128)(2,1)}), bf16[64,16,128]{2,1,0:T(8,128)(2,1)S(1)}, u32[]{:S(2)}, u32[]{:S(2)}) async-start(bf16[64,16,128]{2,1,0:T(8,128)(2,1)} %get-tuple-element.11), calls=%async_computation.2 | async-start | bytes 524288 | tf_op jit(solution)/shard_map/all_to_all | solution.py:242
  95.6 8.5 %collective-permute-start.7 = (bf16[16,1024]{1,0:T(8,128)(2,1)S(1)}, bf16[16,1024]{1,0:T(8,128)(2,1)S(1)}, u32[]{:S(2)}, u32[]{:S(2)}) collective-permute-start(bf16[16,1024]{1,0:T(8,128)(2,1)S(1)} %get-tuple-element.12.refs_0_), channel_id=1, source_target_pairs={{128,0},{256,128},{384,256},{0,384},{129,1},{257,129},{385,257},{1... | collective-permute-start | bytes 98312 | tf_op jit(solution)/shard_map/ppermute | solution.py:20
  99.6 6.5 %collective-permute-start.8 = (bf16[16,1024]{1,0:T(8,128)(2,1)S(1)}, bf16[16,1024]{1,0:T(8,128)(2,1)S(1)}, u32[]{:S(2)}, u32[]{:S(2)}) collective-permute-start(bf16[16,1024]{1,0:T(8,128)(2,1)S(1)} %get-tuple-element.12.refs_0_), channel_id=1, source_target_pairs={{256,0},{384,128},{0,256},{128,384},{257,1},{385,129},{1,257},{129... | collective-permute-start | bytes 98312 | tf_op jit(solution)/shard_map/ppermute | solution.py:20
  101.6 6.2 %collective-permute-start.9 = (bf16[16,1024]{1,0:T(8,128)(2,1)S(1)}, bf16[16,1024]{1,0:T(8,128)(2,1)S(1)}, u32[]{:S(2)}, u32[]{:S(2)}) collective-permute-start(bf16[16,1024]{1,0:T(8,128)(2,1)S(1)} %get-tuple-element.12.refs_0_), channel_id=1, source_target_pairs={{384,0},{0,128},{128,256},{256,384},{385,1},{1,129},{129,257},{257... | collective-permute-start | bytes 98312 | tf_op jit(solution)/shard_map/ppermute | solution.py:20
  109.1 9.3 %collective-permute-start.10 = (f32[56,64]{1,0:T(8,128)S(1)}, f32[56,64]{1,0:T(8,128)S(1)}, u32[]{:S(2)}, u32[]{:S(2)}) collective-permute-start(f32[56,64]{1,0:T(8,128)S(1)} %shard_map.59), channel_id=1, source_target_pairs={{64,0},{0,64},{65,1},{1,65},{66,2},{2,66},{67,3},{3,67},{68,4},{4,... | collective-permute-start | bytes 43016 | tf_op jit(solution)/shard_map/ppermute | solution.py:20

commit v5 on v4

--- a/solution.py
+++ b/solution.py
@@ -143,12 +143,13 @@
 
 
 def documents(which, place, out_ref, *refs):
-    pieces, (total_ref, rows_in, rows_out, sems) = refs[:NX], refs[NX:]
+    pairs, (total_ref, rows_in, rows_out, sems) = refs[:2], refs[2:]
     x, zh = place[0], place[1]
     block = lax.rem(zh + which, NZH)
+    near = x + 1 - 2 * lax.rem(x, 2)
     copies = []
-    for s in range(NX):
-        copies.append(pltpu.make_async_copy(pieces[s], rows_in.at[lax.rem(x + s, NX)], sems.at[s]))
+    for s, source in enumerate((x, near, NX - 1 - x, NX - 1 - near)):
+        copies.append(pltpu.make_async_copy(pairs[s // 2].at[s % 2], rows_in.at[source], sems.at[s]))
         copies[-1].start()
     rows_out[...] = out_ref[...].astype(F32).reshape(64 * 16, 128)
     position = lax.broadcasted_iota(jnp.int32, (1, 256), 1).astype(F32)
@@ -161,9 +162,8 @@
         right = []
         for h in range(2):
             cut = [
-                rows_out[pl.ds((zl * 16 + core) * 16 + block * 8 + g * 2 + h, NY, stride=32), :]
-                for zl in range(NZL)
-                for core in range(NC)
+                rows_out[pl.ds(i * NY * 16 + block * 8 + g * 2 + h, NY, stride=16), :]
+                for i in range(NZL * NC)
             ]
             right.append(jnp.concatenate(cut, axis=0))
         right = jnp.concatenate(right, axis=1).astype(BF16)
@@ -233,15 +233,18 @@
     lens = jnp.pad(doc_lengths.astype(F32), ((0, 0), (0, 124)))
     proj_in, proj_out = call(
         add_up,
-        (jax.ShapeDtypeStruct((16, tokens), BF16), in_hbm((64, 16, 128))),
+        (jax.ShapeDtypeStruct((16, tokens), BF16), in_hbm((NY, 16, 128))),
         [pltpu.VMEM((16, tokens), F32), pltpu.VMEM((16, 128), F32)],
         (place, lens, in_vmem(parts)),
         32 * 16 * 1152,
     )
 
-    proj_out = lax.all_to_all(proj_out, ("zl", "y", "core"), split_axis=0, concat_axis=0, tiled=True)
-    pieces = [proj_in] + [from_offset(proj_in, "x", NX, s) for s in range(1, NX)]
-    operands = (place, in_vmem(proj_out), *pieces)
+    proj_out = lax.all_to_all(proj_out, "y", split_axis=0, concat_axis=0, tiled=True)
+    proj_out = jnp.broadcast_to(proj_out[None], (NZL * NC, NY, 16, 128)).reshape(64, 16, 128)
+    proj_out = lax.all_to_all(proj_out, ("zl", "core"), split_axis=0, concat_axis=0, tiled=True)
+    pair = jnp.stack([proj_in, lax.ppermute(proj_in, "x", [(0, 1), (1, 0), (2, 3), (3, 2)])])
+    far = lax.ppermute(pair, "x", [(0, 3), (3, 0), (1, 2), (2, 1)])
+    operands = (place, in_vmem(proj_out), pair, far)
     totals = [
         call(
             functools.partial(documents, which),
@@ -253,7 +256,7 @@
             ],
             operands,
             2 * 4 * 256 * 256 * 64,
-            in_specs=[SMEM, VMEM] + [ANY] * NX,
+            in_specs=[SMEM, VMEM, ANY, ANY],
         )
         for which in range(NZH)
     ]

time: 120 us -> 130 us (1.083)
  blocking collectives: 0 us -> 13.2 us
  starting transfers between devices: 73.4 us -> 67.7 us
    all_to_all x0 -> x1, blocking collectives: none -> 13.2 us  [body(): lax.all_to_all(proj_out, 'y', split_axis=0, concat_axis=0, tiled=True)]
    ppermute x11 -> x8, starting transfers between devices: 40.5 us -> 32.1 us  [from_offset(): lax.ppermute(value, axis, [((i + offset) % size, i) for i in range(size)])]
    ppermute x0 -> x2, starting transfers between devices: none -> 5.98 us  [the longest x1 4.07 us: body(): far = lax.ppermute(pair, 'x', [(0, 3), (3, 0), (1, 2), (2, 1)])]
    ppermute x0 -> x2, waiting for transfers between devices: none -> 4.87 us  [the longest x1 2.73 us: body(): lax.ppermute(proj_in, 'x', [(0, 1), (1, 0), (2, 3), (3, 2)])]
    ppermute x11 -> x8, waiting for transfers between devices: 6.2 us -> 2.46 us  [from_offset(): lax.ppermute(value, axis, [((i + offset) % size, i) for i in range(size)])]
    all_to_all x1, starting transfers between devices: 9.92 us -> 6.52 us  [body(): lax.all_to_all(proj_out, ('zl', 'core'), split_axis=0, concat_axis=0, til...]
  transfers between devices with their start and end apart: 14 -> 13, of which waited for: 7 -> 5; matrix products, arithmetic and copies ran while one was open for 0% -> 0% of each run, Pallas kernels for 1% -> 1%
where the time goes in v5:
time: 130 us; the launch traced here: 128 us
  starting transfers between devices  67.7 us (52%)
  waiting for transfers between devices  35.2 us (27%)
  blocking collectives  13.2 us (10%)
  Pallas kernels  10.3 us (8%)
    ppermute x8, starting transfers between devices, from_offset(): lax.ppermute(value, axis, [((i + offset) % size, i) for i in range(size)])  32.1 us
    all_to_all x1, waiting for transfers between devices, body(): lax.all_to_all(parts, ('zl', 'y'), split_axis=0, concat_axis=0, tiled=True)  27.9 us
    all_to_all x1, starting transfers between devices, body(): lax.all_to_all(packed, ('zl', 'y'), split_axis=0, concat_axis=0, tiled=True)  13.5 us
    all_to_all x1, blocking collectives, body(): lax.all_to_all(proj_out, 'y', split_axis=0, concat_axis=0, tiled=True)  13.2 us
    pallas_call x5, Pallas kernels, call(): pl.pallas_call(kernel, out_shape=shapes, in_specs=in_specs or [SMEM] + [V...  10.3 us
    all_to_all x1, starting transfers between devices, body(): lax.all_to_all(parts, ('zl', 'y'), split_axis=0, concat_axis=0, tiled=True)  9.59 us
    all_to_all x1, starting transfers between devices, body(): lax.all_to_all(proj_out, ('zl', 'core'), split_axis=0, concat_axis=0, til...  6.52 us
    ppermute x1, starting transfers between devices, body(): far = lax.ppermute(pair, 'x', [(0, 3), (3, 0), (1, 2), (2, 1)])  4.07 us
  transfers between devices with their start and end apart: 13, of which 5 were waited for; matrix products, arithmetic and copies ran while one was open for 0% of the time, Pallas kernels for 1%

profile of v5, /device:TPU:1, one launch (start us, length us, event | category | flops | bytes accessed | tf_op | source)
XLA Modules:
  0.0 128.1 jit_solution(5943064527472347612)
XLA Ops:
  0.0 0.1 pad_add_fusion.place
  0.1 3.4 %shard_map.55 = (bf16[32,16,1024]{2,1,0:T(8,128)(2,1)}, bf16[576,256]{1,0:T(8,128)(2,1)S(1)}) custom-call(s32[3]{0:T(128)S(1)} %pad_add_fusion.place, bf16[56,28672]{1,0:T(8,128)(2,1)} %basis_ref.1, bf16[8,8192]{1,0:T(8,128)(2,1)} %out_rows_ref.1, bf16[448,256]{1,0:T(8,128)(2,1)} %bitcast.10, bf16[256,128]{1,0:T(8,128)(2,1)} %grads_ref.1), custom_call_target="tpu_custom_call" | custom-call | flops 1048576 | bytes 3637260 | tf_op jit(solution)/shard_map/pallas_call | solution.py:25
  3.4 13.5 %all-to-all-start = ((bf16[32,16,1024]{2,1,0:T(8,128)(2,1)}), bf16[32,16,1024]{2,1,0:T(8,128)(2,1)S(1)}, u32[]{:S(2)}, u32[]{:S(2)}) async-start(bf16[32,16,1024]{2,1,0:T(8,128)(2,1)} %get-tuple-element.9), calls=%async_computation | async-start | bytes 2097152 | tf_op jit(solution)/shard_map/all_to_all | solution.py:211
  16.9 4.4 %collective-permute-start = (bf16[576,256]{1,0:T(8,128)(2,1)S(1)}, bf16[576,256]{1,0:T(8,128)(2,1)S(1)}, u32[]{:S(2)}, u32[]{:S(2)}) collective-permute-start(bf16[576,256]{1,0:T(8,128)(2,1)S(1)} %get-tuple-element.10.refs_0_), channel_id=1, source_target_pairs={{128,0},{256,128},{384,256},{0,384},{129,1},{257,129},{385,257},{1... | collective-permute-start | bytes 884744 | tf_op jit(solution)/shard_map/ppermute | solution.py:20
  21.3 2.5 %collective-permute-start.1 = (bf16[576,256]{1,0:T(8,128)(2,1)S(1)}, bf16[576,256]{1,0:T(8,128)(2,1)S(1)}, u32[]{:S(2)}, u32[]{:S(2)}) collective-permute-start(bf16[576,256]{1,0:T(8,128)(2,1)S(1)} %get-tuple-element.10.refs_0_), channel_id=1, source_target_pairs={{256,0},{384,128},{0,256},{128,384},{257,1},{385,129},{1,257},{129... | collective-permute-start | bytes 884744 | tf_op jit(solution)/shard_map/ppermute | solution.py:20
  23.8 2.5 %collective-permute-start.2 = (bf16[576,256]{1,0:T(8,128)(2,1)S(1)}, bf16[576,256]{1,0:T(8,128)(2,1)S(1)}, u32[]{:S(2)}, u32[]{:S(2)}) collective-permute-start(bf16[576,256]{1,0:T(8,128)(2,1)S(1)} %get-tuple-element.10.refs_0_), channel_id=1, source_target_pairs={{384,0},{0,128},{128,256},{256,384},{385,1},{1,129},{129,257},{257... | collective-permute-start | bytes 884744 | tf_op jit(solution)/shard_map/ppermute | solution.py:20
  26.3 3.7 %collective-permute-start.3 = (bf16[576,256]{1,0:T(8,128)(2,1)S(1)}, bf16[576,256]{1,0:T(8,128)(2,1)S(1)}, u32[]{:S(2)}, u32[]{:S(2)}) collective-permute-start(bf16[576,256]{1,0:T(8,128)(2,1)S(1)} %get-tuple-element.10.refs_0_), channel_id=1, source_target_pairs={{1,0},{0,1},{3,2},{2,3},{5,4},{4,5},{7,6},{6,7},{9,8},{8,9},{11,10... | collective-permute-start | bytes 884744 | tf_op jit(solution)/shard_map/ppermute | solution.py:20
  30.0 6.8 %collective-permute-start.4 = (bf16[576,256]{1,0:T(8,128)(2,1)S(1)}, bf16[576,256]{1,0:T(8,128)(2,1)S(1)}, u32[]{:S(2)}, u32[]{:S(2)}) collective-permute-start(bf16[576,256]{1,0:T(8,128)(2,1)S(1)} %collective-permute-done.refs_1_), channel_id=1, source_target_pairs={{1,0},{0,1},{3,2},{2,3},{5,4},{4,5},{7,6},{6,7},{9,8},{8,9},{11,10... | collective-permute-start | bytes 884744 | tf_op jit(solution)/shard_map/ppermute | solution.py:20
  36.8 0.0 collective-permute-done.1.refs_2_
  36.8 1.9 %collective-permute-start.5 = (bf16[576,256]{1,0:T(8,128)(2,1)S(1)}, bf16[576,256]{1,0:T(8,128)(2,1)S(1)}, u32[]{:S(2)}, u32[]{:S(2)}) collective-permute-start(bf16[576,256]{1,0:T(8,128)(2,1)S(1)} %collective-permute-done.1.refs_2_), channel_id=1, source_target_pairs={{1,0},{0,1},{3,2},{2,3},{5,4},{4,5},{7,6},{6,7},{9,8},{8,9},{11,10... | collective-permute-start | bytes 884744 | tf_op jit(solution)/shard_map/ppermute | solution.py:20
  38.7 1.3 collective-permute-done.2.refs_3_
  40.0 2.4 %collective-permute-start.6 = (bf16[576,256]{1,0:T(8,128)(2,1)S(1)}, bf16[576,256]{1,0:T(8,128)(2,1)S(1)}, u32[]{:S(2)}, u32[]{:S(2)}) collective-permute-start(bf16[576,256]{1,0:T(8,128)(2,1)S(1)} %collective-permute-done.2.refs_3_), channel_id=1, source_target_pairs={{1,0},{0,1},{3,2},{2,3},{5,4},{4,5},{7,6},{6,7},{9,8},{8,9},{11,10... | collective-permute-start | bytes 884744 | tf_op jit(solution)/shard_map/ppermute | solution.py:20
  42.4 0.0 collective-permute-done.3.refs_4_
  42.4 0.0 collective-permute-done.5.refs_6_
  42.4 1.2 collective-permute-done.6.refs_7_
  43.6 3.2 %shard_map.56 = bf16[32,16,1152]{2,1,0:T(8,128)(2,1)} custom-call(s32[3]{0:T(128)S(1)} %pad_add_fusion.place, bf16[32,16,1024]{2,1,0:T(8,128)(2,1)S(1)} %all-to-all-done.packed_ref, bf16[576,256]{1,0:T(8,128)(2,1)S(1)} %get-tuple-element.10.refs_0_, bf16[576,256]{1,0:T(8,128)(2,1)S(1)} %collective-permute-done.refs_1_, ...), custom_call_target="tpu_custom_call" | custom-call | flops 1073741824 | bytes 3407884 | tf_op jit(solution)/shard_map/pallas_call | solution.py:25
  46.8 0.0 copy-start
  46.8 9.6 %all-to-all-start.1 = ((bf16[32,16,1152]{2,1,0:T(8,128)(2,1)}), bf16[32,16,1152]{2,1,0:T(8,128)(2,1)S(1)}, u32[]{:S(2)}, u32[]{:S(2)}) async-start(bf16[32,16,1152]{2,1,0:T(8,128)(2,1)} %shard_map.56), calls=%async_computation.1 | async-start | bytes 2359296 | tf_op jit(solution)/shard_map/all_to_all | solution.py:232
  56.4 27.9 %all-to-all-done.1.parts_ref = bf16[32,16,1152]{2,1,0:T(8,128)(2,1)S(1)} async-done(((bf16[32,16,1152]{2,1,0:T(8,128)(2,1)}), bf16[32,16,1152]{2,1,0:T(8,128)(2,1)S(1)}, u32[]{:S(2)}, u32[]{:S(2)}) %all-to-all-start.1) | async-done | bytes 1179680 | tf_op jit(solution)/shard_map/all_to_all | solution.py:232
  84.3 1.3 %shard_map.57 = (bf16[16,1024]{1,0:T(8,128)(2,1)S(1)}, bf16[8,16,128]{2,1,0:T(8,128)(2,1)}) custom-call(s32[3]{0:T(128)S(1)} %pad_add_fusion.place, f32[1,128]{1,0:T(1,128)S(1)} %pad.4.lens_ref, bf16[32,16,1152]{2,1,0:T(8,128)(2,1)S(1)} %all-to-all-done.1.parts_ref), custom_call_target="tpu_custom_call" | custom-call | flops 589824 | bytes 1180172 | tf_op jit(solution)/shard_map/pallas_call | solution.py:25
  85.7 13.2 %all_to_all.20 = bf16[8,16,128]{2,1,0:T(8,128)(2,1)S(1)} all-to-all(bf16[8,16,128]{2,1,0:T(8,128)(2,1)} %get-tuple-element.11), channel_id=1, replica_groups=mesh['x'=4,'zh'=2,'zl'=4,'y'=8,'core'=2] {'y'}, dimensions={0} | all-to-all | bytes 65536 | tf_op jit(solution)/shard_map/all_to_all | solution.py:242
  98.9 0.7 broadcast_in_dim.2
  99.6 6.5 %all-to-all-start.3 = ((bf16[64,16,128]{2,1,0:T(8,128)(2,1)}), bf16[64,16,128]{2,1,0:T(8,128)(2,1)S(1)}, u32[]{:S(2)}, u32[]{:S(2)}) async-start(bf16[64,16,128]{2,1,0:T(8,128)(2,1)} %bitcast.4), calls=%async_computation.3 | async-start | bytes 524288 | tf_op jit(solution)/shard_map/all_to_all | solution.py:244
  106.2 1.9 %collective-permute-start.7 = (bf16[16,1024]{1,0:T(8,128)(2,1)S(1)}, bf16[16,1024]{1,0:T(8,128)(2,1)S(1)}, u32[]{:S(2)}, u32[]{:S(2)}) collective-permute-start(bf16[16,1024]{1,0:T(8,128)(2,1)S(1)} %get-tuple-element.12), channel_id=1, source_target_pairs={{0,128},{128,0},{256,384},{384,256},{1,129},{129,1},{257,385},{385... | collective-permute-start | bytes 98312 | tf_op jit(solution)/shard_map/ppermute | solution.py:245
  108.1 2.7 %collective-permute-done.7 = bf16[16,1024]{1,0:T(8,128)(2,1)S(1)} collective-permute-done((bf16[16,1024]{1,0:T(8,128)(2,1)S(1)}, bf16[16,1024]{1,0:T(8,128)(2,1)S(1)}, u32[]{:S(2)}, u32[]{:S(2)}) %collective-permute-start.7) | collective-permute-done | bytes 32800 | tf_op jit(solution)/shard_map/ppermute | solution.py:245
  110.8 4.1 %collective-permute-start.8 = (bf16[2,16,1024]{2,1,0:T(8,128)(2,1)S(1)}, bf16[2,16,1024]{2,1,0:T(8,128)(2,1)S(1)}, u32[]{:S(2)}, u32[]{:S(2)}) collective-permute-start(bf16[2,16,1024]{2,1,0:T(8,128)(2,1)S(1)} %pad_maximum_fusion.refs_0_), channel_id=1, source_target_pairs={{0,384},{384,0},{128,256},{256,128},{1,385},{385,1},{129,257},{257... | collective-permute-start | bytes 196616 | tf_op jit(solution)/shard_map/ppermute | solution.py:246
  114.9 2.1 %collective-permute-done.8.refs_1_ = bf16[2,16,1024]{2,1,0:T(8,128)(2,1)S(1)} collective-permute-done((bf16[2,16,1024]{2,1,0:T(8,128)(2,1)S(1)}, bf16[2,16,1024]{2,1,0:T(8,128)(2,1)S(1)}, u32[]{:S(2)}, u32[]{:S(2)}) %collective-permute-start.8) | collective-permute-done | bytes 65568 | tf_op jit(solution)/shard_map/ppermute | solution.py:246
  117.0 1.2 shard_map.59
  118.2 8.0 %collective-permute-start.9 = (f32[56,64]{1,0:T(8,128)S(1)}, f32[56,64]{1,0:T(8,128)S(1)}, u32[]{:S(2)}, u32[]{:S(2)}) collective-permute-start(f32[56,64]{1,0:T(8,128)S(1)} %shard_map.59), channel_id=1, source_target_pairs={{64,0},{0,64},{65,1},{1,65},{66,2},{2,66},{67,3},{3,67},{68,4},{4,... | collective-permute-start | bytes 43016 | tf_op jit(solution)/shard_map/ppermute | solution.py:20
  126.2 1.2 shard_map.58
  127.5 0.0 collective-permute-done.9
  127.5 0.6 add_bitcast_fusion
  (8 shorter events, 0.0 us)
Async XLA Ops:
  3.4 40.1 %all-to-all-start = ((bf16[32,16,1024]{2,1,0:T(8,128)(2,1)}), bf16[32,16,1024]{2,1,0:T(8,128)(2,1)S(1)}, u32[]{:S(2)}, u32[]{:S(2)}) async-start(bf16[32,16,1024]{2,1,0:T(8,128)(2,1)} %get-tuple-element.9), calls=%async_computation | async-start | bytes 2097152 | tf_op jit(solution)/shard_map/all_to_all | solution.py:211
  16.9 13.1 %collective-permute-start = (bf16[576,256]{1,0:T(8,128)(2,1)S(1)}, bf16[576,256]{1,0:T(8,128)(2,1)S(1)}, u32[]{:S(2)}, u32[]{:S(2)}) collective-permute-start(bf16[576,256]{1,0:T(8,128)(2,1)S(1)} %get-tuple-element.10.refs_0_), channel_id=1, source_target_pairs={{128,0},{256,128},{384,256},{0,384},{129,1},{257,129},{385,257},{1... | collective-permute-start | bytes 884744 | tf_op jit(solution)/shard_map/ppermute | solution.py:20
  21.3 15.5 %collective-permute-start.1 = (bf16[576,256]{1,0:T(8,128)(2,1)S(1)}, bf16[576,256]{1,0:T(8,128)(2,1)S(1)}, u32[]{:S(2)}, u32[]{:S(2)}) collective-permute-start(bf16[576,256]{1,0:T(8,128)(2,1)S(1)} %get-tuple-element.10.refs_0_), channel_id=1, source_target_pairs={{256,0},{384,128},{0,256},{128,384},{257,1},{385,129},{1,257},{129... | collective-permute-start | bytes 884744 | tf_op jit(solution)/shard_map/ppermute | solution.py:20
  23.8 16.2 %collective-permute-start.2 = (bf16[576,256]{1,0:T(8,128)(2,1)S(1)}, bf16[576,256]{1,0:T(8,128)(2,1)S(1)}, u32[]{:S(2)}, u32[]{:S(2)}) collective-permute-start(bf16[576,256]{1,0:T(8,128)(2,1)S(1)} %get-tuple-element.10.refs_0_), channel_id=1, source_target_pairs={{384,0},{0,128},{128,256},{256,384},{385,1},{1,129},{129,257},{257... | collective-permute-start | bytes 884744 | tf_op jit(solution)/shard_map/ppermute | solution.py:20
  26.3 16.1 %collective-permute-start.3 = (bf16[576,256]{1,0:T(8,128)(2,1)S(1)}, bf16[576,256]{1,0:T(8,128)(2,1)S(1)}, u32[]{:S(2)}, u32[]{:S(2)}) collective-permute-start(bf16[576,256]{1,0:T(8,128)(2,1)S(1)} %get-tuple-element.10.refs_0_), channel_id=1, source_target_pairs={{1,0},{0,1},{3,2},{2,3},{5,4},{4,5},{7,6},{6,7},{9,8},{8,9},{11,10... | collective-permute-start | bytes 884744 | tf_op jit(solution)/shard_map/ppermute | solution.py:20
  30.0 12.4 %collective-permute-start.4 = (bf16[576,256]{1,0:T(8,128)(2,1)S(1)}, bf16[576,256]{1,0:T(8,128)(2,1)S(1)}, u32[]{:S(2)}, u32[]{:S(2)}) collective-permute-start(bf16[576,256]{1,0:T(8,128)(2,1)S(1)} %collective-permute-done.refs_1_), channel_id=1, source_target_pairs={{1,0},{0,1},{3,2},{2,3},{5,4},{4,5},{7,6},{6,7},{9,8},{8,9},{11,10... | collective-permute-start | bytes 884744 | tf_op jit(solution)/shard_map/ppermute | solution.py:20
  36.8 5.6 %collective-permute-start.5 = (bf16[576,256]{1,0:T(8,128)(2,1)S(1)}, bf16[576,256]{1,0:T(8,128)(2,1)S(1)}, u32[]{:S(2)}, u32[]{:S(2)}) collective-permute-start(bf16[576,256]{1,0:T(8,128)(2,1)S(1)} %collective-permute-done.1.refs_2_), channel_id=1, source_target_pairs={{1,0},{0,1},{3,2},{2,3},{5,4},{4,5},{7,6},{6,7},{9,8},{8,9},{11,10... | collective-permute-start | bytes 884744 | tf_op jit(solution)/shard_map/ppermute | solution.py:20
  40.0 3.6 %collective-permute-start.6 = (bf16[576,256]{1,0:T(8,128)(2,1)S(1)}, bf16[576,256]{1,0:T(8,128)(2,1)S(1)}, u32[]{:S(2)}, u32[]{:S(2)}) collective-permute-start(bf16[576,256]{1,0:T(8,128)(2,1)S(1)} %collective-permute-done.2.refs_3_), channel_id=1, source_target_pairs={{1,0},{0,1},{3,2},{2,3},{5,4},{4,5},{7,6},{6,7},{9,8},{8,9},{11,10... | collective-permute-start | bytes 884744 | tf_op jit(solution)/shard_map/ppermute | solution.py:20
  46.8 9.6 %copy-start = (s32[1,4]{1,0:T(1,128)S(1)}, s32[1,4]{1,0:T(1,128)}, u32[]{:S(2)}) copy-start(s32[1,4]{1,0:T(1,128)} %param.9) | copy-start | bytes 52
  46.8 37.5 %all-to-all-start.1 = ((bf16[32,16,1152]{2,1,0:T(8,128)(2,1)}), bf16[32,16,1152]{2,1,0:T(8,128)(2,1)S(1)}, u32[]{:S(2)}, u32[]{:S(2)}) async-start(bf16[32,16,1152]{2,1,0:T(8,128)(2,1)} %shard_map.56), calls=%async_computation.1 | async-start | bytes 2359296 | tf_op jit(solution)/shard_map/all_to_all | solution.py:232
  99.6 17.4 %all-to-all-start.3 = ((bf16[64,16,128]{2,1,0:T(8,128)(2,1)}), bf16[64,16,128]{2,1,0:T(8,128)(2,1)S(1)}, u32[]{:S(2)}, u32[]{:S(2)}) async-start(bf16[64,16,128]{2,1,0:T(8,128)(2,1)} %bitcast.4), calls=%async_computation.3 | async-start | bytes 524288 | tf_op jit(solution)/shard_map/all_to_all | solution.py:244
  106.2 4.6 %collective-permute-start.7 = (bf16[16,1024]{1,0:T(8,128)(2,1)S(1)}, bf16[16,1024]{1,0:T(8,128)(2,1)S(1)}, u32[]{:S(2)}, u32[]{:S(2)}) collective-permute-start(bf16[16,1024]{1,0:T(8,128)(2,1)S(1)} %get-tuple-element.12), channel_id=1, source_target_pairs={{0,128},{128,0},{256,384},{384,256},{1,129},{129,1},{257,385},{385... | collective-permute-start | bytes 98312 | tf_op jit(solution)/shard_map/ppermute | solution.py:245
  110.8 6.2 %collective-permute-start.8 = (bf16[2,16,1024]{2,1,0:T(8,128)(2,1)S(1)}, bf16[2,16,1024]{2,1,0:T(8,128)(2,1)S(1)}, u32[]{:S(2)}, u32[]{:S(2)}) collective-permute-start(bf16[2,16,1024]{2,1,0:T(8,128)(2,1)S(1)} %pad_maximum_fusion.refs_0_), channel_id=1, source_target_pairs={{0,384},{384,0},{128,256},{256,128},{1,385},{385,1},{129,257},{257... | collective-permute-start | bytes 196616 | tf_op jit(solution)/shard_map/ppermute | solution.py:246
  118.2 9.3 %collective-permute-start.9 = (f32[56,64]{1,0:T(8,128)S(1)}, f32[56,64]{1,0:T(8,128)S(1)}, u32[]{:S(2)}, u32[]{:S(2)}) collective-permute-start(f32[56,64]{1,0:T(8,128)S(1)} %shard_map.59), channel_id=1, source_target_pairs={{64,0},{0,64},{65,1},{1,65},{66,2},{2,66},{67,3},{3,67},{68,4},{4,... | collective-permute-start | bytes 43016 | tf_op jit(solution)/shard_map/ppermute | solution.py:20

commit v6 on v4

--- a/solution.py
+++ b/solution.py
@@ -45,9 +45,10 @@
     return pltpu.HBM(shape, BF16)
 
 
-def pack(place, basis_ref, out_rows_ref, acts_ref, grads_ref, packed_ref, payload_ref, *scratch):
+def pack(place, basis_ref, out_rows_ref, grads_ref, packed_ref, turned_ref, *scratch):
     basis, out_rows, grads, turned, packed, sems = scratch
-    fin, fout = acts_ref.shape[0], grads_ref.shape[1]
+    fout = grads_ref.shape[1]
+    fin = basis_ref.shape[1] // (CHIPS * NC)
     width, chips = NC * fin, CHIPS // PARTS
     loads = [
         pltpu.make_async_copy(out_rows_ref, out_rows, sems.at[0]),
@@ -56,18 +57,19 @@
     for i in range(PARTS):
         cols = pl.ds(i * chips * width, chips * width)
         loads.append(pltpu.make_async_copy(basis_ref.at[:, cols], basis.at[i], sems.at[2 + i]))
-    stores = [pltpu.make_async_copy(acts_ref, payload_ref.at[pl.ds(0, fin)], sems.at[2 + PARTS])]
-    for copy in loads + stores:
-        copy.start()
+    for load in loads:
+        load.start()
     loads[0].wait()
     for c in range(CHIPS):
-        out = out_rows[:, c * NC * fout : (c + 1) * NC * fout].astype(F32)
-        out = jnp.concatenate([out[:, :fout], out[:, fout:]], axis=0).astype(BF16)
-        packed[c // chips, c % chips, :, width:] = out
+        half = c // NY % 2
+        rows = out_rows[:, (c - half * NY) * NC * fout : (c - half * NY + 1) * NC * fout].astype(F32)
+        more = out_rows[:, (c - half * NY + NY) * NC * fout : (c - half * NY + NY + 1) * NC * fout].astype(F32)
+        blocks = [v[half * 4 : half * 4 + 4, k * fout : (k + 1) * fout] for v in (rows, more) for k in range(NC)]
+        packed[c // chips, c % chips, :, width:] = jnp.concatenate(blocks, axis=0).astype(BF16)
     loads[1].wait()
     turned[...] = grads[...].astype(F32).T.astype(BF16)
-    stores.append(pltpu.make_async_copy(turned, payload_ref.at[pl.ds(fin, fout)], sems.at[3 + PARTS]))
-    stores[-1].start()
+    stores = [pltpu.make_async_copy(turned, turned_ref, sems.at[3 + PARTS])]
+    stores[0].start()
     for i in range(PARTS):
         loads[2 + i].wait()
         for x in range(NX):
@@ -88,55 +90,60 @@
 
 def project(place, packed_ref, *refs):
     own, other, parts_ref = refs[:NX], refs[NX : 2 * NX], refs[2 * NX]
-    acts, grads, wide, low, *outs, sems = refs[2 * NX + 1 :]
-    x, core = place[0], place[2]
+    acts, grads, thin, wide, *outs, sems = refs[2 * NX + 1 :]
+    x, core, odd = place[0], place[2], place[3]
     fin = acts.shape[0] // NC
     fout = grads.shape[1]
-    tokens, height = acts.shape[1], CHIPS * 16
+    height = CHIPS * 16
     left = packed_ref[:, :, : NC * fin].reshape(height, NC * fin)
-    rows_out = packed_ref[pl.ds(x * 8, 8), :, NC * fin :].astype(F32).reshape(8, NC, 8, fout)
-    rows_out = [rows_out[:, c].reshape(64, fout).astype(BF16) for c in range(NC)]
+    thin[...] = packed_ref[pl.ds(x * NY, NY), :, NC * fin :].astype(F32).reshape(NY * 16, fout)
+    rows_out = []
+    for k in range(2 * NC):
+        cut = [thin[pl.ds(k * 4 + i, NY, stride=16), :] for i in range(4)]
+        rows_out.append(jnp.concatenate(cut, axis=0).astype(BF16))
     results = []
     for s in range(NX):
         cols = slice(s * 256, (s + 1) * 256)
         for pieces, which in ((own, core), (other, 1 - core)):
             acts[pl.ds(pl.multiple_of(which * fin, 16), fin), cols] = pieces[s][:fin, :]
-            grads[which, :, cols] = pieces[s][fin:, :]
+            grads[odd * NC + which, :, cols] = pieces[s][fin : fin + fout, :]
+            grads[(1 - odd) * NC + which, :, cols] = pieces[s][fin + fout :, :]
         part = jnp.dot(left, acts[:, cols], preferred_element_type=F32)
-        out = jnp.zeros((64, 256), F32)
-        for c in range(NC):
-            out += jnp.dot(rows_out[c], grads[c, :, cols], preferred_element_type=F32)
+        out = jnp.zeros((32, 256), F32)
+        for k in range(2 * NC):
+            out += jnp.dot(rows_out[k], grads[k, :, cols], preferred_element_type=F32)
         rest = out - out.astype(BF16).astype(F32)
         for h in range(2):
             block = slice(h * 128, (h + 1) * 128)
             wide[pl.ds(h * height, height), :] = part[:, block]
-            for half in range(2):
-                wide[pl.ds(h * height + 14 + half, CHIPS, stride=16), :] = out[half * 32 : half * 32 + 32, block]
-                low[pl.ds(half * 8 + s * 2 + h, CHIPS, stride=16), :] = rest[half * 32 : half * 32 + 32, block]
+            for i in range(4):
+                wide[pl.ds(h * height + i * 16 + 14, NY, stride=64), :] = out[i * 8 : i * 8 + 8, block]
+                wide[pl.ds(h * height + i * 16 + 15, NY, stride=64), :] = rest[i * 8 : i * 8 + 8, block]
             outs[s][:, :, block] = wide[h * height : (h + 1) * height].astype(BF16).reshape(CHIPS, 16, 128)
         results.append(pltpu.make_async_copy(outs[s], parts_ref.at[:, :, pl.ds(s * 256, 256)], sems.at[s]))
         results[-1].start()
-    outs[NX][...] = low[...].astype(BF16).reshape(CHIPS, 16, 128)
-    results.append(pltpu.make_async_copy(outs[NX], parts_ref.at[:, :, pl.ds(tokens, 128)], sems.at[NX]))
-    results[-1].start()
     for result in results:
         result.wait()
 
 
 def add_up(place, lens_ref, parts_ref, in_ref, out_ref, wide, narrow):
     x = place[0]
-    tokens = wide.shape[1]
-    total = parts_ref[0].astype(F32)
-    for i in range(1, CHIPS):
-        total = total + parts_ref[i].astype(F32)
+    halves = []
+    for odd in range(2):
+        mine = [zl * NY + y for zl in range(odd, NZL, 2) for y in range(NY)]
+        part = parts_ref[mine[0]].astype(F32)
+        for i in mine[1:]:
+            part = part + parts_ref[i].astype(F32)
+        halves.append(part)
+    total = halves[0] + halves[1]
     for s in range(NX):
         source = lax.rem(x + s, NX)
         wide[:, pl.ds(pl.multiple_of(source * 256, 256), 256)] = total[:, s * 256 : (s + 1) * 256]
-        for half in range(2):
+        for odd in range(2):
             for h in range(2):
-                col, row = s * 2 + h, half * 8 + s * 2 + h
-                value = total[14 + half : 15 + half, col * 128 : (col + 1) * 128] + total[row : row + 1, tokens:]
-                narrow[pl.ds(half * 8 + source * 2 + h, 1), :] = value
+                cols = slice((s * 2 + h) * 128, (s * 2 + h + 1) * 128)
+                value = halves[odd][14:15, cols] + halves[odd][15:16, cols]
+                narrow[pl.ds(odd * 8 + source * 2 + h, 1), :] = value
     wide[14:15, :128] = lens_ref[...]
     in_ref[...] = wide[...].astype(BF16)
     out_ref[...] = jnp.broadcast_to(narrow[...].astype(BF16)[None], out_ref.shape)
@@ -161,9 +168,10 @@
         right = []
         for h in range(2):
             cut = [
-                rows_out[pl.ds((zl * 16 + core) * 16 + block * 8 + g * 2 + h, NY, stride=32), :]
-                for zl in range(NZL)
+                rows_out[pl.ds(block * 512 + y * 128 + core * 16 + odd * 8 + g * 2 + h, 4, stride=32), :]
+                for y in range(4)
                 for core in range(NC)
+                for odd in range(2)
             ]
             right.append(jnp.concatenate(cut, axis=0))
         right = jnp.concatenate(right, axis=1).astype(BF16)
@@ -186,15 +194,15 @@
 
 def body(acts, grads, basis_in, basis_out, doc_lengths):
     x, zh, core = lax.axis_index("x"), lax.axis_index("zh"), lax.axis_index("core")
-    place = jnp.stack([x, zh, core]).astype(jnp.int32)
+    place = jnp.stack([x, zh, core, lax.rem(lax.axis_index("zl"), 2)]).astype(jnp.int32)
     tok, fin = acts.shape
     fout = grads.shape[1]
     rows = basis_in.shape[0] // NX
     tokens = NX * tok
 
-    packed, payload = call(
+    packed, grads_t = call(
         pack,
-        (in_hbm((CHIPS, 16, NC * fin + fout)), jax.ShapeDtypeStruct((fin + fout, tok), BF16)),
+        (in_hbm((CHIPS, 16, NC * fin + fout)), jax.ShapeDtypeStruct((fout, tok), BF16)),
         [
             pltpu.VMEM((PARTS, 4 * rows, CHIPS // PARTS * NC * fin), BF16),
             pltpu.VMEM((8, CHIPS * NC * fout), BF16),
@@ -203,27 +211,31 @@
             pltpu.VMEM((PARTS, CHIPS // PARTS, 16, NC * fin + fout), BF16),
             pltpu.SemaphoreType.DMA((2 * PARTS + 4,)),
         ],
-        (place, *map(from_hbm, (basis_in, basis_out, acts.T, grads))),
+        (place, *map(from_hbm, (basis_in, basis_out, grads))),
         1 << 20,
-        in_specs=[SMEM] + [ANY] * 4,
+        in_specs=[SMEM] + [ANY] * 3,
         out_spec=ANY,
     )
     packed = lax.all_to_all(packed, ("zl", "y"), split_axis=0, concat_axis=0, tiled=True)
 
-    own = [payload] + [from_offset(payload, "x", NX, s) for s in range(1, NX)]
+    next_t = lax.ppermute(grads_t, "zl", [(0, 1), (1, 0), (2, 3), (3, 2)])
+    payload = jnp.concatenate([acts.T, grads_t, next_t], axis=0)
+    size = payload.shape[0] // 2
+    right, left = from_offset(payload, "x", NX, 1), from_offset(payload, "x", NX, 3)
+    far = [from_offset(right[:size], "x", NX, 1), from_offset(left[size:], "x", NX, 3)]
+    own = [payload, right, jnp.concatenate(far, axis=0), left]
     other = [from_offset(v, "core", NC, 1) for v in own]
 
     parts = call(
         project,
-        in_hbm((CHIPS, 16, tokens + 128)),
+        in_hbm((CHIPS, 16, tokens)),
         [
             pltpu.VMEM((NC * fin, tokens), BF16),
-            pltpu.VMEM((NC, fout, tokens), BF16),
+            pltpu.VMEM((2 * NC, fout, tokens), BF16),
+            pltpu.VMEM((NY * 16, fout), F32),
             pltpu.VMEM((2 * CHIPS * 16, 128), F32),
-            pltpu.VMEM((CHIPS * 16, 128), F32),
             *[pltpu.VMEM((CHIPS, 16, 256), BF16)] * NX,
-            pltpu.VMEM((CHIPS, 16, 128), BF16),
-            pltpu.SemaphoreType.DMA((5,)),
+            pltpu.SemaphoreType.DMA((NX,)),
         ],
         (place, *map(in_vmem, (packed, *own, *other))),
         2 * 512 * 1024 * 1024,
@@ -236,7 +248,7 @@
         (jax.ShapeDtypeStruct((16, tokens), BF16), in_hbm((64, 16, 128))),
         [pltpu.VMEM((16, tokens), F32), pltpu.VMEM((16, 128), F32)],
         (place, lens, in_vmem(parts)),
-        32 * 16 * 1152,
+        32 * 16 * 1024,
     )
 
     proj_out = lax.all_to_all(proj_out, ("zl", "y", "core"), split_axis=0, concat_axis=0, tiled=True)

time: 120 us -> 148 us (1.23); the launches traced: 119 us -> 145 us
  starting transfers between devices: 73.4 us -> 96.2 us
  local copies, waits for them, and re-layouts: 0.01 us -> 3.52 us
    all_to_all x1, starting transfers between devices: 9.58 us -> 25.7 us  [body(): lax.all_to_all(parts, ('zl', 'y'), split_axis=0, concat_axis=0, tiled=True)]
    ppermute x11 -> x12, starting transfers between devices: 40.5 us -> 45.2 us  [from_offset(): lax.ppermute(value, axis, [((i + offset) % size, i) for i in range(size)])]
    unnamed x2 -> x13, local copies, waits for them, and re-layouts: 0.01 us -> 3.47 us
    ppermute x0 -> x1, starting transfers between devices: none -> 3.14 us  [body(): next_t = lax.ppermute(grads_t, 'zl', [(0, 1), (1, 0), (2, 3), (3, 2)])]
    ppermute x0 -> x1, waiting for transfers between devices: none -> 2.51 us  [body(): next_t = lax.ppermute(grads_t, 'zl', [(0, 1), (1, 0), (2, 3), (3, 2)])]
    all_to_all x1, waiting for transfers between devices: 27.8 us -> 25.9 us  [body(): lax.all_to_all(parts, ('zl', 'y'), split_axis=0, concat_axis=0, tiled=True)]
    ppermute x11 -> x12, waiting for transfers between devices: 6.2 us -> 5.68 us  [from_offset(): lax.ppermute(value, axis, [((i + offset) % size, i) for i in range(size)])]
  transfers between devices with their start and end apart: 14 -> 16, of which waited for: 7 -> 5; matrix products, arithmetic and copies ran while one was open for 0% -> 0% of each run, Pallas kernels for 1% -> 1%
where the time goes in v6:
time: 148 us; the launch traced here: 145 us
  starting transfers between devices  96.2 us (65%)
  waiting for transfers between devices  34.1 us (23%)
  Pallas kernels  10.6 us (7%)
  local copies, waits for them, and re-layouts  3.52 us (2%)
    ppermute x12, starting transfers between devices, from_offset(): lax.ppermute(value, axis, [((i + offset) % size, i) for i in range(size)])  45.2 us
    all_to_all x1, waiting for transfers between devices, body(): lax.all_to_all(parts, ('zl', 'y'), split_axis=0, concat_axis=0, tiled=True)  25.9 us
    all_to_all x1, starting transfers between devices, body(): lax.all_to_all(parts, ('zl', 'y'), split_axis=0, concat_axis=0, tiled=True)  25.7 us
    all_to_all x1, starting transfers between devices, body(): lax.all_to_all(packed, ('zl', 'y'), split_axis=0, concat_axis=0, tiled=True)  13.5 us
    pallas_call x5, Pallas kernels, call(): pl.pallas_call(kernel, out_shape=shapes, in_specs=in_specs or [SMEM] + [V...  10.6 us
    all_to_all x1, starting transfers between devices, body(): lax.all_to_all(proj_out, ('zl', 'y', 'core'), split_axis=0, concat_axis=0...  8.7 us
    ppermute x12, waiting for transfers between devices, from_offset(): lax.ppermute(value, axis, [((i + offset) % size, i) for i in range(size)])  5.68 us
    unnamed x13, local copies, waits for them, and re-layouts  3.47 us
  transfers between devices with their start and end apart: 16, of which 5 were waited for; matrix products, arithmetic and copies ran while one was open for 0% of the time, Pallas kernels for 1%

profile of v6, /device:TPU:1, one launch (start us, length us, event | category | flops | bytes accessed | tf_op | source)
XLA Modules:
  0.0 145.4 jit_solution(656162934471132057)
XLA Ops:
  0.0 0.1 pad_add_fusion.place
  0.1 3.4 %shard_map.55 = (bf16[32,16,1024]{2,1,0:T(8,128)(2,1)}, bf16[128,256]{1,0:T(8,128)(2,1)S(1)}) custom-call(s32[4]{0:T(128)S(1)} %pad_add_fusion.place, bf16[56,28672]{1,0:T(8,128)(2,1)} %basis_ref.1, bf16[8,8192]{1,0:T(8,128)(2,1)} %out_rows_ref.1, bf16[256,128]{1,0:T(8,128)(2,1)} %grads_ref.1), custom_call_target="tpu_custom_call" | custom-call | flops 1048576 | bytes 3407888 | tf_op jit(solution)/shard_map/pallas_call | solution.py:25
  3.5 13.5 %all-to-all-start = ((bf16[32,16,1024]{2,1,0:T(8,128)(2,1)}), bf16[32,16,1024]{2,1,0:T(8,128)(2,1)S(1)}, u32[]{:S(2)}, u32[]{:S(2)}) async-start(bf16[32,16,1024]{2,1,0:T(8,128)(2,1)} %get-tuple-element.9), calls=%async_computation | async-start | bytes 2097152 | tf_op jit(solution)/shard_map/all_to_all | solution.py:219
  16.9 3.1 %collective-permute-start = (bf16[128,256]{1,0:T(8,128)(2,1)S(1)}, bf16[128,256]{1,0:T(8,128)(2,1)S(1)}, u32[]{:S(2)}, u32[]{:S(2)}) collective-permute-start(bf16[128,256]{1,0:T(8,128)(2,1)S(1)} %get-tuple-element.10), channel_id=1, source_target_pairs={{0,16},{16,0},{32,48},{48,32},{1,17},{17,1},{33,49},{49,33},{2,18}... | collective-permute-start | bytes 196616 | tf_op jit(solution)/shard_map/ppermute | solution.py:221
  20.1 2.5 %collective-permute-done = bf16[128,256]{1,0:T(8,128)(2,1)S(1)} collective-permute-done((bf16[128,256]{1,0:T(8,128)(2,1)S(1)}, bf16[128,256]{1,0:T(8,128)(2,1)S(1)}, u32[]{:S(2)}, u32[]{:S(2)}) %collective-permute-start) | collective-permute-done | bytes 65568 | tf_op jit(solution)/shard_map/ppermute | solution.py:221
  22.6 4.4 %collective-permute-start.1 = (bf16[704,256]{1,0:T(8,128)(2,1)S(1)}, bf16[704,256]{1,0:T(8,128)(2,1)S(1)}, u32[]{:S(2)}, u32[]{:S(2)}) collective-permute-start(bf16[704,256]{1,0:T(8,128)(2,1)S(1)} %pad_maximum_fusion.refs_0_), channel_id=1, source_target_pairs={{128,0},{256,128},{384,256},{0,384},{129,1},{257,129},{385,257},{1... | collective-permute-start | bytes 1081352 | tf_op jit(solution)/shard_map/ppermute | solution.py:20
  27.0 1.9 %collective-permute-start.3 = (bf16[704,256]{1,0:T(8,128)(2,1)S(1)}, bf16[704,256]{1,0:T(8,128)(2,1)S(1)}, u32[]{:S(2)}, u32[]{:S(2)}) collective-permute-start(bf16[704,256]{1,0:T(8,128)(2,1)S(1)} %pad_maximum_fusion.refs_0_), channel_id=1, source_target_pairs={{384,0},{0,128},{128,256},{256,384},{385,1},{1,129},{129,257},{257... | collective-permute-start | bytes 1081352 | tf_op jit(solution)/shard_map/ppermute | solution.py:20
  28.9 2.4 %collective-permute-done.1.refs_1_ = bf16[704,256]{1,0:T(8,128)(2,1)S(1)} collective-permute-done((bf16[704,256]{1,0:T(8,128)(2,1)S(1)}, bf16[704,256]{1,0:T(8,128)(2,1)S(1)}, u32[]{:S(2)}, u32[]{:S(2)}) %collective-permute-start.1) | collective-permute-done | bytes 360480 | tf_op jit(solution)/shard_map/ppermute | solution.py:20
  31.4 5.3 %collective-permute-start.2 = (bf16[352,256]{1,0:T(8,128)(2,1)S(1)}, bf16[352,256]{1,0:T(8,128)(2,1)S(1)}, u32[]{:S(2)}, u32[]{:S(2)}) collective-permute-start(bf16[352,256]{1,0:T(8,128)(2,1)S(1)} %slice.8), channel_id=1, source_target_pairs={{128,0},{256,128},{384,256},{0,384},{129,1},{257,129},{385,257},{1... | collective-permute-start | bytes 540680 | tf_op jit(solution)/shard_map/ppermute | solution.py:20
  36.7 1.9 %collective-permute-start.4 = (bf16[352,256]{1,0:T(8,128)(2,1)S(1)}, bf16[352,256]{1,0:T(8,128)(2,1)S(1)}, u32[]{:S(2)}, u32[]{:S(2)}) collective-permute-start(bf16[352,256]{1,0:T(8,128)(2,1)S(1)} %slice.9), channel_id=1, source_target_pairs={{384,0},{0,128},{128,256},{256,384},{385,1},{1,129},{129,257},{257... | collective-permute-start | bytes 540680 | tf_op jit(solution)/shard_map/ppermute | solution.py:20
  38.7 7.1 %collective-permute-start.5 = (bf16[704,256]{1,0:T(8,128)(2,1)S(1)}, bf16[704,256]{1,0:T(8,128)(2,1)S(1)}, u32[]{:S(2)}, u32[]{:S(2)}) collective-permute-start(bf16[704,256]{1,0:T(8,128)(2,1)S(1)} %pad_maximum_fusion.refs_0_), channel_id=1, source_target_pairs={{1,0},{0,1},{3,2},{2,3},{5,4},{4,5},{7,6},{6,7},{9,8},{8,9},{11,10... | collective-permute-start | bytes 1081352 | tf_op jit(solution)/shard_map/ppermute | solution.py:20
  45.8 1.9 %collective-permute-start.8 = (bf16[704,256]{1,0:T(8,128)(2,1)S(1)}, bf16[704,256]{1,0:T(8,128)(2,1)S(1)}, u32[]{:S(2)}, u32[]{:S(2)}) collective-permute-start(bf16[704,256]{1,0:T(8,128)(2,1)S(1)} %collective-permute-done.3.refs_3_), channel_id=1, source_target_pairs={{1,0},{0,1},{3,2},{2,3},{5,4},{4,5},{7,6},{6,7},{9,8},{8,9},{11,10... | collective-permute-start | bytes 1081352 | tf_op jit(solution)/shard_map/ppermute | solution.py:20
  47.7 2.4 %collective-permute-start.6 = (bf16[704,256]{1,0:T(8,128)(2,1)S(1)}, bf16[704,256]{1,0:T(8,128)(2,1)S(1)}, u32[]{:S(2)}, u32[]{:S(2)}) collective-permute-start(bf16[704,256]{1,0:T(8,128)(2,1)S(1)} %collective-permute-done.1.refs_1_), channel_id=1, source_target_pairs={{1,0},{0,1},{3,2},{2,3},{5,4},{4,5},{7,6},{6,7},{9,8},{8,9},{11,10... | collective-permute-start | bytes 1081352 | tf_op jit(solution)/shard_map/ppermute | solution.py:20
  50.2 2.3 %collective-permute-start.7 = (bf16[704,256]{1,0:T(8,128)(2,1)S(1)}, bf16[704,256]{1,0:T(8,128)(2,1)S(1)}, u32[]{:S(2)}, u32[]{:S(2)}) collective-permute-start(bf16[704,256]{1,0:T(8,128)(2,1)S(1)} %constant_dynamic-update-slice_fusion.refs_2_), channel_id=1, source_target_pairs={{1,0},{0,1},{3,2},{2,3},{5,4},{4,5},{7,6},{6,7},{9,8},{8,9},{11,10... | collective-permute-start | bytes 1081352 | tf_op jit(solution)/shard_map/ppermute | solution.py:20
  52.5 0.7 copy-done
  53.3 0.5 collective-permute-done.7.refs_6_
  53.8 0.7 copy-done.2
  54.5 1.0 copy-done.1
  55.5 1.0 copy-done.3
  56.5 3.3 %shard_map.56 = bf16[32,16,1024]{2,1,0:T(8,128)(2,1)} custom-call(s32[4]{0:T(128)S(1)} %pad_add_fusion.place, bf16[32,16,1024]{2,1,0:T(8,128)(2,1)S(1)} %all-to-all-done.packed_ref, bf16[704,256]{1,0:T(8,128)(2,1)S(1)} %pad_maximum_fusion.refs_0_, bf16[704,256]{1,0:T(8,128)(2,1)S(1)} %collective-permute-done.1.refs_1_, ...), custom_call_target="tpu_custom_call" | custom-call | flops 1073741824 | bytes 3932176 | tf_op jit(solution)/shard_map/pallas_call | solution.py:25
  59.8 25.7 %all-to-all-start.1 = ((bf16[32,16,1024]{2,1,0:T(8,128)(2,1)}), bf16[32,16,1024]{2,1,0:T(8,128)(2,1)S(1)}, u32[]{:S(2)}, u32[]{:S(2)}) async-start(bf16[32,16,1024]{2,1,0:T(8,128)(2,1)} %shard_map.56), calls=%async_computation.1 | async-start | bytes 2097152 | tf_op jit(solution)/shard_map/all_to_all | solution.py:244
  85.6 25.9 %all-to-all-done.1.parts_ref = bf16[32,16,1024]{2,1,0:T(8,128)(2,1)S(1)} async-done(((bf16[32,16,1024]{2,1,0:T(8,128)(2,1)}), bf16[32,16,1024]{2,1,0:T(8,128)(2,1)S(1)}, u32[]{:S(2)}, u32[]{:S(2)}) %all-to-all-start.1) | async-done | bytes 1048608 | tf_op jit(solution)/shard_map/all_to_all | solution.py:244
  111.5 1.4 shard_map.57
  112.9 8.7 %all-to-all-start.2 = ((bf16[64,16,128]{2,1,0:T(8,128)(2,1)}), bf16[64,16,128]{2,1,0:T(8,128)(2,1)S(1)}, u32[]{:S(2)}, u32[]{:S(2)}) async-start(bf16[64,16,128]{2,1,0:T(8,128)(2,1)} %get-tuple-element.11), calls=%async_computation.2 | async-start | bytes 524288 | tf_op jit(solution)/shard_map/all_to_all | solution.py:254
  121.6 1.9 %collective-permute-start.11 = (bf16[16,1024]{1,0:T(8,128)(2,1)S(1)}, bf16[16,1024]{1,0:T(8,128)(2,1)S(1)}, u32[]{:S(2)}, u32[]{:S(2)}) collective-permute-start(bf16[16,1024]{1,0:T(8,128)(2,1)S(1)} %get-tuple-element.12.refs_0_), channel_id=1, source_target_pairs={{384,0},{0,128},{128,256},{256,384},{385,1},{1,129},{129,257},{257... | collective-permute-start | bytes 98312 | tf_op jit(solution)/shard_map/ppermute | solution.py:20
  123.5 6.1 %collective-permute-start.10 = (bf16[16,1024]{1,0:T(8,128)(2,1)S(1)}, bf16[16,1024]{1,0:T(8,128)(2,1)S(1)}, u32[]{:S(2)}, u32[]{:S(2)}) collective-permute-start(bf16[16,1024]{1,0:T(8,128)(2,1)S(1)} %get-tuple-element.12.refs_0_), channel_id=1, source_target_pairs={{256,0},{384,128},{0,256},{128,384},{257,1},{385,129},{1,257},{129... | collective-permute-start | bytes 98312 | tf_op jit(solution)/shard_map/ppermute | solution.py:20
  129.7 1.9 %collective-permute-start.9 = (bf16[16,1024]{1,0:T(8,128)(2,1)S(1)}, bf16[16,1024]{1,0:T(8,128)(2,1)S(1)}, u32[]{:S(2)}, u32[]{:S(2)}) collective-permute-start(bf16[16,1024]{1,0:T(8,128)(2,1)S(1)} %get-tuple-element.12.refs_0_), channel_id=1, source_target_pairs={{128,0},{256,128},{384,256},{0,384},{129,1},{257,129},{385,257},{1... | collective-permute-start | bytes 98312 | tf_op jit(solution)/shard_map/ppermute | solution.py:20
  131.6 2.7 %collective-permute-done.9.refs_1_ = bf16[16,1024]{1,0:T(8,128)(2,1)S(1)} collective-permute-done((bf16[16,1024]{1,0:T(8,128)(2,1)S(1)}, bf16[16,1024]{1,0:T(8,128)(2,1)S(1)}, u32[]{:S(2)}, u32[]{:S(2)}) %collective-permute-start.9) | collective-permute-done | bytes 32800 | tf_op jit(solution)/shard_map/ppermute | solution.py:20
  134.3 1.2 shard_map.59
  135.6 7.9 %collective-permute-start.12 = (f32[56,64]{1,0:T(8,128)S(1)}, f32[56,64]{1,0:T(8,128)S(1)}, u32[]{:S(2)}, u32[]{:S(2)}) collective-permute-start(f32[56,64]{1,0:T(8,128)S(1)} %shard_map.59), channel_id=1, source_target_pairs={{64,0},{0,64},{65,1},{1,65},{66,2},{2,66},{67,3},{3,67},{68,4},{4,... | collective-permute-start | bytes 43016 | tf_op jit(solution)/shard_map/ppermute | solution.py:20
  143.5 1.2 shard_map.58
  144.8 0.6 add_bitcast_fusion
  (26 shorter events, 0.1 us)
Async XLA Ops:
  0.0 22.6 %copy-start.4 = (bf16[256,448]{0,1:T(8,128)(2,1)S(1)}, bf16[256,448]{0,1:T(8,128)(2,1)}, u32[]{:S(2)}) copy-start(bf16[256,448]{0,1:T(8,128)(2,1)} %param.5) | copy-start | bytes 688132
  3.5 51.1 %all-to-all-start = ((bf16[32,16,1024]{2,1,0:T(8,128)(2,1)}), bf16[32,16,1024]{2,1,0:T(8,128)(2,1)S(1)}, u32[]{:S(2)}, u32[]{:S(2)}) async-start(bf16[32,16,1024]{2,1,0:T(8,128)(2,1)} %get-tuple-element.9), calls=%async_computation | async-start | bytes 2097152 | tf_op jit(solution)/shard_map/all_to_all | solution.py:219
  16.9 5.7 %collective-permute-start = (bf16[128,256]{1,0:T(8,128)(2,1)S(1)}, bf16[128,256]{1,0:T(8,128)(2,1)S(1)}, u32[]{:S(2)}, u32[]{:S(2)}) collective-permute-start(bf16[128,256]{1,0:T(8,128)(2,1)S(1)} %get-tuple-element.10), channel_id=1, source_target_pairs={{0,16},{16,0},{32,48},{48,32},{1,17},{17,1},{33,49},{49,33},{2,18}... | collective-permute-start | bytes 196616 | tf_op jit(solution)/shard_map/ppermute | solution.py:221
  22.6 8.7 %collective-permute-start.1 = (bf16[704,256]{1,0:T(8,128)(2,1)S(1)}, bf16[704,256]{1,0:T(8,128)(2,1)S(1)}, u32[]{:S(2)}, u32[]{:S(2)}) collective-permute-start(bf16[704,256]{1,0:T(8,128)(2,1)S(1)} %pad_maximum_fusion.refs_0_), channel_id=1, source_target_pairs={{128,0},{256,128},{384,256},{0,384},{129,1},{257,129},{385,257},{1... | collective-permute-start | bytes 1081352 | tf_op jit(solution)/shard_map/ppermute | solution.py:20
  27.0 9.7 %collective-permute-start.3 = (bf16[704,256]{1,0:T(8,128)(2,1)S(1)}, bf16[704,256]{1,0:T(8,128)(2,1)S(1)}, u32[]{:S(2)}, u32[]{:S(2)}) collective-permute-start(bf16[704,256]{1,0:T(8,128)(2,1)S(1)} %pad_maximum_fusion.refs_0_), channel_id=1, source_target_pairs={{384,0},{0,128},{128,256},{256,384},{385,1},{1,129},{129,257},{257... | collective-permute-start | bytes 1081352 | tf_op jit(solution)/shard_map/ppermute | solution.py:20
  31.4 18.8 %collective-permute-start.2 = (bf16[352,256]{1,0:T(8,128)(2,1)S(1)}, bf16[352,256]{1,0:T(8,128)(2,1)S(1)}, u32[]{:S(2)}, u32[]{:S(2)}) collective-permute-start(bf16[352,256]{1,0:T(8,128)(2,1)S(1)} %slice.8), channel_id=1, source_target_pairs={{128,0},{256,128},{384,256},{0,384},{129,1},{257,129},{385,257},{1... | collective-permute-start | bytes 540680 | tf_op jit(solution)/shard_map/ppermute | solution.py:20
  36.7 13.4 %collective-permute-start.4 = (bf16[352,256]{1,0:T(8,128)(2,1)S(1)}, bf16[352,256]{1,0:T(8,128)(2,1)S(1)}, u32[]{:S(2)}, u32[]{:S(2)}) collective-permute-start(bf16[352,256]{1,0:T(8,128)(2,1)S(1)} %slice.9), channel_id=1, source_target_pairs={{384,0},{0,128},{128,256},{256,384},{385,1},{1,129},{129,257},{257... | collective-permute-start | bytes 540680 | tf_op jit(solution)/shard_map/ppermute | solution.py:20
  38.7 13.8 %collective-permute-start.5 = (bf16[704,256]{1,0:T(8,128)(2,1)S(1)}, bf16[704,256]{1,0:T(8,128)(2,1)S(1)}, u32[]{:S(2)}, u32[]{:S(2)}) collective-permute-start(bf16[704,256]{1,0:T(8,128)(2,1)S(1)} %pad_maximum_fusion.refs_0_), channel_id=1, source_target_pairs={{1,0},{0,1},{3,2},{2,3},{5,4},{4,5},{7,6},{6,7},{9,8},{8,9},{11,10... | collective-permute-start | bytes 1081352 | tf_op jit(solution)/shard_map/ppermute | solution.py:20
  45.8 6.7 %collective-permute-start.8 = (bf16[704,256]{1,0:T(8,128)(2,1)S(1)}, bf16[704,256]{1,0:T(8,128)(2,1)S(1)}, u32[]{:S(2)}, u32[]{:S(2)}) collective-permute-start(bf16[704,256]{1,0:T(8,128)(2,1)S(1)} %collective-permute-done.3.refs_3_), channel_id=1, source_target_pairs={{1,0},{0,1},{3,2},{2,3},{5,4},{4,5},{7,6},{6,7},{9,8},{8,9},{11,10... | collective-permute-start | bytes 1081352 | tf_op jit(solution)/shard_map/ppermute | solution.py:20
  47.7 4.8 %collective-permute-start.6 = (bf16[704,256]{1,0:T(8,128)(2,1)S(1)}, bf16[704,256]{1,0:T(8,128)(2,1)S(1)}, u32[]{:S(2)}, u32[]{:S(2)}) collective-permute-start(bf16[704,256]{1,0:T(8,128)(2,1)S(1)} %collective-permute-done.1.refs_1_), channel_id=1, source_target_pairs={{1,0},{0,1},{3,2},{2,3},{5,4},{4,5},{7,6},{6,7},{9,8},{8,9},{11,10... | collective-permute-start | bytes 1081352 | tf_op jit(solution)/shard_map/ppermute | solution.py:20
  50.2 35.4 %copy-start.5 = (s32[1,4]{1,0:T(1,128)S(1)}, s32[1,4]{1,0:T(1,128)}, u32[]{:S(2)}) copy-start(s32[1,4]{1,0:T(1,128)} %param.9) | copy-start | bytes 52
  50.2 3.6 %collective-permute-start.7 = (bf16[704,256]{1,0:T(8,128)(2,1)S(1)}, bf16[704,256]{1,0:T(8,128)(2,1)S(1)}, u32[]{:S(2)}, u32[]{:S(2)}) collective-permute-start(bf16[704,256]{1,0:T(8,128)(2,1)S(1)} %constant_dynamic-update-slice_fusion.refs_2_), channel_id=1, source_target_pairs={{1,0},{0,1},{3,2},{2,3},{5,4},{4,5},{7,6},{6,7},{9,8},{8,9},{11,10... | collective-permute-start | bytes 1081352 | tf_op jit(solution)/shard_map/ppermute | solution.py:20
  52.5 0.7 copy-start
  53.8 0.7 copy-start.2
  54.5 1.0 copy-start.1
  55.5 1.0 copy-start.3
  59.8 51.6 %all-to-all-start.1 = ((bf16[32,16,1024]{2,1,0:T(8,128)(2,1)}), bf16[32,16,1024]{2,1,0:T(8,128)(2,1)S(1)}, u32[]{:S(2)}, u32[]{:S(2)}) async-start(bf16[32,16,1024]{2,1,0:T(8,128)(2,1)} %shard_map.56), calls=%async_computation.1 | async-start | bytes 2097152 | tf_op jit(solution)/shard_map/all_to_all | solution.py:244
  112.9 21.4 %all-to-all-start.2 = ((bf16[64,16,128]{2,1,0:T(8,128)(2,1)}), bf16[64,16,128]{2,1,0:T(8,128)(2,1)S(1)}, u32[]{:S(2)}, u32[]{:S(2)}) async-start(bf16[64,16,128]{2,1,0:T(8,128)(2,1)} %get-tuple-element.11), calls=%async_computation.2 | async-start | bytes 524288 | tf_op jit(solution)/shard_map/all_to_all | solution.py:254
  121.6 10.0 %collective-permute-start.11 = (bf16[16,1024]{1,0:T(8,128)(2,1)S(1)}, bf16[16,1024]{1,0:T(8,128)(2,1)S(1)}, u32[]{:S(2)}, u32[]{:S(2)}) collective-permute-start(bf16[16,1024]{1,0:T(8,128)(2,1)S(1)} %get-tuple-element.12.refs_0_), channel_id=1, source_target_pairs={{384,0},{0,128},{128,256},{256,384},{385,1},{1,129},{129,257},{257... | collective-permute-start | bytes 98312 | tf_op jit(solution)/shard_map/ppermute | solution.py:20
  123.5 8.1 %collective-permute-start.10 = (bf16[16,1024]{1,0:T(8,128)(2,1)S(1)}, bf16[16,1024]{1,0:T(8,128)(2,1)S(1)}, u32[]{:S(2)}, u32[]{:S(2)}) collective-permute-start(bf16[16,1024]{1,0:T(8,128)(2,1)S(1)} %get-tuple-element.12.refs_0_), channel_id=1, source_target_pairs={{256,0},{384,128},{0,256},{128,384},{257,1},{385,129},{1,257},{129... | collective-permute-start | bytes 98312 | tf_op jit(solution)/shard_map/ppermute | solution.py:20
  129.7 4.7 %collective-permute-start.9 = (bf16[16,1024]{1,0:T(8,128)(2,1)S(1)}, bf16[16,1024]{1,0:T(8,128)(2,1)S(1)}, u32[]{:S(2)}, u32[]{:S(2)}) collective-permute-start(bf16[16,1024]{1,0:T(8,128)(2,1)S(1)} %get-tuple-element.12.refs_0_), channel_id=1, source_target_pairs={{128,0},{256,128},{384,256},{0,384},{129,1},{257,129},{385,257},{1... | collective-permute-start | bytes 98312 | tf_op jit(solution)/shard_map/ppermute | solution.py:20
  135.6 9.2 %collective-permute-start.12 = (f32[56,64]{1,0:T(8,128)S(1)}, f32[56,64]{1,0:T(8,128)S(1)}, u32[]{:S(2)}, u32[]{:S(2)}) collective-permute-start(f32[56,64]{1,0:T(8,128)S(1)} %shard_map.59), channel_id=1, source_target_pairs={{64,0},{0,64},{65,1},{1,65},{66,2},{2,66},{67,3},{3,67},{68,4},{4,... | collective-permute-start | bytes 43016 | tf_op jit(solution)/shard_map/ppermute | solution.py:20

commit v7 on v4

--- a/solution.py
+++ b/solution.py
@@ -1,5 +1,3 @@
-import functools
-
 import jax
 import jax.numpy as jnp
 from jax import lax
@@ -76,7 +74,8 @@
             def _():
                 for c in range(chips):
                     rows = basis[i, :, c * width : (c + 1) * width].astype(F32)[x * 14 : (x + 1) * 14]
-                    rows = jnp.concatenate([rows, jnp.zeros((2, width), F32)], axis=0)
+                    none = jnp.zeros((1, width), F32)
+                    rows = jnp.concatenate([rows[:7], none, rows[7:], none], axis=0)
                     packed[i, c, :, :width] = rows.astype(BF16)
 
         there = packed_ref.at[pl.ds(i * chips, chips)]
@@ -110,78 +109,94 @@
         for h in range(2):
             block = slice(h * 128, (h + 1) * 128)
             wide[pl.ds(h * height, height), :] = part[:, block]
-            for half in range(2):
-                wide[pl.ds(h * height + 14 + half, CHIPS, stride=16), :] = out[half * 32 : half * 32 + 32, block]
-                low[pl.ds(half * 8 + s * 2 + h, CHIPS, stride=16), :] = rest[half * 32 : half * 32 + 32, block]
-            outs[s][:, :, block] = wide[h * height : (h + 1) * height].astype(BF16).reshape(CHIPS, 16, 128)
+            for half in range(NZH):
+                mine = out[half * 32 : half * 32 + 32, block], rest[half * 32 : half * 32 + 32, block]
+                wide[pl.ds(h * height + half * 8 + 7, CHIPS, stride=16), :] = mine[0]
+                low[pl.ds(half * 8 + s * 2 + h, CHIPS, stride=16), :] = mine[1]
+            for half in range(NZH):
+                rows = wide[h * height : (h + 1) * height].reshape(CHIPS, NZH, 8, 128)[:, half]
+                outs[s][half * CHIPS : (half + 1) * CHIPS, :, block] = rows.astype(BF16)
         results.append(pltpu.make_async_copy(outs[s], parts_ref.at[:, :, pl.ds(s * 256, 256)], sems.at[s]))
         results[-1].start()
-    outs[NX][...] = low[...].astype(BF16).reshape(CHIPS, 16, 128)
+    for half in range(NZH):
+        rows = low[...].reshape(CHIPS, NZH, 8, 128)[:, half]
+        outs[NX][half * CHIPS : (half + 1) * CHIPS] = rows.astype(BF16)
     results.append(pltpu.make_async_copy(outs[NX], parts_ref.at[:, :, pl.ds(tokens, 128)], sems.at[NX]))
     results[-1].start()
     for result in results:
         result.wait()
 
 
-def add_up(place, lens_ref, parts_ref, in_ref, out_ref, wide, narrow):
-    x = place[0]
-    tokens = wide.shape[1]
-    total = parts_ref[0].astype(F32)
-    for i in range(1, CHIPS):
-        total = total + parts_ref[i].astype(F32)
-    for s in range(NX):
-        source = lax.rem(x + s, NX)
-        wide[:, pl.ds(pl.multiple_of(source * 256, 256), 256)] = total[:, s * 256 : (s + 1) * 256]
-        for half in range(2):
+def add_in(place, lens_ref, parts_ref, in_ref, wide):
+    x, tokens = place[0], wide.shape[1]
+    for half in range(NZH):
+        total = parts_ref[half * CHIPS, :, :tokens].astype(F32)
+        for i in range(1, CHIPS):
+            total = total + parts_ref[half * CHIPS + i, :, :tokens].astype(F32)
+        for s in range(NX):
+            there = pl.ds(pl.multiple_of(lax.rem(x + s, NX) * 256, 256), 256)
+            wide[half * 8 : half * 8 + 8, there] = total[:, s * 256 : (s + 1) * 256]
+    wide[7:8, :128] = lens_ref[...]
+    in_ref[...] = wide[...].astype(BF16)
+
+
+def add_out(place, parts_ref, _, out_ref, narrow):
+    x, tokens = place[0], NX * 256
+    for half in range(NZH):
+        total = parts_ref[half * CHIPS].astype(F32)
+        for i in range(1, CHIPS):
+            total = total + parts_ref[half * CHIPS + i].astype(F32)
+        for s in range(NX):
             for h in range(2):
-                col, row = s * 2 + h, half * 8 + s * 2 + h
-                value = total[14 + half : 15 + half, col * 128 : (col + 1) * 128] + total[row : row + 1, tokens:]
-                narrow[pl.ds(half * 8 + source * 2 + h, 1), :] = value
-    wide[14:15, :128] = lens_ref[...]
-    in_ref[...] = wide[...].astype(BF16)
+                tile = s * 2 + h
+                value = total[7:8, tile * 128 : (tile + 1) * 128] + total[tile : tile + 1, tokens:]
+                narrow[pl.ds(half * 8 + lax.rem(x + s, NX) * 2 + h, 1), :] = value
     out_ref[...] = jnp.broadcast_to(narrow[...].astype(BF16)[None], out_ref.shape)
 
 
-def documents(which, place, out_ref, *refs):
+def documents(place, out_ref, *refs):
     pieces, (total_ref, rows_in, rows_out, sems) = refs[:NX], refs[NX:]
     x, zh = place[0], place[1]
-    block = lax.rem(zh + which, NZH)
     copies = []
     for s in range(NX):
-        copies.append(pltpu.make_async_copy(pieces[s], rows_in.at[lax.rem(x + s, NX)], sems.at[s]))
-        copies[-1].start()
+        for half in range(NZH):
+            there = rows_in.at[lax.rem(x + s, NX), lax.rem(half + zh, NZH)]
+            copies.append(pltpu.make_async_copy(pieces[s].at[half], there, sems.at[s * NZH + half]))
+            copies[-1].start()
     rows_out[...] = out_ref[...].astype(F32).reshape(64 * 16, 128)
     position = lax.broadcasted_iota(jnp.int32, (1, 256), 1).astype(F32)
     for copy in copies:
         copy.wait()
-    total = jnp.zeros((NX * 16, 64), F32)
-    for g in range(NX):
-        left = rows_in[:, :, g * 256 : (g + 1) * 256].astype(F32).reshape(NX * 16, 256)
-        lens = rows_in[g, :, :128].astype(F32)[14:15, :4]
-        right = []
-        for h in range(2):
-            cut = [
-                rows_out[pl.ds((zl * 16 + core) * 16 + block * 8 + g * 2 + h, NY, stride=32), :]
-                for zl in range(NZL)
-                for core in range(NC)
-            ]
-            right.append(jnp.concatenate(cut, axis=0))
-        right = jnp.concatenate(right, axis=1).astype(BF16)
-        masked, start = [], jnp.zeros((1, 1), F32)
-        for d in range(4):
-            end = start + lens[:, d : d + 1]
-            inside = (position >= start) & (position < end)
-            masked.append(jnp.where(inside, left, 0.0).astype(BF16))
-            start = end
-        product = lax.dot_general(
-            jnp.concatenate(masked, axis=0), right, (((1,), (1,)), ((), ())), preferred_element_type=F32
-        )
-        for d in range(4):
-            one = product[d * 64 : (d + 1) * 64]
-            total = total + one * one
+    total = jnp.zeros((64, 64), F32)
+    for half in range(NZH):
+        for g in range(NX):
+            left = rows_in[:, :, :, g * 256 : (g + 1) * 256].astype(F32)
+            left = left[:, :, half * 8 : half * 8 + 8].reshape(64, 256)
+            lens = rows_in[g, half, :, :128].astype(F32)[7:8, :4]
+            right = []
+            for h in range(2):
+                cut = [
+                    rows_out[pl.ds((zl * 16 + core) * 16 + half * 8 + g * 2 + h, NY, stride=32), :]
+                    for zl in range(NZL)
+                    for core in range(NC)
+                ]
+                right.append(jnp.concatenate(cut, axis=0))
+            right = jnp.concatenate(right, axis=1).astype(BF16)
+            masked, start = [], jnp.zeros((1, 1), F32)
+            for d in range(4):
+                end = start + lens[:, d : d + 1]
+                inside = (position >= start) & (position < end)
+                masked.append(jnp.where(inside, left, 0.0).astype(BF16))
+                start = end
+            product = lax.dot_general(
+                jnp.concatenate(masked, axis=0), right, (((1,), (1,)), ((), ())), preferred_element_type=F32
+            )
+            for d in range(4):
+                one = product[d * 64 : (d + 1) * 64]
+                total = total + one * one
     total = total * (1.0 / 2048.0)
-    for i in range(NX):
-        total_ref[i * 14 : (i + 1) * 14, :] = total[i * 16 : i * 16 + 14]
+    for i in range(NX * NZH):
+        total_ref[i * 7 : (i + 1) * 7, :] = total[i * 8 : i * 8 + 7]
 
 
 def body(acts, grads, basis_in, basis_out, doc_lengths):
@@ -215,49 +230,55 @@
 
     parts = call(
         project,
-        in_hbm((CHIPS, 16, tokens + 128)),
+        in_hbm((NZH * CHIPS, 8, tokens + 128)),
         [
             pltpu.VMEM((NC * fin, tokens), BF16),
             pltpu.VMEM((NC, fout, tokens), BF16),
             pltpu.VMEM((2 * CHIPS * 16, 128), F32),
             pltpu.VMEM((CHIPS * 16, 128), F32),
-            *[pltpu.VMEM((CHIPS, 16, 256), BF16)] * NX,
-            pltpu.VMEM((CHIPS, 16, 128), BF16),
+            *[pltpu.VMEM((NZH * CHIPS, 8, 256), BF16)] * NX,
+            pltpu.VMEM((NZH * CHIPS, 8, 128), BF16),
             pltpu.SemaphoreType.DMA((5,)),
         ],
         (place, *map(in_vmem, (packed, *own, *other))),
         2 * 512 * 1024 * 1024,
         out_spec=ANY,
     )
-    parts = lax.all_to_all(parts, ("zl", "y"), split_axis=0, concat_axis=0, tiled=True)
+    parts = lax.all_to_all(parts, ("zh", "zl", "y"), split_axis=0, concat_axis=0, tiled=True)
+    parts = in_vmem(parts)
     lens = jnp.pad(doc_lengths.astype(F32), ((0, 0), (0, 124)))
-    proj_in, proj_out = call(
-        add_up,
-        (jax.ShapeDtypeStruct((16, tokens), BF16), in_hbm((64, 16, 128))),
-        [pltpu.VMEM((16, tokens), F32), pltpu.VMEM((16, 128), F32)],
-        (place, lens, in_vmem(parts)),
-        32 * 16 * 1152,
-    )
-
+    proj_in = call(
+        add_in,
+        jax.ShapeDtypeStruct((16, tokens), BF16),
+        [pltpu.VMEM((16, tokens), F32)],
+        (place, lens, parts),
+        64 * 8 * 1024,
+    )
+    proj_out = call(
+        add_out,
+        in_hbm((64, 16, 128)),
+        [pltpu.VMEM((16, 128), F32)],
+        (place, parts, proj_in),
+        64 * 8 * 1152,
+        in_specs=[SMEM, VMEM, ANY],
+    )
+
+    pair = jnp.stack([proj_in, from_offset(proj_in, "zh", NZH, 1)])
+    pieces = [pair] + [from_offset(pair, "x", NX, s) for s in range(1, NX)]
     proj_out = lax.all_to_all(proj_out, ("zl", "y", "core"), split_axis=0, concat_axis=0, tiled=True)
-    pieces = [proj_in] + [from_offset(proj_in, "x", NX, s) for s in range(1, NX)]
-    operands = (place, in_vmem(proj_out), *pieces)
-    totals = [
-        call(
-            functools.partial(documents, which),
-            jax.ShapeDtypeStruct((NX * rows, 64), F32),
-            [
-                pltpu.VMEM((NX, 16, tokens), BF16),
-                pltpu.VMEM((64 * 16, 128), F32),
-                pltpu.SemaphoreType.DMA((NX,)),
-            ],
-            operands,
-            2 * 4 * 256 * 256 * 64,
-            in_specs=[SMEM, VMEM] + [ANY] * NX,
-        )
-        for which in range(NZH)
-    ]
-    return (totals[0] + from_offset(totals[1], "zh", NZH, 1)).T
+    total = call(
+        documents,
+        jax.ShapeDtypeStruct((NX * rows, 64), F32),
+        [
+            pltpu.VMEM((NX, NZH, 16, tokens), BF16),
+            pltpu.VMEM((64 * 16, 128), F32),
+            pltpu.SemaphoreType.DMA((NX * NZH,)),
+        ],
+        (place, in_vmem(proj_out), *pieces),
+        2 * 8 * 256 * 256 * 64,
+        in_specs=[SMEM, VMEM] + [ANY] * NX,
+    )
+    return total.T
 
 
 def solution(mesh):

time: 120 us -> 129 us (1.075)
  waiting for transfers between devices: 34.2 us -> 43.6 us
    ppermute x11, waiting for transfers between devices: 6.2 us -> 12.8 us  [from_offset(): lax.ppermute(value, axis, [((i + offset) % size, i) for i in range(size)])]
    all_to_all x1, starting transfers between devices: 9.58 us -> 13.3 us  [body(): lax.all_to_all(parts, ('zh', 'zl', 'y'), split_axis=0, concat_axis=0, til...]
    ppermute x11, starting transfers between devices: 40.5 us -> 37 us  [from_offset(): lax.ppermute(value, axis, [((i + offset) % size, i) for i in range(size)])]
    all_to_all x1, waiting for transfers between devices: 27.8 us -> 30.8 us  [body(): lax.all_to_all(parts, ('zh', 'zl', 'y'), split_axis=0, concat_axis=0, til...]
  transfers between devices with their start and end apart: 14 -> 14, of which waited for: 7 -> 5; matrix products, arithmetic and copies ran while one was open for 0% -> 0% of each run, Pallas kernels for 1% -> 0%
where the time goes in v7:
time: 129 us; the launch traced here: 128 us
  starting transfers between devices  72.9 us (57%)
  waiting for transfers between devices  43.6 us (34%)
  Pallas kernels  11 us (9%)
    ppermute x11, starting transfers between devices, from_offset(): lax.ppermute(value, axis, [((i + offset) % size, i) for i in range(size)])  37 us
    all_to_all x1, waiting for transfers between devices, body(): lax.all_to_all(parts, ('zh', 'zl', 'y'), split_axis=0, concat_axis=0, til...  30.8 us
    all_to_all x1, starting transfers between devices, body(): lax.all_to_all(packed, ('zl', 'y'), split_axis=0, concat_axis=0, tiled=True)  13.5 us
    all_to_all x1, starting transfers between devices, body(): lax.all_to_all(parts, ('zh', 'zl', 'y'), split_axis=0, concat_axis=0, til...  13.3 us
    ppermute x11, waiting for transfers between devices, from_offset(): lax.ppermute(value, axis, [((i + offset) % size, i) for i in range(size)])  12.8 us
    pallas_call x5, Pallas kernels, call(): pl.pallas_call(kernel, out_shape=shapes, in_specs=in_specs or [SMEM] + [V...  11 us
    all_to_all x1, starting transfers between devices, body(): lax.all_to_all(proj_out, ('zl', 'y', 'core'), split_axis=0, concat_axis=0...  9.16 us
  transfers between devices with their start and end apart: 14, of which 5 were waited for; matrix products, arithmetic and copies ran while one was open for 0% of the time, Pallas kernels for 0%

profile of v7, /device:TPU:1, one launch (start us, length us, event | category | flops | bytes accessed | tf_op | source)
XLA Modules:
  0.0 127.8 jit_solution(5119016302863329063)
XLA Ops:
  0.0 0.1 pad_add_fusion.place
  0.1 3.4 %shard_map.55 = (bf16[32,16,1024]{2,1,0:T(8,128)(2,1)}, bf16[576,256]{1,0:T(8,128)(2,1)S(1)}) custom-call(s32[3]{0:T(128)S(1)} %pad_add_fusion.place, bf16[56,28672]{1,0:T(8,128)(2,1)} %basis_ref.1, bf16[8,8192]{1,0:T(8,128)(2,1)} %out_rows_ref.1, bf16[448,256]{1,0:T(8,128)(2,1)} %bitcast.8, bf16[256,128]{1,0:T(8,128)(2,1)} %grads_ref.1), custom_call_target="tpu_custom_call" | custom-call | flops 1048576 | bytes 3637260 | tf_op jit(solution)/shard_map/pallas_call | solution.py:23
  3.5 13.5 %all-to-all-start = ((bf16[32,16,1024]{2,1,0:T(8,128)(2,1)}), bf16[32,16,1024]{2,1,0:T(8,128)(2,1)S(1)}, u32[]{:S(2)}, u32[]{:S(2)}) async-start(bf16[32,16,1024]{2,1,0:T(8,128)(2,1)} %get-tuple-element.7), calls=%async_computation | async-start | bytes 2097152 | tf_op jit(solution)/shard_map/all_to_all | solution.py:226
  16.9 4.4 %collective-permute-start = (bf16[576,256]{1,0:T(8,128)(2,1)S(1)}, bf16[576,256]{1,0:T(8,128)(2,1)S(1)}, u32[]{:S(2)}, u32[]{:S(2)}) collective-permute-start(bf16[576,256]{1,0:T(8,128)(2,1)S(1)} %get-tuple-element.8.refs_0_), channel_id=1, source_target_pairs={{128,0},{256,128},{384,256},{0,384},{129,1},{257,129},{385,257},{1... | collective-permute-start | bytes 884744 | tf_op jit(solution)/shard_map/ppermute | solution.py:18
  21.3 2.5 %collective-permute-start.1 = (bf16[576,256]{1,0:T(8,128)(2,1)S(1)}, bf16[576,256]{1,0:T(8,128)(2,1)S(1)}, u32[]{:S(2)}, u32[]{:S(2)}) collective-permute-start(bf16[576,256]{1,0:T(8,128)(2,1)S(1)} %get-tuple-element.8.refs_0_), channel_id=1, source_target_pairs={{256,0},{384,128},{0,256},{128,384},{257,1},{385,129},{1,257},{129... | collective-permute-start | bytes 884744 | tf_op jit(solution)/shard_map/ppermute | solution.py:18
  23.8 2.5 %collective-permute-start.2 = (bf16[576,256]{1,0:T(8,128)(2,1)S(1)}, bf16[576,256]{1,0:T(8,128)(2,1)S(1)}, u32[]{:S(2)}, u32[]{:S(2)}) collective-permute-start(bf16[576,256]{1,0:T(8,128)(2,1)S(1)} %get-tuple-element.8.refs_0_), channel_id=1, source_target_pairs={{384,0},{0,128},{128,256},{256,384},{385,1},{1,129},{129,257},{257... | collective-permute-start | bytes 884744 | tf_op jit(solution)/shard_map/ppermute | solution.py:18
  26.3 3.7 %collective-permute-start.3 = (bf16[576,256]{1,0:T(8,128)(2,1)S(1)}, bf16[576,256]{1,0:T(8,128)(2,1)S(1)}, u32[]{:S(2)}, u32[]{:S(2)}) collective-permute-start(bf16[576,256]{1,0:T(8,128)(2,1)S(1)} %get-tuple-element.8.refs_0_), channel_id=1, source_target_pairs={{1,0},{0,1},{3,2},{2,3},{5,4},{4,5},{7,6},{6,7},{9,8},{8,9},{11,10... | collective-permute-start | bytes 884744 | tf_op jit(solution)/shard_map/ppermute | solution.py:18
  30.0 0.0 collective-permute-done.refs_1_
  30.0 6.8 %collective-permute-start.4 = (bf16[576,256]{1,0:T(8,128)(2,1)S(1)}, bf16[576,256]{1,0:T(8,128)(2,1)S(1)}, u32[]{:S(2)}, u32[]{:S(2)}) collective-permute-start(bf16[576,256]{1,0:T(8,128)(2,1)S(1)} %collective-permute-done.refs_1_), channel_id=1, source_target_pairs={{1,0},{0,1},{3,2},{2,3},{5,4},{4,5},{7,6},{6,7},{9,8},{8,9},{11,10... | collective-permute-start | bytes 884744 | tf_op jit(solution)/shard_map/ppermute | solution.py:18
  36.8 0.0 collective-permute-done.1.refs_2_
  36.8 1.9 %collective-permute-start.5 = (bf16[576,256]{1,0:T(8,128)(2,1)S(1)}, bf16[576,256]{1,0:T(8,128)(2,1)S(1)}, u32[]{:S(2)}, u32[]{:S(2)}) collective-permute-start(bf16[576,256]{1,0:T(8,128)(2,1)S(1)} %collective-permute-done.1.refs_2_), channel_id=1, source_target_pairs={{1,0},{0,1},{3,2},{2,3},{5,4},{4,5},{7,6},{6,7},{9,8},{8,9},{11,10... | collective-permute-start | bytes 884744 | tf_op jit(solution)/shard_map/ppermute | solution.py:18
  38.7 1.3 collective-permute-done.2.refs_3_
  40.0 2.4 %collective-permute-start.6 = (bf16[576,256]{1,0:T(8,128)(2,1)S(1)}, bf16[576,256]{1,0:T(8,128)(2,1)S(1)}, u32[]{:S(2)}, u32[]{:S(2)}) collective-permute-start(bf16[576,256]{1,0:T(8,128)(2,1)S(1)} %collective-permute-done.2.refs_3_), channel_id=1, source_target_pairs={{1,0},{0,1},{3,2},{2,3},{5,4},{4,5},{7,6},{6,7},{9,8},{8,9},{11,10... | collective-permute-start | bytes 884744 | tf_op jit(solution)/shard_map/ppermute | solution.py:18
  42.4 0.0 collective-permute-done.4.refs_5_
  42.4 0.0 collective-permute-done.5.refs_6_
  42.4 1.2 collective-permute-done.6.refs_7_
  43.6 0.0 all-to-all-done.packed_ref
  43.6 3.2 %shard_map.56 = bf16[64,8,1152]{2,1,0:T(8,128)(2,1)} custom-call(s32[3]{0:T(128)S(1)} %pad_add_fusion.place, bf16[32,16,1024]{2,1,0:T(8,128)(2,1)S(1)} %all-to-all-done.packed_ref, bf16[576,256]{1,0:T(8,128)(2,1)S(1)} %get-tuple-element.8.refs_0_, bf16[576,256]{1,0:T(8,128)(2,1)S(1)} %collective-permute-done.refs_1_, ...), custom_call_target="tpu_custom_call" | custom-call | flops 1073741824 | bytes 3407884 | tf_op jit(solution)/shard_map/pallas_call | solution.py:23
  46.8 0.0 copy-start
  46.8 13.3 %all-to-all-start.1 = ((bf16[64,8,1152]{2,1,0:T(8,128)(2,1)}), bf16[64,8,1152]{2,1,0:T(8,128)(2,1)S(1)}, u32[]{:S(2)}, u32[]{:S(2)}) async-start(bf16[64,8,1152]{2,1,0:T(8,128)(2,1)} %shard_map.56), calls=%async_computation.1 | async-start | bytes 2359296 | tf_op jit(solution)/shard_map/all_to_all | solution.py:247
  60.1 30.8 %all-to-all-done.1.parts_ref = bf16[64,8,1152]{2,1,0:T(8,128)(2,1)S(1)} async-done(((bf16[64,8,1152]{2,1,0:T(8,128)(2,1)}), bf16[64,8,1152]{2,1,0:T(8,128)(2,1)S(1)}, u32[]{:S(2)}, u32[]{:S(2)}) %all-to-all-start.1) | async-done | bytes 1179680 | tf_op jit(solution)/shard_map/all_to_all | solution.py:247
  90.9 0.7 shard_map.57._
  91.6 1.4 %shard_map.58 = bf16[64,16,128]{2,1,0:T(8,128)(2,1)} custom-call(s32[3]{0:T(128)S(1)} %pad_add_fusion.place, bf16[64,8,1152]{2,1,0:T(8,128)(2,1)S(1)} %all-to-all-done.1.parts_ref, bf16[16,1024]{1,0:T(8,128)(2,1)S(1)} %shard_map.57._), custom_call_target="tpu_custom_call" | custom-call | flops 589824 | bytes 1212428 | tf_op jit(solution)/shard_map/pallas_call | solution.py:23
  93.0 9.2 %all-to-all-start.2 = ((bf16[64,16,128]{2,1,0:T(8,128)(2,1)}), bf16[64,16,128]{2,1,0:T(8,128)(2,1)S(1)}, u32[]{:S(2)}, u32[]{:S(2)}) async-start(bf16[64,16,128]{2,1,0:T(8,128)(2,1)} %shard_map.58), calls=%async_computation.2 | async-start | bytes 524288 | tf_op jit(solution)/shard_map/all_to_all | solution.py:268
  102.2 3.9 %collective-permute-start.7 = (bf16[16,1024]{1,0:T(8,128)(2,1)S(1)}, bf16[16,1024]{1,0:T(8,128)(2,1)S(1)}, u32[]{:S(2)}, u32[]{:S(2)}) collective-permute-start(bf16[16,1024]{1,0:T(8,128)(2,1)S(1)} %shard_map.57._), channel_id=1, source_target_pairs={{64,0},{0,64},{65,1},{1,65},{66,2},{2,66},{67,3},{3,67},{68,4},{4,... | collective-permute-start | bytes 98312 | tf_op jit(solution)/shard_map/ppermute | solution.py:18
  106.1 6.5 %collective-permute-done.7 = bf16[16,1024]{1,0:T(8,128)(2,1)S(1)} collective-permute-done((bf16[16,1024]{1,0:T(8,128)(2,1)S(1)}, bf16[16,1024]{1,0:T(8,128)(2,1)S(1)}, u32[]{:S(2)}, u32[]{:S(2)}) %collective-permute-start.7) | collective-permute-done | bytes 32800 | tf_op jit(solution)/shard_map/ppermute | solution.py:18
  112.5 1.9 %collective-permute-start.10 = (bf16[2,16,1024]{2,1,0:T(8,128)(2,1)S(1)}, bf16[2,16,1024]{2,1,0:T(8,128)(2,1)S(1)}, u32[]{:S(2)}, u32[]{:S(2)}) collective-permute-start(bf16[2,16,1024]{2,1,0:T(8,128)(2,1)S(1)} %pad_maximum_fusion.refs_0_), channel_id=1, source_target_pairs={{384,0},{0,128},{128,256},{256,384},{385,1},{1,129},{129,257},{257... | collective-permute-start | bytes 196616 | tf_op jit(solution)/shard_map/ppermute | solution.py:18
  114.5 4.6 %collective-permute-start.8 = (bf16[2,16,1024]{2,1,0:T(8,128)(2,1)S(1)}, bf16[2,16,1024]{2,1,0:T(8,128)(2,1)S(1)}, u32[]{:S(2)}, u32[]{:S(2)}) collective-permute-start(bf16[2,16,1024]{2,1,0:T(8,128)(2,1)S(1)} %pad_maximum_fusion.refs_0_), channel_id=1, source_target_pairs={{128,0},{256,128},{384,256},{0,384},{129,1},{257,129},{385,257},{1... | collective-permute-start | bytes 196616 | tf_op jit(solution)/shard_map/ppermute | solution.py:18
  119.0 2.6 %collective-permute-start.9 = (bf16[2,16,1024]{2,1,0:T(8,128)(2,1)S(1)}, bf16[2,16,1024]{2,1,0:T(8,128)(2,1)S(1)}, u32[]{:S(2)}, u32[]{:S(2)}) collective-permute-start(bf16[2,16,1024]{2,1,0:T(8,128)(2,1)S(1)} %pad_maximum_fusion.refs_0_), channel_id=1, source_target_pairs={{256,0},{384,128},{0,256},{128,384},{257,1},{385,129},{1,257},{129... | collective-permute-start | bytes 196616 | tf_op jit(solution)/shard_map/ppermute | solution.py:18
  121.6 0.0 collective-permute-done.10.refs_3_
  121.7 3.9 %collective-permute-done.9.refs_2_ = bf16[2,16,1024]{2,1,0:T(8,128)(2,1)S(1)} collective-permute-done((bf16[2,16,1024]{2,1,0:T(8,128)(2,1)S(1)}, bf16[2,16,1024]{2,1,0:T(8,128)(2,1)S(1)}, u32[]{:S(2)}, u32[]{:S(2)}) %collective-permute-start.9) | collective-permute-done | bytes 65568 | tf_op jit(solution)/shard_map/ppermute | solution.py:18
  125.5 2.2 %shard_map.59 = f32[56,64]{1,0:T(8,128)} custom-call(s32[3]{0:T(128)S(1)} %pad_add_fusion.place, bf16[64,16,128]{2,1,0:T(8,128)(2,1)S(1)} %all-to-all-done.2.out_ref, bf16[2,16,1024]{2,1,0:T(8,128)(2,1)S(1)} %pad_maximum_fusion.refs_0_, bf16[2,16,1024]{2,1,0:T(8,128)(2,1)S(1)} %collective-permute-done.8.refs_1_, ...), custom_call_target="tpu_custom_call" | custom-call | flops 67108864 | bytes 524300 | tf_op jit(solution)/shard_map/pallas_call | solution.py:23
  (7 shorter events, 0.0 us)
Async XLA Ops:
  3.5 40.1 %all-to-all-start = ((bf16[32,16,1024]{2,1,0:T(8,128)(2,1)}), bf16[32,16,1024]{2,1,0:T(8,128)(2,1)S(1)}, u32[]{:S(2)}, u32[]{:S(2)}) async-start(bf16[32,16,1024]{2,1,0:T(8,128)(2,1)} %get-tuple-element.7), calls=%async_computation | async-start | bytes 2097152 | tf_op jit(solution)/shard_map/all_to_all | solution.py:226
  16.9 13.1 %collective-permute-start = (bf16[576,256]{1,0:T(8,128)(2,1)S(1)}, bf16[576,256]{1,0:T(8,128)(2,1)S(1)}, u32[]{:S(2)}, u32[]{:S(2)}) collective-permute-start(bf16[576,256]{1,0:T(8,128)(2,1)S(1)} %get-tuple-element.8.refs_0_), channel_id=1, source_target_pairs={{128,0},{256,128},{384,256},{0,384},{129,1},{257,129},{385,257},{1... | collective-permute-start | bytes 884744 | tf_op jit(solution)/shard_map/ppermute | solution.py:18
  21.3 15.5 %collective-permute-start.1 = (bf16[576,256]{1,0:T(8,128)(2,1)S(1)}, bf16[576,256]{1,0:T(8,128)(2,1)S(1)}, u32[]{:S(2)}, u32[]{:S(2)}) collective-permute-start(bf16[576,256]{1,0:T(8,128)(2,1)S(1)} %get-tuple-element.8.refs_0_), channel_id=1, source_target_pairs={{256,0},{384,128},{0,256},{128,384},{257,1},{385,129},{1,257},{129... | collective-permute-start | bytes 884744 | tf_op jit(solution)/shard_map/ppermute | solution.py:18
  23.8 16.2 %collective-permute-start.2 = (bf16[576,256]{1,0:T(8,128)(2,1)S(1)}, bf16[576,256]{1,0:T(8,128)(2,1)S(1)}, u32[]{:S(2)}, u32[]{:S(2)}) collective-permute-start(bf16[576,256]{1,0:T(8,128)(2,1)S(1)} %get-tuple-element.8.refs_0_), channel_id=1, source_target_pairs={{384,0},{0,128},{128,256},{256,384},{385,1},{1,129},{129,257},{257... | collective-permute-start | bytes 884744 | tf_op jit(solution)/shard_map/ppermute | solution.py:18
  26.3 16.1 %collective-permute-start.3 = (bf16[576,256]{1,0:T(8,128)(2,1)S(1)}, bf16[576,256]{1,0:T(8,128)(2,1)S(1)}, u32[]{:S(2)}, u32[]{:S(2)}) collective-permute-start(bf16[576,256]{1,0:T(8,128)(2,1)S(1)} %get-tuple-element.8.refs_0_), channel_id=1, source_target_pairs={{1,0},{0,1},{3,2},{2,3},{5,4},{4,5},{7,6},{6,7},{9,8},{8,9},{11,10... | collective-permute-start | bytes 884744 | tf_op jit(solution)/shard_map/ppermute | solution.py:18
  30.0 12.4 %collective-permute-start.4 = (bf16[576,256]{1,0:T(8,128)(2,1)S(1)}, bf16[576,256]{1,0:T(8,128)(2,1)S(1)}, u32[]{:S(2)}, u32[]{:S(2)}) collective-permute-start(bf16[576,256]{1,0:T(8,128)(2,1)S(1)} %collective-permute-done.refs_1_), channel_id=1, source_target_pairs={{1,0},{0,1},{3,2},{2,3},{5,4},{4,5},{7,6},{6,7},{9,8},{8,9},{11,10... | collective-permute-start | bytes 884744 | tf_op jit(solution)/shard_map/ppermute | solution.py:18
  36.8 5.6 %collective-permute-start.5 = (bf16[576,256]{1,0:T(8,128)(2,1)S(1)}, bf16[576,256]{1,0:T(8,128)(2,1)S(1)}, u32[]{:S(2)}, u32[]{:S(2)}) collective-permute-start(bf16[576,256]{1,0:T(8,128)(2,1)S(1)} %collective-permute-done.1.refs_2_), channel_id=1, source_target_pairs={{1,0},{0,1},{3,2},{2,3},{5,4},{4,5},{7,6},{6,7},{9,8},{8,9},{11,10... | collective-permute-start | bytes 884744 | tf_op jit(solution)/shard_map/ppermute | solution.py:18
  40.0 3.6 %collective-permute-start.6 = (bf16[576,256]{1,0:T(8,128)(2,1)S(1)}, bf16[576,256]{1,0:T(8,128)(2,1)S(1)}, u32[]{:S(2)}, u32[]{:S(2)}) collective-permute-start(bf16[576,256]{1,0:T(8,128)(2,1)S(1)} %collective-permute-done.2.refs_3_), channel_id=1, source_target_pairs={{1,0},{0,1},{3,2},{2,3},{5,4},{4,5},{7,6},{6,7},{9,8},{8,9},{11,10... | collective-permute-start | bytes 884744 | tf_op jit(solution)/shard_map/ppermute | solution.py:18
  46.8 13.3 %copy-start = (s32[1,4]{1,0:T(1,128)S(1)}, s32[1,4]{1,0:T(1,128)}, u32[]{:S(2)}) copy-start(s32[1,4]{1,0:T(1,128)} %param.9) | copy-start | bytes 52
  46.8 44.1 %all-to-all-start.1 = ((bf16[64,8,1152]{2,1,0:T(8,128)(2,1)}), bf16[64,8,1152]{2,1,0:T(8,128)(2,1)S(1)}, u32[]{:S(2)}, u32[]{:S(2)}) async-start(bf16[64,8,1152]{2,1,0:T(8,128)(2,1)} %shard_map.56), calls=%async_computation.1 | async-start | bytes 2359296 | tf_op jit(solution)/shard_map/all_to_all | solution.py:247
  93.0 32.5 %all-to-all-start.2 = ((bf16[64,16,128]{2,1,0:T(8,128)(2,1)}), bf16[64,16,128]{2,1,0:T(8,128)(2,1)S(1)}, u32[]{:S(2)}, u32[]{:S(2)}) async-start(bf16[64,16,128]{2,1,0:T(8,128)(2,1)} %shard_map.58), calls=%async_computation.2 | async-start | bytes 524288 | tf_op jit(solution)/shard_map/all_to_all | solution.py:268
  102.2 10.3 %collective-permute-start.7 = (bf16[16,1024]{1,0:T(8,128)(2,1)S(1)}, bf16[16,1024]{1,0:T(8,128)(2,1)S(1)}, u32[]{:S(2)}, u32[]{:S(2)}) collective-permute-start(bf16[16,1024]{1,0:T(8,128)(2,1)S(1)} %shard_map.57._), channel_id=1, source_target_pairs={{64,0},{0,64},{65,1},{1,65},{66,2},{2,66},{67,3},{3,67},{68,4},{4,... | collective-permute-start | bytes 98312 | tf_op jit(solution)/shard_map/ppermute | solution.py:18
  112.5 9.1 %collective-permute-start.10 = (bf16[2,16,1024]{2,1,0:T(8,128)(2,1)S(1)}, bf16[2,16,1024]{2,1,0:T(8,128)(2,1)S(1)}, u32[]{:S(2)}, u32[]{:S(2)}) collective-permute-start(bf16[2,16,1024]{2,1,0:T(8,128)(2,1)S(1)} %pad_maximum_fusion.refs_0_), channel_id=1, source_target_pairs={{384,0},{0,128},{128,256},{256,384},{385,1},{1,129},{129,257},{257... | collective-permute-start | bytes 196616 | tf_op jit(solution)/shard_map/ppermute | solution.py:18
  114.5 7.2 %collective-permute-start.8 = (bf16[2,16,1024]{2,1,0:T(8,128)(2,1)S(1)}, bf16[2,16,1024]{2,1,0:T(8,128)(2,1)S(1)}, u32[]{:S(2)}, u32[]{:S(2)}) collective-permute-start(bf16[2,16,1024]{2,1,0:T(8,128)(2,1)S(1)} %pad_maximum_fusion.refs_0_), channel_id=1, source_target_pairs={{128,0},{256,128},{384,256},{0,384},{129,1},{257,129},{385,257},{1... | collective-permute-start | bytes 196616 | tf_op jit(solution)/shard_map/ppermute | solution.py:18
  119.0 6.5 %collective-permute-start.9 = (bf16[2,16,1024]{2,1,0:T(8,128)(2,1)S(1)}, bf16[2,16,1024]{2,1,0:T(8,128)(2,1)S(1)}, u32[]{:S(2)}, u32[]{:S(2)}) collective-permute-start(bf16[2,16,1024]{2,1,0:T(8,128)(2,1)S(1)} %pad_maximum_fusion.refs_0_), channel_id=1, source_target_pairs={{256,0},{384,128},{0,256},{128,384},{257,1},{385,129},{1,257},{129... | collective-permute-start | bytes 196616 | tf_op jit(solution)/shard_map/ppermute | solution.py:18

commit v8 on v4

--- a/solution.py
+++ b/solution.py
@@ -9,7 +9,7 @@
 
 NX, NZH, NZL, NY, NC = 4, 2, 4, 8, 2
 CHIPS = NZL * NY
-PARTS = 8
+ORDER = [yb * 4 + ya for ya in range(4) for yb in range(2)]
 BF16, F32 = jnp.bfloat16, jnp.float32
 SMEM = pl.BlockSpec(memory_space=pltpu.SMEM)
 VMEM = pl.BlockSpec(memory_space=pltpu.VMEM)
@@ -48,39 +48,40 @@
 def pack(place, basis_ref, out_rows_ref, acts_ref, grads_ref, packed_ref, payload_ref, *scratch):
     basis, out_rows, grads, turned, packed, sems = scratch
     fin, fout = acts_ref.shape[0], grads_ref.shape[1]
-    width, chips = NC * fin, CHIPS // PARTS
+    width = NC * fin
     loads = [
         pltpu.make_async_copy(out_rows_ref, out_rows, sems.at[0]),
         pltpu.make_async_copy(grads_ref, grads, sems.at[1]),
     ]
-    for i in range(PARTS):
-        cols = pl.ds(i * chips * width, chips * width)
-        loads.append(pltpu.make_async_copy(basis_ref.at[:, cols], basis.at[i], sems.at[2 + i]))
-    stores = [pltpu.make_async_copy(acts_ref, payload_ref.at[pl.ds(0, fin)], sems.at[2 + PARTS])]
+    for zl in range(NZL):
+        cols = pl.ds(zl * NY * width, NY * width)
+        loads.append(pltpu.make_async_copy(basis_ref.at[:, cols], basis.at[zl], sems.at[2 + zl]))
+    stores = [pltpu.make_async_copy(acts_ref, payload_ref.at[pl.ds(0, fin)], sems.at[2 + NZL])]
     for copy in loads + stores:
         copy.start()
     loads[0].wait()
-    for c in range(CHIPS):
-        out = out_rows[:, c * NC * fout : (c + 1) * NC * fout].astype(F32)
-        out = jnp.concatenate([out[:, :fout], out[:, fout:]], axis=0).astype(BF16)
-        packed[c // chips, c % chips, :, width:] = out
+    for zl in range(NZL):
+        for i, y in enumerate(ORDER):
+            first = (zl * NY + y) * NC * fout
+            out = out_rows[:, first : first + NC * fout].astype(F32)
+            packed[zl, i, :, width:] = jnp.concatenate([out[:, :fout], out[:, fout:]], axis=0).astype(BF16)
     loads[1].wait()
     turned[...] = grads[...].astype(F32).T.astype(BF16)
-    stores.append(pltpu.make_async_copy(turned, payload_ref.at[pl.ds(fin, fout)], sems.at[3 + PARTS]))
+    stores.append(pltpu.make_async_copy(turned, payload_ref.at[pl.ds(fin, fout)], sems.at[3 + NZL]))
     stores[-1].start()
-    for i in range(PARTS):
-        loads[2 + i].wait()
+    for zl in range(NZL):
+        loads[2 + zl].wait()
         for x in range(NX):
 
             @pl.when(place[0] == x)
             def _():
-                for c in range(chips):
-                    rows = basis[i, :, c * width : (c + 1) * width].astype(F32)[x * 14 : (x + 1) * 14]
+                for i, y in enumerate(ORDER):
+                    rows = basis[zl, :, y * width : (y + 1) * width].astype(F32)[x * 14 : (x + 1) * 14]
                     rows = jnp.concatenate([rows, jnp.zeros((2, width), F32)], axis=0)
-                    packed[i, c, :, :width] = rows.astype(BF16)
-
-        there = packed_ref.at[pl.ds(i * chips, chips)]
-        stores.append(pltpu.make_async_copy(packed.at[i], there, sems.at[4 + PARTS + i]))
+                    packed[zl, i, :, :width] = rows.astype(BF16)
+
+        there = packed_ref.at[pl.ds(zl * NY, NY)]
+        stores.append(pltpu.make_async_copy(packed.at[zl], there, sems.at[4 + NZL + zl]))
         stores[-1].start()
     for store in stores:
         store.wait()
@@ -110,9 +111,12 @@
         for h in range(2):
             block = slice(h * 128, (h + 1) * 128)
             wide[pl.ds(h * height, height), :] = part[:, block]
-            for half in range(2):
-                wide[pl.ds(h * height + 14 + half, CHIPS, stride=16), :] = out[half * 32 : half * 32 + 32, block]
-                low[pl.ds(half * 8 + s * 2 + h, CHIPS, stride=16), :] = rest[half * 32 : half * 32 + 32, block]
+            for k, y in enumerate(ORDER):
+                for yb in range(2):
+                    mine = slice(k * 8 + yb * 4, k * 8 + yb * 4 + 4), block
+                    first = ((y % 4) * NY + yb) * 16
+                    wide[pl.ds(h * height + first + 14 + y // 4, 4, stride=32), :] = out[mine]
+                    low[pl.ds(first + y // 4 * 8 + s * 2 + h, 4, stride=32), :] = rest[mine]
             outs[s][:, :, block] = wide[h * height : (h + 1) * height].astype(BF16).reshape(CHIPS, 16, 128)
         results.append(pltpu.make_async_copy(outs[s], parts_ref.at[:, :, pl.ds(s * 256, 256)], sems.at[s]))
         results[-1].start()
@@ -196,19 +200,19 @@
         pack,
         (in_hbm((CHIPS, 16, NC * fin + fout)), jax.ShapeDtypeStruct((fin + fout, tok), BF16)),
         [
-            pltpu.VMEM((PARTS, 4 * rows, CHIPS // PARTS * NC * fin), BF16),
+            pltpu.VMEM((NZL, 4 * rows, NY * NC * fin), BF16),
             pltpu.VMEM((8, CHIPS * NC * fout), BF16),
             pltpu.VMEM((tok, fout), BF16),
             pltpu.VMEM((fout, tok), BF16),
-            pltpu.VMEM((PARTS, CHIPS // PARTS, 16, NC * fin + fout), BF16),
-            pltpu.SemaphoreType.DMA((2 * PARTS + 4,)),
+            pltpu.VMEM((NZL, NY, 16, NC * fin + fout), BF16),
+            pltpu.SemaphoreType.DMA((2 * NZL + 4,)),
         ],
         (place, *map(from_hbm, (basis_in, basis_out, acts.T, grads))),
         1 << 20,
         in_specs=[SMEM] + [ANY] * 4,
         out_spec=ANY,
     )
-    packed = lax.all_to_all(packed, ("zl", "y"), split_axis=0, concat_axis=0, tiled=True)
+    packed = lax.all_to_all(packed, ("zl", "ya", "yb"), split_axis=0, concat_axis=0, tiled=True)
 
     own = [payload] + [from_offset(payload, "x", NX, s) for s in range(1, NX)]
     other = [from_offset(v, "core", NC, 1) for v in own]
@@ -229,7 +233,7 @@
         2 * 512 * 1024 * 1024,
         out_spec=ANY,
     )
-    parts = lax.all_to_all(parts, ("zl", "y"), split_axis=0, concat_axis=0, tiled=True)
+    parts = lax.all_to_all(parts, ("zl", "ya", "yb"), split_axis=0, concat_axis=0, tiled=True)
     lens = jnp.pad(doc_lengths.astype(F32), ((0, 0), (0, 124)))
     proj_in, proj_out = call(
         add_up,
@@ -239,7 +243,7 @@
         32 * 16 * 1152,
     )
 
-    proj_out = lax.all_to_all(proj_out, ("zl", "y", "core"), split_axis=0, concat_axis=0, tiled=True)
+    proj_out = lax.all_to_all(proj_out, ("zl", "yb", "ya", "core"), split_axis=0, concat_axis=0, tiled=True)
     pieces = [proj_in] + [from_offset(proj_in, "x", NX, s) for s in range(1, NX)]
     operands = (place, in_vmem(proj_out), *pieces)
     totals = [
@@ -261,7 +265,7 @@
 
 
 def solution(mesh):
-    fine = Mesh(mesh.devices.reshape(NX, NZH, NZL, NY, NC), ("x", "zh", "zl", "y", "core"))
-    dp, mp = ("x", "zh"), ("zl", "y", "core")
+    fine = Mesh(mesh.devices.reshape(NX, NZH, NZL, 2, 4, NC), ("x", "zh", "zl", "yb", "ya", "core"))
+    dp, mp = ("x", "zh"), ("zl", "yb", "ya", "core")
     in_specs = (P(dp, mp), P(dp, mp), P(mp, None), P(mp, None), P(dp, None))
     return jax.shard_map(body, mesh=fine, in_specs=in_specs, out_specs=P(dp, mp), check_vma=False)

time: 120 us -> 121 us (level)
  waiting for transfers between devices: 34.2 us -> 37 us
  starting transfers between devices: 73.4 us -> 71.2 us
    all_to_all x3, waiting for transfers between devices: 28 us -> 30.8 us  [the longest x1 30.2 us: body(): lax.all_to_all(parts, ('zl', 'ya', 'yb'), split_axis=0, concat_axis=0, ti...]
    all_to_all x3, starting transfers between devices: 33 us -> 30.6 us  [the longest x1 13.5 us: body(): lax.all_to_all(packed, ('zl', 'ya', 'yb'), split_axis=0, concat_axis=0, t...]
  transfers between devices with their start and end apart: 14 -> 14, of which waited for: 7 -> 8; matrix products, arithmetic and copies ran while one was open for 0% -> 0% of each run, Pallas kernels for 1% -> 1%
where the time goes in v8:
time: 121 us; the launch traced here: 120 us
  starting transfers between devices  71.2 us (59%)
  waiting for transfers between devices  37 us (31%)
  Pallas kernels  10.6 us (9%)
    ppermute x11, starting transfers between devices, from_offset(): lax.ppermute(value, axis, [((i + offset) % size, i) for i in range(size)])  40.5 us
    all_to_all x1, waiting for transfers between devices, body(): lax.all_to_all(parts, ('zl', 'ya', 'yb'), split_axis=0, concat_axis=0, ti...  30.2 us
    all_to_all x1, starting transfers between devices, body(): lax.all_to_all(packed, ('zl', 'ya', 'yb'), split_axis=0, concat_axis=0, t...  13.5 us
    pallas_call x5, Pallas kernels, call(): pl.pallas_call(kernel, out_shape=shapes, in_specs=in_specs or [SMEM] + [V...  10.6 us
    all_to_all x1, starting transfers between devices, body(): lax.all_to_all(parts, ('zl', 'ya', 'yb'), split_axis=0, concat_axis=0, ti...  9.07 us
    all_to_all x1, starting transfers between devices, body(): lax.all_to_all(proj_out, ('zl', 'yb', 'ya', 'core'), split_axis=0, concat...  8.08 us
    ppermute x11, waiting for transfers between devices, from_offset(): lax.ppermute(value, axis, [((i + offset) % size, i) for i in range(size)])  6.19 us
  transfers between devices with their start and end apart: 14, of which 8 were waited for; matrix products, arithmetic and copies ran while one was open for 0% of the time, Pallas kernels for 1%

profile of v8, /device:TPU:1, one launch (start us, length us, event | category | flops | bytes accessed | tf_op | source)
XLA Modules:
  0.0 119.6 jit_solution(16413107859899737570)
XLA Ops:
  0.0 0.1 pad_add_fusion.place
  0.1 3.4 %shard_map.55 = (bf16[32,16,1024]{2,1,0:T(8,128)(2,1)}, bf16[576,256]{1,0:T(8,128)(2,1)S(1)}) custom-call(s32[3]{0:T(128)S(1)} %pad_add_fusion.place, bf16[56,28672]{1,0:T(8,128)(2,1)} %basis_ref.1, bf16[8,8192]{1,0:T(8,128)(2,1)} %out_rows_ref.1, bf16[448,256]{1,0:T(8,128)(2,1)} %bitcast.6, bf16[256,128]{1,0:T(8,128)(2,1)} %grads_ref.1), custom_call_target="tpu_custom_call" | custom-call | flops 1048576 | bytes 3637260 | tf_op jit(solution)/shard_map/pallas_call | solution.py:25
  3.5 13.5 %all-to-all-start = ((bf16[32,16,1024]{2,1,0:T(8,128)(2,1)}), bf16[32,16,1024]{2,1,0:T(8,128)(2,1)S(1)}, u32[]{:S(2)}, u32[]{:S(2)}) async-start(bf16[32,16,1024]{2,1,0:T(8,128)(2,1)} %get-tuple-element.9), calls=%async_computation | async-start | bytes 2097152 | tf_op jit(solution)/shard_map/all_to_all | solution.py:215
  16.9 4.4 %collective-permute-start = (bf16[576,256]{1,0:T(8,128)(2,1)S(1)}, bf16[576,256]{1,0:T(8,128)(2,1)S(1)}, u32[]{:S(2)}, u32[]{:S(2)}) collective-permute-start(bf16[576,256]{1,0:T(8,128)(2,1)S(1)} %get-tuple-element.10.refs_0_), channel_id=1, source_target_pairs={{128,0},{256,128},{384,256},{0,384},{129,1},{257,129},{385,257},{1... | collective-permute-start | bytes 884744 | tf_op jit(solution)/shard_map/ppermute | solution.py:20
  21.3 2.5 %collective-permute-start.1 = (bf16[576,256]{1,0:T(8,128)(2,1)S(1)}, bf16[576,256]{1,0:T(8,128)(2,1)S(1)}, u32[]{:S(2)}, u32[]{:S(2)}) collective-permute-start(bf16[576,256]{1,0:T(8,128)(2,1)S(1)} %get-tuple-element.10.refs_0_), channel_id=1, source_target_pairs={{256,0},{384,128},{0,256},{128,384},{257,1},{385,129},{1,257},{129... | collective-permute-start | bytes 884744 | tf_op jit(solution)/shard_map/ppermute | solution.py:20
  23.8 2.5 %collective-permute-start.2 = (bf16[576,256]{1,0:T(8,128)(2,1)S(1)}, bf16[576,256]{1,0:T(8,128)(2,1)S(1)}, u32[]{:S(2)}, u32[]{:S(2)}) collective-permute-start(bf16[576,256]{1,0:T(8,128)(2,1)S(1)} %get-tuple-element.10.refs_0_), channel_id=1, source_target_pairs={{384,0},{0,128},{128,256},{256,384},{385,1},{1,129},{129,257},{257... | collective-permute-start | bytes 884744 | tf_op jit(solution)/shard_map/ppermute | solution.py:20
  26.3 3.7 %collective-permute-start.3 = (bf16[576,256]{1,0:T(8,128)(2,1)S(1)}, bf16[576,256]{1,0:T(8,128)(2,1)S(1)}, u32[]{:S(2)}, u32[]{:S(2)}) collective-permute-start(bf16[576,256]{1,0:T(8,128)(2,1)S(1)} %get-tuple-element.10.refs_0_), channel_id=1, source_target_pairs={{1,0},{0,1},{3,2},{2,3},{5,4},{4,5},{7,6},{6,7},{9,8},{8,9},{11,10... | collective-permute-start | bytes 884744 | tf_op jit(solution)/shard_map/ppermute | solution.py:20
  30.0 0.0 collective-permute-done.refs_1_
  30.1 6.7 %collective-permute-start.4 = (bf16[576,256]{1,0:T(8,128)(2,1)S(1)}, bf16[576,256]{1,0:T(8,128)(2,1)S(1)}, u32[]{:S(2)}, u32[]{:S(2)}) collective-permute-start(bf16[576,256]{1,0:T(8,128)(2,1)S(1)} %collective-permute-done.refs_1_), channel_id=1, source_target_pairs={{1,0},{0,1},{3,2},{2,3},{5,4},{4,5},{7,6},{6,7},{9,8},{8,9},{11,10... | collective-permute-start | bytes 884744 | tf_op jit(solution)/shard_map/ppermute | solution.py:20
  36.8 0.0 collective-permute-done.1.refs_2_
  36.8 1.9 %collective-permute-start.5 = (bf16[576,256]{1,0:T(8,128)(2,1)S(1)}, bf16[576,256]{1,0:T(8,128)(2,1)S(1)}, u32[]{:S(2)}, u32[]{:S(2)}) collective-permute-start(bf16[576,256]{1,0:T(8,128)(2,1)S(1)} %collective-permute-done.1.refs_2_), channel_id=1, source_target_pairs={{1,0},{0,1},{3,2},{2,3},{5,4},{4,5},{7,6},{6,7},{9,8},{8,9},{11,10... | collective-permute-start | bytes 884744 | tf_op jit(solution)/shard_map/ppermute | solution.py:20
  38.7 1.3 %collective-permute-done.2.refs_3_ = bf16[576,256]{1,0:T(8,128)(2,1)S(1)} collective-permute-done((bf16[576,256]{1,0:T(8,128)(2,1)S(1)}, bf16[576,256]{1,0:T(8,128)(2,1)S(1)}, u32[]{:S(2)}, u32[]{:S(2)}) %collective-permute-start.2) | collective-permute-done | bytes 294944 | tf_op jit(solution)/shard_map/ppermute | solution.py:20
  40.0 2.4 %collective-permute-start.6 = (bf16[576,256]{1,0:T(8,128)(2,1)S(1)}, bf16[576,256]{1,0:T(8,128)(2,1)S(1)}, u32[]{:S(2)}, u32[]{:S(2)}) collective-permute-start(bf16[576,256]{1,0:T(8,128)(2,1)S(1)} %collective-permute-done.2.refs_3_), channel_id=1, source_target_pairs={{1,0},{0,1},{3,2},{2,3},{5,4},{4,5},{7,6},{6,7},{9,8},{8,9},{11,10... | collective-permute-start | bytes 884744 | tf_op jit(solution)/shard_map/ppermute | solution.py:20
  42.4 1.2 collective-permute-done.6.refs_7_
  43.6 0.5 all-to-all-done.packed_ref
  44.1 3.3 %shard_map.56 = bf16[32,16,1152]{2,1,0:T(8,128)(2,1)} custom-call(s32[3]{0:T(128)S(1)} %pad_add_fusion.place, bf16[32,16,1024]{2,1,0:T(8,128)(2,1)S(1)} %all-to-all-done.packed_ref, bf16[576,256]{1,0:T(8,128)(2,1)S(1)} %get-tuple-element.10.refs_0_, bf16[576,256]{1,0:T(8,128)(2,1)S(1)} %collective-permute-done.refs_1_, ...), custom_call_target="tpu_custom_call" | custom-call | flops 1073741824 | bytes 3407884 | tf_op jit(solution)/shard_map/pallas_call | solution.py:25
  47.4 0.0 copy-start
  47.4 9.1 %all-to-all-start.1 = ((bf16[32,16,1152]{2,1,0:T(8,128)(2,1)}), bf16[32,16,1152]{2,1,0:T(8,128)(2,1)S(1)}, u32[]{:S(2)}, u32[]{:S(2)}) async-start(bf16[32,16,1152]{2,1,0:T(8,128)(2,1)} %shard_map.56), calls=%async_computation.1 | async-start | bytes 2359296 | tf_op jit(solution)/shard_map/all_to_all | solution.py:236
  56.5 30.2 %all-to-all-done.1.parts_ref = bf16[32,16,1152]{2,1,0:T(8,128)(2,1)S(1)} async-done(((bf16[32,16,1152]{2,1,0:T(8,128)(2,1)}), bf16[32,16,1152]{2,1,0:T(8,128)(2,1)S(1)}, u32[]{:S(2)}, u32[]{:S(2)}) %all-to-all-start.1) | async-done | bytes 1179680 | tf_op jit(solution)/shard_map/all_to_all | solution.py:236
  86.7 1.4 %shard_map.57 = (bf16[16,1024]{1,0:T(8,128)(2,1)S(1)}, bf16[64,16,128]{2,1,0:T(8,128)(2,1)}) custom-call(s32[3]{0:T(128)S(1)} %pad_add_fusion.place, f32[1,128]{1,0:T(1,128)S(1)} %pad.4.lens_ref, bf16[32,16,1152]{2,1,0:T(8,128)(2,1)S(1)} %all-to-all-done.1.parts_ref), custom_call_target="tpu_custom_call" | custom-call | flops 589824 | bytes 1180172 | tf_op jit(solution)/shard_map/pallas_call | solution.py:25
  88.1 8.1 %all-to-all-start.2 = ((bf16[64,16,128]{2,1,0:T(8,128)(2,1)}), bf16[64,16,128]{2,1,0:T(8,128)(2,1)S(1)}, u32[]{:S(2)}, u32[]{:S(2)}) async-start(bf16[64,16,128]{2,1,0:T(8,128)(2,1)} %get-tuple-element.11), calls=%async_computation.2 | async-start | bytes 524288 | tf_op jit(solution)/shard_map/all_to_all | solution.py:246
  96.2 4.1 %collective-permute-start.7 = (bf16[16,1024]{1,0:T(8,128)(2,1)S(1)}, bf16[16,1024]{1,0:T(8,128)(2,1)S(1)}, u32[]{:S(2)}, u32[]{:S(2)}) collective-permute-start(bf16[16,1024]{1,0:T(8,128)(2,1)S(1)} %get-tuple-element.12.refs_0_), channel_id=1, source_target_pairs={{128,0},{256,128},{384,256},{0,384},{129,1},{257,129},{385,257},{1... | collective-permute-start | bytes 98312 | tf_op jit(solution)/shard_map/ppermute | solution.py:20
  100.3 1.9 %collective-permute-start.8 = (bf16[16,1024]{1,0:T(8,128)(2,1)S(1)}, bf16[16,1024]{1,0:T(8,128)(2,1)S(1)}, u32[]{:S(2)}, u32[]{:S(2)}) collective-permute-start(bf16[16,1024]{1,0:T(8,128)(2,1)S(1)} %get-tuple-element.12.refs_0_), channel_id=1, source_target_pairs={{256,0},{384,128},{0,256},{128,384},{257,1},{385,129},{1,257},{129... | collective-permute-start | bytes 98312 | tf_op jit(solution)/shard_map/ppermute | solution.py:20
  102.2 2.5 %collective-permute-start.9 = (bf16[16,1024]{1,0:T(8,128)(2,1)S(1)}, bf16[16,1024]{1,0:T(8,128)(2,1)S(1)}, u32[]{:S(2)}, u32[]{:S(2)}) collective-permute-start(bf16[16,1024]{1,0:T(8,128)(2,1)S(1)} %get-tuple-element.12.refs_0_), channel_id=1, source_target_pairs={{384,0},{0,128},{128,256},{256,384},{385,1},{1,129},{129,257},{257... | collective-permute-start | bytes 98312 | tf_op jit(solution)/shard_map/ppermute | solution.py:20
  104.7 2.0 %collective-permute-done.8.refs_2_ = bf16[16,1024]{1,0:T(8,128)(2,1)S(1)} collective-permute-done((bf16[16,1024]{1,0:T(8,128)(2,1)S(1)}, bf16[16,1024]{1,0:T(8,128)(2,1)S(1)}, u32[]{:S(2)}, u32[]{:S(2)}) %collective-permute-start.8) | collective-permute-done | bytes 32800 | tf_op jit(solution)/shard_map/ppermute | solution.py:20
  106.8 1.6 %collective-permute-done.9.refs_3_ = bf16[16,1024]{1,0:T(8,128)(2,1)S(1)} collective-permute-done((bf16[16,1024]{1,0:T(8,128)(2,1)S(1)}, bf16[16,1024]{1,0:T(8,128)(2,1)S(1)}, u32[]{:S(2)}, u32[]{:S(2)}) %collective-permute-start.9) | collective-permute-done | bytes 32800 | tf_op jit(solution)/shard_map/ppermute | solution.py:20
  108.4 0.1 all-to-all-done.2.out_ref
  108.5 1.2 %shard_map.59 = f32[56,64]{1,0:T(8,128)S(1)} custom-call(s32[3]{0:T(128)S(1)} %pad_add_fusion.place, bf16[64,16,128]{2,1,0:T(8,128)(2,1)S(1)} %all-to-all-done.2.out_ref, bf16[16,1024]{1,0:T(8,128)(2,1)S(1)} %get-tuple-element.12.refs_0_, bf16[16,1024]{1,0:T(8,128)(2,1)S(1)} %collective-permute-done.7.refs_1_, ...), custom_call_target="tpu_custom_call" | custom-call | flops 33554432 | bytes 393228 | tf_op jit(solution)/shard_map/pallas_call | solution.py:25
  109.7 7.9 %collective-permute-start.10 = (f32[56,64]{1,0:T(8,128)S(1)}, f32[56,64]{1,0:T(8,128)S(1)}, u32[]{:S(2)}, u32[]{:S(2)}) collective-permute-start(f32[56,64]{1,0:T(8,128)S(1)} %shard_map.59), channel_id=1, source_target_pairs={{64,0},{0,64},{65,1},{1,65},{66,2},{2,66},{67,3},{3,67},{68,4},{4,... | collective-permute-start | bytes 43016 | tf_op jit(solution)/shard_map/ppermute | solution.py:20
  117.7 1.2 %shard_map.58 = f32[56,64]{1,0:T(8,128)S(1)} custom-call(s32[3]{0:T(128)S(1)} %pad_add_fusion.place, bf16[64,16,128]{2,1,0:T(8,128)(2,1)S(1)} %all-to-all-done.2.out_ref, bf16[16,1024]{1,0:T(8,128)(2,1)S(1)} %get-tuple-element.12.refs_0_, bf16[16,1024]{1,0:T(8,128)(2,1)S(1)} %collective-permute-done.7.refs_1_, ...), custom_call_target="tpu_custom_call" | custom-call | flops 33554432 | bytes 393228 | tf_op jit(solution)/shard_map/pallas_call | solution.py:25
  118.9 0.1 collective-permute-done.10
  119.0 0.6 add_bitcast_fusion
  (7 shorter events, 0.0 us)
Async XLA Ops:
  3.5 40.6 %all-to-all-start = ((bf16[32,16,1024]{2,1,0:T(8,128)(2,1)}), bf16[32,16,1024]{2,1,0:T(8,128)(2,1)S(1)}, u32[]{:S(2)}, u32[]{:S(2)}) async-start(bf16[32,16,1024]{2,1,0:T(8,128)(2,1)} %get-tuple-element.9), calls=%async_computation | async-start | bytes 2097152 | tf_op jit(solution)/shard_map/all_to_all | solution.py:215
  16.9 13.1 %collective-permute-start = (bf16[576,256]{1,0:T(8,128)(2,1)S(1)}, bf16[576,256]{1,0:T(8,128)(2,1)S(1)}, u32[]{:S(2)}, u32[]{:S(2)}) collective-permute-start(bf16[576,256]{1,0:T(8,128)(2,1)S(1)} %get-tuple-element.10.refs_0_), channel_id=1, source_target_pairs={{128,0},{256,128},{384,256},{0,384},{129,1},{257,129},{385,257},{1... | collective-permute-start | bytes 884744 | tf_op jit(solution)/shard_map/ppermute | solution.py:20
  21.3 15.5 %collective-permute-start.1 = (bf16[576,256]{1,0:T(8,128)(2,1)S(1)}, bf16[576,256]{1,0:T(8,128)(2,1)S(1)}, u32[]{:S(2)}, u32[]{:S(2)}) collective-permute-start(bf16[576,256]{1,0:T(8,128)(2,1)S(1)} %get-tuple-element.10.refs_0_), channel_id=1, source_target_pairs={{256,0},{384,128},{0,256},{128,384},{257,1},{385,129},{1,257},{129... | collective-permute-start | bytes 884744 | tf_op jit(solution)/shard_map/ppermute | solution.py:20
  23.8 16.2 %collective-permute-start.2 = (bf16[576,256]{1,0:T(8,128)(2,1)S(1)}, bf16[576,256]{1,0:T(8,128)(2,1)S(1)}, u32[]{:S(2)}, u32[]{:S(2)}) collective-permute-start(bf16[576,256]{1,0:T(8,128)(2,1)S(1)} %get-tuple-element.10.refs_0_), channel_id=1, source_target_pairs={{384,0},{0,128},{128,256},{256,384},{385,1},{1,129},{129,257},{257... | collective-permute-start | bytes 884744 | tf_op jit(solution)/shard_map/ppermute | solution.py:20
  26.3 16.1 %collective-permute-start.3 = (bf16[576,256]{1,0:T(8,128)(2,1)S(1)}, bf16[576,256]{1,0:T(8,128)(2,1)S(1)}, u32[]{:S(2)}, u32[]{:S(2)}) collective-permute-start(bf16[576,256]{1,0:T(8,128)(2,1)S(1)} %get-tuple-element.10.refs_0_), channel_id=1, source_target_pairs={{1,0},{0,1},{3,2},{2,3},{5,4},{4,5},{7,6},{6,7},{9,8},{8,9},{11,10... | collective-permute-start | bytes 884744 | tf_op jit(solution)/shard_map/ppermute | solution.py:20
  30.1 12.4 %collective-permute-start.4 = (bf16[576,256]{1,0:T(8,128)(2,1)S(1)}, bf16[576,256]{1,0:T(8,128)(2,1)S(1)}, u32[]{:S(2)}, u32[]{:S(2)}) collective-permute-start(bf16[576,256]{1,0:T(8,128)(2,1)S(1)} %collective-permute-done.refs_1_), channel_id=1, source_target_pairs={{1,0},{0,1},{3,2},{2,3},{5,4},{4,5},{7,6},{6,7},{9,8},{8,9},{11,10... | collective-permute-start | bytes 884744 | tf_op jit(solution)/shard_map/ppermute | solution.py:20
  36.8 5.6 %collective-permute-start.5 = (bf16[576,256]{1,0:T(8,128)(2,1)S(1)}, bf16[576,256]{1,0:T(8,128)(2,1)S(1)}, u32[]{:S(2)}, u32[]{:S(2)}) collective-permute-start(bf16[576,256]{1,0:T(8,128)(2,1)S(1)} %collective-permute-done.1.refs_2_), channel_id=1, source_target_pairs={{1,0},{0,1},{3,2},{2,3},{5,4},{4,5},{7,6},{6,7},{9,8},{8,9},{11,10... | collective-permute-start | bytes 884744 | tf_op jit(solution)/shard_map/ppermute | solution.py:20
  40.0 3.6 %collective-permute-start.6 = (bf16[576,256]{1,0:T(8,128)(2,1)S(1)}, bf16[576,256]{1,0:T(8,128)(2,1)S(1)}, u32[]{:S(2)}, u32[]{:S(2)}) collective-permute-start(bf16[576,256]{1,0:T(8,128)(2,1)S(1)} %collective-permute-done.2.refs_3_), channel_id=1, source_target_pairs={{1,0},{0,1},{3,2},{2,3},{5,4},{4,5},{7,6},{6,7},{9,8},{8,9},{11,10... | collective-permute-start | bytes 884744 | tf_op jit(solution)/shard_map/ppermute | solution.py:20
  47.4 9.1 %copy-start = (s32[1,4]{1,0:T(1,128)S(1)}, s32[1,4]{1,0:T(1,128)}, u32[]{:S(2)}) copy-start(s32[1,4]{1,0:T(1,128)} %param.9) | copy-start | bytes 52
  47.4 39.3 %all-to-all-start.1 = ((bf16[32,16,1152]{2,1,0:T(8,128)(2,1)}), bf16[32,16,1152]{2,1,0:T(8,128)(2,1)S(1)}, u32[]{:S(2)}, u32[]{:S(2)}) async-start(bf16[32,16,1152]{2,1,0:T(8,128)(2,1)} %shard_map.56), calls=%async_computation.1 | async-start | bytes 2359296 | tf_op jit(solution)/shard_map/all_to_all | solution.py:236
  88.1 20.4 %all-to-all-start.2 = ((bf16[64,16,128]{2,1,0:T(8,128)(2,1)}), bf16[64,16,128]{2,1,0:T(8,128)(2,1)S(1)}, u32[]{:S(2)}, u32[]{:S(2)}) async-start(bf16[64,16,128]{2,1,0:T(8,128)(2,1)} %get-tuple-element.11), calls=%async_computation.2 | async-start | bytes 524288 | tf_op jit(solution)/shard_map/all_to_all | solution.py:246
  96.2 8.5 %collective-permute-start.7 = (bf16[16,1024]{1,0:T(8,128)(2,1)S(1)}, bf16[16,1024]{1,0:T(8,128)(2,1)S(1)}, u32[]{:S(2)}, u32[]{:S(2)}) collective-permute-start(bf16[16,1024]{1,0:T(8,128)(2,1)S(1)} %get-tuple-element.12.refs_0_), channel_id=1, source_target_pairs={{128,0},{256,128},{384,256},{0,384},{129,1},{257,129},{385,257},{1... | collective-permute-start | bytes 98312 | tf_op jit(solution)/shard_map/ppermute | solution.py:20
  100.3 6.5 %collective-permute-start.8 = (bf16[16,1024]{1,0:T(8,128)(2,1)S(1)}, bf16[16,1024]{1,0:T(8,128)(2,1)S(1)}, u32[]{:S(2)}, u32[]{:S(2)}) collective-permute-start(bf16[16,1024]{1,0:T(8,128)(2,1)S(1)} %get-tuple-element.12.refs_0_), channel_id=1, source_target_pairs={{256,0},{384,128},{0,256},{128,384},{257,1},{385,129},{1,257},{129... | collective-permute-start | bytes 98312 | tf_op jit(solution)/shard_map/ppermute | solution.py:20
  102.2 6.2 %collective-permute-start.9 = (bf16[16,1024]{1,0:T(8,128)(2,1)S(1)}, bf16[16,1024]{1,0:T(8,128)(2,1)S(1)}, u32[]{:S(2)}, u32[]{:S(2)}) collective-permute-start(bf16[16,1024]{1,0:T(8,128)(2,1)S(1)} %get-tuple-element.12.refs_0_), channel_id=1, source_target_pairs={{384,0},{0,128},{128,256},{256,384},{385,1},{1,129},{129,257},{257... | collective-permute-start | bytes 98312 | tf_op jit(solution)/shard_map/ppermute | solution.py:20
  109.7 9.3 %collective-permute-start.10 = (f32[56,64]{1,0:T(8,128)S(1)}, f32[56,64]{1,0:T(8,128)S(1)}, u32[]{:S(2)}, u32[]{:S(2)}) collective-permute-start(f32[56,64]{1,0:T(8,128)S(1)} %shard_map.59), channel_id=1, source_target_pairs={{64,0},{0,64},{65,1},{1,65},{66,2},{2,66},{67,3},{3,67},{68,4},{4,... | collective-permute-start | bytes 43016 | tf_op jit(solution)/shard_map/ppermute | solution.py:20

commit v9 on v4

--- a/solution.py
+++ b/solution.py
@@ -1,5 +1,3 @@
-import functools
-
 import jax
 import jax.numpy as jnp
 from jax import lax
@@ -142,26 +140,19 @@
     out_ref[...] = jnp.broadcast_to(narrow[...].astype(BF16)[None], out_ref.shape)
 
 
-def documents(which, place, out_ref, *refs):
-    pieces, (total_ref, rows_in, rows_out, sems) = refs[:NX], refs[NX:]
-    x, zh = place[0], place[1]
-    block = lax.rem(zh + which, NZH)
-    copies = []
-    for s in range(NX):
-        copies.append(pltpu.make_async_copy(pieces[s], rows_in.at[lax.rem(x + s, NX)], sems.at[s]))
-        copies[-1].start()
+def documents(place, out_ref, in_ref, send_ref, keep_ref, rows_out):
+    zh = place[1]
     rows_out[...] = out_ref[...].astype(F32).reshape(64 * 16, 128)
     position = lax.broadcasted_iota(jnp.int32, (1, 256), 1).astype(F32)
-    for copy in copies:
-        copy.wait()
-    total = jnp.zeros((NX * 16, 64), F32)
+    total = jnp.zeros((NX * 16, 128), F32)
     for g in range(NX):
-        left = rows_in[:, :, g * 256 : (g + 1) * 256].astype(F32).reshape(NX * 16, 256)
-        lens = rows_in[g, :, :128].astype(F32)[14:15, :4]
+        left = in_ref[:, :, g * 256 : (g + 1) * 256].astype(F32).reshape(NX * 16, 256)
+        lens = in_ref[g, :, :128].astype(F32)[14:15, :4]
         right = []
         for h in range(2):
             cut = [
                 rows_out[pl.ds((zl * 16 + core) * 16 + block * 8 + g * 2 + h, NY, stride=32), :]
+                for block in (1 - zh, zh)
                 for zl in range(NZL)
                 for core in range(NC)
             ]
@@ -181,7 +172,8 @@
             total = total + one * one
     total = total * (1.0 / 2048.0)
     for i in range(NX):
-        total_ref[i * 14 : (i + 1) * 14, :] = total[i * 16 : i * 16 + 14]
+        send_ref[i * 14 : (i + 1) * 14, :] = total[i * 16 : i * 16 + 14, :64]
+        keep_ref[i * 14 : (i + 1) * 14, :] = total[i * 16 : i * 16 + 14, 64:]
 
 
 def body(acts, grads, basis_in, basis_out, doc_lengths):
@@ -240,24 +232,17 @@
     )
 
     proj_out = lax.all_to_all(proj_out, ("zl", "y", "core"), split_axis=0, concat_axis=0, tiled=True)
-    pieces = [proj_in] + [from_offset(proj_in, "x", NX, s) for s in range(1, NX)]
-    operands = (place, in_vmem(proj_out), *pieces)
-    totals = [
-        call(
-            functools.partial(documents, which),
-            jax.ShapeDtypeStruct((NX * rows, 64), F32),
-            [
-                pltpu.VMEM((NX, 16, tokens), BF16),
-                pltpu.VMEM((64 * 16, 128), F32),
-                pltpu.SemaphoreType.DMA((NX,)),
-            ],
-            operands,
-            2 * 4 * 256 * 256 * 64,
-            in_specs=[SMEM, VMEM] + [ANY] * NX,
-        )
-        for which in range(NZH)
-    ]
-    return (totals[0] + from_offset(totals[1], "zh", NZH, 1)).T
+    proj_in = lax.all_gather(proj_in, "x")
+    block = jax.ShapeDtypeStruct((NX * rows, 64), F32)
+    send, keep = call(
+        documents,
+        (block, block),
+        [pltpu.VMEM((64 * 16, 128), F32)],
+        (place, *map(in_vmem, (proj_out, proj_in))),
+        2 * 4 * 256 * 256 * 128,
+    )
+    both = lax.all_gather(send, "zh")
+    return (keep + jnp.where(zh == 0, both[1], both[0])).T
 
 
 def solution(mesh):

time: 120 us -> 118 us (0.983)
  blocking collectives: 0 us -> 17.9 us
  starting transfers between devices: 73.4 us -> 57.1 us
  waiting for transfers between devices: 34.2 us -> 32.5 us
  Pallas kernels: 10.4 us -> 9.16 us
    all_gather x0 -> x2, blocking collectives: none -> 17.9 us  [the longest x1 9.99 us: body(): proj_in = lax.all_gather(proj_in, 'x')]
    ppermute x11 -> x7, starting transfers between devices: 40.5 us -> 24.1 us  [from_offset(): lax.ppermute(value, axis, [((i + offset) % size, i) for i in range(size)])]
    ppermute x11 -> x7, waiting for transfers between devices: 6.2 us -> 2.42 us  [from_offset(): lax.ppermute(value, axis, [((i + offset) % size, i) for i in range(size)])]
    all_to_all x1, waiting for transfers between devices: 0.14 us -> 2.28 us  [body(): lax.all_to_all(proj_out, ('zl', 'y', 'core'), split_axis=0, concat_axis=0...]
    pallas_call x5 -> x4, Pallas kernels: 10.4 us -> 9.16 us  [call(): pl.pallas_call(kernel, out_shape=shapes, in_specs=in_specs or [SMEM] + [V...]
  transfers between devices with their start and end apart: 14 -> 10, of which waited for: 7 -> 4; matrix products, arithmetic and copies ran while one was open for 0% -> 0% of each run, Pallas kernels for 1% -> 0%
where the time goes in v9:
time: 118 us
  starting transfers between devices  57.1 us (48%)
  waiting for transfers between devices  32.5 us (28%)
  blocking collectives  17.9 us (15%)
  Pallas kernels  9.16 us (8%)
    all_to_all x1, waiting for transfers between devices, body(): lax.all_to_all(parts, ('zl', 'y'), split_axis=0, concat_axis=0, tiled=True)  27.8 us
    ppermute x7, starting transfers between devices, from_offset(): lax.ppermute(value, axis, [((i + offset) % size, i) for i in range(size)])  24.1 us
    all_to_all x1, starting transfers between devices, body(): lax.all_to_all(packed, ('zl', 'y'), split_axis=0, concat_axis=0, tiled=True)  13.5 us
    all_gather x1, blocking collectives, body(): proj_in = lax.all_gather(proj_in, 'x')  9.99 us
    all_to_all x1, starting transfers between devices, body(): lax.all_to_all(proj_out, ('zl', 'y', 'core'), split_axis=0, concat_axis=0...  9.92 us
    all_to_all x1, starting transfers between devices, body(): lax.all_to_all(parts, ('zl', 'y'), split_axis=0, concat_axis=0, tiled=True)  9.58 us
    pallas_call x4, Pallas kernels, call(): pl.pallas_call(kernel, out_shape=shapes, in_specs=in_specs or [SMEM] + [V...  9.16 us
    all_gather x1, blocking collectives, body(): both = lax.all_gather(send, 'zh')  7.91 us
  transfers between devices with their start and end apart: 10, of which 4 were waited for; matrix products, arithmetic and copies ran while one was open for 0% of the time, Pallas kernels for 0%

profile of v9, /device:TPU:1, one launch (start us, length us, event | category | flops | bytes accessed | tf_op | source)
XLA Modules:
  0.0 117.6 jit_solution(16619457199058816372)
XLA Ops:
  0.0 0.1 pad_add_fusion.place
  0.1 3.4 %shard_map.55 = (bf16[32,16,1024]{2,1,0:T(8,128)(2,1)}, bf16[576,256]{1,0:T(8,128)(2,1)S(1)}) custom-call(s32[3]{0:T(128)S(1)} %pad_add_fusion.place, bf16[56,28672]{1,0:T(8,128)(2,1)} %basis_ref.1, bf16[8,8192]{1,0:T(8,128)(2,1)} %out_rows_ref.1, bf16[448,256]{1,0:T(8,128)(2,1)} %bitcast.8, bf16[256,128]{1,0:T(8,128)(2,1)} %grads_ref.1), custom_call_target="tpu_custom_call" | custom-call | flops 1048576 | bytes 3637260 | tf_op jit(solution)/shard_map/pallas_call | solution.py:23
  3.4 13.5 %all-to-all-start = ((bf16[32,16,1024]{2,1,0:T(8,128)(2,1)}), bf16[32,16,1024]{2,1,0:T(8,128)(2,1)S(1)}, u32[]{:S(2)}, u32[]{:S(2)}) async-start(bf16[32,16,1024]{2,1,0:T(8,128)(2,1)} %get-tuple-element.11), calls=%async_computation | async-start | bytes 2097152 | tf_op jit(solution)/shard_map/all_to_all | solution.py:203
  16.9 4.4 %collective-permute-start = (bf16[576,256]{1,0:T(8,128)(2,1)S(1)}, bf16[576,256]{1,0:T(8,128)(2,1)S(1)}, u32[]{:S(2)}, u32[]{:S(2)}) collective-permute-start(bf16[576,256]{1,0:T(8,128)(2,1)S(1)} %get-tuple-element.12.refs_0_), channel_id=1, source_target_pairs={{128,0},{256,128},{384,256},{0,384},{129,1},{257,129},{385,257},{1... | collective-permute-start | bytes 884744 | tf_op jit(solution)/shard_map/ppermute | solution.py:18
  21.3 2.5 %collective-permute-start.1 = (bf16[576,256]{1,0:T(8,128)(2,1)S(1)}, bf16[576,256]{1,0:T(8,128)(2,1)S(1)}, u32[]{:S(2)}, u32[]{:S(2)}) collective-permute-start(bf16[576,256]{1,0:T(8,128)(2,1)S(1)} %get-tuple-element.12.refs_0_), channel_id=1, source_target_pairs={{256,0},{384,128},{0,256},{128,384},{257,1},{385,129},{1,257},{129... | collective-permute-start | bytes 884744 | tf_op jit(solution)/shard_map/ppermute | solution.py:18
  23.8 2.5 %collective-permute-start.2 = (bf16[576,256]{1,0:T(8,128)(2,1)S(1)}, bf16[576,256]{1,0:T(8,128)(2,1)S(1)}, u32[]{:S(2)}, u32[]{:S(2)}) collective-permute-start(bf16[576,256]{1,0:T(8,128)(2,1)S(1)} %get-tuple-element.12.refs_0_), channel_id=1, source_target_pairs={{384,0},{0,128},{128,256},{256,384},{385,1},{1,129},{129,257},{257... | collective-permute-start | bytes 884744 | tf_op jit(solution)/shard_map/ppermute | solution.py:18
  26.3 3.7 %collective-permute-start.3 = (bf16[576,256]{1,0:T(8,128)(2,1)S(1)}, bf16[576,256]{1,0:T(8,128)(2,1)S(1)}, u32[]{:S(2)}, u32[]{:S(2)}) collective-permute-start(bf16[576,256]{1,0:T(8,128)(2,1)S(1)} %get-tuple-element.12.refs_0_), channel_id=1, source_target_pairs={{1,0},{0,1},{3,2},{2,3},{5,4},{4,5},{7,6},{6,7},{9,8},{8,9},{11,10... | collective-permute-start | bytes 884744 | tf_op jit(solution)/shard_map/ppermute | solution.py:18
  30.0 0.0 collective-permute-done.refs_1_
  30.0 6.8 %collective-permute-start.4 = (bf16[576,256]{1,0:T(8,128)(2,1)S(1)}, bf16[576,256]{1,0:T(8,128)(2,1)S(1)}, u32[]{:S(2)}, u32[]{:S(2)}) collective-permute-start(bf16[576,256]{1,0:T(8,128)(2,1)S(1)} %collective-permute-done.refs_1_), channel_id=1, source_target_pairs={{1,0},{0,1},{3,2},{2,3},{5,4},{4,5},{7,6},{6,7},{9,8},{8,9},{11,10... | collective-permute-start | bytes 884744 | tf_op jit(solution)/shard_map/ppermute | solution.py:18
  36.8 0.0 collective-permute-done.1.refs_2_
  36.8 1.9 %collective-permute-start.5 = (bf16[576,256]{1,0:T(8,128)(2,1)S(1)}, bf16[576,256]{1,0:T(8,128)(2,1)S(1)}, u32[]{:S(2)}, u32[]{:S(2)}) collective-permute-start(bf16[576,256]{1,0:T(8,128)(2,1)S(1)} %collective-permute-done.1.refs_2_), channel_id=1, source_target_pairs={{1,0},{0,1},{3,2},{2,3},{5,4},{4,5},{7,6},{6,7},{9,8},{8,9},{11,10... | collective-permute-start | bytes 884744 | tf_op jit(solution)/shard_map/ppermute | solution.py:18
  38.7 1.3 %collective-permute-done.2.refs_3_ = bf16[576,256]{1,0:T(8,128)(2,1)S(1)} collective-permute-done((bf16[576,256]{1,0:T(8,128)(2,1)S(1)}, bf16[576,256]{1,0:T(8,128)(2,1)S(1)}, u32[]{:S(2)}, u32[]{:S(2)}) %collective-permute-start.2) | collective-permute-done | bytes 294944 | tf_op jit(solution)/shard_map/ppermute | solution.py:18
  40.0 2.4 %collective-permute-start.6 = (bf16[576,256]{1,0:T(8,128)(2,1)S(1)}, bf16[576,256]{1,0:T(8,128)(2,1)S(1)}, u32[]{:S(2)}, u32[]{:S(2)}) collective-permute-start(bf16[576,256]{1,0:T(8,128)(2,1)S(1)} %collective-permute-done.2.refs_3_), channel_id=1, source_target_pairs={{1,0},{0,1},{3,2},{2,3},{5,4},{4,5},{7,6},{6,7},{9,8},{8,9},{11,10... | collective-permute-start | bytes 884744 | tf_op jit(solution)/shard_map/ppermute | solution.py:18
  42.4 0.0 collective-permute-done.3.refs_4_
  42.4 0.0 collective-permute-done.4.refs_5_
  42.4 0.0 collective-permute-done.5.refs_6_
  42.4 1.2 collective-permute-done.6.refs_7_
  43.6 0.0 all-to-all-done.packed_ref
  43.6 3.2 %shard_map.56 = bf16[32,16,1152]{2,1,0:T(8,128)(2,1)} custom-call(s32[3]{0:T(128)S(1)} %pad_add_fusion.place, bf16[32,16,1024]{2,1,0:T(8,128)(2,1)S(1)} %all-to-all-done.packed_ref, bf16[576,256]{1,0:T(8,128)(2,1)S(1)} %get-tuple-element.12.refs_0_, bf16[576,256]{1,0:T(8,128)(2,1)S(1)} %collective-permute-done.refs_1_, ...), custom_call_target="tpu_custom_call" | custom-call | flops 1073741824 | bytes 3407884 | tf_op jit(solution)/shard_map/pallas_call | solution.py:23
  46.8 0.0 copy-start
  46.8 9.6 %all-to-all-start.1 = ((bf16[32,16,1152]{2,1,0:T(8,128)(2,1)}), bf16[32,16,1152]{2,1,0:T(8,128)(2,1)S(1)}, u32[]{:S(2)}, u32[]{:S(2)}) async-start(bf16[32,16,1152]{2,1,0:T(8,128)(2,1)} %shard_map.56), calls=%async_computation.1 | async-start | bytes 2359296 | tf_op jit(solution)/shard_map/all_to_all | solution.py:224
  56.4 0.0 copy-done
  56.4 27.8 %all-to-all-done.1.parts_ref = bf16[32,16,1152]{2,1,0:T(8,128)(2,1)S(1)} async-done(((bf16[32,16,1152]{2,1,0:T(8,128)(2,1)}), bf16[32,16,1152]{2,1,0:T(8,128)(2,1)S(1)}, u32[]{:S(2)}, u32[]{:S(2)}) %all-to-all-start.1) | async-done | bytes 1179680 | tf_op jit(solution)/shard_map/all_to_all | solution.py:224
  84.3 1.4 %shard_map.57 = (bf16[16,1024]{1,0:T(8,128)(2,1)S(1)}, bf16[64,16,128]{2,1,0:T(8,128)(2,1)}) custom-call(s32[3]{0:T(128)S(1)} %pad_add_fusion.place, f32[1,128]{1,0:T(1,128)S(1)} %pad.4.lens_ref, bf16[32,16,1152]{2,1,0:T(8,128)(2,1)S(1)} %all-to-all-done.1.parts_ref), custom_call_target="tpu_custom_call" | custom-call | flops 589824 | bytes 1180172 | tf_op jit(solution)/shard_map/pallas_call | solution.py:23
  85.7 9.9 %all-to-all-start.2 = ((bf16[64,16,128]{2,1,0:T(8,128)(2,1)}), bf16[64,16,128]{2,1,0:T(8,128)(2,1)S(1)}, u32[]{:S(2)}, u32[]{:S(2)}) async-start(bf16[64,16,128]{2,1,0:T(8,128)(2,1)} %get-tuple-element.13), calls=%async_computation.2 | async-start | bytes 524288 | tf_op jit(solution)/shard_map/all_to_all | solution.py:234
  95.6 10.0 %all-gather = bf16[64,1024]{1,0:T(8,128)(2,1)S(1)} all-gather(bf16[16,1024]{1,0:T(8,128)(2,1)S(1)} %get-tuple-element.14), channel_id=2, replica_groups=mesh['x'=4,'zh'=2,'zl'=4,'y'=8,'core'=2] {'x'}, dimensions={0}, use_global_device_ids=true | all-gather | bytes 163840 | tf_op jit(solution)/shard_map/all_gather | solution.py:235
  105.6 2.3 %all-to-all-done.2.out_ref = bf16[64,16,128]{2,1,0:T(8,128)(2,1)S(1)} async-done(((bf16[64,16,128]{2,1,0:T(8,128)(2,1)}), bf16[64,16,128]{2,1,0:T(8,128)(2,1)S(1)}, u32[]{:S(2)}, u32[]{:S(2)}) %all-to-all-start.2) | async-done | bytes 262176 | tf_op jit(solution)/shard_map/all_to_all | solution.py:234
  107.9 1.2 shard_map.58
  109.1 7.9 %all-gather.1 = f32[112,64]{1,0:T(8,128)S(1)} all-gather(f32[56,64]{1,0:T(8,128)S(1)} %get-tuple-element.16), channel_id=3, replica_groups=mesh['x'=4,'zh'=2,'zl'=4,'y'=8,'core'=2] {'zh'}, dimensions={0}, use_global_device_ids=true | all-gather | bytes 43008 | tf_op jit(solution)/shard_map/all_gather | solution.py:244
  117.0 0.6 fusion.1
  (2 shorter events, 0.0 us)
Async XLA Ops:
  3.4 40.1 %all-to-all-start = ((bf16[32,16,1024]{2,1,0:T(8,128)(2,1)}), bf16[32,16,1024]{2,1,0:T(8,128)(2,1)S(1)}, u32[]{:S(2)}, u32[]{:S(2)}) async-start(bf16[32,16,1024]{2,1,0:T(8,128)(2,1)} %get-tuple-element.11), calls=%async_computation | async-start | bytes 2097152 | tf_op jit(solution)/shard_map/all_to_all | solution.py:203
  16.9 13.1 %collective-permute-start = (bf16[576,256]{1,0:T(8,128)(2,1)S(1)}, bf16[576,256]{1,0:T(8,128)(2,1)S(1)}, u32[]{:S(2)}, u32[]{:S(2)}) collective-permute-start(bf16[576,256]{1,0:T(8,128)(2,1)S(1)} %get-tuple-element.12.refs_0_), channel_id=1, source_target_pairs={{128,0},{256,128},{384,256},{0,384},{129,1},{257,129},{385,257},{1... | collective-permute-start | bytes 884744 | tf_op jit(solution)/shard_map/ppermute | solution.py:18
  21.3 15.5 %collective-permute-start.1 = (bf16[576,256]{1,0:T(8,128)(2,1)S(1)}, bf16[576,256]{1,0:T(8,128)(2,1)S(1)}, u32[]{:S(2)}, u32[]{:S(2)}) collective-permute-start(bf16[576,256]{1,0:T(8,128)(2,1)S(1)} %get-tuple-element.12.refs_0_), channel_id=1, source_target_pairs={{256,0},{384,128},{0,256},{128,384},{257,1},{385,129},{1,257},{129... | collective-permute-start | bytes 884744 | tf_op jit(solution)/shard_map/ppermute | solution.py:18
  23.8 16.2 %collective-permute-start.2 = (bf16[576,256]{1,0:T(8,128)(2,1)S(1)}, bf16[576,256]{1,0:T(8,128)(2,1)S(1)}, u32[]{:S(2)}, u32[]{:S(2)}) collective-permute-start(bf16[576,256]{1,0:T(8,128)(2,1)S(1)} %get-tuple-element.12.refs_0_), channel_id=1, source_target_pairs={{384,0},{0,128},{128,256},{256,384},{385,1},{1,129},{129,257},{257... | collective-permute-start | bytes 884744 | tf_op jit(solution)/shard_map/ppermute | solution.py:18
  26.3 16.1 %collective-permute-start.3 = (bf16[576,256]{1,0:T(8,128)(2,1)S(1)}, bf16[576,256]{1,0:T(8,128)(2,1)S(1)}, u32[]{:S(2)}, u32[]{:S(2)}) collective-permute-start(bf16[576,256]{1,0:T(8,128)(2,1)S(1)} %get-tuple-element.12.refs_0_), channel_id=1, source_target_pairs={{1,0},{0,1},{3,2},{2,3},{5,4},{4,5},{7,6},{6,7},{9,8},{8,9},{11,10... | collective-permute-start | bytes 884744 | tf_op jit(solution)/shard_map/ppermute | solution.py:18
  30.0 12.4 %collective-permute-start.4 = (bf16[576,256]{1,0:T(8,128)(2,1)S(1)}, bf16[576,256]{1,0:T(8,128)(2,1)S(1)}, u32[]{:S(2)}, u32[]{:S(2)}) collective-permute-start(bf16[576,256]{1,0:T(8,128)(2,1)S(1)} %collective-permute-done.refs_1_), channel_id=1, source_target_pairs={{1,0},{0,1},{3,2},{2,3},{5,4},{4,5},{7,6},{6,7},{9,8},{8,9},{11,10... | collective-permute-start | bytes 884744 | tf_op jit(solution)/shard_map/ppermute | solution.py:18
  36.8 5.6 %collective-permute-start.5 = (bf16[576,256]{1,0:T(8,128)(2,1)S(1)}, bf16[576,256]{1,0:T(8,128)(2,1)S(1)}, u32[]{:S(2)}, u32[]{:S(2)}) collective-permute-start(bf16[576,256]{1,0:T(8,128)(2,1)S(1)} %collective-permute-done.1.refs_2_), channel_id=1, source_target_pairs={{1,0},{0,1},{3,2},{2,3},{5,4},{4,5},{7,6},{6,7},{9,8},{8,9},{11,10... | collective-permute-start | bytes 884744 | tf_op jit(solution)/shard_map/ppermute | solution.py:18
  40.0 3.6 %collective-permute-start.6 = (bf16[576,256]{1,0:T(8,128)(2,1)S(1)}, bf16[576,256]{1,0:T(8,128)(2,1)S(1)}, u32[]{:S(2)}, u32[]{:S(2)}) collective-permute-start(bf16[576,256]{1,0:T(8,128)(2,1)S(1)} %collective-permute-done.2.refs_3_), channel_id=1, source_target_pairs={{1,0},{0,1},{3,2},{2,3},{5,4},{4,5},{7,6},{6,7},{9,8},{8,9},{11,10... | collective-permute-start | bytes 884744 | tf_op jit(solution)/shard_map/ppermute | solution.py:18
  46.8 9.6 %copy-start = (s32[1,4]{1,0:T(1,128)S(1)}, s32[1,4]{1,0:T(1,128)}, u32[]{:S(2)}) copy-start(s32[1,4]{1,0:T(1,128)} %param.9) | copy-start | bytes 52
  46.8 37.5 %all-to-all-start.1 = ((bf16[32,16,1152]{2,1,0:T(8,128)(2,1)}), bf16[32,16,1152]{2,1,0:T(8,128)(2,1)S(1)}, u32[]{:S(2)}, u32[]{:S(2)}) async-start(bf16[32,16,1152]{2,1,0:T(8,128)(2,1)} %shard_map.56), calls=%async_computation.1 | async-start | bytes 2359296 | tf_op jit(solution)/shard_map/all_to_all | solution.py:224
  85.7 22.2 %all-to-all-start.2 = ((bf16[64,16,128]{2,1,0:T(8,128)(2,1)}), bf16[64,16,128]{2,1,0:T(8,128)(2,1)S(1)}, u32[]{:S(2)}, u32[]{:S(2)}) async-start(bf16[64,16,128]{2,1,0:T(8,128)(2,1)} %get-tuple-element.13), calls=%async_computation.2 | async-start | bytes 524288 | tf_op jit(solution)/shard_map/all_to_all | solution.py:234

commit v10 on v9

--- a/solution.py
+++ b/solution.py
@@ -66,20 +66,22 @@
     turned[...] = grads[...].astype(F32).T.astype(BF16)
     stores.append(pltpu.make_async_copy(turned, payload_ref.at[pl.ds(fin, fout)], sems.at[3 + PARTS]))
     stores[-1].start()
-    for i in range(PARTS):
-        loads[2 + i].wait()
-        for x in range(NX):
-
-            @pl.when(place[0] == x)
-            def _():
+    for x in range(NX):
+
+        @pl.when(place[0] == x)
+        def _():
+            for i in range(PARTS):
+                loads[2 + i].wait()
                 for c in range(chips):
                     rows = basis[i, :, c * width : (c + 1) * width].astype(F32)[x * 14 : (x + 1) * 14]
                     rows = jnp.concatenate([rows, jnp.zeros((2, width), F32)], axis=0)
                     packed[i, c, :, :width] = rows.astype(BF16)
-
+                there = packed_ref.at[pl.ds(i * chips, chips)]
+                pltpu.make_async_copy(packed.at[i], there, sems.at[4 + PARTS + i]).start()
+
+    for i in range(PARTS):
         there = packed_ref.at[pl.ds(i * chips, chips)]
         stores.append(pltpu.make_async_copy(packed.at[i], there, sems.at[4 + PARTS + i]))
-        stores[-1].start()
     for store in stores:
         store.wait()
 
@@ -121,23 +123,33 @@
         result.wait()
 
 
-def add_up(place, lens_ref, parts_ref, in_ref, out_ref, wide, narrow):
-    x = place[0]
-    tokens = wide.shape[1]
-    total = parts_ref[0].astype(F32)
+def add_out(place, parts_ref, out_ref, narrow):
+    x, tokens = place[0], NX * 256
+    high = parts_ref[0, :, :tokens].astype(F32)[8:]
+    low = parts_ref[0, :, tokens:].astype(F32)
     for i in range(1, CHIPS):
-        total = total + parts_ref[i].astype(F32)
+        high = high + parts_ref[i, :, :tokens].astype(F32)[8:]
+        low = low + parts_ref[i, :, tokens:].astype(F32)
     for s in range(NX):
         source = lax.rem(x + s, NX)
-        wide[:, pl.ds(pl.multiple_of(source * 256, 256), 256)] = total[:, s * 256 : (s + 1) * 256]
         for half in range(2):
             for h in range(2):
                 col, row = s * 2 + h, half * 8 + s * 2 + h
-                value = total[14 + half : 15 + half, col * 128 : (col + 1) * 128] + total[row : row + 1, tokens:]
+                value = high[6 + half : 7 + half, col * 128 : (col + 1) * 128] + low[row : row + 1]
                 narrow[pl.ds(half * 8 + source * 2 + h, 1), :] = value
+    out_ref[...] = jnp.broadcast_to(narrow[...].astype(BF16)[None], out_ref.shape)
+
+
+def add_in(place, lens_ref, parts_ref, in_ref, wide):
+    x, tokens = place[0], wide.shape[1]
+    total = parts_ref[0, :, :tokens].astype(F32)
+    for i in range(1, CHIPS):
+        total = total + parts_ref[i, :, :tokens].astype(F32)
+    for s in range(NX):
+        there = pl.ds(pl.multiple_of(lax.rem(x + s, NX) * 256, 256), 256)
+        wide[:, there] = total[:, s * 256 : (s + 1) * 256]
     wide[14:15, :128] = lens_ref[...]
     in_ref[...] = wide[...].astype(BF16)
-    out_ref[...] = jnp.broadcast_to(narrow[...].astype(BF16)[None], out_ref.shape)
 
 
 def documents(place, out_ref, in_ref, send_ref, keep_ref, rows_out):
@@ -223,12 +235,14 @@
     )
     parts = lax.all_to_all(parts, ("zl", "y"), split_axis=0, concat_axis=0, tiled=True)
     lens = jnp.pad(doc_lengths.astype(F32), ((0, 0), (0, 124)))
-    proj_in, proj_out = call(
-        add_up,
-        (jax.ShapeDtypeStruct((16, tokens), BF16), in_hbm((64, 16, 128))),
-        [pltpu.VMEM((16, tokens), F32), pltpu.VMEM((16, 128), F32)],
-        (place, lens, in_vmem(parts)),
-        32 * 16 * 1152,
+    parts = in_vmem(parts)
+    proj_out = call(add_out, in_hbm((64, 16, 128)), [pltpu.VMEM((16, 128), F32)], (place, parts), 32 * 16 * 640)
+    proj_in = call(
+        add_in,
+        jax.ShapeDtypeStruct((16, tokens), BF16),
+        [pltpu.VMEM((16, tokens), F32)],
+        (place, lens, parts),
+        32 * 16 * 1024,
     )
 
     proj_out = lax.all_to_all(proj_out, ("zl", "y", "core"), split_axis=0, concat_axis=0, tiled=True)

time: 118 us -> 118 us (level)
  blocking collectives: 17.9 us -> 59.4 us
  waiting for transfers between devices: 32.5 us -> 4.09 us
  starting transfers between devices: 57.1 us -> 43.6 us
    all_to_all x0 -> x1, blocking collectives: none -> 41.5 us  [body(): lax.all_to_all(parts, ('zl', 'y'), split_axis=0, concat_axis=0, tiled=True)]
    all_to_all x1 -> x0, waiting for transfers between devices: 27.8 us -> none  [body(): lax.all_to_all(parts, ('zl', 'y'), split_axis=0, concat_axis=0, tiled=True)]
    all_to_all x1 -> x0, starting transfers between devices: 9.58 us -> none  [body(): lax.all_to_all(parts, ('zl', 'y'), split_axis=0, concat_axis=0, tiled=True)]
    all_to_all x1, starting transfers between devices: 9.92 us -> 5.95 us  [body(): lax.all_to_all(proj_out, ('zl', 'y', 'core'), split_axis=0, concat_axis=0...]
    pallas_call x4 -> x5, Pallas kernels: 9.16 us -> 9.74 us  [call(): pl.pallas_call(kernel, out_shape=shapes, in_specs=in_specs or [SMEM] + [V...]
  transfers between devices with their start and end apart: 10 -> 9, of which waited for: 4 -> 3; matrix products, arithmetic and copies ran while one was open for 0% -> 0% of each run, Pallas kernels for 0% -> 1%
where the time goes in v10:
time: 118 us
  blocking collectives  59.4 us (50%)
  starting transfers between devices  43.6 us (37%)
  Pallas kernels  9.74 us (8%)
  waiting for transfers between devices  4.09 us (3%)
    all_to_all x1, blocking collectives, body(): lax.all_to_all(parts, ('zl', 'y'), split_axis=0, concat_axis=0, tiled=True)  41.5 us
    ppermute x7, starting transfers between devices, from_offset(): lax.ppermute(value, axis, [((i + offset) % size, i) for i in range(size)])  24.1 us
    all_to_all x1, starting transfers between devices, body(): lax.all_to_all(packed, ('zl', 'y'), split_axis=0, concat_axis=0, tiled=True)  13.5 us
    all_gather x1, blocking collectives, body(): proj_in = lax.all_gather(proj_in, 'x')  9.99 us
    pallas_call x5, Pallas kernels, call(): pl.pallas_call(kernel, out_shape=shapes, in_specs=in_specs or [SMEM] + [V...  9.74 us
    all_gather x1, blocking collectives, body(): both = lax.all_gather(send, 'zh')  7.94 us
    all_to_all x1, starting transfers between devices, body(): lax.all_to_all(proj_out, ('zl', 'y', 'core'), split_axis=0, concat_axis=0...  5.95 us
    ppermute x7, waiting for transfers between devices, from_offset(): lax.ppermute(value, axis, [((i + offset) % size, i) for i in range(size)])  2.42 us
  transfers between devices with their start and end apart: 9, of which 3 were waited for; matrix products, arithmetic and copies ran while one was open for 0% of the time, Pallas kernels for 1%

profile of v10, /device:TPU:1, one launch (start us, length us, event | category | flops | bytes accessed | tf_op | source)
XLA Modules:
  0.0 117.7 jit_solution(12394627003028070609)
XLA Ops:
  0.0 0.1 pad_add_fusion.place
  0.1 3.3 %shard_map.55 = (bf16[32,16,1024]{2,1,0:T(8,128)(2,1)}, bf16[576,256]{1,0:T(8,128)(2,1)S(1)}) custom-call(s32[3]{0:T(128)S(1)} %pad_add_fusion.place, bf16[56,28672]{1,0:T(8,128)(2,1)} %basis_ref.1, bf16[8,8192]{1,0:T(8,128)(2,1)} %out_rows_ref.1, bf16[448,256]{1,0:T(8,128)(2,1)} %bitcast.8, bf16[256,128]{1,0:T(8,128)(2,1)} %grads_ref.1), custom_call_target="tpu_custom_call" | custom-call | flops 1048576 | bytes 3637260 | tf_op jit(solution)/shard_map/pallas_call | solution.py:23
  3.4 13.5 %all-to-all-start = ((bf16[32,16,1024]{2,1,0:T(8,128)(2,1)}), bf16[32,16,1024]{2,1,0:T(8,128)(2,1)S(1)}, u32[]{:S(2)}, u32[]{:S(2)}) async-start(bf16[32,16,1024]{2,1,0:T(8,128)(2,1)} %get-tuple-element.9), calls=%async_computation | async-start | bytes 2097152 | tf_op jit(solution)/shard_map/all_to_all | solution.py:215
  16.9 4.4 %collective-permute-start = (bf16[576,256]{1,0:T(8,128)(2,1)S(1)}, bf16[576,256]{1,0:T(8,128)(2,1)S(1)}, u32[]{:S(2)}, u32[]{:S(2)}) collective-permute-start(bf16[576,256]{1,0:T(8,128)(2,1)S(1)} %get-tuple-element.10.refs_0_), channel_id=1, source_target_pairs={{128,0},{256,128},{384,256},{0,384},{129,1},{257,129},{385,257},{1... | collective-permute-start | bytes 884744 | tf_op jit(solution)/shard_map/ppermute | solution.py:18
  21.3 2.4 %collective-permute-start.1 = (bf16[576,256]{1,0:T(8,128)(2,1)S(1)}, bf16[576,256]{1,0:T(8,128)(2,1)S(1)}, u32[]{:S(2)}, u32[]{:S(2)}) collective-permute-start(bf16[576,256]{1,0:T(8,128)(2,1)S(1)} %get-tuple-element.10.refs_0_), channel_id=1, source_target_pairs={{256,0},{384,128},{0,256},{128,384},{257,1},{385,129},{1,257},{129... | collective-permute-start | bytes 884744 | tf_op jit(solution)/shard_map/ppermute | solution.py:18
  23.8 2.5 %collective-permute-start.2 = (bf16[576,256]{1,0:T(8,128)(2,1)S(1)}, bf16[576,256]{1,0:T(8,128)(2,1)S(1)}, u32[]{:S(2)}, u32[]{:S(2)}) collective-permute-start(bf16[576,256]{1,0:T(8,128)(2,1)S(1)} %get-tuple-element.10.refs_0_), channel_id=1, source_target_pairs={{384,0},{0,128},{128,256},{256,384},{385,1},{1,129},{129,257},{257... | collective-permute-start | bytes 884744 | tf_op jit(solution)/shard_map/ppermute | solution.py:18
  26.3 3.7 %collective-permute-start.3 = (bf16[576,256]{1,0:T(8,128)(2,1)S(1)}, bf16[576,256]{1,0:T(8,128)(2,1)S(1)}, u32[]{:S(2)}, u32[]{:S(2)}) collective-permute-start(bf16[576,256]{1,0:T(8,128)(2,1)S(1)} %get-tuple-element.10.refs_0_), channel_id=1, source_target_pairs={{1,0},{0,1},{3,2},{2,3},{5,4},{4,5},{7,6},{6,7},{9,8},{8,9},{11,10... | collective-permute-start | bytes 884744 | tf_op jit(solution)/shard_map/ppermute | solution.py:18
  30.0 0.0 collective-permute-done.refs_1_
  30.0 6.8 %collective-permute-start.4 = (bf16[576,256]{1,0:T(8,128)(2,1)S(1)}, bf16[576,256]{1,0:T(8,128)(2,1)S(1)}, u32[]{:S(2)}, u32[]{:S(2)}) collective-permute-start(bf16[576,256]{1,0:T(8,128)(2,1)S(1)} %collective-permute-done.refs_1_), channel_id=1, source_target_pairs={{1,0},{0,1},{3,2},{2,3},{5,4},{4,5},{7,6},{6,7},{9,8},{8,9},{11,10... | collective-permute-start | bytes 884744 | tf_op jit(solution)/shard_map/ppermute | solution.py:18
  36.8 0.0 collective-permute-done.1.refs_2_
  36.8 1.9 %collective-permute-start.5 = (bf16[576,256]{1,0:T(8,128)(2,1)S(1)}, bf16[576,256]{1,0:T(8,128)(2,1)S(1)}, u32[]{:S(2)}, u32[]{:S(2)}) collective-permute-start(bf16[576,256]{1,0:T(8,128)(2,1)S(1)} %collective-permute-done.1.refs_2_), channel_id=1, source_target_pairs={{1,0},{0,1},{3,2},{2,3},{5,4},{4,5},{7,6},{6,7},{9,8},{8,9},{11,10... | collective-permute-start | bytes 884744 | tf_op jit(solution)/shard_map/ppermute | solution.py:18
  38.7 1.3 %collective-permute-done.2.refs_3_ = bf16[576,256]{1,0:T(8,128)(2,1)S(1)} collective-permute-done((bf16[576,256]{1,0:T(8,128)(2,1)S(1)}, bf16[576,256]{1,0:T(8,128)(2,1)S(1)}, u32[]{:S(2)}, u32[]{:S(2)}) %collective-permute-start.2) | collective-permute-done | bytes 294944 | tf_op jit(solution)/shard_map/ppermute | solution.py:18
  40.0 2.4 %collective-permute-start.6 = (bf16[576,256]{1,0:T(8,128)(2,1)S(1)}, bf16[576,256]{1,0:T(8,128)(2,1)S(1)}, u32[]{:S(2)}, u32[]{:S(2)}) collective-permute-start(bf16[576,256]{1,0:T(8,128)(2,1)S(1)} %collective-permute-done.2.refs_3_), channel_id=1, source_target_pairs={{1,0},{0,1},{3,2},{2,3},{5,4},{4,5},{7,6},{6,7},{9,8},{8,9},{11,10... | collective-permute-start | bytes 884744 | tf_op jit(solution)/shard_map/ppermute | solution.py:18
  42.4 0.0 collective-permute-done.3.refs_4_
  42.4 0.0 collective-permute-done.4.refs_5_
  42.4 0.0 collective-permute-done.5.refs_6_
  42.4 1.2 collective-permute-done.6.refs_7_
  43.5 0.0 all-to-all-done.packed_ref
  43.5 3.2 %shard_map.56 = bf16[32,16,1152]{2,1,0:T(8,128)(2,1)} custom-call(s32[3]{0:T(128)S(1)} %pad_add_fusion.place, bf16[32,16,1024]{2,1,0:T(8,128)(2,1)S(1)} %all-to-all-done.packed_ref, bf16[576,256]{1,0:T(8,128)(2,1)S(1)} %get-tuple-element.10.refs_0_, bf16[576,256]{1,0:T(8,128)(2,1)S(1)} %collective-permute-done.refs_1_, ...), custom_call_target="tpu_custom_call" | custom-call | flops 1073741824 | bytes 3407884 | tf_op jit(solution)/shard_map/pallas_call | solution.py:23
  46.8 41.5 %all_to_all.15.parts_ref = bf16[32,16,1152]{2,1,0:T(8,128)(2,1)S(1)} all-to-all(bf16[32,16,1152]{2,1,0:T(8,128)(2,1)} %shard_map.56), channel_id=1, replica_groups=mesh['x'=4,'zh'=2,'zl'=4,'y'=8,'core'=2] {'zl','y'}, dimensions={0} | all-to-all | bytes 2359296 | tf_op jit(solution)/shard_map/all_to_all | solution.py:236
  88.2 0.0 copy-start
  88.2 1.3 %shard_map.57 = bf16[64,16,128]{2,1,0:T(8,128)(2,1)} custom-call(s32[3]{0:T(128)S(1)} %pad_add_fusion.place, bf16[32,16,1152]{2,1,0:T(8,128)(2,1)S(1)} %all_to_all.15.parts_ref), custom_call_target="tpu_custom_call" | custom-call | flops 327680 | bytes 1179660 | tf_op jit(solution)/shard_map/pallas_call | solution.py:23
  89.6 5.9 %all-to-all-start.2 = ((bf16[64,16,128]{2,1,0:T(8,128)(2,1)}), bf16[64,16,128]{2,1,0:T(8,128)(2,1)S(1)}, u32[]{:S(2)}, u32[]{:S(2)}) async-start(bf16[64,16,128]{2,1,0:T(8,128)(2,1)} %shard_map.57), calls=%async_computation.2 | async-start | bytes 524288 | tf_op jit(solution)/shard_map/all_to_all | solution.py:248
  95.5 0.0 copy-done
  95.6 0.7 shard_map.58
  96.3 10.0 %all-gather = bf16[64,1024]{1,0:T(8,128)(2,1)S(1)} all-gather(bf16[16,1024]{1,0:T(8,128)(2,1)S(1)} %shard_map.58), channel_id=2, replica_groups=mesh['x'=4,'zh'=2,'zl'=4,'y'=8,'core'=2] {'x'}, dimensions={0}, use_global_device_ids=true | all-gather | bytes 163840 | tf_op jit(solution)/shard_map/all_gather | solution.py:249
  106.3 1.7 %all-to-all-done.2.out_ref = bf16[64,16,128]{2,1,0:T(8,128)(2,1)S(1)} async-done(((bf16[64,16,128]{2,1,0:T(8,128)(2,1)}), bf16[64,16,128]{2,1,0:T(8,128)(2,1)S(1)}, u32[]{:S(2)}, u32[]{:S(2)}) %all-to-all-start.2) | async-done | bytes 262176 | tf_op jit(solution)/shard_map/all_to_all | solution.py:248
  107.9 1.2 shard_map.59
  109.1 7.9 %all-gather.1 = f32[112,64]{1,0:T(8,128)S(1)} all-gather(f32[56,64]{1,0:T(8,128)S(1)} %get-tuple-element.12), channel_id=3, replica_groups=mesh['x'=4,'zh'=2,'zl'=4,'y'=8,'core'=2] {'zh'}, dimensions={0}, use_global_device_ids=true | all-gather | bytes 43008 | tf_op jit(solution)/shard_map/all_gather | solution.py:258
  117.0 0.6 fusion.1
  (2 shorter events, 0.0 us)
Async XLA Ops:
  3.4 40.1 %all-to-all-start = ((bf16[32,16,1024]{2,1,0:T(8,128)(2,1)}), bf16[32,16,1024]{2,1,0:T(8,128)(2,1)S(1)}, u32[]{:S(2)}, u32[]{:S(2)}) async-start(bf16[32,16,1024]{2,1,0:T(8,128)(2,1)} %get-tuple-element.9), calls=%async_computation | async-start | bytes 2097152 | tf_op jit(solution)/shard_map/all_to_all | solution.py:215
  16.9 13.1 %collective-permute-start = (bf16[576,256]{1,0:T(8,128)(2,1)S(1)}, bf16[576,256]{1,0:T(8,128)(2,1)S(1)}, u32[]{:S(2)}, u32[]{:S(2)}) collective-permute-start(bf16[576,256]{1,0:T(8,128)(2,1)S(1)} %get-tuple-element.10.refs_0_), channel_id=1, source_target_pairs={{128,0},{256,128},{384,256},{0,384},{129,1},{257,129},{385,257},{1... | collective-permute-start | bytes 884744 | tf_op jit(solution)/shard_map/ppermute | solution.py:18
  21.3 15.5 %collective-permute-start.1 = (bf16[576,256]{1,0:T(8,128)(2,1)S(1)}, bf16[576,256]{1,0:T(8,128)(2,1)S(1)}, u32[]{:S(2)}, u32[]{:S(2)}) collective-permute-start(bf16[576,256]{1,0:T(8,128)(2,1)S(1)} %get-tuple-element.10.refs_0_), channel_id=1, source_target_pairs={{256,0},{384,128},{0,256},{128,384},{257,1},{385,129},{1,257},{129... | collective-permute-start | bytes 884744 | tf_op jit(solution)/shard_map/ppermute | solution.py:18
  23.8 16.2 %collective-permute-start.2 = (bf16[576,256]{1,0:T(8,128)(2,1)S(1)}, bf16[576,256]{1,0:T(8,128)(2,1)S(1)}, u32[]{:S(2)}, u32[]{:S(2)}) collective-permute-start(bf16[576,256]{1,0:T(8,128)(2,1)S(1)} %get-tuple-element.10.refs_0_), channel_id=1, source_target_pairs={{384,0},{0,128},{128,256},{256,384},{385,1},{1,129},{129,257},{257... | collective-permute-start | bytes 884744 | tf_op jit(solution)/shard_map/ppermute | solution.py:18
  26.3 16.1 %collective-permute-start.3 = (bf16[576,256]{1,0:T(8,128)(2,1)S(1)}, bf16[576,256]{1,0:T(8,128)(2,1)S(1)}, u32[]{:S(2)}, u32[]{:S(2)}) collective-permute-start(bf16[576,256]{1,0:T(8,128)(2,1)S(1)} %get-tuple-element.10.refs_0_), channel_id=1, source_target_pairs={{1,0},{0,1},{3,2},{2,3},{5,4},{4,5},{7,6},{6,7},{9,8},{8,9},{11,10... | collective-permute-start | bytes 884744 | tf_op jit(solution)/shard_map/ppermute | solution.py:18
  30.0 12.4 %collective-permute-start.4 = (bf16[576,256]{1,0:T(8,128)(2,1)S(1)}, bf16[576,256]{1,0:T(8,128)(2,1)S(1)}, u32[]{:S(2)}, u32[]{:S(2)}) collective-permute-start(bf16[576,256]{1,0:T(8,128)(2,1)S(1)} %collective-permute-done.refs_1_), channel_id=1, source_target_pairs={{1,0},{0,1},{3,2},{2,3},{5,4},{4,5},{7,6},{6,7},{9,8},{8,9},{11,10... | collective-permute-start | bytes 884744 | tf_op jit(solution)/shard_map/ppermute | solution.py:18
  36.8 5.6 %collective-permute-start.5 = (bf16[576,256]{1,0:T(8,128)(2,1)S(1)}, bf16[576,256]{1,0:T(8,128)(2,1)S(1)}, u32[]{:S(2)}, u32[]{:S(2)}) collective-permute-start(bf16[576,256]{1,0:T(8,128)(2,1)S(1)} %collective-permute-done.1.refs_2_), channel_id=1, source_target_pairs={{1,0},{0,1},{3,2},{2,3},{5,4},{4,5},{7,6},{6,7},{9,8},{8,9},{11,10... | collective-permute-start | bytes 884744 | tf_op jit(solution)/shard_map/ppermute | solution.py:18
  40.0 3.6 %collective-permute-start.6 = (bf16[576,256]{1,0:T(8,128)(2,1)S(1)}, bf16[576,256]{1,0:T(8,128)(2,1)S(1)}, u32[]{:S(2)}, u32[]{:S(2)}) collective-permute-start(bf16[576,256]{1,0:T(8,128)(2,1)S(1)} %collective-permute-done.2.refs_3_), channel_id=1, source_target_pairs={{1,0},{0,1},{3,2},{2,3},{5,4},{4,5},{7,6},{6,7},{9,8},{8,9},{11,10... | collective-permute-start | bytes 884744 | tf_op jit(solution)/shard_map/ppermute | solution.py:18
  88.2 7.3 %copy-start = (s32[1,4]{1,0:T(1,128)S(1)}, s32[1,4]{1,0:T(1,128)}, u32[]{:S(2)}) copy-start(s32[1,4]{1,0:T(1,128)} %param.9) | copy-start | bytes 52
  89.6 18.4 %all-to-all-start.2 = ((bf16[64,16,128]{2,1,0:T(8,128)(2,1)}), bf16[64,16,128]{2,1,0:T(8,128)(2,1)S(1)}, u32[]{:S(2)}, u32[]{:S(2)}) async-start(bf16[64,16,128]{2,1,0:T(8,128)(2,1)} %shard_map.57), calls=%async_computation.2 | async-start | bytes 524288 | tf_op jit(solution)/shard_map/all_to_all | solution.py:248

commit v11 on v9

--- a/solution.py
+++ b/solution.py
@@ -140,8 +140,7 @@
     out_ref[...] = jnp.broadcast_to(narrow[...].astype(BF16)[None], out_ref.shape)
 
 
-def documents(place, out_ref, in_ref, send_ref, keep_ref, rows_out):
-    zh = place[1]
+def documents(place, out_ref, in_ref, both_ref, rows_out):
     rows_out[...] = out_ref[...].astype(F32).reshape(64 * 16, 128)
     position = lax.broadcasted_iota(jnp.int32, (1, 256), 1).astype(F32)
     total = jnp.zeros((NX * 16, 128), F32)
@@ -152,7 +151,7 @@
         for h in range(2):
             cut = [
                 rows_out[pl.ds((zl * 16 + core) * 16 + block * 8 + g * 2 + h, NY, stride=32), :]
-                for block in (1 - zh, zh)
+                for block in range(NZH)
                 for zl in range(NZL)
                 for core in range(NC)
             ]
@@ -172,8 +171,8 @@
             total = total + one * one
     total = total * (1.0 / 2048.0)
     for i in range(NX):
-        send_ref[i * 14 : (i + 1) * 14, :] = total[i * 16 : i * 16 + 14, :64]
-        keep_ref[i * 14 : (i + 1) * 14, :] = total[i * 16 : i * 16 + 14, 64:]
+        for block in range(NZH):
+            both_ref[block, i * 14 : (i + 1) * 14, :] = total[i * 16 : i * 16 + 14, block * 64 : (block + 1) * 64]
 
 
 def body(acts, grads, basis_in, basis_out, doc_lengths):
@@ -233,16 +232,15 @@
 
     proj_out = lax.all_to_all(proj_out, ("zl", "y", "core"), split_axis=0, concat_axis=0, tiled=True)
     proj_in = lax.all_gather(proj_in, "x")
-    block = jax.ShapeDtypeStruct((NX * rows, 64), F32)
-    send, keep = call(
+    both = call(
         documents,
-        (block, block),
+        jax.ShapeDtypeStruct((NZH, NX * rows, 64), F32),
         [pltpu.VMEM((64 * 16, 128), F32)],
         (place, *map(in_vmem, (proj_out, proj_in))),
         2 * 4 * 256 * 256 * 128,
     )
-    both = lax.all_gather(send, "zh")
-    return (keep + jnp.where(zh == 0, both[1], both[0])).T
+    both = lax.all_to_all(both, "zh", split_axis=0, concat_axis=0, tiled=True)
+    return (both[0] + both[1]).T
 
 
 def solution(mesh):

time: 118 us -> 126 us (1.068)
  blocking collectives: 17.9 us -> 23.8 us
    all_to_all x0 -> x1, blocking collectives: none -> 13.8 us  [body(): both = lax.all_to_all(both, 'zh', split_axis=0, concat_axis=0, tiled=True)]
    all_gather x1 -> x0, blocking collectives: 7.91 us -> none  [body(): both = lax.all_gather(send, 'zh')]
where the time goes in v11:
time: 126 us; the launch traced here: 125 us
  starting transfers between devices  57.1 us (45%)
  waiting for transfers between devices  32.5 us (26%)
  blocking collectives  23.8 us (19%)
  Pallas kernels  9.15 us (7%)
  other arithmetic  1.42 us (1%)
    all_to_all x1, waiting for transfers between devices, body(): lax.all_to_all(parts, ('zl', 'y'), split_axis=0, concat_axis=0, tiled=True)  27.8 us
    ppermute x7, starting transfers between devices, from_offset(): lax.ppermute(value, axis, [((i + offset) % size, i) for i in range(size)])  24.1 us
    all_to_all x1, blocking collectives, body(): both = lax.all_to_all(both, 'zh', split_axis=0, concat_axis=0, tiled=True)  13.8 us
    all_to_all x1, starting transfers between devices, body(): lax.all_to_all(packed, ('zl', 'y'), split_axis=0, concat_axis=0, tiled=True)  13.5 us
    all_gather x1, blocking collectives, body(): proj_in = lax.all_gather(proj_in, 'x')  9.99 us
    all_to_all x1, starting transfers between devices, body(): lax.all_to_all(proj_out, ('zl', 'y', 'core'), split_axis=0, concat_axis=0...  9.94 us
    all_to_all x1, starting transfers between devices, body(): lax.all_to_all(parts, ('zl', 'y'), split_axis=0, concat_axis=0, tiled=True)  9.58 us
    pallas_call x4, Pallas kernels, call(): pl.pallas_call(kernel, out_shape=shapes, in_specs=in_specs or [SMEM] + [V...  9.15 us
  transfers between devices with their start and end apart: 10, of which 4 were waited for; matrix products, arithmetic and copies ran while one was open for 0% of the time, Pallas kernels for 0%

profile of v11, /device:TPU:1, one launch (start us, length us, event | category | flops | bytes accessed | tf_op | source)
XLA Modules:
  0.0 124.9 jit_solution(5952211126393197751)
XLA Ops:
  0.0 0.1 pad_add_fusion.place
  0.1 3.3 %shard_map.55 = (bf16[32,16,1024]{2,1,0:T(8,128)(2,1)}, bf16[576,256]{1,0:T(8,128)(2,1)S(1)}) custom-call(s32[3]{0:T(128)S(1)} %pad_add_fusion.place, bf16[56,28672]{1,0:T(8,128)(2,1)} %basis_ref.1, bf16[8,8192]{1,0:T(8,128)(2,1)} %out_rows_ref.1, bf16[448,256]{1,0:T(8,128)(2,1)} %bitcast.10, bf16[256,128]{1,0:T(8,128)(2,1)} %grads_ref.1), custom_call_target="tpu_custom_call" | custom-call | flops 1048576 | bytes 3637260 | tf_op jit(solution)/shard_map/pallas_call | solution.py:23
  3.4 13.5 %all-to-all-start = ((bf16[32,16,1024]{2,1,0:T(8,128)(2,1)}), bf16[32,16,1024]{2,1,0:T(8,128)(2,1)S(1)}, u32[]{:S(2)}, u32[]{:S(2)}) async-start(bf16[32,16,1024]{2,1,0:T(8,128)(2,1)} %get-tuple-element.9), calls=%async_computation | async-start | bytes 2097152 | tf_op jit(solution)/shard_map/all_to_all | solution.py:202
  16.9 4.4 %collective-permute-start = (bf16[576,256]{1,0:T(8,128)(2,1)S(1)}, bf16[576,256]{1,0:T(8,128)(2,1)S(1)}, u32[]{:S(2)}, u32[]{:S(2)}) collective-permute-start(bf16[576,256]{1,0:T(8,128)(2,1)S(1)} %get-tuple-element.10.refs_0_), channel_id=1, source_target_pairs={{128,0},{256,128},{384,256},{0,384},{129,1},{257,129},{385,257},{1... | collective-permute-start | bytes 884744 | tf_op jit(solution)/shard_map/ppermute | solution.py:18
  21.3 2.5 %collective-permute-start.1 = (bf16[576,256]{1,0:T(8,128)(2,1)S(1)}, bf16[576,256]{1,0:T(8,128)(2,1)S(1)}, u32[]{:S(2)}, u32[]{:S(2)}) collective-permute-start(bf16[576,256]{1,0:T(8,128)(2,1)S(1)} %get-tuple-element.10.refs_0_), channel_id=1, source_target_pairs={{256,0},{384,128},{0,256},{128,384},{257,1},{385,129},{1,257},{129... | collective-permute-start | bytes 884744 | tf_op jit(solution)/shard_map/ppermute | solution.py:18
  23.8 2.5 %collective-permute-start.2 = (bf16[576,256]{1,0:T(8,128)(2,1)S(1)}, bf16[576,256]{1,0:T(8,128)(2,1)S(1)}, u32[]{:S(2)}, u32[]{:S(2)}) collective-permute-start(bf16[576,256]{1,0:T(8,128)(2,1)S(1)} %get-tuple-element.10.refs_0_), channel_id=1, source_target_pairs={{384,0},{0,128},{128,256},{256,384},{385,1},{1,129},{129,257},{257... | collective-permute-start | bytes 884744 | tf_op jit(solution)/shard_map/ppermute | solution.py:18
  26.3 3.7 %collective-permute-start.3 = (bf16[576,256]{1,0:T(8,128)(2,1)S(1)}, bf16[576,256]{1,0:T(8,128)(2,1)S(1)}, u32[]{:S(2)}, u32[]{:S(2)}) collective-permute-start(bf16[576,256]{1,0:T(8,128)(2,1)S(1)} %get-tuple-element.10.refs_0_), channel_id=1, source_target_pairs={{1,0},{0,1},{3,2},{2,3},{5,4},{4,5},{7,6},{6,7},{9,8},{8,9},{11,10... | collective-permute-start | bytes 884744 | tf_op jit(solution)/shard_map/ppermute | solution.py:18
  30.0 0.0 collective-permute-done.refs_1_
  30.0 6.8 %collective-permute-start.4 = (bf16[576,256]{1,0:T(8,128)(2,1)S(1)}, bf16[576,256]{1,0:T(8,128)(2,1)S(1)}, u32[]{:S(2)}, u32[]{:S(2)}) collective-permute-start(bf16[576,256]{1,0:T(8,128)(2,1)S(1)} %collective-permute-done.refs_1_), channel_id=1, source_target_pairs={{1,0},{0,1},{3,2},{2,3},{5,4},{4,5},{7,6},{6,7},{9,8},{8,9},{11,10... | collective-permute-start | bytes 884744 | tf_op jit(solution)/shard_map/ppermute | solution.py:18
  36.8 0.0 collective-permute-done.1.refs_2_
  36.8 1.9 %collective-permute-start.5 = (bf16[576,256]{1,0:T(8,128)(2,1)S(1)}, bf16[576,256]{1,0:T(8,128)(2,1)S(1)}, u32[]{:S(2)}, u32[]{:S(2)}) collective-permute-start(bf16[576,256]{1,0:T(8,128)(2,1)S(1)} %collective-permute-done.1.refs_2_), channel_id=1, source_target_pairs={{1,0},{0,1},{3,2},{2,3},{5,4},{4,5},{7,6},{6,7},{9,8},{8,9},{11,10... | collective-permute-start | bytes 884744 | tf_op jit(solution)/shard_map/ppermute | solution.py:18
  38.7 1.3 %collective-permute-done.2.refs_3_ = bf16[576,256]{1,0:T(8,128)(2,1)S(1)} collective-permute-done((bf16[576,256]{1,0:T(8,128)(2,1)S(1)}, bf16[576,256]{1,0:T(8,128)(2,1)S(1)}, u32[]{:S(2)}, u32[]{:S(2)}) %collective-permute-start.2) | collective-permute-done | bytes 294944 | tf_op jit(solution)/shard_map/ppermute | solution.py:18
  40.0 2.4 %collective-permute-start.6 = (bf16[576,256]{1,0:T(8,128)(2,1)S(1)}, bf16[576,256]{1,0:T(8,128)(2,1)S(1)}, u32[]{:S(2)}, u32[]{:S(2)}) collective-permute-start(bf16[576,256]{1,0:T(8,128)(2,1)S(1)} %collective-permute-done.2.refs_3_), channel_id=1, source_target_pairs={{1,0},{0,1},{3,2},{2,3},{5,4},{4,5},{7,6},{6,7},{9,8},{8,9},{11,10... | collective-permute-start | bytes 884744 | tf_op jit(solution)/shard_map/ppermute | solution.py:18
  42.4 0.0 collective-permute-done.3.refs_4_
  42.4 0.0 collective-permute-done.4.refs_5_
  42.4 0.0 collective-permute-done.5.refs_6_
  42.4 1.2 collective-permute-done.6.refs_7_
  43.5 3.2 %shard_map.56 = bf16[32,16,1152]{2,1,0:T(8,128)(2,1)} custom-call(s32[3]{0:T(128)S(1)} %pad_add_fusion.place, bf16[32,16,1024]{2,1,0:T(8,128)(2,1)S(1)} %all-to-all-done.packed_ref, bf16[576,256]{1,0:T(8,128)(2,1)S(1)} %get-tuple-element.10.refs_0_, bf16[576,256]{1,0:T(8,128)(2,1)S(1)} %collective-permute-done.refs_1_, ...), custom_call_target="tpu_custom_call" | custom-call | flops 1073741824 | bytes 3407884 | tf_op jit(solution)/shard_map/pallas_call | solution.py:23
  46.8 0.0 copy-start
  46.8 9.6 %all-to-all-start.1 = ((bf16[32,16,1152]{2,1,0:T(8,128)(2,1)}), bf16[32,16,1152]{2,1,0:T(8,128)(2,1)S(1)}, u32[]{:S(2)}, u32[]{:S(2)}) async-start(bf16[32,16,1152]{2,1,0:T(8,128)(2,1)} %shard_map.56), calls=%async_computation.1 | async-start | bytes 2359296 | tf_op jit(solution)/shard_map/all_to_all | solution.py:223
  56.4 27.8 %all-to-all-done.1.parts_ref = bf16[32,16,1152]{2,1,0:T(8,128)(2,1)S(1)} async-done(((bf16[32,16,1152]{2,1,0:T(8,128)(2,1)}), bf16[32,16,1152]{2,1,0:T(8,128)(2,1)S(1)}, u32[]{:S(2)}, u32[]{:S(2)}) %all-to-all-start.1) | async-done | bytes 1179680 | tf_op jit(solution)/shard_map/all_to_all | solution.py:223
  84.2 1.4 %shard_map.57 = (bf16[16,1024]{1,0:T(8,128)(2,1)S(1)}, bf16[64,16,128]{2,1,0:T(8,128)(2,1)}) custom-call(s32[3]{0:T(128)S(1)} %pad_add_fusion.place, f32[1,128]{1,0:T(1,128)S(1)} %pad.4.lens_ref, bf16[32,16,1152]{2,1,0:T(8,128)(2,1)S(1)} %all-to-all-done.1.parts_ref), custom_call_target="tpu_custom_call" | custom-call | flops 589824 | bytes 1180172 | tf_op jit(solution)/shard_map/pallas_call | solution.py:23
  85.6 9.9 %all-to-all-start.2 = ((bf16[64,16,128]{2,1,0:T(8,128)(2,1)}), bf16[64,16,128]{2,1,0:T(8,128)(2,1)S(1)}, u32[]{:S(2)}, u32[]{:S(2)}) async-start(bf16[64,16,128]{2,1,0:T(8,128)(2,1)} %get-tuple-element.11), calls=%async_computation.2 | async-start | bytes 524288 | tf_op jit(solution)/shard_map/all_to_all | solution.py:233
  95.6 10.0 %all-gather = bf16[64,1024]{1,0:T(8,128)(2,1)S(1)} all-gather(bf16[16,1024]{1,0:T(8,128)(2,1)S(1)} %get-tuple-element.12), channel_id=2, replica_groups=mesh['x'=4,'zh'=2,'zl'=4,'y'=8,'core'=2] {'x'}, dimensions={0}, use_global_device_ids=true | all-gather | bytes 163840 | tf_op jit(solution)/shard_map/all_gather | solution.py:234
  105.6 2.3 %all-to-all-done.2.out_ref = bf16[64,16,128]{2,1,0:T(8,128)(2,1)S(1)} async-done(((bf16[64,16,128]{2,1,0:T(8,128)(2,1)}), bf16[64,16,128]{2,1,0:T(8,128)(2,1)S(1)}, u32[]{:S(2)}, u32[]{:S(2)}) %all-to-all-start.2) | async-done | bytes 262176 | tf_op jit(solution)/shard_map/all_to_all | solution.py:233
  107.9 1.2 shard_map.58
  109.0 0.1 reshape.2
  109.1 13.8 %all_to_all.20 = f32[2,1,3584]{2,1,0:T(1,128)S(1)} all-to-all(f32[2,1,3584]{2,1,0:T(1,128)S(1)} %reshape.2), channel_id=1, replica_groups=mesh['x'=4,'zh'=2,'zl'=4,'y'=8,'core'=2] {'zh'}, dimensions={0} | all-to-all | bytes 57344 | tf_op jit(solution)/shard_map/all_to_all | solution.py:242
  122.9 0.5 broadcast.2
  123.4 0.7 reduce
  124.2 0.1 reshape.3
  124.3 0.6 fusion
  (4 shorter events, 0.0 us)
Async XLA Ops:
  3.4 40.1 %all-to-all-start = ((bf16[32,16,1024]{2,1,0:T(8,128)(2,1)}), bf16[32,16,1024]{2,1,0:T(8,128)(2,1)S(1)}, u32[]{:S(2)}, u32[]{:S(2)}) async-start(bf16[32,16,1024]{2,1,0:T(8,128)(2,1)} %get-tuple-element.9), calls=%async_computation | async-start | bytes 2097152 | tf_op jit(solution)/shard_map/all_to_all | solution.py:202
  16.9 13.1 %collective-permute-start = (bf16[576,256]{1,0:T(8,128)(2,1)S(1)}, bf16[576,256]{1,0:T(8,128)(2,1)S(1)}, u32[]{:S(2)}, u32[]{:S(2)}) collective-permute-start(bf16[576,256]{1,0:T(8,128)(2,1)S(1)} %get-tuple-element.10.refs_0_), channel_id=1, source_target_pairs={{128,0},{256,128},{384,256},{0,384},{129,1},{257,129},{385,257},{1... | collective-permute-start | bytes 884744 | tf_op jit(solution)/shard_map/ppermute | solution.py:18
  21.3 15.5 %collective-permute-start.1 = (bf16[576,256]{1,0:T(8,128)(2,1)S(1)}, bf16[576,256]{1,0:T(8,128)(2,1)S(1)}, u32[]{:S(2)}, u32[]{:S(2)}) collective-permute-start(bf16[576,256]{1,0:T(8,128)(2,1)S(1)} %get-tuple-element.10.refs_0_), channel_id=1, source_target_pairs={{256,0},{384,128},{0,256},{128,384},{257,1},{385,129},{1,257},{129... | collective-permute-start | bytes 884744 | tf_op jit(solution)/shard_map/ppermute | solution.py:18
  23.8 16.2 %collective-permute-start.2 = (bf16[576,256]{1,0:T(8,128)(2,1)S(1)}, bf16[576,256]{1,0:T(8,128)(2,1)S(1)}, u32[]{:S(2)}, u32[]{:S(2)}) collective-permute-start(bf16[576,256]{1,0:T(8,128)(2,1)S(1)} %get-tuple-element.10.refs_0_), channel_id=1, source_target_pairs={{384,0},{0,128},{128,256},{256,384},{385,1},{1,129},{129,257},{257... | collective-permute-start | bytes 884744 | tf_op jit(solution)/shard_map/ppermute | solution.py:18
  26.3 16.1 %collective-permute-start.3 = (bf16[576,256]{1,0:T(8,128)(2,1)S(1)}, bf16[576,256]{1,0:T(8,128)(2,1)S(1)}, u32[]{:S(2)}, u32[]{:S(2)}) collective-permute-start(bf16[576,256]{1,0:T(8,128)(2,1)S(1)} %get-tuple-element.10.refs_0_), channel_id=1, source_target_pairs={{1,0},{0,1},{3,2},{2,3},{5,4},{4,5},{7,6},{6,7},{9,8},{8,9},{11,10... | collective-permute-start | bytes 884744 | tf_op jit(solution)/shard_map/ppermute | solution.py:18
  30.0 12.4 %collective-permute-start.4 = (bf16[576,256]{1,0:T(8,128)(2,1)S(1)}, bf16[576,256]{1,0:T(8,128)(2,1)S(1)}, u32[]{:S(2)}, u32[]{:S(2)}) collective-permute-start(bf16[576,256]{1,0:T(8,128)(2,1)S(1)} %collective-permute-done.refs_1_), channel_id=1, source_target_pairs={{1,0},{0,1},{3,2},{2,3},{5,4},{4,5},{7,6},{6,7},{9,8},{8,9},{11,10... | collective-permute-start | bytes 884744 | tf_op jit(solution)/shard_map/ppermute | solution.py:18
  36.8 5.6 %collective-permute-start.5 = (bf16[576,256]{1,0:T(8,128)(2,1)S(1)}, bf16[576,256]{1,0:T(8,128)(2,1)S(1)}, u32[]{:S(2)}, u32[]{:S(2)}) collective-permute-start(bf16[576,256]{1,0:T(8,128)(2,1)S(1)} %collective-permute-done.1.refs_2_), channel_id=1, source_target_pairs={{1,0},{0,1},{3,2},{2,3},{5,4},{4,5},{7,6},{6,7},{9,8},{8,9},{11,10... | collective-permute-start | bytes 884744 | tf_op jit(solution)/shard_map/ppermute | solution.py:18
  40.0 3.6 %collective-permute-start.6 = (bf16[576,256]{1,0:T(8,128)(2,1)S(1)}, bf16[576,256]{1,0:T(8,128)(2,1)S(1)}, u32[]{:S(2)}, u32[]{:S(2)}) collective-permute-start(bf16[576,256]{1,0:T(8,128)(2,1)S(1)} %collective-permute-done.2.refs_3_), channel_id=1, source_target_pairs={{1,0},{0,1},{3,2},{2,3},{5,4},{4,5},{7,6},{6,7},{9,8},{8,9},{11,10... | collective-permute-start | bytes 884744 | tf_op jit(solution)/shard_map/ppermute | solution.py:18
  46.8 9.6 %copy-start = (s32[1,4]{1,0:T(1,128)S(1)}, s32[1,4]{1,0:T(1,128)}, u32[]{:S(2)}) copy-start(s32[1,4]{1,0:T(1,128)} %param.9) | copy-start | bytes 52
  46.8 37.4 %all-to-all-start.1 = ((bf16[32,16,1152]{2,1,0:T(8,128)(2,1)}), bf16[32,16,1152]{2,1,0:T(8,128)(2,1)S(1)}, u32[]{:S(2)}, u32[]{:S(2)}) async-start(bf16[32,16,1152]{2,1,0:T(8,128)(2,1)} %shard_map.56), calls=%async_computation.1 | async-start | bytes 2359296 | tf_op jit(solution)/shard_map/all_to_all | solution.py:223
  85.6 22.2 %all-to-all-start.2 = ((bf16[64,16,128]{2,1,0:T(8,128)(2,1)}), bf16[64,16,128]{2,1,0:T(8,128)(2,1)S(1)}, u32[]{:S(2)}, u32[]{:S(2)}) async-start(bf16[64,16,128]{2,1,0:T(8,128)(2,1)} %get-tuple-element.11), calls=%async_computation.2 | async-start | bytes 524288 | tf_op jit(solution)/shard_map/all_to_all | solution.py:233

commit v12 on v9

--- a/solution.py
+++ b/solution.py
@@ -86,24 +86,25 @@
 
 def project(place, packed_ref, *refs):
     own, other, parts_ref = refs[:NX], refs[NX : 2 * NX], refs[2 * NX]
-    acts, grads, wide, low, *outs, sems = refs[2 * NX + 1 :]
+    wide, low, *outs, sems = refs[2 * NX + 1 :]
     x, core = place[0], place[2]
-    fin = acts.shape[0] // NC
-    fout = grads.shape[1]
-    tokens, height = acts.shape[1], CHIPS * 16
+    fout = parts_ref.shape[2] - NX * 256
+    fin = own[0].shape[0] - fout
+    tokens, height = NX * 256, CHIPS * 16
+
+    def by_core(halves):
+        return jnp.where(core == 0, halves[0], halves[1]), jnp.where(core == 0, halves[1], halves[0])
+
     left = packed_ref[:, :, : NC * fin].reshape(height, NC * fin)
+    left = by_core([left[:, c * fin : (c + 1) * fin] for c in range(NC)])
     rows_out = packed_ref[pl.ds(x * 8, 8), :, NC * fin :].astype(F32).reshape(8, NC, 8, fout)
-    rows_out = [rows_out[:, c].reshape(64, fout).astype(BF16) for c in range(NC)]
+    rows_out = by_core([rows_out[:, c].reshape(64, fout).astype(BF16) for c in range(NC)])
     results = []
     for s in range(NX):
-        cols = slice(s * 256, (s + 1) * 256)
-        for pieces, which in ((own, core), (other, 1 - core)):
-            acts[pl.ds(pl.multiple_of(which * fin, 16), fin), cols] = pieces[s][:fin, :]
-            grads[which, :, cols] = pieces[s][fin:, :]
-        part = jnp.dot(left, acts[:, cols], preferred_element_type=F32)
-        out = jnp.zeros((64, 256), F32)
-        for c in range(NC):
-            out += jnp.dot(rows_out[c], grads[c, :, cols], preferred_element_type=F32)
+        part, out = 0.0, 0.0
+        for k, pieces in enumerate((own, other)):
+            part += jnp.dot(left[k], pieces[s][:fin, :], preferred_element_type=F32)
+            out += jnp.dot(rows_out[k], pieces[s][fin:, :], preferred_element_type=F32)
         rest = out - out.astype(BF16).astype(F32)
         for h in range(2):
             block = slice(h * 128, (h + 1) * 128)
@@ -209,8 +210,6 @@
         project,
         in_hbm((CHIPS, 16, tokens + 128)),
         [
-            pltpu.VMEM((NC * fin, tokens), BF16),
-            pltpu.VMEM((NC, fout, tokens), BF16),
             pltpu.VMEM((2 * CHIPS * 16, 128), F32),
             pltpu.VMEM((CHIPS * 16, 128), F32),
             *[pltpu.VMEM((CHIPS, 16, 256), BF16)] * NX,

time: 118 us -> 118 us (level)
  no operation moved by 1% of the time
where the time goes in v12:
time: 118 us; the launch traced here: 117 us
  starting transfers between devices  57.1 us (48%)
  waiting for transfers between devices  32.5 us (28%)
  blocking collectives  17.9 us (15%)
  Pallas kernels  8.95 us (8%)
    all_to_all x1, waiting for transfers between devices, body(): lax.all_to_all(parts, ('zl', 'y'), split_axis=0, concat_axis=0, tiled=True)  27.8 us
    ppermute x7, starting transfers between devices, from_offset(): lax.ppermute(value, axis, [((i + offset) % size, i) for i in range(size)])  24.1 us
    all_to_all x1, starting transfers between devices, body(): lax.all_to_all(packed, ('zl', 'y'), split_axis=0, concat_axis=0, tiled=True)  13.5 us
    all_gather x1, blocking collectives, body(): proj_in = lax.all_gather(proj_in, 'x')  9.99 us
    all_to_all x1, starting transfers between devices, body(): lax.all_to_all(proj_out, ('zl', 'y', 'core'), split_axis=0, concat_axis=0...  9.94 us
    all_to_all x1, starting transfers between devices, body(): lax.all_to_all(parts, ('zl', 'y'), split_axis=0, concat_axis=0, tiled=True)  9.58 us
    pallas_call x4, Pallas kernels, call(): pl.pallas_call(kernel, out_shape=shapes, in_specs=in_specs or [SMEM] + [V...  8.95 us
    all_gather x1, blocking collectives, body(): both = lax.all_gather(send, 'zh')  7.93 us
  transfers between devices with their start and end apart: 10, of which 4 were waited for; matrix products, arithmetic and copies ran while one was open for 0% of the time, Pallas kernels for 0%

profile of v12, /device:TPU:1, one launch (start us, length us, event | category | flops | bytes accessed | tf_op | source)
XLA Modules:
  0.0 117.4 jit_solution(12213200870080242681)
XLA Ops:
  0.0 0.1 pad_add_fusion.place
  0.1 3.4 %shard_map.55 = (bf16[32,16,1024]{2,1,0:T(8,128)(2,1)}, bf16[576,256]{1,0:T(8,128)(2,1)S(1)}) custom-call(s32[3]{0:T(128)S(1)} %pad_add_fusion.place, bf16[56,28672]{1,0:T(8,128)(2,1)} %basis_ref.1, bf16[8,8192]{1,0:T(8,128)(2,1)} %out_rows_ref.1, bf16[448,256]{1,0:T(8,128)(2,1)} %bitcast.8, bf16[256,128]{1,0:T(8,128)(2,1)} %grads_ref.1), custom_call_target="tpu_custom_call" | custom-call | flops 1048576 | bytes 3637260 | tf_op jit(solution)/shard_map/pallas_call | solution.py:23
  3.4 13.5 %all-to-all-start = ((bf16[32,16,1024]{2,1,0:T(8,128)(2,1)}), bf16[32,16,1024]{2,1,0:T(8,128)(2,1)S(1)}, u32[]{:S(2)}, u32[]{:S(2)}) async-start(bf16[32,16,1024]{2,1,0:T(8,128)(2,1)} %get-tuple-element.11), calls=%async_computation | async-start | bytes 2097152 | tf_op jit(solution)/shard_map/all_to_all | solution.py:204
  16.9 4.4 %collective-permute-start = (bf16[576,256]{1,0:T(8,128)(2,1)S(1)}, bf16[576,256]{1,0:T(8,128)(2,1)S(1)}, u32[]{:S(2)}, u32[]{:S(2)}) collective-permute-start(bf16[576,256]{1,0:T(8,128)(2,1)S(1)} %get-tuple-element.12.refs_0_), channel_id=1, source_target_pairs={{128,0},{256,128},{384,256},{0,384},{129,1},{257,129},{385,257},{1... | collective-permute-start | bytes 884744 | tf_op jit(solution)/shard_map/ppermute | solution.py:18
  21.3 2.5 %collective-permute-start.1 = (bf16[576,256]{1,0:T(8,128)(2,1)S(1)}, bf16[576,256]{1,0:T(8,128)(2,1)S(1)}, u32[]{:S(2)}, u32[]{:S(2)}) collective-permute-start(bf16[576,256]{1,0:T(8,128)(2,1)S(1)} %get-tuple-element.12.refs_0_), channel_id=1, source_target_pairs={{256,0},{384,128},{0,256},{128,384},{257,1},{385,129},{1,257},{129... | collective-permute-start | bytes 884744 | tf_op jit(solution)/shard_map/ppermute | solution.py:18
  23.8 2.5 %collective-permute-start.2 = (bf16[576,256]{1,0:T(8,128)(2,1)S(1)}, bf16[576,256]{1,0:T(8,128)(2,1)S(1)}, u32[]{:S(2)}, u32[]{:S(2)}) collective-permute-start(bf16[576,256]{1,0:T(8,128)(2,1)S(1)} %get-tuple-element.12.refs_0_), channel_id=1, source_target_pairs={{384,0},{0,128},{128,256},{256,384},{385,1},{1,129},{129,257},{257... | collective-permute-start | bytes 884744 | tf_op jit(solution)/shard_map/ppermute | solution.py:18
  26.3 3.7 %collective-permute-start.3 = (bf16[576,256]{1,0:T(8,128)(2,1)S(1)}, bf16[576,256]{1,0:T(8,128)(2,1)S(1)}, u32[]{:S(2)}, u32[]{:S(2)}) collective-permute-start(bf16[576,256]{1,0:T(8,128)(2,1)S(1)} %get-tuple-element.12.refs_0_), channel_id=1, source_target_pairs={{1,0},{0,1},{3,2},{2,3},{5,4},{4,5},{7,6},{6,7},{9,8},{8,9},{11,10... | collective-permute-start | bytes 884744 | tf_op jit(solution)/shard_map/ppermute | solution.py:18
  30.0 0.0 collective-permute-done.refs_1_
  30.0 6.8 %collective-permute-start.4 = (bf16[576,256]{1,0:T(8,128)(2,1)S(1)}, bf16[576,256]{1,0:T(8,128)(2,1)S(1)}, u32[]{:S(2)}, u32[]{:S(2)}) collective-permute-start(bf16[576,256]{1,0:T(8,128)(2,1)S(1)} %collective-permute-done.refs_1_), channel_id=1, source_target_pairs={{1,0},{0,1},{3,2},{2,3},{5,4},{4,5},{7,6},{6,7},{9,8},{8,9},{11,10... | collective-permute-start | bytes 884744 | tf_op jit(solution)/shard_map/ppermute | solution.py:18
  36.8 0.0 collective-permute-done.1.refs_2_
  36.8 1.9 %collective-permute-start.5 = (bf16[576,256]{1,0:T(8,128)(2,1)S(1)}, bf16[576,256]{1,0:T(8,128)(2,1)S(1)}, u32[]{:S(2)}, u32[]{:S(2)}) collective-permute-start(bf16[576,256]{1,0:T(8,128)(2,1)S(1)} %collective-permute-done.1.refs_2_), channel_id=1, source_target_pairs={{1,0},{0,1},{3,2},{2,3},{5,4},{4,5},{7,6},{6,7},{9,8},{8,9},{11,10... | collective-permute-start | bytes 884744 | tf_op jit(solution)/shard_map/ppermute | solution.py:18
  38.7 1.3 %collective-permute-done.2.refs_3_ = bf16[576,256]{1,0:T(8,128)(2,1)S(1)} collective-permute-done((bf16[576,256]{1,0:T(8,128)(2,1)S(1)}, bf16[576,256]{1,0:T(8,128)(2,1)S(1)}, u32[]{:S(2)}, u32[]{:S(2)}) %collective-permute-start.2) | collective-permute-done | bytes 294944 | tf_op jit(solution)/shard_map/ppermute | solution.py:18
  40.0 2.4 %collective-permute-start.6 = (bf16[576,256]{1,0:T(8,128)(2,1)S(1)}, bf16[576,256]{1,0:T(8,128)(2,1)S(1)}, u32[]{:S(2)}, u32[]{:S(2)}) collective-permute-start(bf16[576,256]{1,0:T(8,128)(2,1)S(1)} %collective-permute-done.2.refs_3_), channel_id=1, source_target_pairs={{1,0},{0,1},{3,2},{2,3},{5,4},{4,5},{7,6},{6,7},{9,8},{8,9},{11,10... | collective-permute-start | bytes 884744 | tf_op jit(solution)/shard_map/ppermute | solution.py:18
  42.4 0.0 collective-permute-done.3.refs_4_
  42.4 0.0 collective-permute-done.4.refs_5_
  42.4 0.0 collective-permute-done.5.refs_6_
  42.4 1.2 collective-permute-done.6.refs_7_
  43.6 0.0 all-to-all-done.packed_ref
  43.6 3.0 %shard_map.56 = bf16[32,16,1152]{2,1,0:T(8,128)(2,1)} custom-call(s32[3]{0:T(128)S(1)} %pad_add_fusion.place, bf16[32,16,1024]{2,1,0:T(8,128)(2,1)S(1)} %all-to-all-done.packed_ref, bf16[576,256]{1,0:T(8,128)(2,1)S(1)} %get-tuple-element.12.refs_0_, bf16[576,256]{1,0:T(8,128)(2,1)S(1)} %collective-permute-done.refs_1_, ...), custom_call_target="tpu_custom_call" | custom-call | flops 1073741824 | bytes 3407884 | tf_op jit(solution)/shard_map/pallas_call | solution.py:23
  46.6 0.0 copy-start
  46.6 9.6 %all-to-all-start.1 = ((bf16[32,16,1152]{2,1,0:T(8,128)(2,1)}), bf16[32,16,1152]{2,1,0:T(8,128)(2,1)S(1)}, u32[]{:S(2)}, u32[]{:S(2)}) async-start(bf16[32,16,1152]{2,1,0:T(8,128)(2,1)} %shard_map.56), calls=%async_computation.1 | async-start | bytes 2359296 | tf_op jit(solution)/shard_map/all_to_all | solution.py:223
  56.2 0.0 copy-done
  56.2 27.8 %all-to-all-done.1.parts_ref = bf16[32,16,1152]{2,1,0:T(8,128)(2,1)S(1)} async-done(((bf16[32,16,1152]{2,1,0:T(8,128)(2,1)}), bf16[32,16,1152]{2,1,0:T(8,128)(2,1)S(1)}, u32[]{:S(2)}, u32[]{:S(2)}) %all-to-all-start.1) | async-done | bytes 1179680 | tf_op jit(solution)/shard_map/all_to_all | solution.py:223
  84.0 1.4 %shard_map.57 = (bf16[16,1024]{1,0:T(8,128)(2,1)S(1)}, bf16[64,16,128]{2,1,0:T(8,128)(2,1)}) custom-call(s32[3]{0:T(128)S(1)} %pad_add_fusion.place, f32[1,128]{1,0:T(1,128)S(1)} %pad.4.lens_ref, bf16[32,16,1152]{2,1,0:T(8,128)(2,1)S(1)} %all-to-all-done.1.parts_ref), custom_call_target="tpu_custom_call" | custom-call | flops 589824 | bytes 1180172 | tf_op jit(solution)/shard_map/pallas_call | solution.py:23
  85.4 9.9 %all-to-all-start.2 = ((bf16[64,16,128]{2,1,0:T(8,128)(2,1)}), bf16[64,16,128]{2,1,0:T(8,128)(2,1)S(1)}, u32[]{:S(2)}, u32[]{:S(2)}) async-start(bf16[64,16,128]{2,1,0:T(8,128)(2,1)} %get-tuple-element.13), calls=%async_computation.2 | async-start | bytes 524288 | tf_op jit(solution)/shard_map/all_to_all | solution.py:233
  95.4 10.0 %all-gather = bf16[64,1024]{1,0:T(8,128)(2,1)S(1)} all-gather(bf16[16,1024]{1,0:T(8,128)(2,1)S(1)} %get-tuple-element.14), channel_id=2, replica_groups=mesh['x'=4,'zh'=2,'zl'=4,'y'=8,'core'=2] {'x'}, dimensions={0}, use_global_device_ids=true | all-gather | bytes 163840 | tf_op jit(solution)/shard_map/all_gather | solution.py:234
  105.4 2.3 %all-to-all-done.2.out_ref = bf16[64,16,128]{2,1,0:T(8,128)(2,1)S(1)} async-done(((bf16[64,16,128]{2,1,0:T(8,128)(2,1)}), bf16[64,16,128]{2,1,0:T(8,128)(2,1)S(1)}, u32[]{:S(2)}, u32[]{:S(2)}) %all-to-all-start.2) | async-done | bytes 262176 | tf_op jit(solution)/shard_map/all_to_all | solution.py:233
  107.7 1.2 shard_map.58
  108.8 7.9 %all-gather.1 = f32[112,64]{1,0:T(8,128)S(1)} all-gather(f32[56,64]{1,0:T(8,128)S(1)} %get-tuple-element.16), channel_id=3, replica_groups=mesh['x'=4,'zh'=2,'zl'=4,'y'=8,'core'=2] {'zh'}, dimensions={0}, use_global_device_ids=true | all-gather | bytes 43008 | tf_op jit(solution)/shard_map/all_gather | solution.py:243
  116.8 0.6 fusion.1
  (2 shorter events, 0.0 us)
Async XLA Ops:
  3.4 40.1 %all-to-all-start = ((bf16[32,16,1024]{2,1,0:T(8,128)(2,1)}), bf16[32,16,1024]{2,1,0:T(8,128)(2,1)S(1)}, u32[]{:S(2)}, u32[]{:S(2)}) async-start(bf16[32,16,1024]{2,1,0:T(8,128)(2,1)} %get-tuple-element.11), calls=%async_computation | async-start | bytes 2097152 | tf_op jit(solution)/shard_map/all_to_all | solution.py:204
  16.9 13.1 %collective-permute-start = (bf16[576,256]{1,0:T(8,128)(2,1)S(1)}, bf16[576,256]{1,0:T(8,128)(2,1)S(1)}, u32[]{:S(2)}, u32[]{:S(2)}) collective-permute-start(bf16[576,256]{1,0:T(8,128)(2,1)S(1)} %get-tuple-element.12.refs_0_), channel_id=1, source_target_pairs={{128,0},{256,128},{384,256},{0,384},{129,1},{257,129},{385,257},{1... | collective-permute-start | bytes 884744 | tf_op jit(solution)/shard_map/ppermute | solution.py:18
  21.3 15.5 %collective-permute-start.1 = (bf16[576,256]{1,0:T(8,128)(2,1)S(1)}, bf16[576,256]{1,0:T(8,128)(2,1)S(1)}, u32[]{:S(2)}, u32[]{:S(2)}) collective-permute-start(bf16[576,256]{1,0:T(8,128)(2,1)S(1)} %get-tuple-element.12.refs_0_), channel_id=1, source_target_pairs={{256,0},{384,128},{0,256},{128,384},{257,1},{385,129},{1,257},{129... | collective-permute-start | bytes 884744 | tf_op jit(solution)/shard_map/ppermute | solution.py:18
  23.8 16.2 %collective-permute-start.2 = (bf16[576,256]{1,0:T(8,128)(2,1)S(1)}, bf16[576,256]{1,0:T(8,128)(2,1)S(1)}, u32[]{:S(2)}, u32[]{:S(2)}) collective-permute-start(bf16[576,256]{1,0:T(8,128)(2,1)S(1)} %get-tuple-element.12.refs_0_), channel_id=1, source_target_pairs={{384,0},{0,128},{128,256},{256,384},{385,1},{1,129},{129,257},{257... | collective-permute-start | bytes 884744 | tf_op jit(solution)/shard_map/ppermute | solution.py:18
  26.3 16.1 %collective-permute-start.3 = (bf16[576,256]{1,0:T(8,128)(2,1)S(1)}, bf16[576,256]{1,0:T(8,128)(2,1)S(1)}, u32[]{:S(2)}, u32[]{:S(2)}) collective-permute-start(bf16[576,256]{1,0:T(8,128)(2,1)S(1)} %get-tuple-element.12.refs_0_), channel_id=1, source_target_pairs={{1,0},{0,1},{3,2},{2,3},{5,4},{4,5},{7,6},{6,7},{9,8},{8,9},{11,10... | collective-permute-start | bytes 884744 | tf_op jit(solution)/shard_map/ppermute | solution.py:18
  30.0 12.4 %collective-permute-start.4 = (bf16[576,256]{1,0:T(8,128)(2,1)S(1)}, bf16[576,256]{1,0:T(8,128)(2,1)S(1)}, u32[]{:S(2)}, u32[]{:S(2)}) collective-permute-start(bf16[576,256]{1,0:T(8,128)(2,1)S(1)} %collective-permute-done.refs_1_), channel_id=1, source_target_pairs={{1,0},{0,1},{3,2},{2,3},{5,4},{4,5},{7,6},{6,7},{9,8},{8,9},{11,10... | collective-permute-start | bytes 884744 | tf_op jit(solution)/shard_map/ppermute | solution.py:18
  36.8 5.6 %collective-permute-start.5 = (bf16[576,256]{1,0:T(8,128)(2,1)S(1)}, bf16[576,256]{1,0:T(8,128)(2,1)S(1)}, u32[]{:S(2)}, u32[]{:S(2)}) collective-permute-start(bf16[576,256]{1,0:T(8,128)(2,1)S(1)} %collective-permute-done.1.refs_2_), channel_id=1, source_target_pairs={{1,0},{0,1},{3,2},{2,3},{5,4},{4,5},{7,6},{6,7},{9,8},{8,9},{11,10... | collective-permute-start | bytes 884744 | tf_op jit(solution)/shard_map/ppermute | solution.py:18
  40.0 3.6 %collective-permute-start.6 = (bf16[576,256]{1,0:T(8,128)(2,1)S(1)}, bf16[576,256]{1,0:T(8,128)(2,1)S(1)}, u32[]{:S(2)}, u32[]{:S(2)}) collective-permute-start(bf16[576,256]{1,0:T(8,128)(2,1)S(1)} %collective-permute-done.2.refs_3_), channel_id=1, source_target_pairs={{1,0},{0,1},{3,2},{2,3},{5,4},{4,5},{7,6},{6,7},{9,8},{8,9},{11,10... | collective-permute-start | bytes 884744 | tf_op jit(solution)/shard_map/ppermute | solution.py:18
  46.6 9.6 %copy-start = (s32[1,4]{1,0:T(1,128)S(1)}, s32[1,4]{1,0:T(1,128)}, u32[]{:S(2)}) copy-start(s32[1,4]{1,0:T(1,128)} %param.9) | copy-start | bytes 52
  46.6 37.4 %all-to-all-start.1 = ((bf16[32,16,1152]{2,1,0:T(8,128)(2,1)}), bf16[32,16,1152]{2,1,0:T(8,128)(2,1)S(1)}, u32[]{:S(2)}, u32[]{:S(2)}) async-start(bf16[32,16,1152]{2,1,0:T(8,128)(2,1)} %shard_map.56), calls=%async_computation.1 | async-start | bytes 2359296 | tf_op jit(solution)/shard_map/all_to_all | solution.py:223
  85.4 22.2 %all-to-all-start.2 = ((bf16[64,16,128]{2,1,0:T(8,128)(2,1)}), bf16[64,16,128]{2,1,0:T(8,128)(2,1)S(1)}, u32[]{:S(2)}, u32[]{:S(2)}) async-start(bf16[64,16,128]{2,1,0:T(8,128)(2,1)} %get-tuple-element.13), calls=%async_computation.2 | async-start | bytes 524288 | tf_op jit(solution)/shard_map/all_to_all | solution.py:233

commit v13 on v12

--- a/solution.py
+++ b/solution.py
@@ -99,46 +99,62 @@
     left = by_core([left[:, c * fin : (c + 1) * fin] for c in range(NC)])
     rows_out = packed_ref[pl.ds(x * 8, 8), :, NC * fin :].astype(F32).reshape(8, NC, 8, fout)
     rows_out = by_core([rows_out[:, c].reshape(64, fout).astype(BF16) for c in range(NC)])
-    results = []
-    for s in range(NX):
-        part, out = 0.0, 0.0
+    results, highs = [], []
+    for s in range(NX):
+        out = 0.0
+        for k, pieces in enumerate((own, other)):
+            out += jnp.dot(rows_out[k], pieces[s][fin:, :], preferred_element_type=F32)
+        highs.append(out)
+        rest = out - out.astype(BF16).astype(F32)
+        for h in range(2):
+            for half in range(2):
+                value = rest[half * 32 : half * 32 + 32, h * 128 : (h + 1) * 128]
+                low[pl.ds(half * 8 + s * 2 + h, CHIPS, stride=16), :] = value
+    outs[NX][...] = low[...].astype(BF16).reshape(CHIPS, 16, 128)
+    results.append(pltpu.make_async_copy(outs[NX], parts_ref.at[:, :, pl.ds(tokens, 128)], sems.at[NX]))
+    results[-1].start()
+    for s in range(NX):
+        part = 0.0
         for k, pieces in enumerate((own, other)):
             part += jnp.dot(left[k], pieces[s][:fin, :], preferred_element_type=F32)
-            out += jnp.dot(rows_out[k], pieces[s][fin:, :], preferred_element_type=F32)
-        rest = out - out.astype(BF16).astype(F32)
         for h in range(2):
             block = slice(h * 128, (h + 1) * 128)
             wide[pl.ds(h * height, height), :] = part[:, block]
             for half in range(2):
-                wide[pl.ds(h * height + 14 + half, CHIPS, stride=16), :] = out[half * 32 : half * 32 + 32, block]
-                low[pl.ds(half * 8 + s * 2 + h, CHIPS, stride=16), :] = rest[half * 32 : half * 32 + 32, block]
+                value = highs[s][half * 32 : half * 32 + 32, block]
+                wide[pl.ds(h * height + 14 + half, CHIPS, stride=16), :] = value
             outs[s][:, :, block] = wide[h * height : (h + 1) * height].astype(BF16).reshape(CHIPS, 16, 128)
         results.append(pltpu.make_async_copy(outs[s], parts_ref.at[:, :, pl.ds(s * 256, 256)], sems.at[s]))
         results[-1].start()
-    outs[NX][...] = low[...].astype(BF16).reshape(CHIPS, 16, 128)
-    results.append(pltpu.make_async_copy(outs[NX], parts_ref.at[:, :, pl.ds(tokens, 128)], sems.at[NX]))
-    results[-1].start()
     for result in results:
         result.wait()
 
 
-def add_up(place, lens_ref, parts_ref, in_ref, out_ref, wide, narrow):
+def add_up(place, lens_ref, parts_ref, in_ref, out_ref, wide, narrow, rows_in, spread, sems):
     x = place[0]
     tokens = wide.shape[1]
     total = parts_ref[0].astype(F32)
     for i in range(1, CHIPS):
         total = total + parts_ref[i].astype(F32)
-    for s in range(NX):
-        source = lax.rem(x + s, NX)
-        wide[:, pl.ds(pl.multiple_of(source * 256, 256), 256)] = total[:, s * 256 : (s + 1) * 256]
+    sources = [lax.rem(x + s, NX) for s in range(NX)]
+    for s in range(NX):
         for half in range(2):
             for h in range(2):
                 col, row = s * 2 + h, half * 8 + s * 2 + h
                 value = total[14 + half : 15 + half, col * 128 : (col + 1) * 128] + total[row : row + 1, tokens:]
-                narrow[pl.ds(half * 8 + source * 2 + h, 1), :] = value
+                narrow[pl.ds(half * 8 + sources[s] * 2 + h, 1), :] = value
+    spread[...] = jnp.broadcast_to(narrow[...].astype(BF16)[None], spread.shape)
+    first = pltpu.make_async_copy(spread, out_ref, sems.at[0])
+    first.start()
+    for s in range(NX):
+        there = pl.ds(pl.multiple_of(sources[s] * 256, 256), 256)
+        wide[:, there] = total[:, s * 256 : (s + 1) * 256]
     wide[14:15, :128] = lens_ref[...]
-    in_ref[...] = wide[...].astype(BF16)
-    out_ref[...] = jnp.broadcast_to(narrow[...].astype(BF16)[None], out_ref.shape)
+    rows_in[...] = wide[...].astype(BF16)
+    second = pltpu.make_async_copy(rows_in, in_ref, sems.at[1])
+    second.start()
+    first.wait()
+    second.wait()
 
 
 def documents(place, out_ref, in_ref, send_ref, keep_ref, rows_out):
@@ -225,9 +241,16 @@
     proj_in, proj_out = call(
         add_up,
         (jax.ShapeDtypeStruct((16, tokens), BF16), in_hbm((64, 16, 128))),
-        [pltpu.VMEM((16, tokens), F32), pltpu.VMEM((16, 128), F32)],
+        [
+            pltpu.VMEM((16, tokens), F32),
+            pltpu.VMEM((16, 128), F32),
+            pltpu.VMEM((16, tokens), BF16),
+            pltpu.VMEM((64, 16, 128), BF16),
+            pltpu.SemaphoreType.DMA((2,)),
+        ],
         (place, lens, in_vmem(parts)),
         32 * 16 * 1152,
+        out_spec=ANY,
     )
 
     proj_out = lax.all_to_all(proj_out, ("zl", "y", "core"), split_axis=0, concat_axis=0, tiled=True)

time: 118 us -> 118 us (level)
  no operation moved by 1% of the time
where the time goes in v13:
time: 118 us; the launch traced here: 117 us
  starting transfers between devices  57 us (48%)
  waiting for transfers between devices  32.6 us (28%)
  blocking collectives  17.9 us (15%)
  Pallas kernels  9.03 us (8%)
    all_to_all x1, waiting for transfers between devices, body(): lax.all_to_all(parts, ('zl', 'y'), split_axis=0, concat_axis=0, tiled=True)  27.9 us
    ppermute x7, starting transfers between devices, from_offset(): lax.ppermute(value, axis, [((i + offset) % size, i) for i in range(size)])  24.1 us
    all_to_all x1, starting transfers between devices, body(): lax.all_to_all(packed, ('zl', 'y'), split_axis=0, concat_axis=0, tiled=True)  13.5 us
    all_gather x1, blocking collectives, body(): proj_in = lax.all_gather(proj_in, 'x')  9.99 us
    all_to_all x1, starting transfers between devices, body(): lax.all_to_all(proj_out, ('zl', 'y', 'core'), split_axis=0, concat_axis=0...  9.87 us
    all_to_all x1, starting transfers between devices, body(): lax.all_to_all(parts, ('zl', 'y'), split_axis=0, concat_axis=0, tiled=True)  9.59 us
    pallas_call x4, Pallas kernels, call(): pl.pallas_call(kernel, out_shape=shapes, in_specs=in_specs or [SMEM] + [V...  9.03 us
    all_gather x1, blocking collectives, body(): both = lax.all_gather(send, 'zh')  7.94 us
  transfers between devices with their start and end apart: 10, of which 4 were waited for; matrix products, arithmetic and copies ran while one was open for 0% of the time, Pallas kernels for 0%

profile of v13, /device:TPU:1, one launch (start us, length us, event | category | flops | bytes accessed | tf_op | source)
XLA Modules:
  0.0 117.5 jit_solution(16844429991528450777)
XLA Ops:
  0.0 0.1 pad_add_fusion.place
  0.1 3.4 %shard_map.55 = (bf16[32,16,1024]{2,1,0:T(8,128)(2,1)}, bf16[576,256]{1,0:T(8,128)(2,1)S(1)}) custom-call(s32[3]{0:T(128)S(1)} %pad_add_fusion.place, bf16[56,28672]{1,0:T(8,128)(2,1)} %basis_ref.1, bf16[8,8192]{1,0:T(8,128)(2,1)} %out_rows_ref.1, bf16[448,256]{1,0:T(8,128)(2,1)} %bitcast.8, bf16[256,128]{1,0:T(8,128)(2,1)} %grads_ref.1), custom_call_target="tpu_custom_call" | custom-call | flops 1048576 | bytes 3637260 | tf_op jit(solution)/shard_map/pallas_call | solution.py:23
  3.4 13.5 %all-to-all-start = ((bf16[32,16,1024]{2,1,0:T(8,128)(2,1)}), bf16[32,16,1024]{2,1,0:T(8,128)(2,1)S(1)}, u32[]{:S(2)}, u32[]{:S(2)}) async-start(bf16[32,16,1024]{2,1,0:T(8,128)(2,1)} %get-tuple-element.11), calls=%async_computation | async-start | bytes 2097152 | tf_op jit(solution)/shard_map/all_to_all | solution.py:220
  16.9 4.4 %collective-permute-start = (bf16[576,256]{1,0:T(8,128)(2,1)S(1)}, bf16[576,256]{1,0:T(8,128)(2,1)S(1)}, u32[]{:S(2)}, u32[]{:S(2)}) collective-permute-start(bf16[576,256]{1,0:T(8,128)(2,1)S(1)} %get-tuple-element.12.refs_0_), channel_id=1, source_target_pairs={{128,0},{256,128},{384,256},{0,384},{129,1},{257,129},{385,257},{1... | collective-permute-start | bytes 884744 | tf_op jit(solution)/shard_map/ppermute | solution.py:18
  21.3 2.5 %collective-permute-start.1 = (bf16[576,256]{1,0:T(8,128)(2,1)S(1)}, bf16[576,256]{1,0:T(8,128)(2,1)S(1)}, u32[]{:S(2)}, u32[]{:S(2)}) collective-permute-start(bf16[576,256]{1,0:T(8,128)(2,1)S(1)} %get-tuple-element.12.refs_0_), channel_id=1, source_target_pairs={{256,0},{384,128},{0,256},{128,384},{257,1},{385,129},{1,257},{129... | collective-permute-start | bytes 884744 | tf_op jit(solution)/shard_map/ppermute | solution.py:18
  23.8 2.5 %collective-permute-start.2 = (bf16[576,256]{1,0:T(8,128)(2,1)S(1)}, bf16[576,256]{1,0:T(8,128)(2,1)S(1)}, u32[]{:S(2)}, u32[]{:S(2)}) collective-permute-start(bf16[576,256]{1,0:T(8,128)(2,1)S(1)} %get-tuple-element.12.refs_0_), channel_id=1, source_target_pairs={{384,0},{0,128},{128,256},{256,384},{385,1},{1,129},{129,257},{257... | collective-permute-start | bytes 884744 | tf_op jit(solution)/shard_map/ppermute | solution.py:18
  26.3 3.7 %collective-permute-start.3 = (bf16[576,256]{1,0:T(8,128)(2,1)S(1)}, bf16[576,256]{1,0:T(8,128)(2,1)S(1)}, u32[]{:S(2)}, u32[]{:S(2)}) collective-permute-start(bf16[576,256]{1,0:T(8,128)(2,1)S(1)} %get-tuple-element.12.refs_0_), channel_id=1, source_target_pairs={{1,0},{0,1},{3,2},{2,3},{5,4},{4,5},{7,6},{6,7},{9,8},{8,9},{11,10... | collective-permute-start | bytes 884744 | tf_op jit(solution)/shard_map/ppermute | solution.py:18
  30.0 0.0 collective-permute-done.refs_1_
  30.0 6.8 %collective-permute-start.4 = (bf16[576,256]{1,0:T(8,128)(2,1)S(1)}, bf16[576,256]{1,0:T(8,128)(2,1)S(1)}, u32[]{:S(2)}, u32[]{:S(2)}) collective-permute-start(bf16[576,256]{1,0:T(8,128)(2,1)S(1)} %collective-permute-done.refs_1_), channel_id=1, source_target_pairs={{1,0},{0,1},{3,2},{2,3},{5,4},{4,5},{7,6},{6,7},{9,8},{8,9},{11,10... | collective-permute-start | bytes 884744 | tf_op jit(solution)/shard_map/ppermute | solution.py:18
  36.8 0.0 collective-permute-done.1.refs_2_
  36.8 1.9 %collective-permute-start.5 = (bf16[576,256]{1,0:T(8,128)(2,1)S(1)}, bf16[576,256]{1,0:T(8,128)(2,1)S(1)}, u32[]{:S(2)}, u32[]{:S(2)}) collective-permute-start(bf16[576,256]{1,0:T(8,128)(2,1)S(1)} %collective-permute-done.1.refs_2_), channel_id=1, source_target_pairs={{1,0},{0,1},{3,2},{2,3},{5,4},{4,5},{7,6},{6,7},{9,8},{8,9},{11,10... | collective-permute-start | bytes 884744 | tf_op jit(solution)/shard_map/ppermute | solution.py:18
  38.7 1.3 %collective-permute-done.2.refs_3_ = bf16[576,256]{1,0:T(8,128)(2,1)S(1)} collective-permute-done((bf16[576,256]{1,0:T(8,128)(2,1)S(1)}, bf16[576,256]{1,0:T(8,128)(2,1)S(1)}, u32[]{:S(2)}, u32[]{:S(2)}) %collective-permute-start.2) | collective-permute-done | bytes 294944 | tf_op jit(solution)/shard_map/ppermute | solution.py:18
  40.0 2.4 %collective-permute-start.6 = (bf16[576,256]{1,0:T(8,128)(2,1)S(1)}, bf16[576,256]{1,0:T(8,128)(2,1)S(1)}, u32[]{:S(2)}, u32[]{:S(2)}) collective-permute-start(bf16[576,256]{1,0:T(8,128)(2,1)S(1)} %collective-permute-done.2.refs_3_), channel_id=1, source_target_pairs={{1,0},{0,1},{3,2},{2,3},{5,4},{4,5},{7,6},{6,7},{9,8},{8,9},{11,10... | collective-permute-start | bytes 884744 | tf_op jit(solution)/shard_map/ppermute | solution.py:18
  42.4 0.0 collective-permute-done.3.refs_4_
  42.4 0.0 collective-permute-done.4.refs_5_
  42.4 0.0 collective-permute-done.5.refs_6_
  42.4 1.2 collective-permute-done.6.refs_7_
  43.6 0.0 all-to-all-done.packed_ref
  43.6 3.1 %shard_map.56 = bf16[32,16,1152]{2,1,0:T(8,128)(2,1)} custom-call(s32[3]{0:T(128)S(1)} %pad_add_fusion.place, bf16[32,16,1024]{2,1,0:T(8,128)(2,1)S(1)} %all-to-all-done.packed_ref, bf16[576,256]{1,0:T(8,128)(2,1)S(1)} %get-tuple-element.12.refs_0_, bf16[576,256]{1,0:T(8,128)(2,1)S(1)} %collective-permute-done.refs_1_, ...), custom_call_target="tpu_custom_call" | custom-call | flops 1073741824 | bytes 3407884 | tf_op jit(solution)/shard_map/pallas_call | solution.py:23
  46.6 0.0 copy-start
  46.6 9.6 %all-to-all-start.1 = ((bf16[32,16,1152]{2,1,0:T(8,128)(2,1)}), bf16[32,16,1152]{2,1,0:T(8,128)(2,1)S(1)}, u32[]{:S(2)}, u32[]{:S(2)}) async-start(bf16[32,16,1152]{2,1,0:T(8,128)(2,1)} %shard_map.56), calls=%async_computation.1 | async-start | bytes 2359296 | tf_op jit(solution)/shard_map/all_to_all | solution.py:239
  56.2 0.0 copy-done
  56.3 27.9 %all-to-all-done.1.parts_ref = bf16[32,16,1152]{2,1,0:T(8,128)(2,1)S(1)} async-done(((bf16[32,16,1152]{2,1,0:T(8,128)(2,1)}), bf16[32,16,1152]{2,1,0:T(8,128)(2,1)S(1)}, u32[]{:S(2)}, u32[]{:S(2)}) %all-to-all-start.1) | async-done | bytes 1179680 | tf_op jit(solution)/shard_map/all_to_all | solution.py:239
  84.2 1.4 %shard_map.57 = (bf16[16,1024]{1,0:T(8,128)(2,1)S(1)}, bf16[64,16,128]{2,1,0:T(8,128)(2,1)}) custom-call(s32[3]{0:T(128)S(1)} %pad_add_fusion.place, f32[1,128]{1,0:T(1,128)S(1)} %pad.4.lens_ref, bf16[32,16,1152]{2,1,0:T(8,128)(2,1)S(1)} %all-to-all-done.1.parts_ref), custom_call_target="tpu_custom_call" | custom-call | flops 589824 | bytes 1180172 | tf_op jit(solution)/shard_map/pallas_call | solution.py:23
  85.6 9.9 %all-to-all-start.2 = ((bf16[64,16,128]{2,1,0:T(8,128)(2,1)}), bf16[64,16,128]{2,1,0:T(8,128)(2,1)S(1)}, u32[]{:S(2)}, u32[]{:S(2)}) async-start(bf16[64,16,128]{2,1,0:T(8,128)(2,1)} %get-tuple-element.13), calls=%async_computation.2 | async-start | bytes 524288 | tf_op jit(solution)/shard_map/all_to_all | solution.py:256
  95.5 10.0 %all-gather = bf16[64,1024]{1,0:T(8,128)(2,1)S(1)} all-gather(bf16[16,1024]{1,0:T(8,128)(2,1)S(1)} %get-tuple-element.14), channel_id=2, replica_groups=mesh['x'=4,'zh'=2,'zl'=4,'y'=8,'core'=2] {'x'}, dimensions={0}, use_global_device_ids=true | all-gather | bytes 163840 | tf_op jit(solution)/shard_map/all_gather | solution.py:257
  105.5 2.3 %all-to-all-done.2.out_ref = bf16[64,16,128]{2,1,0:T(8,128)(2,1)S(1)} async-done(((bf16[64,16,128]{2,1,0:T(8,128)(2,1)}), bf16[64,16,128]{2,1,0:T(8,128)(2,1)S(1)}, u32[]{:S(2)}, u32[]{:S(2)}) %all-to-all-start.2) | async-done | bytes 262176 | tf_op jit(solution)/shard_map/all_to_all | solution.py:256
  107.8 1.2 shard_map.58
  108.9 7.9 %all-gather.1 = f32[112,64]{1,0:T(8,128)S(1)} all-gather(f32[56,64]{1,0:T(8,128)S(1)} %get-tuple-element.16), channel_id=3, replica_groups=mesh['x'=4,'zh'=2,'zl'=4,'y'=8,'core'=2] {'zh'}, dimensions={0}, use_global_device_ids=true | all-gather | bytes 43008 | tf_op jit(solution)/shard_map/all_gather | solution.py:266
  116.9 0.6 fusion.1
  (2 shorter events, 0.0 us)
Async XLA Ops:
  3.4 40.1 %all-to-all-start = ((bf16[32,16,1024]{2,1,0:T(8,128)(2,1)}), bf16[32,16,1024]{2,1,0:T(8,128)(2,1)S(1)}, u32[]{:S(2)}, u32[]{:S(2)}) async-start(bf16[32,16,1024]{2,1,0:T(8,128)(2,1)} %get-tuple-element.11), calls=%async_computation | async-start | bytes 2097152 | tf_op jit(solution)/shard_map/all_to_all | solution.py:220
  16.9 13.1 %collective-permute-start = (bf16[576,256]{1,0:T(8,128)(2,1)S(1)}, bf16[576,256]{1,0:T(8,128)(2,1)S(1)}, u32[]{:S(2)}, u32[]{:S(2)}) collective-permute-start(bf16[576,256]{1,0:T(8,128)(2,1)S(1)} %get-tuple-element.12.refs_0_), channel_id=1, source_target_pairs={{128,0},{256,128},{384,256},{0,384},{129,1},{257,129},{385,257},{1... | collective-permute-start | bytes 884744 | tf_op jit(solution)/shard_map/ppermute | solution.py:18
  21.3 15.5 %collective-permute-start.1 = (bf16[576,256]{1,0:T(8,128)(2,1)S(1)}, bf16[576,256]{1,0:T(8,128)(2,1)S(1)}, u32[]{:S(2)}, u32[]{:S(2)}) collective-permute-start(bf16[576,256]{1,0:T(8,128)(2,1)S(1)} %get-tuple-element.12.refs_0_), channel_id=1, source_target_pairs={{256,0},{384,128},{0,256},{128,384},{257,1},{385,129},{1,257},{129... | collective-permute-start | bytes 884744 | tf_op jit(solution)/shard_map/ppermute | solution.py:18
  23.8 16.2 %collective-permute-start.2 = (bf16[576,256]{1,0:T(8,128)(2,1)S(1)}, bf16[576,256]{1,0:T(8,128)(2,1)S(1)}, u32[]{:S(2)}, u32[]{:S(2)}) collective-permute-start(bf16[576,256]{1,0:T(8,128)(2,1)S(1)} %get-tuple-element.12.refs_0_), channel_id=1, source_target_pairs={{384,0},{0,128},{128,256},{256,384},{385,1},{1,129},{129,257},{257... | collective-permute-start | bytes 884744 | tf_op jit(solution)/shard_map/ppermute | solution.py:18
  26.3 16.1 %collective-permute-start.3 = (bf16[576,256]{1,0:T(8,128)(2,1)S(1)}, bf16[576,256]{1,0:T(8,128)(2,1)S(1)}, u32[]{:S(2)}, u32[]{:S(2)}) collective-permute-start(bf16[576,256]{1,0:T(8,128)(2,1)S(1)} %get-tuple-element.12.refs_0_), channel_id=1, source_target_pairs={{1,0},{0,1},{3,2},{2,3},{5,4},{4,5},{7,6},{6,7},{9,8},{8,9},{11,10... | collective-permute-start | bytes 884744 | tf_op jit(solution)/shard_map/ppermute | solution.py:18
  30.0 12.4 %collective-permute-start.4 = (bf16[576,256]{1,0:T(8,128)(2,1)S(1)}, bf16[576,256]{1,0:T(8,128)(2,1)S(1)}, u32[]{:S(2)}, u32[]{:S(2)}) collective-permute-start(bf16[576,256]{1,0:T(8,128)(2,1)S(1)} %collective-permute-done.refs_1_), channel_id=1, source_target_pairs={{1,0},{0,1},{3,2},{2,3},{5,4},{4,5},{7,6},{6,7},{9,8},{8,9},{11,10... | collective-permute-start | bytes 884744 | tf_op jit(solution)/shard_map/ppermute | solution.py:18
  36.8 5.6 %collective-permute-start.5 = (bf16[576,256]{1,0:T(8,128)(2,1)S(1)}, bf16[576,256]{1,0:T(8,128)(2,1)S(1)}, u32[]{:S(2)}, u32[]{:S(2)}) collective-permute-start(bf16[576,256]{1,0:T(8,128)(2,1)S(1)} %collective-permute-done.1.refs_2_), channel_id=1, source_target_pairs={{1,0},{0,1},{3,2},{2,3},{5,4},{4,5},{7,6},{6,7},{9,8},{8,9},{11,10... | collective-permute-start | bytes 884744 | tf_op jit(solution)/shard_map/ppermute | solution.py:18
  40.0 3.6 %collective-permute-start.6 = (bf16[576,256]{1,0:T(8,128)(2,1)S(1)}, bf16[576,256]{1,0:T(8,128)(2,1)S(1)}, u32[]{:S(2)}, u32[]{:S(2)}) collective-permute-start(bf16[576,256]{1,0:T(8,128)(2,1)S(1)} %collective-permute-done.2.refs_3_), channel_id=1, source_target_pairs={{1,0},{0,1},{3,2},{2,3},{5,4},{4,5},{7,6},{6,7},{9,8},{8,9},{11,10... | collective-permute-start | bytes 884744 | tf_op jit(solution)/shard_map/ppermute | solution.py:18
  46.6 9.6 %copy-start = (s32[1,4]{1,0:T(1,128)S(1)}, s32[1,4]{1,0:T(1,128)}, u32[]{:S(2)}) copy-start(s32[1,4]{1,0:T(1,128)} %param.9) | copy-start | bytes 52
  46.6 37.5 %all-to-all-start.1 = ((bf16[32,16,1152]{2,1,0:T(8,128)(2,1)}), bf16[32,16,1152]{2,1,0:T(8,128)(2,1)S(1)}, u32[]{:S(2)}, u32[]{:S(2)}) async-start(bf16[32,16,1152]{2,1,0:T(8,128)(2,1)} %shard_map.56), calls=%async_computation.1 | async-start | bytes 2359296 | tf_op jit(solution)/shard_map/all_to_all | solution.py:239
  85.6 22.2 %all-to-all-start.2 = ((bf16[64,16,128]{2,1,0:T(8,128)(2,1)}), bf16[64,16,128]{2,1,0:T(8,128)(2,1)S(1)}, u32[]{:S(2)}, u32[]{:S(2)}) async-start(bf16[64,16,128]{2,1,0:T(8,128)(2,1)} %get-tuple-element.13), calls=%async_computation.2 | async-start | bytes 524288 | tf_op jit(solution)/shard_map/all_to_all | solution.py:256

commit v14 on v12

--- a/solution.py
+++ b/solution.py
@@ -7,7 +7,7 @@
 
 NX, NZH, NZL, NY, NC = 4, 2, 4, 8, 2
 CHIPS = NZL * NY
-PARTS = 8
+PARTS = 16
 BF16, F32 = jnp.bfloat16, jnp.float32
 SMEM = pl.BlockSpec(memory_space=pltpu.SMEM)
 VMEM = pl.BlockSpec(memory_space=pltpu.VMEM)

time: 118 us -> 118 us (level)
  no operation moved by 1% of the time
where the time goes in v14:
time: 118 us
  starting transfers between devices  57.1 us (48%)
  waiting for transfers between devices  32.5 us (28%)
  blocking collectives  17.9 us (15%)
  Pallas kernels  9.11 us (8%)
    all_to_all x1, waiting for transfers between devices, body(): lax.all_to_all(parts, ('zl', 'y'), split_axis=0, concat_axis=0, tiled=True)  27.8 us
    ppermute x7, starting transfers between devices, from_offset(): lax.ppermute(value, axis, [((i + offset) % size, i) for i in range(size)])  24.1 us
    all_to_all x1, starting transfers between devices, body(): lax.all_to_all(packed, ('zl', 'y'), split_axis=0, concat_axis=0, tiled=True)  13.5 us
    all_gather x1, blocking collectives, body(): proj_in = lax.all_gather(proj_in, 'x')  9.99 us
    all_to_all x1, starting transfers between devices, body(): lax.all_to_all(proj_out, ('zl', 'y', 'core'), split_axis=0, concat_axis=0...  9.92 us
    all_to_all x1, starting transfers between devices, body(): lax.all_to_all(parts, ('zl', 'y'), split_axis=0, concat_axis=0, tiled=True)  9.58 us
    pallas_call x4, Pallas kernels, call(): pl.pallas_call(kernel, out_shape=shapes, in_specs=in_specs or [SMEM] + [V...  9.11 us
    all_gather x1, blocking collectives, body(): both = lax.all_gather(send, 'zh')  7.93 us
  transfers between devices with their start and end apart: 10, of which 4 were waited for; matrix products, arithmetic and copies ran while one was open for 0% of the time, Pallas kernels for 0%

profile of v14, /device:TPU:1, one launch (start us, length us, event | category | flops | bytes accessed | tf_op | source)
XLA Modules:
  0.0 117.6 jit_solution(9080146704069738613)
XLA Ops:
  0.0 0.1 pad_add_fusion.place
  0.1 3.5 %shard_map.55 = (bf16[32,16,1024]{2,1,0:T(8,128)(2,1)}, bf16[576,256]{1,0:T(8,128)(2,1)S(1)}) custom-call(s32[3]{0:T(128)S(1)} %pad_add_fusion.place, bf16[56,28672]{1,0:T(8,128)(2,1)} %basis_ref.1, bf16[8,8192]{1,0:T(8,128)(2,1)} %out_rows_ref.1, bf16[448,256]{1,0:T(8,128)(2,1)} %bitcast.8, bf16[256,128]{1,0:T(8,128)(2,1)} %grads_ref.1), custom_call_target="tpu_custom_call" | custom-call | flops 1048576 | bytes 3637260 | tf_op jit(solution)/shard_map/pallas_call | solution.py:23
  3.6 13.5 %all-to-all-start = ((bf16[32,16,1024]{2,1,0:T(8,128)(2,1)}), bf16[32,16,1024]{2,1,0:T(8,128)(2,1)S(1)}, u32[]{:S(2)}, u32[]{:S(2)}) async-start(bf16[32,16,1024]{2,1,0:T(8,128)(2,1)} %get-tuple-element.11), calls=%async_computation | async-start | bytes 2097152 | tf_op jit(solution)/shard_map/all_to_all | solution.py:204
  17.1 4.4 %collective-permute-start = (bf16[576,256]{1,0:T(8,128)(2,1)S(1)}, bf16[576,256]{1,0:T(8,128)(2,1)S(1)}, u32[]{:S(2)}, u32[]{:S(2)}) collective-permute-start(bf16[576,256]{1,0:T(8,128)(2,1)S(1)} %get-tuple-element.12.refs_0_), channel_id=1, source_target_pairs={{128,0},{256,128},{384,256},{0,384},{129,1},{257,129},{385,257},{1... | collective-permute-start | bytes 884744 | tf_op jit(solution)/shard_map/ppermute | solution.py:18
  21.5 2.4 %collective-permute-start.1 = (bf16[576,256]{1,0:T(8,128)(2,1)S(1)}, bf16[576,256]{1,0:T(8,128)(2,1)S(1)}, u32[]{:S(2)}, u32[]{:S(2)}) collective-permute-start(bf16[576,256]{1,0:T(8,128)(2,1)S(1)} %get-tuple-element.12.refs_0_), channel_id=1, source_target_pairs={{256,0},{384,128},{0,256},{128,384},{257,1},{385,129},{1,257},{129... | collective-permute-start | bytes 884744 | tf_op jit(solution)/shard_map/ppermute | solution.py:18
  23.9 2.5 %collective-permute-start.2 = (bf16[576,256]{1,0:T(8,128)(2,1)S(1)}, bf16[576,256]{1,0:T(8,128)(2,1)S(1)}, u32[]{:S(2)}, u32[]{:S(2)}) collective-permute-start(bf16[576,256]{1,0:T(8,128)(2,1)S(1)} %get-tuple-element.12.refs_0_), channel_id=1, source_target_pairs={{384,0},{0,128},{128,256},{256,384},{385,1},{1,129},{129,257},{257... | collective-permute-start | bytes 884744 | tf_op jit(solution)/shard_map/ppermute | solution.py:18
  26.5 3.7 %collective-permute-start.3 = (bf16[576,256]{1,0:T(8,128)(2,1)S(1)}, bf16[576,256]{1,0:T(8,128)(2,1)S(1)}, u32[]{:S(2)}, u32[]{:S(2)}) collective-permute-start(bf16[576,256]{1,0:T(8,128)(2,1)S(1)} %get-tuple-element.12.refs_0_), channel_id=1, source_target_pairs={{1,0},{0,1},{3,2},{2,3},{5,4},{4,5},{7,6},{6,7},{9,8},{8,9},{11,10... | collective-permute-start | bytes 884744 | tf_op jit(solution)/shard_map/ppermute | solution.py:18
  30.2 0.0 collective-permute-done.refs_1_
  30.2 6.8 %collective-permute-start.4 = (bf16[576,256]{1,0:T(8,128)(2,1)S(1)}, bf16[576,256]{1,0:T(8,128)(2,1)S(1)}, u32[]{:S(2)}, u32[]{:S(2)}) collective-permute-start(bf16[576,256]{1,0:T(8,128)(2,1)S(1)} %collective-permute-done.refs_1_), channel_id=1, source_target_pairs={{1,0},{0,1},{3,2},{2,3},{5,4},{4,5},{7,6},{6,7},{9,8},{8,9},{11,10... | collective-permute-start | bytes 884744 | tf_op jit(solution)/shard_map/ppermute | solution.py:18
  36.9 0.0 collective-permute-done.1.refs_2_
  37.0 1.9 %collective-permute-start.5 = (bf16[576,256]{1,0:T(8,128)(2,1)S(1)}, bf16[576,256]{1,0:T(8,128)(2,1)S(1)}, u32[]{:S(2)}, u32[]{:S(2)}) collective-permute-start(bf16[576,256]{1,0:T(8,128)(2,1)S(1)} %collective-permute-done.1.refs_2_), channel_id=1, source_target_pairs={{1,0},{0,1},{3,2},{2,3},{5,4},{4,5},{7,6},{6,7},{9,8},{8,9},{11,10... | collective-permute-start | bytes 884744 | tf_op jit(solution)/shard_map/ppermute | solution.py:18
  38.9 1.3 %collective-permute-done.2.refs_3_ = bf16[576,256]{1,0:T(8,128)(2,1)S(1)} collective-permute-done((bf16[576,256]{1,0:T(8,128)(2,1)S(1)}, bf16[576,256]{1,0:T(8,128)(2,1)S(1)}, u32[]{:S(2)}, u32[]{:S(2)}) %collective-permute-start.2) | collective-permute-done | bytes 294944 | tf_op jit(solution)/shard_map/ppermute | solution.py:18
  40.1 2.4 %collective-permute-start.6 = (bf16[576,256]{1,0:T(8,128)(2,1)S(1)}, bf16[576,256]{1,0:T(8,128)(2,1)S(1)}, u32[]{:S(2)}, u32[]{:S(2)}) collective-permute-start(bf16[576,256]{1,0:T(8,128)(2,1)S(1)} %collective-permute-done.2.refs_3_), channel_id=1, source_target_pairs={{1,0},{0,1},{3,2},{2,3},{5,4},{4,5},{7,6},{6,7},{9,8},{8,9},{11,10... | collective-permute-start | bytes 884744 | tf_op jit(solution)/shard_map/ppermute | solution.py:18
  42.5 0.0 collective-permute-done.3.refs_4_
  42.5 0.0 collective-permute-done.4.refs_5_
  42.6 0.0 collective-permute-done.5.refs_6_
  42.6 1.2 collective-permute-done.6.refs_7_
  43.7 0.0 all-to-all-done.packed_ref
  43.7 3.0 %shard_map.56 = bf16[32,16,1152]{2,1,0:T(8,128)(2,1)} custom-call(s32[3]{0:T(128)S(1)} %pad_add_fusion.place, bf16[32,16,1024]{2,1,0:T(8,128)(2,1)S(1)} %all-to-all-done.packed_ref, bf16[576,256]{1,0:T(8,128)(2,1)S(1)} %get-tuple-element.12.refs_0_, bf16[576,256]{1,0:T(8,128)(2,1)S(1)} %collective-permute-done.refs_1_, ...), custom_call_target="tpu_custom_call" | custom-call | flops 1073741824 | bytes 3407884 | tf_op jit(solution)/shard_map/pallas_call | solution.py:23
  46.7 0.0 copy-start
  46.8 9.6 %all-to-all-start.1 = ((bf16[32,16,1152]{2,1,0:T(8,128)(2,1)}), bf16[32,16,1152]{2,1,0:T(8,128)(2,1)S(1)}, u32[]{:S(2)}, u32[]{:S(2)}) async-start(bf16[32,16,1152]{2,1,0:T(8,128)(2,1)} %shard_map.56), calls=%async_computation.1 | async-start | bytes 2359296 | tf_op jit(solution)/shard_map/all_to_all | solution.py:223
  56.3 0.0 copy-done
  56.4 27.8 %all-to-all-done.1.parts_ref = bf16[32,16,1152]{2,1,0:T(8,128)(2,1)S(1)} async-done(((bf16[32,16,1152]{2,1,0:T(8,128)(2,1)}), bf16[32,16,1152]{2,1,0:T(8,128)(2,1)S(1)}, u32[]{:S(2)}, u32[]{:S(2)}) %all-to-all-start.1) | async-done | bytes 1179680 | tf_op jit(solution)/shard_map/all_to_all | solution.py:223
  84.2 1.4 %shard_map.57 = (bf16[16,1024]{1,0:T(8,128)(2,1)S(1)}, bf16[64,16,128]{2,1,0:T(8,128)(2,1)}) custom-call(s32[3]{0:T(128)S(1)} %pad_add_fusion.place, f32[1,128]{1,0:T(1,128)S(1)} %pad.4.lens_ref, bf16[32,16,1152]{2,1,0:T(8,128)(2,1)S(1)} %all-to-all-done.1.parts_ref), custom_call_target="tpu_custom_call" | custom-call | flops 589824 | bytes 1180172 | tf_op jit(solution)/shard_map/pallas_call | solution.py:23
  85.6 9.9 %all-to-all-start.2 = ((bf16[64,16,128]{2,1,0:T(8,128)(2,1)}), bf16[64,16,128]{2,1,0:T(8,128)(2,1)S(1)}, u32[]{:S(2)}, u32[]{:S(2)}) async-start(bf16[64,16,128]{2,1,0:T(8,128)(2,1)} %get-tuple-element.13), calls=%async_computation.2 | async-start | bytes 524288 | tf_op jit(solution)/shard_map/all_to_all | solution.py:233
  95.6 10.0 %all-gather = bf16[64,1024]{1,0:T(8,128)(2,1)S(1)} all-gather(bf16[16,1024]{1,0:T(8,128)(2,1)S(1)} %get-tuple-element.14), channel_id=2, replica_groups=mesh['x'=4,'zh'=2,'zl'=4,'y'=8,'core'=2] {'x'}, dimensions={0}, use_global_device_ids=true | all-gather | bytes 163840 | tf_op jit(solution)/shard_map/all_gather | solution.py:234
  105.6 2.3 %all-to-all-done.2.out_ref = bf16[64,16,128]{2,1,0:T(8,128)(2,1)S(1)} async-done(((bf16[64,16,128]{2,1,0:T(8,128)(2,1)}), bf16[64,16,128]{2,1,0:T(8,128)(2,1)S(1)}, u32[]{:S(2)}, u32[]{:S(2)}) %all-to-all-start.2) | async-done | bytes 262176 | tf_op jit(solution)/shard_map/all_to_all | solution.py:233
  107.8 1.2 shard_map.58
  109.0 7.9 %all-gather.1 = f32[112,64]{1,0:T(8,128)S(1)} all-gather(f32[56,64]{1,0:T(8,128)S(1)} %get-tuple-element.16), channel_id=3, replica_groups=mesh['x'=4,'zh'=2,'zl'=4,'y'=8,'core'=2] {'zh'}, dimensions={0}, use_global_device_ids=true | all-gather | bytes 43008 | tf_op jit(solution)/shard_map/all_gather | solution.py:243
  116.9 0.6 fusion.1
  (2 shorter events, 0.0 us)
Async XLA Ops:
  3.6 40.1 %all-to-all-start = ((bf16[32,16,1024]{2,1,0:T(8,128)(2,1)}), bf16[32,16,1024]{2,1,0:T(8,128)(2,1)S(1)}, u32[]{:S(2)}, u32[]{:S(2)}) async-start(bf16[32,16,1024]{2,1,0:T(8,128)(2,1)} %get-tuple-element.11), calls=%async_computation | async-start | bytes 2097152 | tf_op jit(solution)/shard_map/all_to_all | solution.py:204
  17.1 13.1 %collective-permute-start = (bf16[576,256]{1,0:T(8,128)(2,1)S(1)}, bf16[576,256]{1,0:T(8,128)(2,1)S(1)}, u32[]{:S(2)}, u32[]{:S(2)}) collective-permute-start(bf16[576,256]{1,0:T(8,128)(2,1)S(1)} %get-tuple-element.12.refs_0_), channel_id=1, source_target_pairs={{128,0},{256,128},{384,256},{0,384},{129,1},{257,129},{385,257},{1... | collective-permute-start | bytes 884744 | tf_op jit(solution)/shard_map/ppermute | solution.py:18
  21.5 15.5 %collective-permute-start.1 = (bf16[576,256]{1,0:T(8,128)(2,1)S(1)}, bf16[576,256]{1,0:T(8,128)(2,1)S(1)}, u32[]{:S(2)}, u32[]{:S(2)}) collective-permute-start(bf16[576,256]{1,0:T(8,128)(2,1)S(1)} %get-tuple-element.12.refs_0_), channel_id=1, source_target_pairs={{256,0},{384,128},{0,256},{128,384},{257,1},{385,129},{1,257},{129... | collective-permute-start | bytes 884744 | tf_op jit(solution)/shard_map/ppermute | solution.py:18
  23.9 16.2 %collective-permute-start.2 = (bf16[576,256]{1,0:T(8,128)(2,1)S(1)}, bf16[576,256]{1,0:T(8,128)(2,1)S(1)}, u32[]{:S(2)}, u32[]{:S(2)}) collective-permute-start(bf16[576,256]{1,0:T(8,128)(2,1)S(1)} %get-tuple-element.12.refs_0_), channel_id=1, source_target_pairs={{384,0},{0,128},{128,256},{256,384},{385,1},{1,129},{129,257},{257... | collective-permute-start | bytes 884744 | tf_op jit(solution)/shard_map/ppermute | solution.py:18
  26.5 16.1 %collective-permute-start.3 = (bf16[576,256]{1,0:T(8,128)(2,1)S(1)}, bf16[576,256]{1,0:T(8,128)(2,1)S(1)}, u32[]{:S(2)}, u32[]{:S(2)}) collective-permute-start(bf16[576,256]{1,0:T(8,128)(2,1)S(1)} %get-tuple-element.12.refs_0_), channel_id=1, source_target_pairs={{1,0},{0,1},{3,2},{2,3},{5,4},{4,5},{7,6},{6,7},{9,8},{8,9},{11,10... | collective-permute-start | bytes 884744 | tf_op jit(solution)/shard_map/ppermute | solution.py:18
  30.2 12.4 %collective-permute-start.4 = (bf16[576,256]{1,0:T(8,128)(2,1)S(1)}, bf16[576,256]{1,0:T(8,128)(2,1)S(1)}, u32[]{:S(2)}, u32[]{:S(2)}) collective-permute-start(bf16[576,256]{1,0:T(8,128)(2,1)S(1)} %collective-permute-done.refs_1_), channel_id=1, source_target_pairs={{1,0},{0,1},{3,2},{2,3},{5,4},{4,5},{7,6},{6,7},{9,8},{8,9},{11,10... | collective-permute-start | bytes 884744 | tf_op jit(solution)/shard_map/ppermute | solution.py:18
  37.0 5.6 %collective-permute-start.5 = (bf16[576,256]{1,0:T(8,128)(2,1)S(1)}, bf16[576,256]{1,0:T(8,128)(2,1)S(1)}, u32[]{:S(2)}, u32[]{:S(2)}) collective-permute-start(bf16[576,256]{1,0:T(8,128)(2,1)S(1)} %collective-permute-done.1.refs_2_), channel_id=1, source_target_pairs={{1,0},{0,1},{3,2},{2,3},{5,4},{4,5},{7,6},{6,7},{9,8},{8,9},{11,10... | collective-permute-start | bytes 884744 | tf_op jit(solution)/shard_map/ppermute | solution.py:18
  40.1 3.6 %collective-permute-start.6 = (bf16[576,256]{1,0:T(8,128)(2,1)S(1)}, bf16[576,256]{1,0:T(8,128)(2,1)S(1)}, u32[]{:S(2)}, u32[]{:S(2)}) collective-permute-start(bf16[576,256]{1,0:T(8,128)(2,1)S(1)} %collective-permute-done.2.refs_3_), channel_id=1, source_target_pairs={{1,0},{0,1},{3,2},{2,3},{5,4},{4,5},{7,6},{6,7},{9,8},{8,9},{11,10... | collective-permute-start | bytes 884744 | tf_op jit(solution)/shard_map/ppermute | solution.py:18
  46.7 9.6 %copy-start = (s32[1,4]{1,0:T(1,128)S(1)}, s32[1,4]{1,0:T(1,128)}, u32[]{:S(2)}) copy-start(s32[1,4]{1,0:T(1,128)} %param.9) | copy-start | bytes 52
  46.8 37.5 %all-to-all-start.1 = ((bf16[32,16,1152]{2,1,0:T(8,128)(2,1)}), bf16[32,16,1152]{2,1,0:T(8,128)(2,1)S(1)}, u32[]{:S(2)}, u32[]{:S(2)}) async-start(bf16[32,16,1152]{2,1,0:T(8,128)(2,1)} %shard_map.56), calls=%async_computation.1 | async-start | bytes 2359296 | tf_op jit(solution)/shard_map/all_to_all | solution.py:223
  85.6 22.2 %all-to-all-start.2 = ((bf16[64,16,128]{2,1,0:T(8,128)(2,1)}), bf16[64,16,128]{2,1,0:T(8,128)(2,1)S(1)}, u32[]{:S(2)}, u32[]{:S(2)}) async-start(bf16[64,16,128]{2,1,0:T(8,128)(2,1)} %get-tuple-element.13), calls=%async_computation.2 | async-start | bytes 524288 | tf_op jit(solution)/shard_map/all_to_all | solution.py:233
